TPU v7x, 32 devices: a whole 2x2x4 slice. The times are simulated.
32 devices in a mesh: section: 2 (over core), space: 16 (over z, y, x).
Axes of the slice: x: 2, y: 2, z: 4, core: 2. Of those that a mesh axis runs over, the one named last changes fastest.
Arguments:
- fwd_in: bfloat16 [2, 64, 8, 8, 256], P('section', 'space'), may hold values from -6 to 6
- bwd_act: bfloat16 [2, 64, 8, 8, 256], P('section', 'space'), may hold values from -6 to 6
- bwd_grad: bfloat16 [2, 64, 8, 8, 256], P('section', 'space'), may hold values from -6 to 6
- fresh: bfloat16 [64, 8, 8, 256], P('space'), may hold values from -6 to 6
- target: bfloat16 [64, 8, 8, 256], P('space'), may hold values from -6 to 6
- w_first: bfloat16 [2, 27, 128, 128], P('section'), may hold values from -0.109375 to 0.109375
- w_second: bfloat16 [2, 27, 128, 128], P('section'), may hold values from -0.109375 to 0.109375
Outputs:
- fwd_out: bfloat16 [2, 64, 8, 8, 256], P('section', 'space')
- back_act: bfloat16 [2, 64, 8, 8, 256], P('section', 'space')
- back_grad: bfloat16 [2, 64, 8, 8, 256], P('section', 'space')
- grad_first: float32 [2, 3456, 128], P('section', 'space')
- grad_second: float32 [2, 3456, 128], P('section', 'space')
All inputs are finite; a program needn't handle non-finite values.
Results may differ from a plain program's by a relative error of at most 0.01.
Values may be sent and summed in bfloat16 or wider, within the bound.
No kernel may reach another device: no remote copies, remote signals or barrier semaphores. Data moves between devices by JAX's collectives and lax.ppermute only.
A program may use at most 64 MiB of HBM per device.

v0:
```python
import math

import jax
import jax.numpy as jnp
from jax import lax
from jax.sharding import PartitionSpec as P


def extended(block, sides, width):
    for axis, dim in sides:
        count = lax.axis_size(axis)
        forward = [(i, i + 1) for i in range(count - 1)]
        backward = [(target, source) for source, target in forward]
        low = lax.ppermute(
            lax.slice_in_dim(block, block.shape[dim] - width, None, axis=dim), axis, forward
        )
        high = lax.ppermute(lax.slice_in_dim(block, 0, width, axis=dim), axis, backward)
        block = jnp.concatenate([low, block, high], axis=dim)
    return block


def from_behind(block, axis, distance):
    devices = range(lax.axis_size(axis))
    route = [(i - distance, i) for i in devices if i - distance in devices]
    return lax.ppermute(block, axis, route)


def smooth_gate(value):
    return 0.5 * value * (1.0 + jax.scipy.special.erf(value * 0.7071067811865476))


def gate_slope(value):
    return (
        0.5 * (1.0 + jax.scipy.special.erf(value * 0.7071067811865476))
        + value * jnp.exp(-0.5 * value * value) * 0.3989422804014327
    )


def pad_sides(field):
    return jnp.pad(field, ((0, 0), (1, 1), (1, 1), (0, 0)))


def joint_extend(fields):
    width = fields[0].shape[-1]
    merged = extended(jnp.concatenate(fields, axis=-1), (("space", 0),), 1)
    padded = pad_sides(merged)
    return tuple((padded[..., index * width : (index + 1) * width] for index in range(len(fields))))


def depth_stack(padded):
    depth = padded.shape[2] - 2
    return jnp.concatenate([padded[:, :, shift : shift + depth, :] for shift in range(3)], axis=-1)


def convolve(padded, weights):
    rows_x = padded.shape[0] - 2
    rows_y = padded.shape[1] - 2
    depth = padded.shape[2] - 2
    width = weights.shape[2]
    stacked = depth_stack(padded)
    wide = weights.reshape(9, 3 * weights.shape[1], width)
    total = jnp.zeros((rows_x * rows_y * depth, width), jnp.float32)
    for across in range(3):
        for down in range(3):
            block = stacked[across : across + rows_x, down : down + rows_y].reshape(
                -1, stacked.shape[-1]
            )
            total = total + jnp.dot(
                block, wide[across * 3 + down], preferred_element_type=jnp.float32
            )
    return total.reshape(rows_x, rows_y, depth, width)


def correlate(padded, incoming):
    rows_x = padded.shape[0] - 2
    rows_y = padded.shape[1] - 2
    stacked = depth_stack(padded)
    flat = incoming.reshape(-1, incoming.shape[-1])
    blocks = []
    for across in range(3):
        for down in range(3):
            block = stacked[across : across + rows_x, down : down + rows_y].reshape(
                -1, stacked.shape[-1]
            )
            blocks.append(
                lax.dot_general(
                    block, flat, (((0,), (0,)), ((), ())), preferred_element_type=jnp.float32
                )
            )
    return jnp.concatenate(blocks, axis=0)


def shards(fwd_in, bwd_act, bwd_grad, fresh, target, w_first, w_second):
    width = w_first.shape[2]
    first = w_first[0]
    second = w_second[0]
    first_back = jnp.transpose(first[::-1], (0, 2, 1))
    second_back = jnp.transpose(second[::-1], (0, 2, 1))
    last_section = lax.axis_size("section") - 1
    place = lax.axis_index("section")

    def tick(state, act, grad):
        x_one = state[..., :width].astype(jnp.float32)
        x_two = state[..., width:].astype(jnp.float32)
        y_one = act[..., :width].astype(jnp.float32)
        y_two = act[..., width:].astype(jnp.float32)
        d_one = grad[..., :width].astype(jnp.float32)
        d_two = grad[..., width:]
        h_in = smooth_gate(x_two).astype(jnp.bfloat16)
        g_out = smooth_gate(y_one).astype(jnp.bfloat16)
        h_pad, g_pad, d_pad = joint_extend((h_in, g_out, d_two))
        new_one = (x_one + convolve(h_pad, first)).astype(jnp.bfloat16)
        back_two = (y_two - convolve(g_pad, second)).astype(jnp.bfloat16)
        carry_one = (d_one + gate_slope(y_one) * convolve(d_pad, second_back)).astype(jnp.bfloat16)
        h_mid = smooth_gate(new_one.astype(jnp.float32)).astype(jnp.bfloat16)
        g_back = smooth_gate(back_two.astype(jnp.float32)).astype(jnp.bfloat16)
        m_pad, b_pad, c_pad = joint_extend((h_mid, g_back, carry_one))
        new_two = (x_two + convolve(m_pad, second)).astype(jnp.bfloat16)
        back_one = (y_one - convolve(b_pad, first)).astype(jnp.bfloat16)
        carry_two = (
            d_two.astype(jnp.float32)
            + gate_slope(back_two.astype(jnp.float32)) * convolve(c_pad, first_back)
        ).astype(jnp.bfloat16)
        forward = jnp.concatenate([new_one, new_two], axis=-1)
        rebuilt = jnp.concatenate([back_one, back_two], axis=-1)
        passed = jnp.concatenate([carry_one, carry_two], axis=-1)
        return (forward, rebuilt, passed, (b_pad, carry_one), (g_pad, d_two))

    fwd_one, rebuilt_one, passed_one, first_pair_one, second_pair_one = tick(
        fwd_in[0], bwd_act[0], bwd_grad[0]
    )
    lifted = from_behind(fwd_one, "section", 1)
    lowered = from_behind(jnp.stack([rebuilt_one, passed_one]), "section", -1)
    state_two = jnp.where(place == 0, fresh, lifted)
    own_grad = (fwd_one.astype(jnp.float32) - target.astype(jnp.float32)).astype(jnp.bfloat16)
    act_two = jnp.where(place == last_section, fwd_one, lowered[0])
    grad_two = jnp.where(place == last_section, own_grad, lowered[1])
    fwd_two, rebuilt_two, passed_two, first_pair_two, second_pair_two = tick(
        state_two, act_two, grad_two
    )
    cell_total = fwd_in.shape[1] * lax.axis_size("space") * fwd_in.shape[2] * fwd_in.shape[3]
    factor = 1.0 / math.sqrt(cell_total)
    first_sum = correlate(first_pair_one[0], first_pair_one[1]) + correlate(
        first_pair_two[0], first_pair_two[1]
    )
    second_sum = correlate(second_pair_one[0], second_pair_one[1]) + correlate(
        second_pair_two[0], second_pair_two[1]
    )
    first_total, second_total = (
        lax.psum_scatter(first_sum, "space", scatter_dimension=0, tiled=True),
        lax.psum_scatter(second_sum, "space", scatter_dimension=0, tiled=True),
    )
    return (
        fwd_two[None],
        rebuilt_two[None],
        passed_two[None],
        (first_total * factor)[None],
        (second_total * factor)[None],
    )


def solution(mesh):
    placed = (
        P("section", "space", None, None, None),
        P("section", "space", None, None, None),
        P("section", "space", None, None, None),
        P("space", None, None, None),
        P("space", None, None, None),
        P("section", None, None, None),
        P("section", None, None, None),
    )
    return jax.shard_map(
        shards,
        mesh=mesh,
        in_specs=placed,
        out_specs=(
            P("section", "space", None, None, None),
            P("section", "space", None, None, None),
            P("section", "space", None, None, None),
            P("section", "space", None),
            P("section", "space", None),
        ),
        check_vma=False,
    )
```

profile of v0, /device:TPU:0, one launch (start us, length us, event | category | flops | bytes accessed | tf_op | source)
XLA Modules:
  0.0 357.2 jit_solution(694295543393715532)
XLA Ops:
  7.2 0.9 slice.1015
  8.1 1.0 fusion.56
  9.8 1.3 collective-permute-start.1
  11.1 6.2 %collective-permute-start = (bf16[1,8,8,384]{3,2,1,0:T(8,128)(2,1)}, bf16[1,8,8,384]{3,2,1,0:T(8,128)(2,1)}, u32[]{:S(2)}, u32[]{:S(2)}) collective-permute-start(bf16[1,8,8,384]{3,2,1,0:T(8,128)(2,1)} %get-tuple-element.201), channel_id=1, source_target_pairs={{0,1},{1,2},{2,3},{3,4},{4,5},{5,6},{6,7},{7,8},{8,9},{9,10},{10,1... | collective-permute-start | bytes 147464 | tf_op jit(solution)/shard_map/ppermute | solution.py:14
  17.4 1.3 fusion.129
  18.7 1.3 copy.14
  20.0 0.9 fusion.128
  20.9 1.3 copy.15
  22.6 0.9 fusion.127
  23.6 1.1 select_maximum_fusion.12
  32.7 1.3 collective-permute-start.3
  34.0 4.8 %collective-permute-start.2 = (bf16[1,8,8,384]{3,2,1,0:T(8,128)(2,1)S(1)}, bf16[1,8,8,384]{3,2,1,0:T(8,128)(2,1)S(1)}, u32[]{:S(2)}, u32[]{:S(2)}) collective-permute-start(bf16[1,8,8,384]{3,2,1,0:T(8,128)(2,1)S(1)} %get-tuple-element.199), channel_id=1, source_target_pairs={{0,1},{1,2},{2,3},{3,4},{4,5},{5,6},{6,7},{7,8},{8,9},{9,10},{10,1... | collective-permute-start | bytes 147464 | tf_op jit(solution)/shard_map/ppermute | solution.py:14
  47.0 1.5 collective-permute-start.5
  53.3 3.1 collective-permute-start.4
  56.4 0.9 collective-permute-done.4
  57.4 1.3 collective-permute-start.7
  58.7 5.5 %collective-permute-start.6 = (bf16[1,8,8,384]{3,2,1,0:T(8,128)(2,1)S(1)}, bf16[1,8,8,384]{3,2,1,0:T(8,128)(2,1)S(1)}, u32[]{:S(2)}, u32[]{:S(2)}) collective-permute-start(bf16[1,8,8,384]{3,2,1,0:T(8,128)(2,1)S(1)} %get-tuple-element.197), channel_id=1, source_target_pairs={{0,1},{1,2},{2,3},{3,4},{4,5},{5,6},{6,7},{7,8},{8,9},{9,10},{10,1... | collective-permute-start | bytes 147464 | tf_op jit(solution)/shard_map/ppermute | solution.py:14
  64.5 1.4 collective-permute-done.6
  76.0 1.3 collective-permute-start.9
  77.3 6.1 %collective-permute-start.8 = (bf16[1,8,8,384]{3,2,1,0:T(8,128)(2,1)}, bf16[1,8,8,384]{3,2,1,0:T(8,128)(2,1)}, u32[]{:S(2)}, u32[]{:S(2)}) collective-permute-start(bf16[1,8,8,384]{3,2,1,0:T(8,128)(2,1)} %get-tuple-element.195), channel_id=1, source_target_pairs={{0,1},{1,2},{2,3},{3,4},{4,5},{5,6},{6,7},{7,8},{8,9},{9,10},{10,1... | collective-permute-start | bytes 147464 | tf_op jit(solution)/shard_map/ppermute | solution.py:14
  85.5 1.4 add.487
  87.8 1.1 select_maximum_fusion
  89.0 1.0 fusion.131
  90.3 0.9 fusion.136
  94.1 0.9 convolution_add_fusion.11
  95.6 1.4 add.486
  97.1 1.1 pad_maximum_fusion.11
  98.2 1.2 convolution_add_fusion.10
  107.1 111.4 %reduce-scatter.9.cloned.1.call-done = f32[216,128]{1,0:T(8,128)} async-done(((f32[3456,128]{1,0:T(8,128)}), f32[216,128]{1,0:T(8,128)}) %reduce-scatter.9.cloned.1.call-update) | async-done | bytes 110608
  218.5 1.5 multiply_bitcast_fusion
  220.0 128.8 %reduce-scatter.7.cloned.1.call-done = f32[216,128]{1,0:T(8,128)} async-done(((f32[3456,128]{1,0:T(8,128)}), f32[216,128]{1,0:T(8,128)}) %reduce-scatter.7.cloned.1.call-update) | async-done | bytes 110608
  348.8 1.5 multiply_bitcast_fusion.1
  (363 shorter events, 44.9 us)
Async XLA Ops:
  7.2 11.5 %copy-start = (bf16[1,27,128,128]{3,2,1,0:T(8,128)(2,1)S(1)}, bf16[1,27,128,128]{3,2,1,0:T(8,128)(2,1)}, u32[]{:S(2)}) copy-start(bf16[1,27,128,128]{3,2,1,0:T(8,128)(2,1)} %param.13) | copy-start | bytes 2654212
  7.2 211.3 %reduce-scatter.9.cloned.1.call-start = ((), (), s32[]{:S(2)}) async-start(), calls=%async_computation.3 | async-start | bytes 1880064
  8.1 2.9 copy-start.62
  9.8 13.7 %collective-permute-start.1 = (bf16[1,8,8,384]{3,2,1,0:T(8,128)(2,1)}, bf16[1,8,8,384]{3,2,1,0:T(8,128)(2,1)}, u32[]{:S(2)}, u32[]{:S(2)}) collective-permute-start(bf16[1,8,8,384]{3,2,1,0:T(8,128)(2,1)} %get-tuple-element.202), channel_id=1, source_target_pairs={{1,0},{2,1},{3,2},{4,3},{5,4},{6,5},{7,6},{8,7},{9,8},{10,9},{11,1... | collective-permute-start | bytes 147464 | tf_op jit(solution)/shard_map/ppermute | solution.py:17
  11.1 8.9 %copy-start.1 = (bf16[1,27,128,128]{3,2,1,0:T(8,128)(2,1)S(1)}, bf16[1,27,128,128]{3,2,1,0:T(8,128)(2,1)}, u32[]{:S(2)}) copy-start(bf16[1,27,128,128]{3,2,1,0:T(8,128)(2,1)} %param.12) | copy-start | bytes 2654212
  11.1 12.4 %collective-permute-start = (bf16[1,8,8,384]{3,2,1,0:T(8,128)(2,1)}, bf16[1,8,8,384]{3,2,1,0:T(8,128)(2,1)}, u32[]{:S(2)}, u32[]{:S(2)}) collective-permute-start(bf16[1,8,8,384]{3,2,1,0:T(8,128)(2,1)} %get-tuple-element.201), channel_id=1, source_target_pairs={{0,1},{1,2},{2,3},{3,4},{4,5},{5,6},{6,7},{7,8},{8,9},{9,10},{10,1... | collective-permute-start | bytes 147464 | tf_op jit(solution)/shard_map/ppermute | solution.py:14
  22.4 6.5 %copy-start.51 = (bf16[3,128,128]{2,1,0:T(8,128)(2,1)}, bf16[3,128,128]{2,1,0:T(8,128)(2,1)S(1)}, u32[]{:S(2)}) copy-start(bf16[3,128,128]{2,1,0:T(8,128)(2,1)S(1)} %get-tuple-element.48) | copy-start | bytes 294916
  22.4 8.4 %copy-start.49 = (bf16[3,128,128]{2,1,0:T(8,128)(2,1)}, bf16[3,128,128]{2,1,0:T(8,128)(2,1)S(1)}, u32[]{:S(2)}) copy-start(bf16[3,128,128]{2,1,0:T(8,128)(2,1)S(1)} %get-tuple-element.47) | copy-start | bytes 294916
  22.4 8.6 %copy-start.47 = (bf16[3,128,128]{2,1,0:T(8,128)(2,1)}, bf16[3,128,128]{2,1,0:T(8,128)(2,1)S(1)}, u32[]{:S(2)}) copy-start(bf16[3,128,128]{2,1,0:T(8,128)(2,1)S(1)} %get-tuple-element.46) | copy-start | bytes 294916
  22.4 8.8 %copy-start.45 = (bf16[3,128,128]{2,1,0:T(8,128)(2,1)}, bf16[3,128,128]{2,1,0:T(8,128)(2,1)S(1)}, u32[]{:S(2)}) copy-start(bf16[3,128,128]{2,1,0:T(8,128)(2,1)S(1)} %get-tuple-element.45) | copy-start | bytes 294916
  22.4 9.0 %copy-start.43 = (bf16[3,128,128]{2,1,0:T(8,128)(2,1)}, bf16[3,128,128]{2,1,0:T(8,128)(2,1)S(1)}, u32[]{:S(2)}) copy-start(bf16[3,128,128]{2,1,0:T(8,128)(2,1)S(1)} %get-tuple-element.44) | copy-start | bytes 294916
  22.5 9.3 %copy-start.41 = (bf16[3,128,128]{2,1,0:T(8,128)(2,1)}, bf16[3,128,128]{2,1,0:T(8,128)(2,1)S(1)}, u32[]{:S(2)}) copy-start(bf16[3,128,128]{2,1,0:T(8,128)(2,1)S(1)} %get-tuple-element.43) | copy-start | bytes 294916
  22.5 9.5 %copy-start.39 = (bf16[3,128,128]{2,1,0:T(8,128)(2,1)}, bf16[3,128,128]{2,1,0:T(8,128)(2,1)S(1)}, u32[]{:S(2)}) copy-start(bf16[3,128,128]{2,1,0:T(8,128)(2,1)S(1)} %get-tuple-element.42) | copy-start | bytes 294916
  22.5 9.7 %copy-start.37 = (bf16[3,128,128]{2,1,0:T(8,128)(2,1)}, bf16[3,128,128]{2,1,0:T(8,128)(2,1)S(1)}, u32[]{:S(2)}) copy-start(bf16[3,128,128]{2,1,0:T(8,128)(2,1)S(1)} %get-tuple-element.41) | copy-start | bytes 294916
  22.5 9.9 %copy-start.35 = (bf16[3,128,128]{2,1,0:T(8,128)(2,1)}, bf16[3,128,128]{2,1,0:T(8,128)(2,1)S(1)}, u32[]{:S(2)}) copy-start(bf16[3,128,128]{2,1,0:T(8,128)(2,1)S(1)} %get-tuple-element.40) | copy-start | bytes 294916
  32.7 8.3 %collective-permute-start.3 = (bf16[1,8,8,384]{3,2,1,0:T(8,128)(2,1)S(1)}, bf16[1,8,8,384]{3,2,1,0:T(8,128)(2,1)S(1)}, u32[]{:S(2)}, u32[]{:S(2)}) collective-permute-start(bf16[1,8,8,384]{3,2,1,0:T(8,128)(2,1)S(1)} %get-tuple-element.200), channel_id=1, source_target_pairs={{1,0},{2,1},{3,2},{4,3},{5,4},{6,5},{7,6},{8,7},{9,8},{10,9},{11,1... | collective-permute-start | bytes 147464 | tf_op jit(solution)/shard_map/ppermute | solution.py:17
  34.0 7.0 %collective-permute-start.2 = (bf16[1,8,8,384]{3,2,1,0:T(8,128)(2,1)S(1)}, bf16[1,8,8,384]{3,2,1,0:T(8,128)(2,1)S(1)}, u32[]{:S(2)}, u32[]{:S(2)}) collective-permute-start(bf16[1,8,8,384]{3,2,1,0:T(8,128)(2,1)S(1)} %get-tuple-element.199), channel_id=1, source_target_pairs={{0,1},{1,2},{2,3},{3,4},{4,5},{5,6},{6,7},{7,8},{8,9},{9,10},{10,1... | collective-permute-start | bytes 147464 | tf_op jit(solution)/shard_map/ppermute | solution.py:14
  47.0 5.5 %collective-permute-start.5 = (bf16[2,4,8,8,256]{4,3,2,1,0:T(8,128)(2,1)S(1)}, bf16[2,4,8,8,256]{4,3,2,1,0:T(8,128)(2,1)S(1)}, u32[]{:S(2)}, u32[]{:S(2)}) collective-permute-start(bf16[2,4,8,8,256]{4,3,2,1,0:T(8,128)(2,1)S(1)} %pad_maximum_fusion.12), channel_id=1, source_target_pairs={{16,0},{17,1},{18,2},{19,3},{20,4},{21,5},{22,6},{23,7},{24,8},{25... | collective-permute-start | bytes 786440 | tf_op jit(solution)/shard_map/ppermute | solution.py:25
  52.3 5.1 %copy-start.76 = (bf16[4,8,8,256]{3,2,1,0:T(8,128)(2,1)S(1)}, bf16[4,8,8,256]{3,2,1,0:T(8,128)(2,1)}, u32[]{:S(2)}) copy-start(bf16[4,8,8,256]{3,2,1,0:T(8,128)(2,1)} %param.10) | copy-start | bytes 393220
  53.3 21.3 %copy-start.13 = (bf16[4,8,8,256]{3,2,1,0:T(8,128)(2,1)}, bf16[4,8,8,256]{3,2,1,0:T(8,128)(2,1)S(1)}, u32[]{:S(2)}) copy-start(bf16[4,8,8,256]{3,2,1,0:T(8,128)(2,1)S(1)} %get-tuple-element.85) | copy-start | bytes 393220
  53.3 32.0 %copy-start.53 = (bf16[4,8,8,256]{3,2,1,0:T(8,128)(2,1)}, bf16[4,8,8,256]{3,2,1,0:T(8,128)(2,1)S(1)}, u32[]{:S(2)}) copy-start(bf16[4,8,8,256]{3,2,1,0:T(8,128)(2,1)S(1)} %get-tuple-element.86) | copy-start | bytes 393220
  53.3 4.0 %collective-permute-start.4 = (bf16[4,8,8,256]{3,2,1,0:T(8,128)(2,1)S(1)}, bf16[4,8,8,256]{3,2,1,0:T(8,128)(2,1)S(1)}, u32[]{:S(2)}, u32[]{:S(2)}) collective-permute-start(bf16[4,8,8,256]{3,2,1,0:T(8,128)(2,1)S(1)} %get-tuple-element.204), channel_id=1, source_target_pairs={{0,16},{1,17},{2,18},{3,19},{4,20},{5,21},{6,22},{7,23},{8,24},{9,... | collective-permute-start | bytes 393224 | tf_op jit(solution)/shard_map/ppermute | solution.py:25
  57.3 13.1 %copy-start.55 = (bf16[4,8,8,256]{3,2,1,0:T(8,128)(2,1)}, bf16[4,8,8,256]{3,2,1,0:T(8,128)(2,1)S(1)}, u32[]{:S(2)}) copy-start(bf16[4,8,8,256]{3,2,1,0:T(8,128)(2,1)S(1)} %broadcast_select_fusion) | copy-start | bytes 393220
  57.4 7.1 %collective-permute-start.7 = (bf16[1,8,8,384]{3,2,1,0:T(8,128)(2,1)S(1)}, bf16[1,8,8,384]{3,2,1,0:T(8,128)(2,1)S(1)}, u32[]{:S(2)}, u32[]{:S(2)}) collective-permute-start(bf16[1,8,8,384]{3,2,1,0:T(8,128)(2,1)S(1)} %get-tuple-element.198), channel_id=1, source_target_pairs={{1,0},{2,1},{3,2},{4,3},{5,4},{6,5},{7,6},{8,7},{9,8},{10,9},{11,1... | collective-permute-start | bytes 147464 | tf_op jit(solution)/shard_map/ppermute | solution.py:17
  58.7 7.2 %collective-permute-start.6 = (bf16[1,8,8,384]{3,2,1,0:T(8,128)(2,1)S(1)}, bf16[1,8,8,384]{3,2,1,0:T(8,128)(2,1)S(1)}, u32[]{:S(2)}, u32[]{:S(2)}) collective-permute-start(bf16[1,8,8,384]{3,2,1,0:T(8,128)(2,1)S(1)} %get-tuple-element.197), channel_id=1, source_target_pairs={{0,1},{1,2},{2,3},{3,4},{4,5},{5,6},{6,7},{7,8},{8,9},{9,10},{10,1... | collective-permute-start | bytes 147464 | tf_op jit(solution)/shard_map/ppermute | solution.py:14
  71.1 4.2 %copy-start.58 = (bf16[4,8,8,128]{3,2,1,0:T(8,128)(2,1)}, bf16[4,8,8,128]{3,2,1,0:T(8,128)(2,1)S(1)}, u32[]{:S(2)}) copy-start(bf16[4,8,8,128]{3,2,1,0:T(8,128)(2,1)S(1)} %get-tuple-element.5) | copy-start | bytes 196612
  75.3 8.6 %copy-start.15 = (bf16[4,8,8,128]{3,2,1,0:T(8,128)(2,1)}, bf16[4,8,8,128]{3,2,1,0:T(8,128)(2,1)S(1)}, u32[]{:S(2)}) copy-start(bf16[4,8,8,128]{3,2,1,0:T(8,128)(2,1)S(1)} %get-tuple-element.203) | copy-start | bytes 196612
  75.3 8.6 %copy-start.60 = (bf16[4,8,8,128]{3,2,1,0:T(8,128)(2,1)}, bf16[4,8,8,128]{3,2,1,0:T(8,128)(2,1)S(1)}, u32[]{:S(2)}) copy-start(bf16[4,8,8,128]{3,2,1,0:T(8,128)(2,1)S(1)} %get-tuple-element.7) | copy-start | bytes 196612
  76.0 11.3 %collective-permute-start.9 = (bf16[1,8,8,384]{3,2,1,0:T(8,128)(2,1)}, bf16[1,8,8,384]{3,2,1,0:T(8,128)(2,1)}, u32[]{:S(2)}, u32[]{:S(2)}) collective-permute-start(bf16[1,8,8,384]{3,2,1,0:T(8,128)(2,1)} %get-tuple-element.196), channel_id=1, source_target_pairs={{1,0},{2,1},{3,2},{4,3},{5,4},{6,5},{7,6},{8,7},{9,8},{10,9},{11,1... | collective-permute-start | bytes 147464 | tf_op jit(solution)/shard_map/ppermute | solution.py:17
  77.3 10.0 %collective-permute-start.8 = (bf16[1,8,8,384]{3,2,1,0:T(8,128)(2,1)}, bf16[1,8,8,384]{3,2,1,0:T(8,128)(2,1)}, u32[]{:S(2)}, u32[]{:S(2)}) collective-permute-start(bf16[1,8,8,384]{3,2,1,0:T(8,128)(2,1)} %get-tuple-element.195), channel_id=1, source_target_pairs={{0,1},{1,2},{2,3},{3,4},{4,5},{5,6},{6,7},{7,8},{8,9},{9,10},{10,1... | collective-permute-start | bytes 147464 | tf_op jit(solution)/shard_map/ppermute | solution.py:14
  87.0 261.8 %reduce-scatter.7.cloned.1.call-start = ((), (), s32[]{:S(2)}) async-start(), calls=%async_computation.2 | async-start | bytes 1880064
  97.1 2.7 copy-start.14
  (57 other events, 78.9 us)
Sparse Core Ops, SparseCore 0:
  87.1 131.3 reduce-scatter.8
  223.4 125.4 reduce-scatter.6
where the time goes:
time: 358 us; the launch traced here: 357 us
  waiting for transfers between devices  243 us (68%)
  starting transfers between devices  32.6 us (9%)
  matrix products  32.3 us (9%)
  other arithmetic  17 us (5%)
  between operations  16.6 us (5%)
  local copies, waits for them, and re-layouts  16.1 us (4%)
    unnamed x4, waiting for transfers between devices  240 us
    dot_general x108, matrix products, convolve(): jnp.dot(block, wide[across * 3 + down], preferred_element_type=jnp.float32)  23 us
    ppermute x4, starting transfers between devices, extended(): lax.ppermute(lax.slice_in_dim(block, block.shape[dim] - width, None, axis...  22.6 us
    dot_general x36, matrix products, correlate(): lax.dot_general(block, flat, (((0,), (0,)), ((), ())), preferred_element_...  9.31 us
    unnamed x156, local copies, waits for them, and re-layouts  7.32 us
  transfers between devices with their start and end apart: 12, of which 4 were waited for; matrix products, arithmetic and copies ran while one was open for 10% of the time, Pallas kernels for 0%

commit v1 on v0

--- a/solution.py
+++ b/solution.py
@@ -88,6 +88,39 @@
                 )
             )
     return jnp.concatenate(blocks, axis=0)
+
+
+def reduce_blocks(grads):
+    count = lax.axis_size("space")
+    bits = [1 << level for level in range(count.bit_length() - 1)]
+    spot = lax.axis_index("space")
+    rows = grads.shape[1]
+    ways = 3 if rows % 3 == 0 else 1
+    span = rows // ways
+    parts = []
+    for way in range(ways):
+        shift = way % len(bits)
+        order = bits[shift:] + bits[:shift]
+        part = grads[:, way * span : (way + 1) * span].reshape(
+            [2] * len(bits) + [span, grads.shape[2]]
+        )
+        parts.append((part, order))
+    for step in range(len(bits)):
+        fresh_parts = []
+        for part, order in parts:
+            bit = order[step]
+            left = sorted(order[step:], reverse=True)
+            axis = left.index(bit)
+            mine = (spot // bit) % 2
+            keep = lax.dynamic_index_in_dim(part, mine, axis, keepdims=False)
+            send = lax.dynamic_index_in_dim(part, 1 - mine, axis, keepdims=False)
+            got = lax.ppermute(send, "space", [(i, i ^ bit) for i in range(count)])
+            total = keep.astype(jnp.float32) + got.astype(jnp.float32)
+            if step < len(bits) - 1:
+                total = total.astype(jnp.bfloat16)
+            fresh_parts.append((total, order))
+        parts = fresh_parts
+    return jnp.concatenate([part for part, _ in parts], axis=0)
 
 
 def shards(fwd_in, bwd_act, bwd_grad, fresh, target, w_first, w_second):
@@ -146,16 +179,20 @@
     second_sum = correlate(second_pair_one[0], second_pair_one[1]) + correlate(
         second_pair_two[0], second_pair_two[1]
     )
-    first_total, second_total = (
-        lax.psum_scatter(first_sum, "space", scatter_dimension=0, tiled=True),
-        lax.psum_scatter(second_sum, "space", scatter_dimension=0, tiled=True),
-    )
+    count = lax.axis_size("space")
+    blocks = jnp.concatenate(
+        [(part * factor).astype(jnp.bfloat16).reshape(count, -1, width) for part in (first_sum, second_sum)],
+        axis=1,
+    )
+    total = reduce_blocks(blocks)
+    rows = total.shape[0] // 2
+    first_total, second_total = total[:rows], total[rows:]
     return (
         fwd_two[None],
         rebuilt_two[None],
         passed_two[None],
-        (first_total * factor)[None],
-        (second_total * factor)[None],
+        first_total[None],
+        second_total[None],
     )
 
 

time: 358 us -> 122 us (0.34)
  waiting for transfers between devices: 243 us -> 15.6 us
  starting transfers between devices: 32.6 us -> 51.8 us
  between operations: 16.6 us -> 2.89 us
  other arithmetic: 17 us -> 9 us
  local copies, waits for them, and re-layouts: 16.1 us -> 11.8 us
    unnamed x4 -> x0, waiting for transfers between devices: 240 us -> none
    ppermute x0 -> x12, starting transfers between devices: none -> 19.9 us  [reduce_blocks(): got = lax.ppermute(send, 'space', [(i, i ^ bit) for i in range(count)])]
    ppermute x0 -> x12, waiting for transfers between devices: none -> 13.2 us  [reduce_blocks(): got = lax.ppermute(send, 'space', [(i, i ^ bit) for i in range(count)])]
    unnamed x156 -> x46, local copies, waits for them, and re-layouts: 7.32 us -> 4.48 us
  transfers between devices with their start and end apart: 12 -> 22, of which waited for: 4 -> 10; matrix products, arithmetic and copies ran while one was open for 10% -> 14% of each run, Pallas kernels for 0% -> 0%
where the time goes in v1:
time: 122 us
  starting transfers between devices  51.8 us (42%)
  matrix products  30.6 us (25%)
  waiting for transfers between devices  15.6 us (13%)
  local copies, waits for them, and re-layouts  11.8 us (10%)
  other arithmetic  9 us (7%)
  between operations  2.89 us (2%)
    ppermute x4, starting transfers between devices, extended(): lax.ppermute(lax.slice_in_dim(block, block.shape[dim] - width, None, axis...  22.2 us
    dot_general x108, matrix products, convolve(): jnp.dot(block, wide[across * 3 + down], preferred_element_type=jnp.float32)  21.3 us
    ppermute x12, starting transfers between devices, reduce_blocks(): got = lax.ppermute(send, 'space', [(i, i ^ bit) for i in range(count)])  19.9 us
    ppermute x12, waiting for transfers between devices, reduce_blocks(): got = lax.ppermute(send, 'space', [(i, i ^ bit) for i in range(count)])  13.2 us
    dot_general x36, matrix products, correlate(): lax.dot_general(block, flat, (((0,), (0,)), ((), ())), preferred_element_...  9.32 us
    ppermute x4, starting transfers between devices, extended(): lax.ppermute(lax.slice_in_dim(block, 0, width, axis=dim), axis, backward)  5.16 us
    ppermute x2, starting transfers between devices, from_behind(): return lax.ppermute(block, axis, route)  4.52 us
    unnamed x46, local copies, waits for them, and re-layouts  4.48 us
  transfers between devices with their start and end apart: 22, of which 10 were waited for; matrix products, arithmetic and copies ran while one was open for 14% of the time, Pallas kernels for 0%

profile of v1, /device:TPU:0, one launch (start us, length us, event | category | flops | bytes accessed | tf_op | source)
XLA Modules:
  0.0 121.7 jit_solution(17795667498377838458)
XLA Ops:
  0.6 0.9 slice.1037
  1.6 1.0 fusion.65
  3.2 1.3 %collective-permute-start.1 = (bf16[1,8,8,384]{3,2,1,0:T(8,128)(2,1)}, bf16[1,8,8,384]{3,2,1,0:T(8,128)(2,1)}, u32[]{:S(2)}, u32[]{:S(2)}) collective-permute-start(bf16[1,8,8,384]{3,2,1,0:T(8,128)(2,1)} %get-tuple-element.209), channel_id=1, source_target_pairs={{1,0},{2,1},{3,2},{4,3},{5,4},{6,5},{7,6},{8,7},{9,8},{10,9},{11,1... | collective-permute-start | bytes 147464 | tf_op jit(solution)/shard_map/ppermute | solution.py:17
  4.6 6.2 %collective-permute-start = (bf16[1,8,8,384]{3,2,1,0:T(8,128)(2,1)}, bf16[1,8,8,384]{3,2,1,0:T(8,128)(2,1)}, u32[]{:S(2)}, u32[]{:S(2)}) collective-permute-start(bf16[1,8,8,384]{3,2,1,0:T(8,128)(2,1)} %get-tuple-element.208), channel_id=1, source_target_pairs={{0,1},{1,2},{2,3},{3,4},{4,5},{5,6},{6,7},{7,8},{8,9},{9,10},{10,1... | collective-permute-start | bytes 147464 | tf_op jit(solution)/shard_map/ppermute | solution.py:14
  10.8 1.9 %fusion.141 = (bf16[1,3,128,128]{3,2,1,0:T(8,128)(2,1)S(1)}, bf16[1,3,128,128]{3,2,1,0:T(8,128)(2,1)S(1)}, bf16[1,3,128,128]{3,2,1,0:T(8,128)(2,1)S(1)}, bf16[1,...) fusion(bf16[1,27,128,128]{3,2,1,0:T(8,128)(2,1)} %param.13), kind=kLoop, calls=%fused_computation.399 | loop fusion | bytes 1769472 | tf_op jit(solution)/shard_map/slice | solution.py:69
  12.7 1.3 %copy.12 = bf16[1,27,128,128]{2,3,1,0:T(8,128)(2,1)S(1)} copy(bf16[1,27,128,128]{3,2,1,0:T(8,128)(2,1)S(1)} %copy-done) | data formatting | bytes 1769472 | tf_op args[6]
  14.0 0.9 fusion.140
  14.9 1.3 %copy.13 = bf16[1,27,128,128]{2,3,1,0:T(8,128)(2,1)S(1)} copy(bf16[1,27,128,128]{3,2,1,0:T(8,128)(2,1)S(1)} %copy-done.1) | data formatting | bytes 1769472 | tf_op args[5]
  17.3 1.1 select_maximum_fusion.12
  26.3 1.3 %collective-permute-start.3 = (bf16[1,8,8,384]{3,2,1,0:T(8,128)(2,1)S(1)}, bf16[1,8,8,384]{3,2,1,0:T(8,128)(2,1)S(1)}, u32[]{:S(2)}, u32[]{:S(2)}) collective-permute-start(bf16[1,8,8,384]{3,2,1,0:T(8,128)(2,1)S(1)} %get-tuple-element.207), channel_id=1, source_target_pairs={{1,0},{2,1},{3,2},{4,3},{5,4},{6,5},{7,6},{8,7},{9,8},{10,9},{11,1... | collective-permute-start | bytes 147464 | tf_op jit(solution)/shard_map/ppermute | solution.py:17
  27.6 4.8 %collective-permute-start.2 = (bf16[1,8,8,384]{3,2,1,0:T(8,128)(2,1)S(1)}, bf16[1,8,8,384]{3,2,1,0:T(8,128)(2,1)S(1)}, u32[]{:S(2)}, u32[]{:S(2)}) collective-permute-start(bf16[1,8,8,384]{3,2,1,0:T(8,128)(2,1)S(1)} %get-tuple-element.206), channel_id=1, source_target_pairs={{0,1},{1,2},{2,3},{3,4},{4,5},{5,6},{6,7},{7,8},{8,9},{9,10},{10,1... | collective-permute-start | bytes 147464 | tf_op jit(solution)/shard_map/ppermute | solution.py:14
  39.8 1.5 %collective-permute-start.5 = (bf16[2,4,8,8,256]{4,3,2,1,0:T(8,128)(2,1)S(1)}, bf16[2,4,8,8,256]{4,3,2,1,0:T(8,128)(2,1)S(1)}, u32[]{:S(2)}, u32[]{:S(2)}) collective-permute-start(bf16[2,4,8,8,256]{4,3,2,1,0:T(8,128)(2,1)S(1)} %pad_maximum_fusion.13), channel_id=1, source_target_pairs={{16,0},{17,1},{18,2},{19,3},{20,4},{21,5},{22,6},{23,7},{24,8},{25... | collective-permute-start | bytes 786440 | tf_op jit(solution)/shard_map/ppermute | solution.py:25
  46.0 3.0 %collective-permute-start.4 = (bf16[4,8,8,256]{3,2,1,0:T(8,128)(2,1)S(1)}, bf16[4,8,8,256]{3,2,1,0:T(8,128)(2,1)S(1)}, u32[]{:S(2)}, u32[]{:S(2)}) collective-permute-start(bf16[4,8,8,256]{3,2,1,0:T(8,128)(2,1)S(1)} %get-tuple-element.211), channel_id=1, source_target_pairs={{0,16},{1,17},{2,18},{3,19},{4,20},{5,21},{6,22},{7,23},{8,24},{9,... | collective-permute-start | bytes 393224 | tf_op jit(solution)/shard_map/ppermute | solution.py:25
  49.1 0.9 collective-permute-done.4
  50.1 1.3 %collective-permute-start.7 = (bf16[1,8,8,384]{3,2,1,0:T(8,128)(2,1)S(1)}, bf16[1,8,8,384]{3,2,1,0:T(8,128)(2,1)S(1)}, u32[]{:S(2)}, u32[]{:S(2)}) collective-permute-start(bf16[1,8,8,384]{3,2,1,0:T(8,128)(2,1)S(1)} %get-tuple-element.205), channel_id=1, source_target_pairs={{1,0},{2,1},{3,2},{4,3},{5,4},{6,5},{7,6},{8,7},{9,8},{10,9},{11,1... | collective-permute-start | bytes 147464 | tf_op jit(solution)/shard_map/ppermute | solution.py:17
  51.4 5.5 %collective-permute-start.6 = (bf16[1,8,8,384]{3,2,1,0:T(8,128)(2,1)S(1)}, bf16[1,8,8,384]{3,2,1,0:T(8,128)(2,1)S(1)}, u32[]{:S(2)}, u32[]{:S(2)}) collective-permute-start(bf16[1,8,8,384]{3,2,1,0:T(8,128)(2,1)S(1)} %get-tuple-element.204), channel_id=1, source_target_pairs={{0,1},{1,2},{2,3},{3,4},{4,5},{5,6},{6,7},{7,8},{8,9},{9,10},{10,1... | collective-permute-start | bytes 147464 | tf_op jit(solution)/shard_map/ppermute | solution.py:14
  57.2 1.4 %collective-permute-done.6 = bf16[1,8,8,384]{3,2,1,0:T(8,128)(2,1)S(1)} collective-permute-done((bf16[1,8,8,384]{3,2,1,0:T(8,128)(2,1)S(1)}, bf16[1,8,8,384]{3,2,1,0:T(8,128)(2,1)S(1)}, u32[]{:S(2)}, u32[]{:S(2)}) %collective-permute-start.6) | collective-permute-done | bytes 49184 | tf_op jit(solution)/shard_map/ppermute | solution.py:14
  65.9 1.3 %collective-permute-start.9 = (bf16[1,8,8,384]{3,2,1,0:T(8,128)(2,1)S(1)}, bf16[1,8,8,384]{3,2,1,0:T(8,128)(2,1)S(1)}, u32[]{:S(2)}, u32[]{:S(2)}) collective-permute-start(bf16[1,8,8,384]{3,2,1,0:T(8,128)(2,1)S(1)} %get-tuple-element.203), channel_id=1, source_target_pairs={{1,0},{2,1},{3,2},{4,3},{5,4},{6,5},{7,6},{8,7},{9,8},{10,9},{11,1... | collective-permute-start | bytes 147464 | tf_op jit(solution)/shard_map/ppermute | solution.py:17
  67.2 5.7 %collective-permute-start.8 = (bf16[1,8,8,384]{3,2,1,0:T(8,128)(2,1)S(1)}, bf16[1,8,8,384]{3,2,1,0:T(8,128)(2,1)S(1)}, u32[]{:S(2)}, u32[]{:S(2)}) collective-permute-start(bf16[1,8,8,384]{3,2,1,0:T(8,128)(2,1)S(1)} %get-tuple-element.202), channel_id=1, source_target_pairs={{0,1},{1,2},{2,3},{3,4},{4,5},{5,6},{6,7},{7,8},{8,9},{9,10},{10,1... | collective-permute-start | bytes 147464 | tf_op jit(solution)/shard_map/ppermute | solution.py:14
  84.7 8.8 %collective-permute-start.18 = (bf16[2,2,2,144,128]{4,3,1,2,0:T(8,128)(2,1)S(1)}, bf16[2,2,2,144,128]{4,3,1,2,0:T(8,128)(2,1)S(1)}, u32[]{:S(2)}, u32[]{:S(2)}) collective-permute-start(bf16[2,2,2,144,128]{4,3,1,2,0:T(8,128)(2,1)S(1)} %bitcast.960), channel_id=1, source_target_pairs={{0,4},{1,5},{2,6},{3,7},{4,0},{5,1},{6,2},{7,3},{8,12},{9,13},{10,... | collective-permute-start | bytes 884744 | tf_op jit(solution)/shard_map/ppermute | solution.py:117
  93.5 0.7 collective-permute-start.14
  97.2 1.3 %collective-permute-done.18 = bf16[2,2,2,144,128]{4,3,1,2,0:T(8,128)(2,1)S(1)} collective-permute-done((bf16[2,2,2,144,128]{4,3,1,2,0:T(8,128)(2,1)S(1)}, bf16[2,2,2,144,128]{4,3,1,2,0:T(8,128)(2,1)S(1)}, u32[]{:S(2)}, u32[]{:S(2)}) %collective-permute-start.18) | collective-permute-done | bytes 294944 | tf_op jit(solution)/shard_map/ppermute | solution.py:117
  98.7 3.1 %collective-permute-start.19 = (bf16[2,2,144,128]{3,2,0,1:T(8,128)(2,1)S(1)}, bf16[2,2,144,128]{3,2,0,1:T(8,128)(2,1)S(1)}, u32[]{:S(2)}, u32[]{:S(2)}) collective-permute-start(bf16[2,2,144,128]{3,2,0,1:T(8,128)(2,1)S(1)} %dynamic-slice_bitcast_fusion.1), channel_id=1, source_target_pairs={{0,8},{1,9},{2,10},{3,11},{4,12},{5,13},{6,14},{7,15},{8,0},{9,1},... | collective-permute-start | bytes 442376 | tf_op jit(solution)/shard_map/ppermute | solution.py:117
  101.9 1.4 %collective-permute-start.15 = (bf16[2,2,144,128]{3,2,1,0:T(8,128)(2,1)S(1)}, bf16[2,2,144,128]{3,2,1,0:T(8,128)(2,1)S(1)}, u32[]{:S(2)}, u32[]{:S(2)}) collective-permute-start(bf16[2,2,144,128]{3,2,1,0:T(8,128)(2,1)S(1)} %dynamic-slice_bitcast_fusion.2), channel_id=1, source_target_pairs={{0,4},{1,5},{2,6},{3,7},{4,0},{5,1},{6,2},{7,3},{8,12},{9,13},{10,... | collective-permute-start | bytes 442376 | tf_op jit(solution)/shard_map/ppermute | solution.py:117
  103.4 0.7 collective-permute-start.11
  104.1 2.5 %collective-permute-done.19 = bf16[2,2,144,128]{3,2,0,1:T(8,128)(2,1)S(1)} collective-permute-done((bf16[2,2,144,128]{3,2,0,1:T(8,128)(2,1)S(1)}, bf16[2,2,144,128]{3,2,0,1:T(8,128)(2,1)S(1)}, u32[]{:S(2)}, u32[]{:S(2)}) %collective-permute-start.19) | collective-permute-done | bytes 147488 | tf_op jit(solution)/shard_map/ppermute | solution.py:117
  106.9 2.1 %collective-permute-done.15 = bf16[2,2,144,128]{3,2,1,0:T(8,128)(2,1)S(1)} collective-permute-done((bf16[2,2,144,128]{3,2,1,0:T(8,128)(2,1)S(1)}, bf16[2,2,144,128]{3,2,1,0:T(8,128)(2,1)S(1)}, u32[]{:S(2)}, u32[]{:S(2)}) %collective-permute-start.15) | collective-permute-done | bytes 147488 | tf_op jit(solution)/shard_map/ppermute | solution.py:117
  109.3 3.5 %collective-permute-start.12 = (bf16[2,144,128]{2,1,0:T(8,128)(2,1)S(1)}, bf16[2,144,128]{2,1,0:T(8,128)(2,1)S(1)}, u32[]{:S(2)}, u32[]{:S(2)}) collective-permute-start(bf16[2,144,128]{2,1,0:T(8,128)(2,1)S(1)} %dynamic-slice_bitcast_fusion.6), channel_id=1, source_target_pairs={{0,4},{1,5},{2,6},{3,7},{4,0},{5,1},{6,2},{7,3},{8,12},{9,13},{10,... | collective-permute-start | bytes 221192 | tf_op jit(solution)/shard_map/ppermute | solution.py:117
  112.9 2.6 %collective-permute-done.16 = bf16[2,144,128]{2,1,0:T(8,128)(2,1)S(1)} collective-permute-done((bf16[2,144,128]{2,1,0:T(8,128)(2,1)S(1)}, bf16[2,144,128]{2,1,0:T(8,128)(2,1)S(1)}, u32[]{:S(2)}, u32[]{:S(2)}) %collective-permute-start.16) | collective-permute-done | bytes 73760 | tf_op jit(solution)/shard_map/ppermute | solution.py:117
  116.8 2.7 %collective-permute-done.17 = bf16[144,128]{1,0:T(8,128)(2,1)S(1)} collective-permute-done((bf16[144,128]{1,0:T(8,128)(2,1)S(1)}, bf16[144,128]{1,0:T(8,128)(2,1)S(1)}, u32[]{:S(2)}, u32[]{:S(2)}) %collective-permute-start.17) | collective-permute-done | bytes 36896 | tf_op jit(solution)/shard_map/ppermute | solution.py:117
  119.5 1.5 %collective-permute-done.13 = bf16[144,128]{1,0:T(8,128)(2,1)S(1)} collective-permute-done((bf16[144,128]{1,0:T(8,128)(2,1)S(1)}, bf16[144,128]{1,0:T(8,128)(2,1)S(1)}, u32[]{:S(2)}, u32[]{:S(2)}) %collective-permute-start.13) | collective-permute-done | bytes 36896 | tf_op jit(solution)/shard_map/ppermute | solution.py:117
  121.0 0.7 fusion.118
  (297 shorter events, 44.7 us)
Async XLA Ops:
  0.6 12.1 %copy-start = (bf16[1,27,128,128]{3,2,1,0:T(8,128)(2,1)S(1)}, bf16[1,27,128,128]{3,2,1,0:T(8,128)(2,1)}, u32[]{:S(2)}) copy-start(bf16[1,27,128,128]{3,2,1,0:T(8,128)(2,1)} %param.13) | copy-start | bytes 2654212
  1.6 2.9 %copy-start.11 = (bf16[4,8,8,128]{3,2,1,0:T(8,128)(2,1)}, bf16[4,8,8,128]{3,2,1,0:T(8,128)(2,1)S(1)}, u32[]{:S(2)}) copy-start(bf16[4,8,8,128]{3,2,1,0:T(8,128)(2,1)S(1)} %slice.1037) | copy-start | bytes 196612
  2.5 2.0 %copy-start.13 = (bf16[4,8,8,128]{3,2,1,0:T(8,128)(2,1)}, bf16[4,8,8,128]{3,2,1,0:T(8,128)(2,1)S(1)}, u32[]{:S(2)}) copy-start(bf16[4,8,8,128]{3,2,1,0:T(8,128)(2,1)S(1)} %get-tuple-element.215) | copy-start | bytes 196612
  2.5 2.0 %copy-start.15 = (bf16[4,8,8,128]{3,2,1,0:T(8,128)(2,1)}, bf16[4,8,8,128]{3,2,1,0:T(8,128)(2,1)S(1)}, u32[]{:S(2)}) copy-start(bf16[4,8,8,128]{3,2,1,0:T(8,128)(2,1)S(1)} %get-tuple-element.216) | copy-start | bytes 196612
  3.2 13.5 %collective-permute-start.1 = (bf16[1,8,8,384]{3,2,1,0:T(8,128)(2,1)}, bf16[1,8,8,384]{3,2,1,0:T(8,128)(2,1)}, u32[]{:S(2)}, u32[]{:S(2)}) collective-permute-start(bf16[1,8,8,384]{3,2,1,0:T(8,128)(2,1)} %get-tuple-element.209), channel_id=1, source_target_pairs={{1,0},{2,1},{3,2},{4,3},{5,4},{6,5},{7,6},{8,7},{9,8},{10,9},{11,1... | collective-permute-start | bytes 147464 | tf_op jit(solution)/shard_map/ppermute | solution.py:17
  4.5 9.5 %copy-start.1 = (bf16[1,27,128,128]{3,2,1,0:T(8,128)(2,1)S(1)}, bf16[1,27,128,128]{3,2,1,0:T(8,128)(2,1)}, u32[]{:S(2)}) copy-start(bf16[1,27,128,128]{3,2,1,0:T(8,128)(2,1)} %param.12) | copy-start | bytes 2654212
  4.6 12.2 %collective-permute-start = (bf16[1,8,8,384]{3,2,1,0:T(8,128)(2,1)}, bf16[1,8,8,384]{3,2,1,0:T(8,128)(2,1)}, u32[]{:S(2)}, u32[]{:S(2)}) collective-permute-start(bf16[1,8,8,384]{3,2,1,0:T(8,128)(2,1)} %get-tuple-element.208), channel_id=1, source_target_pairs={{0,1},{1,2},{2,3},{3,4},{4,5},{5,6},{6,7},{7,8},{8,9},{9,10},{10,1... | collective-permute-start | bytes 147464 | tf_op jit(solution)/shard_map/ppermute | solution.py:14
  16.7 2.0 %copy-start.18 = (bf16[1,4,8,8,256]{4,3,2,1,0:T(8,128)(2,1)S(1)}, bf16[1,4,8,8,256]{4,3,2,1,0:T(8,128)(2,1)}, u32[]{:S(2)}) copy-start(bf16[1,4,8,8,256]{4,3,2,1,0:T(8,128)(2,1)} %param.9) | copy-start | bytes 393220
  19.7 1.6 %copy-start.5 = (bf16[1,3,128,128]{3,2,1,0:T(8,128)(2,1)S(1)}, bf16[1,3,128,128]{3,2,1,0:T(8,128)(2,1)}, u32[]{:S(2)}) copy-start(bf16[1,3,128,128]{3,2,1,0:T(8,128)(2,1)} %get-tuple-element.29) | copy-start | bytes 294916
  19.7 1.8 %copy-start.4 = (bf16[1,3,128,128]{3,2,1,0:T(8,128)(2,1)S(1)}, bf16[1,3,128,128]{3,2,1,0:T(8,128)(2,1)}, u32[]{:S(2)}) copy-start(bf16[1,3,128,128]{3,2,1,0:T(8,128)(2,1)} %get-tuple-element.28) | copy-start | bytes 294916
  19.7 2.0 %copy-start.3 = (bf16[1,3,128,128]{3,2,1,0:T(8,128)(2,1)S(1)}, bf16[1,3,128,128]{3,2,1,0:T(8,128)(2,1)}, u32[]{:S(2)}) copy-start(bf16[1,3,128,128]{3,2,1,0:T(8,128)(2,1)} %get-tuple-element.27) | copy-start | bytes 294916
  26.3 8.3 %collective-permute-start.3 = (bf16[1,8,8,384]{3,2,1,0:T(8,128)(2,1)S(1)}, bf16[1,8,8,384]{3,2,1,0:T(8,128)(2,1)S(1)}, u32[]{:S(2)}, u32[]{:S(2)}) collective-permute-start(bf16[1,8,8,384]{3,2,1,0:T(8,128)(2,1)S(1)} %get-tuple-element.207), channel_id=1, source_target_pairs={{1,0},{2,1},{3,2},{4,3},{5,4},{6,5},{7,6},{8,7},{9,8},{10,9},{11,1... | collective-permute-start | bytes 147464 | tf_op jit(solution)/shard_map/ppermute | solution.py:17
  27.6 7.0 %collective-permute-start.2 = (bf16[1,8,8,384]{3,2,1,0:T(8,128)(2,1)S(1)}, bf16[1,8,8,384]{3,2,1,0:T(8,128)(2,1)S(1)}, u32[]{:S(2)}, u32[]{:S(2)}) collective-permute-start(bf16[1,8,8,384]{3,2,1,0:T(8,128)(2,1)S(1)} %get-tuple-element.206), channel_id=1, source_target_pairs={{0,1},{1,2},{2,3},{3,4},{4,5},{5,6},{6,7},{7,8},{8,9},{9,10},{10,1... | collective-permute-start | bytes 147464 | tf_op jit(solution)/shard_map/ppermute | solution.py:14
  39.8 5.5 %collective-permute-start.5 = (bf16[2,4,8,8,256]{4,3,2,1,0:T(8,128)(2,1)S(1)}, bf16[2,4,8,8,256]{4,3,2,1,0:T(8,128)(2,1)S(1)}, u32[]{:S(2)}, u32[]{:S(2)}) collective-permute-start(bf16[2,4,8,8,256]{4,3,2,1,0:T(8,128)(2,1)S(1)} %pad_maximum_fusion.13), channel_id=1, source_target_pairs={{16,0},{17,1},{18,2},{19,3},{20,4},{21,5},{22,6},{23,7},{24,8},{25... | collective-permute-start | bytes 786440 | tf_op jit(solution)/shard_map/ppermute | solution.py:25
  45.0 5.0 %copy-start.21 = (bf16[4,8,8,256]{3,2,1,0:T(8,128)(2,1)S(1)}, bf16[4,8,8,256]{3,2,1,0:T(8,128)(2,1)}, u32[]{:S(2)}) copy-start(bf16[4,8,8,256]{3,2,1,0:T(8,128)(2,1)} %param.10) | copy-start | bytes 393220
  46.0 4.0 %collective-permute-start.4 = (bf16[4,8,8,256]{3,2,1,0:T(8,128)(2,1)S(1)}, bf16[4,8,8,256]{3,2,1,0:T(8,128)(2,1)S(1)}, u32[]{:S(2)}, u32[]{:S(2)}) collective-permute-start(bf16[4,8,8,256]{3,2,1,0:T(8,128)(2,1)S(1)} %get-tuple-element.211), channel_id=1, source_target_pairs={{0,16},{1,17},{2,18},{3,19},{4,20},{5,21},{6,22},{7,23},{8,24},{9,... | collective-permute-start | bytes 393224 | tf_op jit(solution)/shard_map/ppermute | solution.py:25
  50.1 7.1 %collective-permute-start.7 = (bf16[1,8,8,384]{3,2,1,0:T(8,128)(2,1)S(1)}, bf16[1,8,8,384]{3,2,1,0:T(8,128)(2,1)S(1)}, u32[]{:S(2)}, u32[]{:S(2)}) collective-permute-start(bf16[1,8,8,384]{3,2,1,0:T(8,128)(2,1)S(1)} %get-tuple-element.205), channel_id=1, source_target_pairs={{1,0},{2,1},{3,2},{4,3},{5,4},{6,5},{7,6},{8,7},{9,8},{10,9},{11,1... | collective-permute-start | bytes 147464 | tf_op jit(solution)/shard_map/ppermute | solution.py:17
  51.4 7.2 %collective-permute-start.6 = (bf16[1,8,8,384]{3,2,1,0:T(8,128)(2,1)S(1)}, bf16[1,8,8,384]{3,2,1,0:T(8,128)(2,1)S(1)}, u32[]{:S(2)}, u32[]{:S(2)}) collective-permute-start(bf16[1,8,8,384]{3,2,1,0:T(8,128)(2,1)S(1)} %get-tuple-element.204), channel_id=1, source_target_pairs={{0,1},{1,2},{2,3},{3,4},{4,5},{5,6},{6,7},{7,8},{8,9},{9,10},{10,1... | collective-permute-start | bytes 147464 | tf_op jit(solution)/shard_map/ppermute | solution.py:14
  65.9 9.3 %collective-permute-start.9 = (bf16[1,8,8,384]{3,2,1,0:T(8,128)(2,1)S(1)}, bf16[1,8,8,384]{3,2,1,0:T(8,128)(2,1)S(1)}, u32[]{:S(2)}, u32[]{:S(2)}) collective-permute-start(bf16[1,8,8,384]{3,2,1,0:T(8,128)(2,1)S(1)} %get-tuple-element.203), channel_id=1, source_target_pairs={{1,0},{2,1},{3,2},{4,3},{5,4},{6,5},{7,6},{8,7},{9,8},{10,9},{11,1... | collective-permute-start | bytes 147464 | tf_op jit(solution)/shard_map/ppermute | solution.py:17
  67.2 8.0 %collective-permute-start.8 = (bf16[1,8,8,384]{3,2,1,0:T(8,128)(2,1)S(1)}, bf16[1,8,8,384]{3,2,1,0:T(8,128)(2,1)S(1)}, u32[]{:S(2)}, u32[]{:S(2)}) collective-permute-start(bf16[1,8,8,384]{3,2,1,0:T(8,128)(2,1)S(1)} %get-tuple-element.202), channel_id=1, source_target_pairs={{0,1},{1,2},{2,3},{3,4},{4,5},{5,6},{6,7},{7,8},{8,9},{9,10},{10,1... | collective-permute-start | bytes 147464 | tf_op jit(solution)/shard_map/ppermute | solution.py:14
  84.7 13.9 %collective-permute-start.18 = (bf16[2,2,2,144,128]{4,3,1,2,0:T(8,128)(2,1)S(1)}, bf16[2,2,2,144,128]{4,3,1,2,0:T(8,128)(2,1)S(1)}, u32[]{:S(2)}, u32[]{:S(2)}) collective-permute-start(bf16[2,2,2,144,128]{4,3,1,2,0:T(8,128)(2,1)S(1)} %bitcast.960), channel_id=1, source_target_pairs={{0,4},{1,5},{2,6},{3,7},{4,0},{5,1},{6,2},{7,3},{8,12},{9,13},{10,... | collective-permute-start | bytes 884744 | tf_op jit(solution)/shard_map/ppermute | solution.py:117
  93.5 8.2 %collective-permute-start.14 = (bf16[2,2,2,144,128]{4,3,2,0,1:T(8,128)(2,1)S(1)}, bf16[2,2,2,144,128]{4,3,2,0,1:T(8,128)(2,1)S(1)}, u32[]{:S(2)}, u32[]{:S(2)}) collective-permute-start(bf16[2,2,2,144,128]{4,3,2,0,1:T(8,128)(2,1)S(1)} %bitcast.959), channel_id=1, source_target_pairs={{0,2},{1,3},{2,0},{3,1},{4,6},{5,7},{6,4},{7,5},{8,10},{9,11},{10,... | collective-permute-start | bytes 884744 | tf_op jit(solution)/shard_map/ppermute | solution.py:117
  94.2 9.0 %collective-permute-start.10 = (bf16[2,2,2,144,128]{4,3,2,1,0:T(8,128)(2,1)S(1)}, bf16[2,2,2,144,128]{4,3,2,1,0:T(8,128)(2,1)S(1)}, u32[]{:S(2)}, u32[]{:S(2)}) collective-permute-start(bf16[2,2,2,144,128]{4,3,2,1,0:T(8,128)(2,1)S(1)} %dynamic-slice_bitcast_fusion), channel_id=1, source_target_pairs={{0,1},{1,0},{2,3},{3,2},{4,5},{5,4},{6,7},{7,6},{8,9},{9,8},{10,11... | collective-permute-start | bytes 884744 | tf_op jit(solution)/shard_map/ppermute | solution.py:117
  98.7 7.9 %collective-permute-start.19 = (bf16[2,2,144,128]{3,2,0,1:T(8,128)(2,1)S(1)}, bf16[2,2,144,128]{3,2,0,1:T(8,128)(2,1)S(1)}, u32[]{:S(2)}, u32[]{:S(2)}) collective-permute-start(bf16[2,2,144,128]{3,2,0,1:T(8,128)(2,1)S(1)} %dynamic-slice_bitcast_fusion.1), channel_id=1, source_target_pairs={{0,8},{1,9},{2,10},{3,11},{4,12},{5,13},{6,14},{7,15},{8,0},{9,1},... | collective-permute-start | bytes 442376 | tf_op jit(solution)/shard_map/ppermute | solution.py:117
  101.9 7.2 %collective-permute-start.15 = (bf16[2,2,144,128]{3,2,1,0:T(8,128)(2,1)S(1)}, bf16[2,2,144,128]{3,2,1,0:T(8,128)(2,1)S(1)}, u32[]{:S(2)}, u32[]{:S(2)}) collective-permute-start(bf16[2,2,144,128]{3,2,1,0:T(8,128)(2,1)S(1)} %dynamic-slice_bitcast_fusion.2), channel_id=1, source_target_pairs={{0,4},{1,5},{2,6},{3,7},{4,0},{5,1},{6,2},{7,3},{8,12},{9,13},{10,... | collective-permute-start | bytes 442376 | tf_op jit(solution)/shard_map/ppermute | solution.py:117
  103.4 5.8 %collective-permute-start.11 = (bf16[2,2,144,128]{3,2,1,0:T(8,128)(2,1)S(1)}, bf16[2,2,144,128]{3,2,1,0:T(8,128)(2,1)S(1)}, u32[]{:S(2)}, u32[]{:S(2)}) collective-permute-start(bf16[2,2,144,128]{3,2,1,0:T(8,128)(2,1)S(1)} %dynamic-slice_bitcast_fusion.3), channel_id=1, source_target_pairs={{0,2},{1,3},{2,0},{3,1},{4,6},{5,7},{6,4},{7,5},{8,10},{9,11},{10,... | collective-permute-start | bytes 442376 | tf_op jit(solution)/shard_map/ppermute | solution.py:117
  106.6 6.1 %collective-permute-start.20 = (bf16[2,144,128]{2,1,0:T(8,128)(2,1)S(1)}, bf16[2,144,128]{2,1,0:T(8,128)(2,1)S(1)}, u32[]{:S(2)}, u32[]{:S(2)}) collective-permute-start(bf16[2,144,128]{2,1,0:T(8,128)(2,1)S(1)} %dynamic-slice_bitcast_fusion.4), channel_id=1, source_target_pairs={{0,1},{1,0},{2,3},{3,2},{4,5},{5,4},{6,7},{7,6},{8,9},{9,8},{10,11... | collective-permute-start | bytes 221192 | tf_op jit(solution)/shard_map/ppermute | solution.py:117
  109.1 6.3 %collective-permute-start.16 = (bf16[2,144,128]{2,1,0:T(8,128)(2,1)S(1)}, bf16[2,144,128]{2,1,0:T(8,128)(2,1)S(1)}, u32[]{:S(2)}, u32[]{:S(2)}) collective-permute-start(bf16[2,144,128]{2,1,0:T(8,128)(2,1)S(1)} %dynamic-slice_bitcast_fusion.5), channel_id=1, source_target_pairs={{0,8},{1,9},{2,10},{3,11},{4,12},{5,13},{6,14},{7,15},{8,0},{9,1},... | collective-permute-start | bytes 221192 | tf_op jit(solution)/shard_map/ppermute | solution.py:117
  109.3 6.8 %collective-permute-start.12 = (bf16[2,144,128]{2,1,0:T(8,128)(2,1)S(1)}, bf16[2,144,128]{2,1,0:T(8,128)(2,1)S(1)}, u32[]{:S(2)}, u32[]{:S(2)}) collective-permute-start(bf16[2,144,128]{2,1,0:T(8,128)(2,1)S(1)} %dynamic-slice_bitcast_fusion.6), channel_id=1, source_target_pairs={{0,4},{1,5},{2,6},{3,7},{4,0},{5,1},{6,2},{7,3},{8,12},{9,13},{10,... | collective-permute-start | bytes 221192 | tf_op jit(solution)/shard_map/ppermute | solution.py:117
  112.8 4.0 %collective-permute-start.21 = (bf16[144,128]{1,0:T(8,128)(2,1)S(1)}, bf16[144,128]{1,0:T(8,128)(2,1)S(1)}, u32[]{:S(2)}, u32[]{:S(2)}) collective-permute-start(bf16[144,128]{1,0:T(8,128)(2,1)S(1)} %dynamic-slice_bitcast_fusion.7), channel_id=1, source_target_pairs={{0,2},{1,3},{2,0},{3,1},{4,6},{5,7},{6,4},{7,5},{8,10},{9,11},{10,... | collective-permute-start | bytes 110600 | tf_op jit(solution)/shard_map/ppermute | solution.py:117
  115.5 4.0 %collective-permute-start.17 = (bf16[144,128]{1,0:T(8,128)(2,1)S(1)}, bf16[144,128]{1,0:T(8,128)(2,1)S(1)}, u32[]{:S(2)}, u32[]{:S(2)}) collective-permute-start(bf16[144,128]{1,0:T(8,128)(2,1)S(1)} %dynamic-slice_bitcast_fusion.8), channel_id=1, source_target_pairs={{0,1},{1,0},{2,3},{3,2},{4,5},{5,4},{6,7},{7,6},{8,9},{9,8},{10,11... | collective-permute-start | bytes 110600 | tf_op jit(solution)/shard_map/ppermute | solution.py:117
  116.1 4.9 %collective-permute-start.13 = (bf16[144,128]{1,0:T(8,128)(2,1)S(1)}, bf16[144,128]{1,0:T(8,128)(2,1)S(1)}, u32[]{:S(2)}, u32[]{:S(2)}) collective-permute-start(bf16[144,128]{1,0:T(8,128)(2,1)S(1)} %dynamic-slice_bitcast_fusion.9), channel_id=1, source_target_pairs={{0,8},{1,9},{2,10},{3,11},{4,12},{5,13},{6,14},{7,15},{8,0},{9,1},... | collective-permute-start | bytes 110600 | tf_op jit(solution)/shard_map/ppermute | solution.py:117
  (12 other events, 13.6 us)

commit v2 on v1

v2 whole, which is shorter than its diff:
```python
import functools
import math

import jax
import jax.numpy as jnp
from jax import lax
from jax.experimental import pallas as pl
from jax.experimental.pallas import tpu as pltpu
from jax.sharding import PartitionSpec as P

VMEM = pltpu.CompilerParams(vmem_limit_bytes=48 * 1024 * 1024)
F32 = jnp.float32
BF16 = jnp.bfloat16


def half_erf(value):
    return 0.5 * (1.0 + lax.erf(value * 0.7071067811865476))


def smooth_gate(value):
    return value * half_erf(value)


def gate_slope(value, half):
    return half + value * jnp.exp(-0.5 * value * value) * 0.3989422804014327


def fill_shifts(stack, field, ydim, zdim):
    rows, width = field.shape
    cells = field.reshape(rows // zdim, zdim, width)
    depth = lax.broadcasted_iota(jnp.int32, cells.shape, 1)
    before = jnp.where(depth == 0, 0.0, pltpu.roll(cells, 1, 1))
    after = jnp.where(depth == zdim - 1, 0.0, pltpu.roll(cells, zdim - 1, 1))
    for across, moved in enumerate((before, cells, after)):
        moved = moved.reshape(rows // (ydim * zdim), ydim, zdim, width)
        blank = jnp.zeros_like(moved[:, :1])
        shifted = (
            jnp.concatenate([blank, moved[:, :-1]], axis=1),
            moved,
            jnp.concatenate([moved[:, 1:], blank], axis=1),
        )
        for down in range(3):
            at = (3 * down + across) * width
            stack[0:rows, at : at + width] = shifted[down].reshape(rows, width).astype(BF16)


def convolve(stack, weights, rows, plane):
    total = None
    for step in range(3):
        part = jnp.dot(
            stack[step * plane : step * plane + rows, :],
            weights[step],
            preferred_element_type=F32,
        )
        total = part if total is None else total + part
    return total


def pack_edges(state, act, grad, low, high, plane):
    width = state.shape[1] // 2
    cells = state.shape[0]
    left, right = slice(0, width), slice(width, 2 * width)
    for index, (source, half) in enumerate(((state, right), (act, left), (grad, right))):
        at = index * 2 * plane
        low[at : at + 2 * plane, :] = source[0 : 2 * plane, half]
        high[at : at + 2 * plane, :] = source[cells - 2 * plane : cells, half]
    for index, (source, half) in enumerate(((state, left), (act, right), (grad, left))):
        at = (6 + index) * plane
        low[at : at + plane, :] = source[0:plane, half]
        high[at : at + plane, :] = source[cells - plane : cells, half]


def edges_kernel(plane, state, act, grad, low, high):
    pack_edges(state, act, grad, low, high, plane)


def first_kernel(ydim, zdim, flags, state, act, grad, below, above, first, second, second_back,
                 new_one, back_two, mid, back, carry, gate, stack):
    plane = ydim * zdim
    cells, double = state.shape
    width = double // 2
    inner = cells + 2 * plane
    outer = cells + 4 * plane
    left, right = slice(0, width), slice(width, double)

    def two(source, half, index):
        at = index * 2 * plane
        return jnp.concatenate(
            [below[at : at + 2 * plane, :], source[:, half], above[at : at + 2 * plane, :]], axis=0
        ).astype(F32)

    def one(source, half, index):
        at = (6 + index) * plane
        return jnp.concatenate(
            [below[at : at + plane, :], source[:, half], above[at : at + plane, :]], axis=0
        ).astype(F32)

    low_flag, high_flag = flags[0], flags[1]

    def store_masked(ref, value):
        ref[0:plane, :] = (value[0:plane].astype(F32) * low_flag).astype(BF16)
        ref[plane : plane + cells, :] = value[plane : plane + cells]
        ref[plane + cells : inner, :] = (value[plane + cells :].astype(F32) * high_flag).astype(BF16)

    core = slice(plane, plane + cells)
    fill_shifts(stack, smooth_gate(two(state, right, 0)), ydim, zdim)
    f_one = (one(state, left, 0) + convolve(stack, first, inner, plane)).astype(BF16)
    new_one[...] = f_one[core]
    store_masked(mid, smooth_gate(f_one.astype(F32)).astype(BF16))

    y_one = two(act, left, 1)
    half = half_erf(y_one)
    gated = y_one * half
    gate[...] = gated[plane : plane + inner].astype(BF16)
    fill_shifts(stack, gated, ydim, zdim)
    r_two = (one(act, right, 1) - convolve(stack, second, inner, plane)).astype(BF16)
    back_two[...] = r_two[core]
    store_masked(back, smooth_gate(r_two.astype(F32)).astype(BF16))

    fill_shifts(stack, two(grad, right, 2), ydim, zdim)
    slope = gate_slope(y_one[plane : plane + inner], half[plane : plane + inner])
    e_one = (one(grad, left, 2) + slope * convolve(stack, second_back, inner, plane)).astype(BF16)
    store_masked(carry, e_one)


def second_kernel(ydim, zdim, state, act, grad, new_one, back_two, mid, back, carry, first, second,
                  first_back, forward, rebuilt, passed, stack):
    plane = ydim * zdim
    cells, double = state.shape
    width = double // 2
    left, right = slice(0, width), slice(width, double)
    forward[:, left] = new_one[...]
    rebuilt[:, right] = back_two[...]
    passed[:, left] = carry[plane : plane + cells, :]

    fill_shifts(stack, back[...].astype(F32), ydim, zdim)
    rebuilt[:, left] = (
        act[:, left].astype(F32) - convolve(stack, first, cells, plane)
    ).astype(BF16)
    fill_shifts(stack, carry[...].astype(F32), ydim, zdim)
    r_two = back_two[...].astype(F32)
    passed[:, right] = (
        grad[:, right].astype(F32)
        + gate_slope(r_two, half_erf(r_two)) * convolve(stack, first_back, cells, plane)
    ).astype(BF16)
    fill_shifts(stack, mid[...].astype(F32), ydim, zdim)
    forward[:, right] = (
        state[:, right].astype(F32) + convolve(stack, second, cells, plane)
    ).astype(BF16)


def correlate(stack, field, cotangent, ydim, zdim, emit):
    plane = ydim * zdim
    cells, width = cotangent.shape
    fill_shifts(stack, cotangent, ydim, zdim)
    for step in range(3):
        product = lax.dot_general(
            field[step * plane : step * plane + cells, :],
            stack[0:cells, :],
            (((0,), (0,)), ((), ())),
            preferred_element_type=F32,
        )
        for place in range(9):
            emit(9 * step + 8 - place, product[:, place * width : (place + 1) * width])


def corr_kernel(ydim, zdim, factor, last, *refs):
    if last:
        grad, back, carry, gate, so_far, out, stack = refs
    else:
        grad, back, carry, gate, out, stack = refs
    plane = ydim * zdim
    cells, double = grad.shape
    width = double // 2

    def store(which):
        def emit(k, block):
            at = slice(k * width, (k + 1) * width)
            if last:
                out[which, at, :] = ((block + so_far[which, at, :]) * factor).astype(out.dtype)
            else:
                out[which, at, :] = block

        return emit

    own = carry[plane : plane + cells, :].astype(F32)
    correlate(stack, back, own, ydim, zdim, store(0))
    correlate(stack, gate, grad[:, width:].astype(F32), ydim, zdim, store(1))


def whole(count):
    return [pl.BlockSpec(memory_space=pltpu.VMEM)] * count


def reduce_blocks(grads):
    count = lax.axis_size("space")
    bits = [1 << level for level in range(count.bit_length() - 1)]
    spot = lax.axis_index("space")
    rows = grads.shape[1]
    ways = 3 if rows % 3 == 0 else 1
    span = rows // ways
    parts = []
    for way in range(ways):
        shift = way % len(bits)
        order = bits[shift:] + bits[:shift]
        part = grads[:, way * span : (way + 1) * span].reshape(
            [2] * len(bits) + [span, grads.shape[2]]
        )
        parts.append((part, order))
    for step in range(len(bits)):
        fresh_parts = []
        for part, order in parts:
            bit = order[step]
            left = sorted(order[step:], reverse=True)
            axis = left.index(bit)
            mine = (spot // bit) % 2
            keep = lax.dynamic_index_in_dim(part, mine, axis, keepdims=False)
            send = lax.dynamic_index_in_dim(part, 1 - mine, axis, keepdims=False)
            got = lax.ppermute(send, "space", [(i, i ^ bit) for i in range(count)])
            total = keep.astype(jnp.float32) + got.astype(jnp.float32)
            if step < len(bits) - 1:
                total = total.astype(jnp.bfloat16)
            fresh_parts.append((total, order))
        parts = fresh_parts
    return jnp.concatenate([part for part, _ in parts], axis=0)


def shards(fwd_in, bwd_act, bwd_grad, fresh, target, w_first, w_second):
    width = w_first.shape[2]
    layers, ydim, zdim = fwd_in.shape[1:4]
    plane = ydim * zdim
    cells = layers * plane
    shape = fwd_in.shape[1:]
    flat = lambda block: block.reshape(cells, 2 * width)
    first = w_first[0].reshape(3, 9 * width, width)
    second = w_second[0].reshape(3, 9 * width, width)
    first_back = jnp.transpose(w_first[0][::-1], (0, 2, 1)).reshape(3, 9 * width, width)
    second_back = jnp.transpose(w_second[0][::-1], (0, 2, 1)).reshape(3, 9 * width, width)
    last_section = lax.axis_size("section") - 1
    place = lax.axis_index("section")
    count = lax.axis_size("space")
    spot = lax.axis_index("space")
    flags = jnp.stack([spot > 0, spot < count - 1]).astype(F32)
    up = [(i, i + 1) for i in range(count - 1)]
    down = [(i + 1, i) for i in range(count - 1)]
    array = jax.ShapeDtypeStruct
    edge = array((9 * plane, width), BF16)
    tile = array((cells, width), BF16)
    wide = array((cells + 2 * plane, width), BF16)
    state_shape = array((cells, 2 * width), BF16)
    offsets = 27 * width

    def exchange(low, high):
        below = lax.ppermute(high, "space", up)
        above = lax.ppermute(low, "space", down)
        return below, above

    def edges(state, act, grad):
        return pl.pallas_call(
            functools.partial(edges_kernel, plane),
            out_shape=(edge, edge),
            in_specs=whole(3),
            out_specs=tuple(whole(2)),
            compiler_params=VMEM,
            name="edges",
        )(state, act, grad)

    def tick_first(state, act, grad, below, above):
        return pl.pallas_call(
            functools.partial(first_kernel, ydim, zdim),
            out_shape=(tile, tile, wide, wide, wide, wide),
            in_specs=[pl.BlockSpec(memory_space=pltpu.SMEM)] + whole(8),
            out_specs=tuple(whole(6)),
            scratch_shapes=[pltpu.VMEM((cells + 4 * plane, 9 * width), BF16)],
            compiler_params=VMEM,
            name="tick_first",
        )(flags, state, act, grad, below, above, first, second, second_back)

    def tick_second(state, act, grad, made):
        new_one, back_two, mid, back, carry, _ = made
        return pl.pallas_call(
            functools.partial(second_kernel, ydim, zdim),
            out_shape=(state_shape,) * 3,
            in_specs=whole(11),
            out_specs=tuple(whole(3)),
            scratch_shapes=[pltpu.VMEM((cells + 2 * plane, 9 * width), BF16)],
            compiler_params=VMEM,
            name="tick_second",
        )(state, act, grad, new_one, back_two, mid, back, carry, first, second, first_back)

    def weight_grads(grad, made, so_far, factor):
        last = so_far is not None
        extra = (so_far,) if last else ()
        return pl.pallas_call(
            functools.partial(corr_kernel, ydim, zdim, factor, last),
            out_shape=array((2, offsets, width), BF16 if last else F32),
            in_specs=whole(4 + len(extra)),
            out_specs=whole(1)[0],
            scratch_shapes=[pltpu.VMEM((cells, 9 * width), BF16)],
            compiler_params=VMEM,
            name="weight_grads",
        )(grad, made[3], made[4], made[5], *extra)

    state, act, grad = flat(fwd_in), flat(bwd_act), flat(bwd_grad)
    below, above = exchange(*edges(state, act, grad))
    made_one = tick_first(state, act, grad, below, above)
    forward, rebuilt, passed = tick_second(state, act, grad, made_one)
    lifted = lax.ppermute(forward, "section", [(s, s + 1) for s in range(last_section)])
    lowered = lax.ppermute(
        jnp.stack([rebuilt, passed]), "section", [(s + 1, s) for s in range(last_section)]
    )
    own_grad = (forward.astype(F32) - flat(target).astype(F32)).astype(BF16)
    state_two = jnp.where(place == 0, flat(fresh), lifted)
    act_two = jnp.where(place == last_section, forward, lowered[0])
    grad_two = jnp.where(place == last_section, own_grad, lowered[1])
    below, above = exchange(*edges(state_two, act_two, grad_two))
    so_far = weight_grads(grad, made_one, None, None)
    made_two = tick_first(state_two, act_two, grad_two, below, above)
    cell_total = cells * count
    sums = weight_grads(grad_two, made_two, so_far, 1.0 / math.sqrt(cell_total))
    forward, rebuilt, passed = tick_second(state_two, act_two, grad_two, made_two)
    blocks = jnp.concatenate([sums[0].reshape(count, -1, width), sums[1].reshape(count, -1, width)], axis=1)
    total = reduce_blocks(blocks)
    rows = total.shape[0] // 2
    return (
        forward.reshape((1,) + shape),
        rebuilt.reshape((1,) + shape),
        passed.reshape((1,) + shape),
        total[:rows][None],
        total[rows:][None],
    )


def solution(mesh):
    placed = (
        P("section", "space", None, None, None),
        P("section", "space", None, None, None),
        P("section", "space", None, None, None),
        P("space", None, None, None),
        P("space", None, None, None),
        P("section", None, None, None),
        P("section", None, None, None),
    )
    return jax.shard_map(
        shards,
        mesh=mesh,
        in_specs=placed,
        out_specs=(
            P("section", "space", None, None, None),
            P("section", "space", None, None, None),
            P("section", "space", None, None, None),
            P("section", "space", None),
            P("section", "space", None),
        ),
        check_vma=False,
    )
```

time: 122 us -> 91.3 us (0.75)
  matrix products: 30.6 us -> 0 us
  starting transfers between devices: 51.8 us -> 35.6 us
  Pallas kernels: 0 us -> 14.8 us
  local copies, waits for them, and re-layouts: 11.8 us -> 18.9 us
  other arithmetic: 9 us -> 6.3 us
  between operations: 2.89 us -> 1.19 us
  waiting for transfers between devices: 15.6 us -> 13.9 us
    dot_general x144 -> x0, matrix products: 30.6 us -> none  [the longest x108 21.3 us: convolve(): jnp.dot(block, wide[across * 3 + down], preferred_element_type=jnp.float32)]
    ppermute x10 -> x6, starting transfers between devices: 31.9 us -> 15.7 us  [the longest x2 9.75 us: exchange(): below = lax.ppermute(high, 'space', up)]
    pallas_call x0 -> x8, Pallas kernels: none -> 14.8 us  [the longest x2 6.89 us: tick_first(): pl.pallas_call(functools.partial(first_kernel, ydim, zdim), out_shape=(ti...]
    slice x22 -> x1, local copies, waits for them, and re-layouts: 6.87 us -> 0.12 us  [shards(): sums[0].reshape(count, -1, width)]
    unnamed x46 -> x72, local copies, waits for them, and re-layouts: 4.48 us -> 10.5 us
    transpose x2 -> x4, local copies, waits for them, and re-layouts: 0.17 us -> 5.49 us  [the longest x2 2.94 us: shards(): jnp.transpose(w_first[0][::-1], (0, 2, 1)).reshape(3, 9 * width, width)]
    ppermute x12, waiting for transfers between devices: 13.2 us -> 8.64 us  [reduce_blocks(): got = lax.ppermute(send, 'space', [(i, i ^ bit) for i in range(count)])]
    ppermute x10 -> x6, waiting for transfers between devices: 2.4 us -> 5.23 us  [the longest x2 3.72 us: exchange(): above = lax.ppermute(low, 'space', down)]
  transfers between devices with their start and end apart: 22 -> 18, of which waited for: 10 -> 8; matrix products, arithmetic and copies ran while one was open for 14% -> 11% of each run, Pallas kernels for 0% -> 3%
where the time goes in v2:
time: 91.3 us; the launch traced here: 90.6 us
  starting transfers between devices  35.6 us (39%)
  local copies, waits for them, and re-layouts  18.9 us (21%)
  Pallas kernels  14.8 us (16%)
  waiting for transfers between devices  13.9 us (15%)
  other arithmetic  6.3 us (7%)
  between operations  1.19 us (1%)
    ppermute x12, starting transfers between devices, reduce_blocks(): got = lax.ppermute(send, 'space', [(i, i ^ bit) for i in range(count)])  19.9 us
    unnamed x72, local copies, waits for them, and re-layouts  10.5 us
    ppermute x2, starting transfers between devices, exchange(): below = lax.ppermute(high, 'space', up)  9.75 us
    ppermute x12, waiting for transfers between devices, reduce_blocks(): got = lax.ppermute(send, 'space', [(i, i ^ bit) for i in range(count)])  8.64 us
    pallas_call x2, Pallas kernels, tick_first(): pl.pallas_call(functools.partial(first_kernel, ydim, zdim), out_shape=(ti...  6.89 us
    pallas_call x2, Pallas kernels, tick_second(): pl.pallas_call(functools.partial(second_kernel, ydim, zdim), out_shape=(s...  4.66 us
    ppermute x2, waiting for transfers between devices, exchange(): above = lax.ppermute(low, 'space', down)  3.72 us
    transpose x2, local copies, waits for them, and re-layouts, shards(): jnp.transpose(w_first[0][::-1], (0, 2, 1)).reshape(3, 9 * width, width)  2.94 us
  transfers between devices with their start and end apart: 18, of which 8 were waited for; matrix products, arithmetic and copies ran while one was open for 11% of the time, Pallas kernels for 3%

profile of v2, /device:TPU:0, one launch (start us, length us, event | category | flops | bytes accessed | tf_op | source)
XLA Modules:
  0.0 90.6 jit_solution(1339557040095154065)
XLA Ops:
  4.2 5.5 %collective-permute-start = (bf16[576,128]{1,0:T(8,128)(2,1)}, bf16[576,128]{1,0:T(8,128)(2,1)}, u32[]{:S(2)}, u32[]{:S(2)}) collective-permute-start(bf16[576,128]{1,0:T(8,128)(2,1)} %get-tuple-element.27), channel_id=1, source_target_pairs={{0,1},{1,2},{2,3},{3,4},{4,5},{5,6},{6,7},{7,8},{8,9},{9,10},{10,1... | collective-permute-start | bytes 442376 | tf_op jit(solution)/shard_map/ppermute | solution.py:254
  9.7 1.3 %collective-permute-start.1 = (bf16[576,128]{1,0:T(8,128)(2,1)}, bf16[576,128]{1,0:T(8,128)(2,1)}, u32[]{:S(2)}, u32[]{:S(2)}) collective-permute-start(bf16[576,128]{1,0:T(8,128)(2,1)} %get-tuple-element.28), channel_id=1, source_target_pairs={{1,0},{2,1},{3,2},{4,3},{5,4},{6,5},{7,6},{8,7},{9,8},{10,9},{11,1... | collective-permute-start | bytes 442376 | tf_op jit(solution)/shard_map/ppermute | solution.py:255
  11.0 1.3 %reverse_bitcast_fusion.1 = bf16[27,128,128]{1,2,0:T(8,128)(2,1)S(1)} fusion(bf16[27,128,128]{2,1,0:T(8,128)(2,1)} %bitcast.113), kind=kLoop, calls=%fused_computation.1 | loop fusion | bytes 1769472 | tf_op jit(solution)/shard_map/transpose | solution.py:238
  12.3 1.0 %reverse_bitcast_fusion = bf16[27,128,128]{1,2,0:T(8,128)(2,1)} fusion(bf16[27,128,128]{2,1,0:T(8,128)(2,1)S(1)} %bitcast.108), kind=kLoop, calls=%fused_computation | loop fusion | bytes 1769472 | tf_op jit(solution)/shard_map/transpose | solution.py:237
  13.3 1.3 %copy.14 = bf16[27,128,128]{2,1,0:T(8,128)(2,1)S(1)} copy(bf16[27,128,128]{1,2,0:T(8,128)(2,1)S(1)} %reverse_bitcast_fusion.1) | data formatting | bytes 1769472 | tf_op jit(solution)/shard_map/transpose | solution.py:238
  14.6 1.9 %copy.15 = bf16[27,128,128]{2,1,0:T(8,128)(2,1)S(1)} copy(bf16[27,128,128]{1,2,0:T(8,128)(2,1)} %reverse_bitcast_fusion) | data formatting | bytes 1769472 | tf_op jit(solution)/shard_map/transpose | solution.py:237
  20.3 3.4 %tick_first.2 = (bf16[256,128]{1,0:T(8,128)(2,1)S(1)}, bf16[256,128]{1,0:T(8,128)(2,1)S(1)}, bf16[384,128]{1,0:T(8,128)(2,1)S(1)}, bf16[384,128]{1,0:T(8,128)(2,...) custom-call(f32[2]{0:T(128)S(1)} %add_convert_fusion.flags, bf16[256,256]{1,0:T(8,128)(2,1)S(1)} %bitcast.127, ...), custom_call_target="tpu_custom_call" | custom-call | tf_op jit(solution)/shard_map/tick_first/pallas_call | solution.py:269
  24.4 2.3 %tick_second.2 = (bf16[256,256]{1,0:T(8,128)(2,1)}, bf16[256,256]{1,0:T(8,128)(2,1)S(1)}, bf16[256,256]{1,0:T(8,128)(2,1)S(1)}) custom-call(bf16[256,256]{1,0:T(8,128)(2,1)S(1)} %bitcast.128, bf16[256,256]{1,0:T(8,128)(2,1)S(1)} %bitcast.131, bf16[256,256]{1,0:T(8,128)(2,1)S(1)} %bitcast.124, bf16[256,128]{1,0:T(8,128)(2,1)S(1)} %get-tuple-element.29.new_one, ...), custom_call_target="tpu_custom_call" | custom-call | tf_op jit(solution)/shard_map/tick_second/pallas_call | solution.py:281
  26.7 1.9 %collective-permute-start.2 = (bf16[256,256]{1,0:T(8,128)(2,1)}, bf16[256,256]{1,0:T(8,128)(2,1)}, u32[]{:S(2)}, u32[]{:S(2)}) collective-permute-start(bf16[256,256]{1,0:T(8,128)(2,1)} %get-tuple-element.34), channel_id=1, source_target_pairs={{0,16},{1,17},{2,18},{3,19},{4,20},{5,21},{6,22},{7,23},{8,24},{9,... | collective-permute-start | bytes 393224 | tf_op jit(solution)/shard_map/ppermute | solution.py:308
  29.4 1.3 %collective-permute-start.3 = (bf16[2,256,256]{2,1,0:T(8,128)(2,1)}, bf16[2,256,256]{2,1,0:T(8,128)(2,1)}, u32[]{:S(2)}, u32[]{:S(2)}) collective-permute-start(bf16[2,256,256]{2,1,0:T(8,128)(2,1)} %pad_maximum_fusion.1), channel_id=1, source_target_pairs={{16,0},{17,1},{18,2},{19,3},{20,4},{21,5},{22,6},{23,7},{24,8},{25... | collective-permute-start | bytes 786440 | tf_op jit(solution)/shard_map/ppermute | solution.py:309
  31.6 1.5 %collective-permute-done.3 = bf16[2,256,256]{2,1,0:T(8,128)(2,1)} collective-permute-done((bf16[2,256,256]{2,1,0:T(8,128)(2,1)}, bf16[2,256,256]{2,1,0:T(8,128)(2,1)}, u32[]{:S(2)}, u32[]{:S(2)}) %collective-permute-start.3) | collective-permute-done | bytes 262176 | tf_op jit(solution)/shard_map/ppermute | solution.py:309
  33.1 1.2 %fusion.10 = (bf16[256,256]{1,0:T(8,128)(2,1)S(1)}, bf16[256,256]{1,0:T(8,128)(2,1)S(1)}) fusion(bf16[256,256]{1,0:T(8,128)(2,1)} %get-tuple-element.34, bf16[2,256,256]{2,1,0:T(8,128)(2,1)} %collective-permute-done.3, bf16[4,8,8,256]{3,2,1,0:T(8,128)(2,1)} %param.11, pred[]{:T(512)S(6)} %eq.21), kind=kLoop, calls=%fused_computation.32 | loop fusion | flops 393216 | bytes 786433 | tf_op jit(solution)/shard_map/jit(_where)/select_n | solution.py:315
  35.8 4.3 %collective-permute-start.4 = (bf16[576,128]{1,0:T(8,128)(2,1)}, bf16[576,128]{1,0:T(8,128)(2,1)}, u32[]{:S(2)}, u32[]{:S(2)}) collective-permute-start(bf16[576,128]{1,0:T(8,128)(2,1)} %get-tuple-element.37), channel_id=1, source_target_pairs={{0,1},{1,2},{2,3},{3,4},{4,5},{5,6},{6,7},{7,8},{8,9},{9,10},{10,1... | collective-permute-start | bytes 442376 | tf_op jit(solution)/shard_map/ppermute | solution.py:254
  40.1 1.5 %collective-permute-start.5 = (bf16[576,128]{1,0:T(8,128)(2,1)}, bf16[576,128]{1,0:T(8,128)(2,1)}, u32[]{:S(2)}, u32[]{:S(2)}) collective-permute-start(bf16[576,128]{1,0:T(8,128)(2,1)} %get-tuple-element.38), channel_id=1, source_target_pairs={{1,0},{2,1},{3,2},{4,3},{5,4},{6,5},{7,6},{8,7},{9,8},{10,9},{11,1... | collective-permute-start | bytes 442376 | tf_op jit(solution)/shard_map/ppermute | solution.py:255
  46.0 2.8 %collective-permute-done.5.above = bf16[576,128]{1,0:T(8,128)(2,1)} collective-permute-done((bf16[576,128]{1,0:T(8,128)(2,1)}, bf16[576,128]{1,0:T(8,128)(2,1)}, u32[]{:S(2)}, u32[]{:S(2)}) %collective-permute-start.5) | collective-permute-done | bytes 147488 | tf_op jit(solution)/shard_map/ppermute | solution.py:255
  48.8 3.4 %tick_first.3 = (bf16[256,128]{1,0:T(8,128)(2,1)S(1)}, bf16[256,128]{1,0:T(8,128)(2,1)S(1)}, bf16[384,128]{1,0:T(8,128)(2,1)S(1)}, bf16[384,128]{1,0:T(8,128)(2,...) custom-call(f32[2]{0:T(128)S(1)} %add_convert_fusion.flags, bf16[256,256]{1,0:T(8,128)(2,1)S(1)} %copy-done.9, ...), custom_call_target="tpu_custom_call" | custom-call | tf_op jit(solution)/shard_map/tick_first/pallas_call | solution.py:269
  53.3 1.2 %fusion.15 = (bf16[16,144,128]{2,1,0:T(8,128)(2,1)S(1)}, bf16[16,144,128]{2,1,0:T(8,128)(2,1)}, bf16[16,144,128]{2,1,0:T(8,128)(2,1)}) fusion(bf16[16,216,128]{2,1,0:T(8,128)(2,1)S(1)} %bitcast.135, bf16[16,216,128]{2,1,0:T(8,128)(2,1)S(1)} %bitcast.134), kind=kLoop, calls=%fused_computation.56 | loop fusion | flops 1179648 | bytes 4718592 | tf_op jit(solution)/shard_map/slice | solution.py:206
  56.1 2.4 %collective-permute-start.14 = (bf16[2,2,2,144,128]{4,3,1,2,0:T(8,128)(2,1)}, bf16[2,2,2,144,128]{4,3,1,2,0:T(8,128)(2,1)}, u32[]{:S(2)}, u32[]{:S(2)}) collective-permute-start(bf16[2,2,2,144,128]{4,3,1,2,0:T(8,128)(2,1)} %bitcast.106), channel_id=1, source_target_pairs={{0,4},{1,5},{2,6},{3,7},{4,0},{5,1},{6,2},{7,3},{8,12},{9,13},{10,... | collective-permute-start | bytes 884744 | tf_op jit(solution)/shard_map/ppermute | solution.py:219
  58.5 1.2 %constant_dynamic-slice_fusion.3 = (bf16[2,2,1,2,144,128]{5,4,3,2,1,0:T(8,128)(2,1)S(1)}, bf16[2,2,1,2,144,128]{5,4,3,2,1,0:T(8,128)(2,1)S(1)}) fusion(bf16[2,2,2,2,144,128]{5,4,3,2,1,0:T(8,128)(2,1)} %bitcast.138, s32[]{:T(128)S(6)} %select_n.131, s32[]{:T(128)S(6)} %select_n.132), kind=kLoop, calls=%fused_computation.53 | loop fusion | bytes 1179656 | tf_op jit(solution)/shard_map/jit(dynamic_index_in_dim)/dynamic_slice | solution.py:217
  59.7 1.5 %collective-permute-start.10 = (bf16[2,2,2,144,128]{4,3,2,0,1:T(8,128)(2,1)S(1)}, bf16[2,2,2,144,128]{4,3,2,0,1:T(8,128)(2,1)S(1)}, u32[]{:S(2)}, u32[]{:S(2)}) collective-permute-start(bf16[2,2,2,144,128]{4,3,2,0,1:T(8,128)(2,1)S(1)} %bitcast.140), channel_id=1, source_target_pairs={{0,2},{1,3},{2,0},{3,1},{4,6},{5,7},{6,4},{7,5},{8,10},{9,11},{10,... | collective-permute-start | bytes 884744 | tf_op jit(solution)/shard_map/ppermute | solution.py:219
  61.2 2.5 %collective-permute-start.6 = (bf16[2,2,2,144,128]{4,3,2,1,0:T(8,128)(2,1)S(1)}, bf16[2,2,2,144,128]{4,3,2,1,0:T(8,128)(2,1)S(1)}, u32[]{:S(2)}, u32[]{:S(2)}) collective-permute-start(bf16[2,2,2,144,128]{4,3,2,1,0:T(8,128)(2,1)S(1)} %dynamic-slice_bitcast_fusion), channel_id=1, source_target_pairs={{0,1},{1,0},{2,3},{3,2},{4,5},{5,4},{6,7},{7,6},{8,9},{9,8},{10,11... | collective-permute-start | bytes 884744 | tf_op jit(solution)/shard_map/ppermute | solution.py:219
  63.8 2.3 %tick_second.3 = (bf16[256,256]{1,0:T(8,128)(2,1)}, bf16[256,256]{1,0:T(8,128)(2,1)}, bf16[256,256]{1,0:T(8,128)(2,1)}) custom-call(bf16[256,256]{1,0:T(8,128)(2,1)S(1)} %copy-done.10, bf16[256,256]{1,0:T(8,128)(2,1)S(1)} %copy-done.13, bf16[256,256]{1,0:T(8,128)(2,1)S(1)} %copy-done.4, bf16[256,128]{1,0:T(8,128)(2,1)S(1)} %copy-done.31, ...), custom_call_target="tpu_custom_call" | custom-call | tf_op jit(solution)/shard_map/tick_second/pallas_call | solution.py:281
  67.2 2.6 %collective-permute-start.15 = (bf16[2,2,144,128]{3,2,0,1:T(8,128)(2,1)S(1)}, bf16[2,2,144,128]{3,2,0,1:T(8,128)(2,1)S(1)}, u32[]{:S(2)}, u32[]{:S(2)}) collective-permute-start(bf16[2,2,144,128]{3,2,0,1:T(8,128)(2,1)S(1)} %dynamic-slice_bitcast_fusion.1), channel_id=1, source_target_pairs={{0,8},{1,9},{2,10},{3,11},{4,12},{5,13},{6,14},{7,15},{8,0},{9,1},... | collective-permute-start | bytes 442376 | tf_op jit(solution)/shard_map/ppermute | solution.py:219
  69.9 1.6 %collective-permute-start.11 = (bf16[2,2,144,128]{3,2,1,0:T(8,128)(2,1)S(1)}, bf16[2,2,144,128]{3,2,1,0:T(8,128)(2,1)S(1)}, u32[]{:S(2)}, u32[]{:S(2)}) collective-permute-start(bf16[2,2,144,128]{3,2,1,0:T(8,128)(2,1)S(1)} %dynamic-slice_bitcast_fusion.2), channel_id=1, source_target_pairs={{0,4},{1,5},{2,6},{3,7},{4,0},{5,1},{6,2},{7,3},{8,12},{9,13},{10,... | collective-permute-start | bytes 442376 | tf_op jit(solution)/shard_map/ppermute | solution.py:219
  71.6 1.7 %collective-permute-start.7 = (bf16[2,2,144,128]{3,2,1,0:T(8,128)(2,1)S(1)}, bf16[2,2,144,128]{3,2,1,0:T(8,128)(2,1)S(1)}, u32[]{:S(2)}, u32[]{:S(2)}) collective-permute-start(bf16[2,2,144,128]{3,2,1,0:T(8,128)(2,1)S(1)} %dynamic-slice_bitcast_fusion.3), channel_id=1, source_target_pairs={{0,2},{1,3},{2,0},{3,1},{4,6},{5,7},{6,4},{7,5},{8,10},{9,11},{10,... | collective-permute-start | bytes 442376 | tf_op jit(solution)/shard_map/ppermute | solution.py:219
  73.3 2.9 %collective-permute-done.15 = bf16[2,2,144,128]{3,2,0,1:T(8,128)(2,1)S(1)} collective-permute-done((bf16[2,2,144,128]{3,2,0,1:T(8,128)(2,1)S(1)}, bf16[2,2,144,128]{3,2,0,1:T(8,128)(2,1)S(1)}, u32[]{:S(2)}, u32[]{:S(2)}) %collective-permute-start.15) | collective-permute-done | bytes 147488 | tf_op jit(solution)/shard_map/ppermute | solution.py:219
  77.0 1.2 %collective-permute-start.12 = (bf16[2,144,128]{2,1,0:T(8,128)(2,1)S(1)}, bf16[2,144,128]{2,1,0:T(8,128)(2,1)S(1)}, u32[]{:S(2)}, u32[]{:S(2)}) collective-permute-start(bf16[2,144,128]{2,1,0:T(8,128)(2,1)S(1)} %dynamic-slice_bitcast_fusion.5), channel_id=1, source_target_pairs={{0,8},{1,9},{2,10},{3,11},{4,12},{5,13},{6,14},{7,15},{8,0},{9,1},... | collective-permute-start | bytes 221192 | tf_op jit(solution)/shard_map/ppermute | solution.py:219
  78.2 2.3 %collective-permute-start.8 = (bf16[2,144,128]{2,1,0:T(8,128)(2,1)S(1)}, bf16[2,144,128]{2,1,0:T(8,128)(2,1)S(1)}, u32[]{:S(2)}, u32[]{:S(2)}) collective-permute-start(bf16[2,144,128]{2,1,0:T(8,128)(2,1)S(1)} %dynamic-slice_bitcast_fusion.6), channel_id=1, source_target_pairs={{0,4},{1,5},{2,6},{3,7},{4,0},{5,1},{6,2},{7,3},{8,12},{9,13},{10,... | collective-permute-start | bytes 221192 | tf_op jit(solution)/shard_map/ppermute | solution.py:219
  80.7 1.9 %collective-permute-start.17 = (bf16[144,128]{1,0:T(8,128)(2,1)S(1)}, bf16[144,128]{1,0:T(8,128)(2,1)S(1)}, u32[]{:S(2)}, u32[]{:S(2)}) collective-permute-start(bf16[144,128]{1,0:T(8,128)(2,1)S(1)} %dynamic-slice_bitcast_fusion.7), channel_id=1, source_target_pairs={{0,2},{1,3},{2,0},{3,1},{4,6},{5,7},{6,4},{7,5},{8,10},{9,11},{10,... | collective-permute-start | bytes 110600 | tf_op jit(solution)/shard_map/ppermute | solution.py:219
  83.2 1.5 %collective-permute-start.13 = (bf16[144,128]{1,0:T(8,128)(2,1)S(1)}, bf16[144,128]{1,0:T(8,128)(2,1)S(1)}, u32[]{:S(2)}, u32[]{:S(2)}) collective-permute-start(bf16[144,128]{1,0:T(8,128)(2,1)S(1)} %dynamic-slice_bitcast_fusion.8), channel_id=1, source_target_pairs={{0,1},{1,0},{2,3},{3,2},{4,5},{5,4},{6,7},{7,6},{8,9},{9,8},{10,11... | collective-permute-start | bytes 110600 | tf_op jit(solution)/shard_map/ppermute | solution.py:219
  84.9 2.3 %collective-permute-done.13 = bf16[144,128]{1,0:T(8,128)(2,1)S(1)} collective-permute-done((bf16[144,128]{1,0:T(8,128)(2,1)S(1)}, bf16[144,128]{1,0:T(8,128)(2,1)S(1)}, u32[]{:S(2)}, u32[]{:S(2)}) %collective-permute-start.13) | collective-permute-done | bytes 36896 | tf_op jit(solution)/shard_map/ppermute | solution.py:219
  87.3 2.6 %collective-permute-done.9 = bf16[144,128]{1,0:T(8,128)(2,1)S(1)} collective-permute-done((bf16[144,128]{1,0:T(8,128)(2,1)S(1)}, bf16[144,128]{1,0:T(8,128)(2,1)S(1)}, u32[]{:S(2)}, u32[]{:S(2)}) %collective-permute-start.9) | collective-permute-done | bytes 36896 | tf_op jit(solution)/shard_map/ppermute | solution.py:219
  (121 shorter events, 21.8 us)
Async XLA Ops:
  0.6 11.6 %copy-start = (bf16[1,27,128,128]{3,2,1,0:T(8,128)(2,1)S(1)}, bf16[1,27,128,128]{3,2,1,0:T(8,128)(2,1)}, u32[]{:S(2)}) copy-start(bf16[1,27,128,128]{3,2,1,0:T(8,128)(2,1)} %param.12) | copy-start | bytes 2654212
  4.2 12.4 %collective-permute-start = (bf16[576,128]{1,0:T(8,128)(2,1)}, bf16[576,128]{1,0:T(8,128)(2,1)}, u32[]{:S(2)}, u32[]{:S(2)}) collective-permute-start(bf16[576,128]{1,0:T(8,128)(2,1)} %get-tuple-element.27), channel_id=1, source_target_pairs={{0,1},{1,2},{2,3},{3,4},{4,5},{5,6},{6,7},{7,8},{8,9},{9,10},{10,1... | collective-permute-start | bytes 442376 | tf_op jit(solution)/shard_map/ppermute | solution.py:254
  9.7 7.9 %collective-permute-start.1 = (bf16[576,128]{1,0:T(8,128)(2,1)}, bf16[576,128]{1,0:T(8,128)(2,1)}, u32[]{:S(2)}, u32[]{:S(2)}) collective-permute-start(bf16[576,128]{1,0:T(8,128)(2,1)} %get-tuple-element.28), channel_id=1, source_target_pairs={{1,0},{2,1},{3,2},{4,3},{5,4},{6,5},{7,6},{8,7},{9,8},{10,9},{11,1... | collective-permute-start | bytes 442376 | tf_op jit(solution)/shard_map/ppermute | solution.py:255
  13.3 4.3 %copy-start.1 = (bf16[1,27,128,128]{3,2,1,0:T(8,128)(2,1)S(1)}, bf16[1,27,128,128]{3,2,1,0:T(8,128)(2,1)}, u32[]{:S(2)}) copy-start(bf16[1,27,128,128]{3,2,1,0:T(8,128)(2,1)} %param.13) | copy-start | bytes 2654212
  24.4 5.0 %copy-start.22 = (bf16[384,128]{1,0:T(8,128)(2,1)}, bf16[384,128]{1,0:T(8,128)(2,1)S(1)}, u32[]{:S(2)}) copy-start(bf16[384,128]{1,0:T(8,128)(2,1)S(1)} %get-tuple-element.32.back.refs_1_) | copy-start | bytes 294916
  24.4 5.0 %copy-start.24 = (bf16[384,128]{1,0:T(8,128)(2,1)}, bf16[384,128]{1,0:T(8,128)(2,1)S(1)}, u32[]{:S(2)}) copy-start(bf16[384,128]{1,0:T(8,128)(2,1)S(1)} %get-tuple-element.33.carry.refs_2_) | copy-start | bytes 294916
  26.7 4.0 %collective-permute-start.2 = (bf16[256,256]{1,0:T(8,128)(2,1)}, bf16[256,256]{1,0:T(8,128)(2,1)}, u32[]{:S(2)}, u32[]{:S(2)}) collective-permute-start(bf16[256,256]{1,0:T(8,128)(2,1)} %get-tuple-element.34), channel_id=1, source_target_pairs={{0,16},{1,17},{2,18},{3,19},{4,20},{5,21},{6,22},{7,23},{8,24},{9,... | collective-permute-start | bytes 393224 | tf_op jit(solution)/shard_map/ppermute | solution.py:308
  29.4 3.8 %collective-permute-start.3 = (bf16[2,256,256]{2,1,0:T(8,128)(2,1)}, bf16[2,256,256]{2,1,0:T(8,128)(2,1)}, u32[]{:S(2)}, u32[]{:S(2)}) collective-permute-start(bf16[2,256,256]{2,1,0:T(8,128)(2,1)} %pad_maximum_fusion.1), channel_id=1, source_target_pairs={{16,0},{17,1},{18,2},{19,3},{20,4},{21,5},{22,6},{23,7},{24,8},{25... | collective-permute-start | bytes 786440 | tf_op jit(solution)/shard_map/ppermute | solution.py:309
  35.8 10.2 %collective-permute-start.4 = (bf16[576,128]{1,0:T(8,128)(2,1)}, bf16[576,128]{1,0:T(8,128)(2,1)}, u32[]{:S(2)}, u32[]{:S(2)}) collective-permute-start(bf16[576,128]{1,0:T(8,128)(2,1)} %get-tuple-element.37), channel_id=1, source_target_pairs={{0,1},{1,2},{2,3},{3,4},{4,5},{5,6},{6,7},{7,8},{8,9},{9,10},{10,1... | collective-permute-start | bytes 442376 | tf_op jit(solution)/shard_map/ppermute | solution.py:254
  40.1 8.7 %collective-permute-start.5 = (bf16[576,128]{1,0:T(8,128)(2,1)}, bf16[576,128]{1,0:T(8,128)(2,1)}, u32[]{:S(2)}, u32[]{:S(2)}) collective-permute-start(bf16[576,128]{1,0:T(8,128)(2,1)} %get-tuple-element.38), channel_id=1, source_target_pairs={{1,0},{2,1},{3,2},{4,3},{5,4},{6,5},{7,6},{8,7},{9,8},{10,9},{11,1... | collective-permute-start | bytes 442376 | tf_op jit(solution)/shard_map/ppermute | solution.py:255
  45.2 3.6 %copy-start.12 = (bf16[256,256]{1,0:T(8,128)(2,1)S(1)}, bf16[256,256]{1,0:T(8,128)(2,1)}, u32[]{:S(2)}) copy-start(bf16[256,256]{1,0:T(8,128)(2,1)} %copy-done.11) | copy-start | bytes 393220
  55.3 8.5 %copy-start.4 = (bf16[256,256]{1,0:T(8,128)(2,1)S(1)}, bf16[256,256]{1,0:T(8,128)(2,1)}, u32[]{:S(2)}) copy-start(bf16[256,256]{1,0:T(8,128)(2,1)} %copy-done.2) | copy-start | bytes 393220
  55.3 8.5 %copy-start.10 = (bf16[256,256]{1,0:T(8,128)(2,1)S(1)}, bf16[256,256]{1,0:T(8,128)(2,1)}, u32[]{:S(2)}) copy-start(bf16[256,256]{1,0:T(8,128)(2,1)} %copy-done.8) | copy-start | bytes 393220
  55.3 8.5 %copy-start.13 = (bf16[256,256]{1,0:T(8,128)(2,1)S(1)}, bf16[256,256]{1,0:T(8,128)(2,1)}, u32[]{:S(2)}) copy-start(bf16[256,256]{1,0:T(8,128)(2,1)} %copy-done.11) | copy-start | bytes 393220
  55.3 8.5 %copy-start.19 = (bf16[384,128]{1,0:T(8,128)(2,1)S(1)}, bf16[384,128]{1,0:T(8,128)(2,1)}, u32[]{:S(2)}) copy-start(bf16[384,128]{1,0:T(8,128)(2,1)} %copy-done.18) | copy-start | bytes 294916
  55.3 8.5 %copy-start.21 = (bf16[384,128]{1,0:T(8,128)(2,1)S(1)}, bf16[384,128]{1,0:T(8,128)(2,1)}, u32[]{:S(2)}) copy-start(bf16[384,128]{1,0:T(8,128)(2,1)} %copy-done.20) | copy-start | bytes 294916
  55.3 8.5 %copy-start.27 = (bf16[384,128]{1,0:T(8,128)(2,1)S(1)}, bf16[384,128]{1,0:T(8,128)(2,1)}, u32[]{:S(2)}) copy-start(bf16[384,128]{1,0:T(8,128)(2,1)} %copy-done.26) | copy-start | bytes 294916
  55.3 8.5 %copy-start.31 = (bf16[256,128]{1,0:T(8,128)(2,1)S(1)}, bf16[256,128]{1,0:T(8,128)(2,1)}, u32[]{:S(2)}) copy-start(bf16[256,128]{1,0:T(8,128)(2,1)} %copy-done.30) | copy-start | bytes 196612
  55.3 8.5 %copy-start.33 = (bf16[256,128]{1,0:T(8,128)(2,1)S(1)}, bf16[256,128]{1,0:T(8,128)(2,1)}, u32[]{:S(2)}) copy-start(bf16[256,128]{1,0:T(8,128)(2,1)} %copy-done.32) | copy-start | bytes 196612
  56.1 10.0 %collective-permute-start.14 = (bf16[2,2,2,144,128]{4,3,1,2,0:T(8,128)(2,1)}, bf16[2,2,2,144,128]{4,3,1,2,0:T(8,128)(2,1)}, u32[]{:S(2)}, u32[]{:S(2)}) collective-permute-start(bf16[2,2,2,144,128]{4,3,1,2,0:T(8,128)(2,1)} %bitcast.106), channel_id=1, source_target_pairs={{0,4},{1,5},{2,6},{3,7},{4,0},{5,1},{6,2},{7,3},{8,12},{9,13},{10,... | collective-permute-start | bytes 884744 | tf_op jit(solution)/shard_map/ppermute | solution.py:219
  59.7 10.1 %collective-permute-start.10 = (bf16[2,2,2,144,128]{4,3,2,0,1:T(8,128)(2,1)S(1)}, bf16[2,2,2,144,128]{4,3,2,0,1:T(8,128)(2,1)S(1)}, u32[]{:S(2)}, u32[]{:S(2)}) collective-permute-start(bf16[2,2,2,144,128]{4,3,2,0,1:T(8,128)(2,1)S(1)} %bitcast.140), channel_id=1, source_target_pairs={{0,2},{1,3},{2,0},{3,1},{4,6},{5,7},{6,4},{7,5},{8,10},{9,11},{10,... | collective-permute-start | bytes 884744 | tf_op jit(solution)/shard_map/ppermute | solution.py:219
  61.2 4.9 %copy-start.35 = (bf16[2,1,2,2,144,128]{5,4,3,2,1,0:T(8,128)(2,1)S(1)}, bf16[2,1,2,2,144,128]{5,4,3,2,1,0:T(8,128)(2,1)}, u32[]{:S(2)}) copy-start(bf16[2,1,2,2,144,128]{5,4,3,2,1,0:T(8,128)(2,1)} %get-tuple-element.54) | copy-start | bytes 884740
  61.2 10.3 %collective-permute-start.6 = (bf16[2,2,2,144,128]{4,3,2,1,0:T(8,128)(2,1)S(1)}, bf16[2,2,2,144,128]{4,3,2,1,0:T(8,128)(2,1)S(1)}, u32[]{:S(2)}, u32[]{:S(2)}) collective-permute-start(bf16[2,2,2,144,128]{4,3,2,1,0:T(8,128)(2,1)S(1)} %dynamic-slice_bitcast_fusion), channel_id=1, source_target_pairs={{0,1},{1,0},{2,3},{3,2},{4,5},{5,4},{6,7},{7,6},{8,9},{9,8},{10,11... | collective-permute-start | bytes 884744 | tf_op jit(solution)/shard_map/ppermute | solution.py:219
  67.2 9.0 %collective-permute-start.15 = (bf16[2,2,144,128]{3,2,0,1:T(8,128)(2,1)S(1)}, bf16[2,2,144,128]{3,2,0,1:T(8,128)(2,1)S(1)}, u32[]{:S(2)}, u32[]{:S(2)}) collective-permute-start(bf16[2,2,144,128]{3,2,0,1:T(8,128)(2,1)S(1)} %dynamic-slice_bitcast_fusion.1), channel_id=1, source_target_pairs={{0,8},{1,9},{2,10},{3,11},{4,12},{5,13},{6,14},{7,15},{8,0},{9,1},... | collective-permute-start | bytes 442376 | tf_op jit(solution)/shard_map/ppermute | solution.py:219
  69.9 7.0 %collective-permute-start.11 = (bf16[2,2,144,128]{3,2,1,0:T(8,128)(2,1)S(1)}, bf16[2,2,144,128]{3,2,1,0:T(8,128)(2,1)S(1)}, u32[]{:S(2)}, u32[]{:S(2)}) collective-permute-start(bf16[2,2,144,128]{3,2,1,0:T(8,128)(2,1)S(1)} %dynamic-slice_bitcast_fusion.2), channel_id=1, source_target_pairs={{0,4},{1,5},{2,6},{3,7},{4,0},{5,1},{6,2},{7,3},{8,12},{9,13},{10,... | collective-permute-start | bytes 442376 | tf_op jit(solution)/shard_map/ppermute | solution.py:219
  71.6 6.5 %collective-permute-start.7 = (bf16[2,2,144,128]{3,2,1,0:T(8,128)(2,1)S(1)}, bf16[2,2,144,128]{3,2,1,0:T(8,128)(2,1)S(1)}, u32[]{:S(2)}, u32[]{:S(2)}) collective-permute-start(bf16[2,2,144,128]{3,2,1,0:T(8,128)(2,1)S(1)} %dynamic-slice_bitcast_fusion.3), channel_id=1, source_target_pairs={{0,2},{1,3},{2,0},{3,1},{4,6},{5,7},{6,4},{7,5},{8,10},{9,11},{10,... | collective-permute-start | bytes 442376 | tf_op jit(solution)/shard_map/ppermute | solution.py:219
  76.3 4.4 %collective-permute-start.16 = (bf16[2,144,128]{2,1,0:T(8,128)(2,1)S(1)}, bf16[2,144,128]{2,1,0:T(8,128)(2,1)S(1)}, u32[]{:S(2)}, u32[]{:S(2)}) collective-permute-start(bf16[2,144,128]{2,1,0:T(8,128)(2,1)S(1)} %dynamic-slice_bitcast_fusion.4), channel_id=1, source_target_pairs={{0,1},{1,0},{2,3},{3,2},{4,5},{5,4},{6,7},{7,6},{8,9},{9,8},{10,11... | collective-permute-start | bytes 221192 | tf_op jit(solution)/shard_map/ppermute | solution.py:219
  77.0 6.2 %collective-permute-start.12 = (bf16[2,144,128]{2,1,0:T(8,128)(2,1)S(1)}, bf16[2,144,128]{2,1,0:T(8,128)(2,1)S(1)}, u32[]{:S(2)}, u32[]{:S(2)}) collective-permute-start(bf16[2,144,128]{2,1,0:T(8,128)(2,1)S(1)} %dynamic-slice_bitcast_fusion.5), channel_id=1, source_target_pairs={{0,8},{1,9},{2,10},{3,11},{4,12},{5,13},{6,14},{7,15},{8,0},{9,1},... | collective-permute-start | bytes 221192 | tf_op jit(solution)/shard_map/ppermute | solution.py:219
  78.2 6.5 %collective-permute-start.8 = (bf16[2,144,128]{2,1,0:T(8,128)(2,1)S(1)}, bf16[2,144,128]{2,1,0:T(8,128)(2,1)S(1)}, u32[]{:S(2)}, u32[]{:S(2)}) collective-permute-start(bf16[2,144,128]{2,1,0:T(8,128)(2,1)S(1)} %dynamic-slice_bitcast_fusion.6), channel_id=1, source_target_pairs={{0,4},{1,5},{2,6},{3,7},{4,0},{5,1},{6,2},{7,3},{8,12},{9,13},{10,... | collective-permute-start | bytes 221192 | tf_op jit(solution)/shard_map/ppermute | solution.py:219
  80.7 4.2 %collective-permute-start.17 = (bf16[144,128]{1,0:T(8,128)(2,1)S(1)}, bf16[144,128]{1,0:T(8,128)(2,1)S(1)}, u32[]{:S(2)}, u32[]{:S(2)}) collective-permute-start(bf16[144,128]{1,0:T(8,128)(2,1)S(1)} %dynamic-slice_bitcast_fusion.7), channel_id=1, source_target_pairs={{0,2},{1,3},{2,0},{3,1},{4,6},{5,7},{6,4},{7,5},{8,10},{9,11},{10,... | collective-permute-start | bytes 110600 | tf_op jit(solution)/shard_map/ppermute | solution.py:219
  83.2 4.0 %collective-permute-start.13 = (bf16[144,128]{1,0:T(8,128)(2,1)S(1)}, bf16[144,128]{1,0:T(8,128)(2,1)S(1)}, u32[]{:S(2)}, u32[]{:S(2)}) collective-permute-start(bf16[144,128]{1,0:T(8,128)(2,1)S(1)} %dynamic-slice_bitcast_fusion.8), channel_id=1, source_target_pairs={{0,1},{1,0},{2,3},{3,2},{4,5},{5,4},{6,7},{7,6},{8,9},{9,8},{10,11... | collective-permute-start | bytes 110600 | tf_op jit(solution)/shard_map/ppermute | solution.py:219
  84.8 5.1 %collective-permute-start.9 = (bf16[144,128]{1,0:T(8,128)(2,1)S(1)}, bf16[144,128]{1,0:T(8,128)(2,1)S(1)}, u32[]{:S(2)}, u32[]{:S(2)}) collective-permute-start(bf16[144,128]{1,0:T(8,128)(2,1)S(1)} %dynamic-slice_bitcast_fusion.9), channel_id=1, source_target_pairs={{0,8},{1,9},{2,10},{3,11},{4,12},{5,13},{6,14},{7,15},{8,0},{9,1},... | collective-permute-start | bytes 110600 | tf_op jit(solution)/shard_map/ppermute | solution.py:219
  (22 other events, 29.8 us)

commit v3 on v2

--- a/solution.py
+++ b/solution.py
@@ -8,7 +8,7 @@
 from jax.experimental.pallas import tpu as pltpu
 from jax.sharding import PartitionSpec as P
 
-VMEM = pltpu.CompilerParams(vmem_limit_bytes=48 * 1024 * 1024)
+VMEM = pltpu.CompilerParams(vmem_limit_bytes=20 * 1024 * 1024)
 F32 = jnp.float32
 BF16 = jnp.bfloat16
 
@@ -70,7 +70,38 @@
         high[at : at + plane, :] = source[cells - plane : cells, half]
 
 
-def edges_kernel(plane, state, act, grad, low, high):
+def edges_kernel(plane, state, act, grad, low, high, sems):
+    width = state.shape[1] // 2
+    cells = state.shape[0]
+    left, right = pl.ds(0, width), pl.ds(width, width)
+    moves = []
+    for index, (source, half) in enumerate(((state, right), (act, left), (grad, right))):
+        moves.append((source, half, 2 * plane, index * 2 * plane))
+    for index, (source, half) in enumerate(((state, left), (act, right), (grad, left))):
+        moves.append((source, half, plane, (6 + index) * plane))
+    copies = []
+    for source, half, size, at in moves:
+        for start, out in ((0, low), (cells - size, high)):
+            copies.append(
+                pltpu.make_async_copy(
+                    source.at[pl.ds(start, size), half],
+                    out.at[pl.ds(at, size), :],
+                    sems.at[len(copies)],
+                )
+            )
+    for copy in copies:
+        copy.start()
+    for copy in copies:
+        copy.wait()
+
+
+def join_kernel(plane, places, forward, lifted, lowered, fresh, target, state, act, grad, low, high):
+    first_place, last_place = places[0] == 0, places[0] == places[1]
+    state[...] = jnp.where(first_place, fresh[...], lifted[0])
+    own = forward[...]
+    act[...] = jnp.where(last_place, own, lowered[0])
+    error = (own.astype(F32) - target[...].astype(F32)).astype(BF16)
+    grad[...] = jnp.where(last_place, error, lowered[1])
     pack_edges(state, act, grad, low, high, plane)
 
 
@@ -149,6 +180,29 @@
     ).astype(BF16)
 
 
+def tick_kernel(ydim, zdim, paired, places, flags, state_in, act_in, grad_in, below, above, first,
+                second, first_back, second_back, forward, sent, back, carry, gate, state, act, grad,
+                new_one, back_two, mid, rebuilt, stack, sems):
+    copies = [
+        pltpu.make_async_copy(source, target, sems.at[index])
+        for index, (source, target) in enumerate(
+            ((state_in, state), (act_in, act), (grad_in, grad))
+        )
+    ]
+    for copy in copies:
+        copy.start()
+    for copy in copies:
+        copy.wait()
+    first_kernel(ydim, zdim, flags, state, act, grad, below, above, first, second, second_back,
+                 new_one, back_two, mid, back, carry, gate, stack)
+    second_kernel(ydim, zdim, state, act, grad, new_one, back_two, mid, back, carry, first, second,
+                  first_back, forward, rebuilt, sent.at[1], stack)
+    if paired:
+        sent[0] = jnp.where(places[0] == 0, forward[...], rebuilt[...])
+    else:
+        sent[0] = rebuilt[...]
+
+
 def correlate(stack, field, cotangent, ydim, zdim, emit):
     plane = ydim * zdim
     cells, width = cotangent.shape
@@ -164,65 +218,111 @@
             emit(9 * step + 8 - place, product[:, place * width : (place + 1) * width])
 
 
-def corr_kernel(ydim, zdim, factor, last, *refs):
-    if last:
-        grad, back, carry, gate, so_far, out, stack = refs
-    else:
-        grad, back, carry, gate, out, stack = refs
+def both_grads(ydim, zdim, grad, back, carry, gate, stack, put):
     plane = ydim * zdim
     cells, double = grad.shape
     width = double // 2
 
     def store(which):
-        def emit(k, block):
-            at = slice(k * width, (k + 1) * width)
-            if last:
-                out[which, at, :] = ((block + so_far[which, at, :]) * factor).astype(out.dtype)
-            else:
-                out[which, at, :] = block
-
-        return emit
+        return lambda k, block: put(which, slice(k * width, (k + 1) * width), block)
 
     own = carry[plane : plane + cells, :].astype(F32)
     correlate(stack, back, own, ydim, zdim, store(0))
     correlate(stack, gate, grad[:, width:].astype(F32), ydim, zdim, store(1))
 
 
+def corr_kernel(ydim, zdim, grad, back, carry, gate, out, stack):
+    def put(which, at, block):
+        out[which, at, :] = block
+
+    both_grads(ydim, zdim, grad, back, carry, gate, stack, put)
+
+
+def ways_of(count, rows):
+    bits = [1 << level for level in range(count.bit_length() - 1)]
+    ways = 3
+    span = 2 * rows // ways
+    return [(way * span, span, bits[way % len(bits) :] + bits[: way % len(bits)]) for way in range(ways)]
+
+
+def last_kernel(ydim, zdim, factor, count, direct, spot, flags, state, act, grad, below, above, first,
+                second, second_back, so_far, new_one, back_two, mid, back, carry, *refs):
+    refs, (gate, stack, sums) = refs[:-3], refs[-3:]
+    first_kernel(ydim, zdim, flags, state, act, grad, below, above, first, second, second_back,
+                 new_one, back_two, mid, back, carry, gate, stack)
+
+    def put(which, at, block):
+        sums[which, at, :] = (block + so_far[which, at, :]) * factor
+
+    both_grads(ydim, zdim, grad, back, carry, gate, stack, put)
+    if not direct:
+        refs[0][...] = sums[...].astype(BF16)
+        return
+    rows = sums.shape[1] // count
+    for index, (start, span, order) in enumerate(ways_of(count, rows)):
+        mine = (spot[0] // order[0]) % 2
+        for kept in range(2):
+            side = mine if kept else 1 - mine
+            out = refs[2 * index + (0 if kept else 1)]
+            for j in range(count // 2):
+                fixed = sum(
+                    bit for level, bit in enumerate(order[1:]) if (j >> (len(order) - 2 - level)) & 1
+                )
+                block = fixed + side * order[0]
+                pieces = []
+                for which in range(2):
+                    lower = max(start, which * rows)
+                    upper = min(start + span, (which + 1) * rows)
+                    if lower < upper:
+                        at = pl.multiple_of(block * rows + (lower - which * rows), 8)
+                        pieces.append(sums[which, pl.ds(at, upper - lower), :])
+                value = pieces[0] if len(pieces) == 1 else jnp.concatenate(pieces, axis=0)
+                out[j] = value.astype(BF16)
+
+
 def whole(count):
     return [pl.BlockSpec(memory_space=pltpu.VMEM)] * count
 
 
-def reduce_blocks(grads):
-    count = lax.axis_size("space")
-    bits = [1 << level for level in range(count.bit_length() - 1)]
+def split_blocks(sums, count):
+    blocks = jnp.concatenate([part.reshape(count, -1, part.shape[-1]) for part in sums], axis=1)
     spot = lax.axis_index("space")
-    rows = grads.shape[1]
-    ways = 3 if rows % 3 == 0 else 1
-    span = rows // ways
-    parts = []
-    for way in range(ways):
-        shift = way % len(bits)
-        order = bits[shift:] + bits[:shift]
-        part = grads[:, way * span : (way + 1) * span].reshape(
-            [2] * len(bits) + [span, grads.shape[2]]
-        )
-        parts.append((part, order))
-    for step in range(len(bits)):
-        fresh_parts = []
-        for part, order in parts:
+    halves = []
+    for start, span, order in ways_of(count, blocks.shape[1] // 2):
+        part = blocks[:, start : start + span]
+        part = part.reshape([2] * len(order) + list(part.shape[1:]))
+        levels = [len(order) - bit.bit_length() for bit in order]
+        part = jnp.transpose(part, levels + [len(order), len(order) + 1])
+        part = part.reshape((2, count // 2) + part.shape[-2:])
+        mine = (spot // order[0]) % 2
+        for side in (mine, 1 - mine):
+            halves.append(lax.dynamic_index_in_dim(part, side, 0, keepdims=False))
+    return halves
+
+
+def reduce_blocks(halves, count, rows):
+    spot = lax.axis_index("space")
+    ways = [
+        (halves[2 * way], halves[2 * way + 1], order)
+        for way, (_, _, order) in enumerate(ways_of(count, rows))
+    ]
+    for step in range(count.bit_length() - 1):
+        later = []
+        for keep, send, order in ways:
             bit = order[step]
-            left = sorted(order[step:], reverse=True)
-            axis = left.index(bit)
-            mine = (spot // bit) % 2
-            keep = lax.dynamic_index_in_dim(part, mine, axis, keepdims=False)
-            send = lax.dynamic_index_in_dim(part, 1 - mine, axis, keepdims=False)
             got = lax.ppermute(send, "space", [(i, i ^ bit) for i in range(count)])
-            total = keep.astype(jnp.float32) + got.astype(jnp.float32)
-            if step < len(bits) - 1:
-                total = total.astype(jnp.bfloat16)
-            fresh_parts.append((total, order))
-        parts = fresh_parts
-    return jnp.concatenate([part for part, _ in parts], axis=0)
+            total = keep.astype(F32) + got.astype(F32)
+            if step + 1 < len(order):
+                total = total.astype(BF16)
+                total = total.reshape((2, total.shape[0] // 2) + total.shape[1:])
+                mine = (spot // order[step + 1]) % 2
+                keep = lax.dynamic_index_in_dim(total, mine, 0, keepdims=False)
+                send = lax.dynamic_index_in_dim(total, 1 - mine, 0, keepdims=False)
+            else:
+                keep, send = total[0], None
+            later.append((keep, send, order))
+        ways = later
+    return jnp.concatenate([keep for keep, _, _ in ways], axis=0)
 
 
 def shards(fwd_in, bwd_act, bwd_grad, fresh, target, w_first, w_second):
@@ -255,73 +355,93 @@
         above = lax.ppermute(low, "space", down)
         return below, above
 
-    def edges(state, act, grad):
-        return pl.pallas_call(
-            functools.partial(edges_kernel, plane),
-            out_shape=(edge, edge),
-            in_specs=whole(3),
-            out_specs=tuple(whole(2)),
-            compiler_params=VMEM,
-            name="edges",
-        )(state, act, grad)
-
-    def tick_first(state, act, grad, below, above):
-        return pl.pallas_call(
-            functools.partial(first_kernel, ydim, zdim),
-            out_shape=(tile, tile, wide, wide, wide, wide),
-            in_specs=[pl.BlockSpec(memory_space=pltpu.SMEM)] + whole(8),
-            out_specs=tuple(whole(6)),
-            scratch_shapes=[pltpu.VMEM((cells + 4 * plane, 9 * width), BF16)],
-            compiler_params=VMEM,
-            name="tick_first",
-        )(flags, state, act, grad, below, above, first, second, second_back)
-
-    def tick_second(state, act, grad, made):
-        new_one, back_two, mid, back, carry, _ = made
-        return pl.pallas_call(
-            functools.partial(second_kernel, ydim, zdim),
-            out_shape=(state_shape,) * 3,
-            in_specs=whole(11),
-            out_specs=tuple(whole(3)),
-            scratch_shapes=[pltpu.VMEM((cells + 2 * plane, 9 * width), BF16)],
-            compiler_params=VMEM,
-            name="tick_second",
-        )(state, act, grad, new_one, back_two, mid, back, carry, first, second, first_back)
-
-    def weight_grads(grad, made, so_far, factor):
-        last = so_far is not None
-        extra = (so_far,) if last else ()
-        return pl.pallas_call(
-            functools.partial(corr_kernel, ydim, zdim, factor, last),
-            out_shape=array((2, offsets, width), BF16 if last else F32),
-            in_specs=whole(4 + len(extra)),
-            out_specs=whole(1)[0],
-            scratch_shapes=[pltpu.VMEM((cells, 9 * width), BF16)],
-            compiler_params=VMEM,
-            name="weight_grads",
-        )(grad, made[3], made[4], made[5], *extra)
-
     state, act, grad = flat(fwd_in), flat(bwd_act), flat(bwd_grad)
-    below, above = exchange(*edges(state, act, grad))
-    made_one = tick_first(state, act, grad, below, above)
-    forward, rebuilt, passed = tick_second(state, act, grad, made_one)
-    lifted = lax.ppermute(forward, "section", [(s, s + 1) for s in range(last_section)])
-    lowered = lax.ppermute(
-        jnp.stack([rebuilt, passed]), "section", [(s + 1, s) for s in range(last_section)]
-    )
-    own_grad = (forward.astype(F32) - flat(target).astype(F32)).astype(BF16)
-    state_two = jnp.where(place == 0, flat(fresh), lifted)
-    act_two = jnp.where(place == last_section, forward, lowered[0])
-    grad_two = jnp.where(place == last_section, own_grad, lowered[1])
-    below, above = exchange(*edges(state_two, act_two, grad_two))
-    so_far = weight_grads(grad, made_one, None, None)
-    made_two = tick_first(state_two, act_two, grad_two, below, above)
-    cell_total = cells * count
-    sums = weight_grads(grad_two, made_two, so_far, 1.0 / math.sqrt(cell_total))
-    forward, rebuilt, passed = tick_second(state_two, act_two, grad_two, made_two)
-    blocks = jnp.concatenate([sums[0].reshape(count, -1, width), sums[1].reshape(count, -1, width)], axis=1)
-    total = reduce_blocks(blocks)
-    rows = total.shape[0] // 2
+    smem = pl.BlockSpec(memory_space=pltpu.SMEM)
+    hbm = pl.BlockSpec(memory_space=pltpu.HBM)
+    scratch = lambda like: pltpu.VMEM(like.shape, like.dtype)
+    inner_stack = pltpu.VMEM((cells + 2 * plane, 9 * width), BF16)
+    outer_stack = pltpu.VMEM((cells + 4 * plane, 9 * width), BF16)
+    places = jnp.stack([place, jnp.full_like(place, last_section)]).astype(jnp.int32)
+
+    low, high = pl.pallas_call(
+        functools.partial(edges_kernel, plane),
+        out_shape=(edge, edge),
+        in_specs=[hbm] * 3,
+        out_specs=(hbm, hbm),
+        scratch_shapes=[pltpu.SemaphoreType.DMA((12,))],
+        compiler_params=VMEM,
+        name="edges",
+    )(state, act, grad)
+    below, above = exchange(low, high)
+
+    paired = last_section == 1
+    forward, sent, back, carry, gate = pl.pallas_call(
+        functools.partial(tick_kernel, ydim, zdim, paired),
+        out_shape=(state_shape, array((2, cells, 2 * width), BF16), wide, wide, wide),
+        in_specs=[smem] * 2 + [hbm] * 3 + whole(6),
+        out_specs=tuple(whole(5)),
+        scratch_shapes=[scratch(state_shape)] * 3
+        + [scratch(tile), scratch(tile), scratch(wide), scratch(state_shape), outer_stack]
+        + [pltpu.SemaphoreType.DMA((3,))],
+        compiler_params=VMEM,
+        name="tick_one",
+    )(places, flags, state, act, grad, below, above, first, second, first_back, second_back)
+    if paired:
+        lifted = lowered = lax.ppermute(sent, "section", [(0, 1), (1, 0)])
+    else:
+        lifted = lax.ppermute(forward[None], "section", [(s, s + 1) for s in range(last_section)])
+        lowered = lax.ppermute(sent, "section", [(s + 1, s) for s in range(last_section)])
+
+    state_two, act_two, grad_two, low, high = pl.pallas_call(
+        functools.partial(join_kernel, plane),
+        out_shape=(state_shape,) * 3 + (edge, edge),
+        in_specs=[smem] + whole(5),
+        out_specs=tuple(whole(5)),
+        compiler_params=VMEM,
+        name="join",
+    )(places, forward, lifted, lowered, flat(fresh), flat(target))
+    below, above = exchange(low, high)
+
+    so_far = pl.pallas_call(
+        functools.partial(corr_kernel, ydim, zdim),
+        out_shape=array((2, offsets, width), F32),
+        in_specs=whole(4),
+        out_specs=whole(1)[0],
+        scratch_shapes=[pltpu.VMEM((cells, 9 * width), BF16)],
+        compiler_params=VMEM,
+        name="weight_grads",
+    )(grad, back, carry, gate)
+
+    rows = offsets // count
+    direct = rows % 24 == 0
+    if direct:
+        span = 2 * rows // 3
+        outs = (array((count // 2, span, width), BF16),) * 6
+    else:
+        outs = (array((2, offsets, width), BF16),)
+    factor = 1.0 / math.sqrt(cells * count)
+    made = pl.pallas_call(
+        functools.partial(last_kernel, ydim, zdim, factor, count, direct),
+        out_shape=(tile, tile, wide, wide, wide) + outs,
+        in_specs=[smem] * 2 + whole(9),
+        out_specs=tuple(whole(5 + len(outs))),
+        scratch_shapes=[scratch(wide), outer_stack, pltpu.VMEM((2, offsets, width), F32)],
+        compiler_params=VMEM,
+        name="tick_two_first",
+    )(spot.astype(jnp.int32).reshape(1), flags, state_two, act_two, grad_two, below, above, first,
+      second, second_back, so_far)
+    forward, rebuilt, passed = pl.pallas_call(
+        functools.partial(second_kernel, ydim, zdim),
+        out_shape=(state_shape,) * 3,
+        in_specs=whole(11),
+        out_specs=tuple(whole(3)),
+        scratch_shapes=[inner_stack],
+        compiler_params=VMEM,
+        cost_estimate=pl.CostEstimate(flops=2 * 81 * cells * width * width, bytes_accessed=4000000, transcendentals=0),
+        name="tick_two_second",
+    )(state_two, act_two, grad_two, *made[:5], first, second, first_back)
+    halves = made[5:] if direct else split_blocks(made[5], count)
+    total = reduce_blocks(halves, count, rows)
     return (
         forward.reshape((1,) + shape),
         rebuilt.reshape((1,) + shape),

time: 91.3 us -> 90.1 us (0.987)
  local copies, waits for them, and re-layouts: 18.9 us -> 26.2 us
  starting transfers between devices: 35.6 us -> 28.5 us
  other arithmetic: 6.3 us -> 1.32 us
  waiting for transfers between devices: 13.9 us -> 16.9 us
    unnamed x72 -> x70, local copies, waits for them, and re-layouts: 10.5 us -> 19.3 us
    ppermute x12, starting transfers between devices: 19.9 us -> 15.6 us  [reduce_blocks(): got = lax.ppermute(send, 'space', [(i, i ^ bit) for i in range(count)])]
    ppermute x2 -> x1, starting transfers between devices: 3.22 us -> 0.07 us  [shards(): lifted = lowered = lax.ppermute(sent, 'section', [(0, 1), (1, 0)])]
    dynamic_slice x4 -> x0, local copies, waits for them, and re-layouts: 2.67 us -> none  [the longest x2 1.9 us: reduce_blocks(): keep = lax.dynamic_index_in_dim(part, mine, axis, keepdims=False)]
    select_n x2 -> x0, other arithmetic: 2.17 us -> none  [the longest x1 1.24 us: shards(): grad_two = jnp.where(place == last_section, own_grad, lowered[1])]
    ppermute x2, waiting for transfers between devices: 3.72 us -> 5.35 us  [exchange(): above = lax.ppermute(low, 'space', down)]
    transpose x2, local copies, waits for them, and re-layouts: 2.55 us -> 4.11 us  [shards(): jnp.transpose(w_second[0][::-1], (0, 2, 1)).reshape(3, 9 * width, width)]
    slice x1 -> x0, other arithmetic: 1.16 us -> none  [reduce_blocks(): grads[:, way * span:(way + 1) * span]]
  transfers between devices with their start and end apart: 18 -> 17, of which waited for: 8 -> 9; matrix products, arithmetic and copies ran while one was open for 11% -> 8% of each run, Pallas kernels for 3% -> 4%
where the time goes in v3:
time: 90.1 us; the launch traced here: 89.5 us
  starting transfers between devices  28.5 us (32%)
  local copies, waits for them, and re-layouts  26.2 us (29%)
  waiting for transfers between devices  16.9 us (19%)
  Pallas kernels  15.5 us (17%)
  other arithmetic  1.32 us (1%)
  between operations  1 us (1%)
    unnamed x70, local copies, waits for them, and re-layouts  19.3 us
    ppermute x12, starting transfers between devices, reduce_blocks(): got = lax.ppermute(send, 'space', [(i, i ^ bit) for i in range(count)])  15.6 us
    ppermute x2, starting transfers between devices, exchange(): below = lax.ppermute(high, 'space', up)  10.1 us
    ppermute x12, waiting for transfers between devices, reduce_blocks(): got = lax.ppermute(send, 'space', [(i, i ^ bit) for i in range(count)])  9.03 us
    pallas_call x1, Pallas kernels, shards(): pl.pallas_call(functools.partial(tick_kernel, ydim, zdim, paired), out_sh...  5.87 us
    ppermute x2, waiting for transfers between devices, exchange(): above = lax.ppermute(low, 'space', down)  5.35 us
    pallas_call x1, Pallas kernels, shards(): pl.pallas_call(functools.partial(last_kernel, ydim, zdim, factor, count,...  4.99 us
    transpose x2, local copies, waits for them, and re-layouts, shards(): jnp.transpose(w_second[0][::-1], (0, 2, 1)).reshape(3, 9 * width, width)  4.11 us
  transfers between devices with their start and end apart: 17, of which 9 were waited for; matrix products, arithmetic and copies ran while one was open for 8% of the time, Pallas kernels for 4%

profile of v3, /device:TPU:0, one launch (start us, length us, event | category | flops | bytes accessed | tf_op | source)
XLA Modules:
  0.0 89.5 jit_solution(15925336457781974986)
XLA Ops:
  1.5 0.9 %copy-done.5 = bf16[1,4,8,8,256]{4,3,2,1,0:T(8,128)(2,1)S(1)} copy-done((bf16[1,4,8,8,256]{4,3,2,1,0:T(8,128)(2,1)S(1)}, bf16[1,4,8,8,256]{4,3,2,1,0:T(8,128)(2,1)}, u32[]{:S(2)}) %copy-start.5) | copy-done | bytes 131096
  2.4 0.9 %copy-done.7 = bf16[1,4,8,8,256]{4,3,2,1,0:T(8,128)(2,1)S(1)} copy-done((bf16[1,4,8,8,256]{4,3,2,1,0:T(8,128)(2,1)S(1)}, bf16[1,4,8,8,256]{4,3,2,1,0:T(8,128)(2,1)}, u32[]{:S(2)}) %copy-start.7) | copy-done | bytes 131096
  4.2 5.5 %collective-permute-start = (bf16[576,128]{1,0:T(8,128)(2,1)}, bf16[576,128]{1,0:T(8,128)(2,1)}, u32[]{:S(2)}, u32[]{:S(2)}) collective-permute-start(bf16[576,128]{1,0:T(8,128)(2,1)} %get-tuple-element.31), channel_id=1, source_target_pairs={{0,1},{1,2},{2,3},{3,4},{4,5},{5,6},{6,7},{7,8},{8,9},{9,10},{10,1... | collective-permute-start | bytes 442376 | tf_op jit(solution)/shard_map/ppermute | solution.py:354
  9.7 1.3 %collective-permute-start.1 = (bf16[576,128]{1,0:T(8,128)(2,1)}, bf16[576,128]{1,0:T(8,128)(2,1)}, u32[]{:S(2)}, u32[]{:S(2)}) collective-permute-start(bf16[576,128]{1,0:T(8,128)(2,1)} %get-tuple-element.32), channel_id=1, source_target_pairs={{1,0},{2,1},{3,2},{4,3},{5,4},{6,5},{7,6},{8,7},{9,8},{10,9},{11,1... | collective-permute-start | bytes 442376 | tf_op jit(solution)/shard_map/ppermute | solution.py:355
  11.0 1.4 %reverse_bitcast_fusion.1 = bf16[27,128,128]{1,2,0:T(8,128)(2,1)S(1)} fusion(bf16[27,128,128]{2,1,0:T(8,128)(2,1)} %bitcast.68), kind=kLoop, calls=%fused_computation.1 | loop fusion | bytes 1769472 | tf_op jit(solution)/shard_map/transpose | solution.py:337
  12.4 2.2 %reverse_bitcast_fusion = bf16[27,128,128]{1,2,0:T(8,128)(2,1)} fusion(bf16[27,128,128]{2,1,0:T(8,128)(2,1)} %bitcast.72), kind=kLoop, calls=%fused_computation | loop fusion | bytes 1769472 | tf_op jit(solution)/shard_map/transpose | solution.py:338
  14.7 1.3 %copy.12 = bf16[27,128,128]{2,1,0:T(8,128)(2,1)S(1)} copy(bf16[27,128,128]{1,2,0:T(8,128)(2,1)S(1)} %reverse_bitcast_fusion.1) | data formatting | bytes 1769472 | tf_op jit(solution)/shard_map/transpose | solution.py:337
  16.0 1.9 %copy.13 = bf16[27,128,128]{2,1,0:T(8,128)(2,1)S(1)} copy(bf16[27,128,128]{1,2,0:T(8,128)(2,1)} %reverse_bitcast_fusion) | data formatting | bytes 1769472 | tf_op jit(solution)/shard_map/transpose | solution.py:338
  18.9 0.9 %copy-done.6 = bf16[1,4,8,8,256]{4,3,2,1,0:T(8,128)(2,1)S(1)} copy-done((bf16[1,4,8,8,256]{4,3,2,1,0:T(8,128)(2,1)S(1)}, bf16[1,4,8,8,256]{4,3,2,1,0:T(8,128)(2,1)}, u32[]{:S(2)}) %copy-start.6) | copy-done | bytes 131096
  19.8 0.9 %copy-done.8 = bf16[1,4,8,8,256]{4,3,2,1,0:T(8,128)(2,1)S(1)} copy-done((bf16[1,4,8,8,256]{4,3,2,1,0:T(8,128)(2,1)S(1)}, bf16[1,4,8,8,256]{4,3,2,1,0:T(8,128)(2,1)}, u32[]{:S(2)}) %copy-start.8) | copy-done | bytes 131096
  20.7 5.9 %tick_one.1 = (bf16[256,256]{1,0:T(8,128)(2,1)S(1)}, bf16[2,256,256]{2,1,0:T(8,128)(2,1)S(1)}, bf16[384,128]{1,0:T(8,128)(2,1)S(1)}, bf16[384,128]{1,0:T(8,128)(2,1)S(1)}, bf16[384,128]{1,0:T(8,128)(2,1)S(1)}) custom-call(s32[2]{0:T(128)S(1)} %pad_add_fusion.places, f32[2]{0:T(128)S(1)} %add_convert_fusion.3.flags, bf16[256,256]{1,0:T(8,128)(2,1)S(1)} %bitcast.84, ...), custom_call_target="tpu_custom_call" | custom-call | tf_op jit(solution)/shard_map/tick_one/pallas_call | solution.py:378
  26.7 1.5 %collective-permute-done.2.lifted.lowered = bf16[2,256,256]{2,1,0:T(8,128)(2,1)S(1)} collective-permute-done((bf16[2,256,256]{2,1,0:T(8,128)(2,1)S(1)}, bf16[2,256,256]{2,1,0:T(8,128)(2,1)S(1)}, u32[]{:S(2)}, u32[]{:S(2)}) %collective-permute-start.2) | collective-permute-done | bytes 262176 | tf_op jit(solution)/shard_map/ppermute | solution.py:390
  28.9 4.6 %collective-permute-start.3 = (bf16[576,128]{1,0:T(8,128)(2,1)S(1)}, bf16[576,128]{1,0:T(8,128)(2,1)S(1)}, u32[]{:S(2)}, u32[]{:S(2)}) collective-permute-start(bf16[576,128]{1,0:T(8,128)(2,1)S(1)} %get-tuple-element.38), channel_id=1, source_target_pairs={{0,1},{1,2},{2,3},{3,4},{4,5},{5,6},{6,7},{7,8},{8,9},{9,10},{10,1... | collective-permute-start | bytes 442376 | tf_op jit(solution)/shard_map/ppermute | solution.py:354
  33.5 1.5 %collective-permute-start.4 = (bf16[576,128]{1,0:T(8,128)(2,1)S(1)}, bf16[576,128]{1,0:T(8,128)(2,1)S(1)}, u32[]{:S(2)}, u32[]{:S(2)}) collective-permute-start(bf16[576,128]{1,0:T(8,128)(2,1)S(1)} %get-tuple-element.39), channel_id=1, source_target_pairs={{1,0},{2,1},{3,2},{4,3},{5,4},{6,5},{7,6},{8,7},{9,8},{10,9},{11,1... | collective-permute-start | bytes 442376 | tf_op jit(solution)/shard_map/ppermute | solution.py:355
  35.8 1.1 %collective-permute-done.3.below = bf16[576,128]{1,0:T(8,128)(2,1)S(1)} collective-permute-done((bf16[576,128]{1,0:T(8,128)(2,1)S(1)}, bf16[576,128]{1,0:T(8,128)(2,1)S(1)}, u32[]{:S(2)}, u32[]{:S(2)}) %collective-permute-start.3) | collective-permute-done | bytes 147488 | tf_op jit(solution)/shard_map/ppermute | solution.py:354
  36.8 5.3 %collective-permute-done.4.above = bf16[576,128]{1,0:T(8,128)(2,1)S(1)} collective-permute-done((bf16[576,128]{1,0:T(8,128)(2,1)S(1)}, bf16[576,128]{1,0:T(8,128)(2,1)S(1)}, u32[]{:S(2)}, u32[]{:S(2)}) %collective-permute-start.4) | collective-permute-done | bytes 147488 | tf_op jit(solution)/shard_map/ppermute | solution.py:355
  42.2 5.0 %tick_two_first.1 = (bf16[256,128]{1,0:T(8,128)(2,1)S(1)}, bf16[256,128]{1,0:T(8,128)(2,1)S(1)}, bf16[384,128]{1,0:T(8,128)(2,1)S(1)}, bf16[384,128]{1,0:T(8,128...) custom-call(s32[1]{0:T(128)} %bitcast.16.spot, ...), custom_call_target="tpu_custom_call" | custom-call | tf_op jit(solution)/shard_map/tick_two_first/pallas_call | solution.py:423
  54.0 1.4 %collective-permute-start.5 = (bf16[8,144,128]{2,1,0:T(8,128)(2,1)}, bf16[8,144,128]{2,1,0:T(8,128)(2,1)S(1)}, u32[]{:S(2)}, u32[]{:S(2)}) collective-permute-start(bf16[8,144,128]{2,1,0:T(8,128)(2,1)} %get-tuple-element.52), channel_id=1, source_target_pairs={{0,1},{1,0},{2,3},{3,2},{4,5},{5,4},{6,7},{7,6},{8,9},{9,8},{10,11... | collective-permute-start | bytes 884744 | tf_op jit(solution)/shard_map/ppermute | solution.py:313
  55.4 3.3 %collective-permute-start.9 = (bf16[8,144,128]{2,1,0:T(8,128)(2,1)}, bf16[8,144,128]{2,1,0:T(8,128)(2,1)S(1)}, u32[]{:S(2)}, u32[]{:S(2)}) collective-permute-start(bf16[8,144,128]{2,1,0:T(8,128)(2,1)} %copy-done.34), channel_id=1, source_target_pairs={{0,2},{1,3},{2,0},{3,1},{4,6},{5,7},{6,4},{7,5},{8,10},{9,11},{10,... | collective-permute-start | bytes 884744 | tf_op jit(solution)/shard_map/ppermute | solution.py:313
  58.7 1.6 %collective-permute-start.13 = (bf16[8,144,128]{2,1,0:T(8,128)(2,1)}, bf16[8,144,128]{2,1,0:T(8,128)(2,1)S(1)}, u32[]{:S(2)}, u32[]{:S(2)}) collective-permute-start(bf16[8,144,128]{2,1,0:T(8,128)(2,1)} %copy-done.33), channel_id=1, source_target_pairs={{0,4},{1,5},{2,6},{3,7},{4,0},{5,1},{6,2},{7,3},{8,12},{9,13},{10,... | collective-permute-start | bytes 884744 | tf_op jit(solution)/shard_map/ppermute | solution.py:313
  60.3 0.9 %copy-done.10 = bf16[256,256]{1,0:T(8,128)(2,1)S(1)} copy-done((bf16[256,256]{1,0:T(8,128)(2,1)S(1)}, bf16[256,256]{1,0:T(8,128)(2,1)}, u32[]{:S(2)}) %copy-start.10) | copy-done | bytes 131096
  61.2 0.9 %copy-done.12 = bf16[256,256]{1,0:T(8,128)(2,1)S(1)} copy-done((bf16[256,256]{1,0:T(8,128)(2,1)S(1)}, bf16[256,256]{1,0:T(8,128)(2,1)}, u32[]{:S(2)}) %copy-start.12) | copy-done | bytes 131096
  62.1 0.9 %copy-done.14 = bf16[256,256]{1,0:T(8,128)(2,1)S(1)} copy-done((bf16[256,256]{1,0:T(8,128)(2,1)S(1)}, bf16[256,256]{1,0:T(8,128)(2,1)}, u32[]{:S(2)}) %copy-start.14) | copy-done | bytes 131096
  67.3 2.3 %tick_two_second.1 = (bf16[256,256]{1,0:T(8,128)(2,1)}, bf16[256,256]{1,0:T(8,128)(2,1)}, bf16[256,256]{1,0:T(8,128)(2,1)}) custom-call(bf16[256,256]{1,0:T(8,128)(2,1)S(1)} %copy-done.10, bf16[256,256]{1,0:T(8,128)(2,1)S(1)} %copy-done.12, bf16[256,256]{1,0:T(8,128)(2,1)S(1)} %copy-done.14, bf16[256,128]{1,0:T(8,128)(2,1)S(1)} %copy-done.30, ...), custom_call_target="tpu_custom_call" | custom-call | flops 679477248 | bytes 4000000 | tf_op jit(solution)/shard_map/tick_two_second/pallas_call | solution.py:433
  70.6 2.7 %collective-permute-start.14 = (bf16[4,144,128]{2,1,0:T(8,128)(2,1)S(1)}, bf16[4,144,128]{2,1,0:T(8,128)(2,1)S(1)}, u32[]{:S(2)}, u32[]{:S(2)}) collective-permute-start(bf16[4,144,128]{2,1,0:T(8,128)(2,1)S(1)} %dynamic-slice_bitcast_fusion), channel_id=1, source_target_pairs={{0,8},{1,9},{2,10},{3,11},{4,12},{5,13},{6,14},{7,15},{8,0},{9,1},... | collective-permute-start | bytes 442376 | tf_op jit(solution)/shard_map/ppermute | solution.py:313
  73.3 1.7 %collective-permute-done.6 = bf16[4,144,128]{2,1,0:T(8,128)(2,1)S(1)} collective-permute-done((bf16[4,144,128]{2,1,0:T(8,128)(2,1)S(1)}, bf16[4,144,128]{2,1,0:T(8,128)(2,1)S(1)}, u32[]{:S(2)}, u32[]{:S(2)}) %collective-permute-start.6) | collective-permute-done | bytes 147488 | tf_op jit(solution)/shard_map/ppermute | solution.py:313
  75.6 2.2 %collective-permute-done.10 = bf16[4,144,128]{2,1,0:T(8,128)(2,1)S(1)} collective-permute-done((bf16[4,144,128]{2,1,0:T(8,128)(2,1)S(1)}, bf16[4,144,128]{2,1,0:T(8,128)(2,1)S(1)}, u32[]{:S(2)}, u32[]{:S(2)}) %collective-permute-start.10) | collective-permute-done | bytes 147488 | tf_op jit(solution)/shard_map/ppermute | solution.py:313
  77.9 1.1 %collective-permute-start.11 = (bf16[2,144,128]{2,1,0:T(8,128)(2,1)S(1)}, bf16[2,144,128]{2,1,0:T(8,128)(2,1)S(1)}, u32[]{:S(2)}, u32[]{:S(2)}) collective-permute-start(bf16[2,144,128]{2,1,0:T(8,128)(2,1)S(1)} %dynamic-slice_bitcast_fusion.4), channel_id=1, source_target_pairs={{0,8},{1,9},{2,10},{3,11},{4,12},{5,13},{6,14},{7,15},{8,0},{9,1},... | collective-permute-start | bytes 221192 | tf_op jit(solution)/shard_map/ppermute | solution.py:313
  79.5 2.4 %collective-permute-start.8 = (bf16[1,144,128]{2,1,0:T(8,128)(2,1)S(1)}, bf16[1,144,128]{2,1,0:T(8,128)(2,1)S(1)}, u32[]{:S(2)}, u32[]{:S(2)}) collective-permute-start(bf16[1,144,128]{2,1,0:T(8,128)(2,1)S(1)} %constant_dynamic-slice_fusion.2), channel_id=1, source_target_pairs={{0,8},{1,9},{2,10},{3,11},{4,12},{5,13},{6,14},{7,15},{8,0},{9,1},... | collective-permute-start | bytes 110600 | tf_op jit(solution)/shard_map/ppermute | solution.py:313
  81.9 2.4 %collective-permute-done.11 = bf16[2,144,128]{2,1,0:T(8,128)(2,1)S(1)} collective-permute-done((bf16[2,144,128]{2,1,0:T(8,128)(2,1)S(1)}, bf16[2,144,128]{2,1,0:T(8,128)(2,1)S(1)}, u32[]{:S(2)}, u32[]{:S(2)}) %collective-permute-start.11) | collective-permute-done | bytes 73760 | tf_op jit(solution)/shard_map/ppermute | solution.py:313
  84.8 1.4 %collective-permute-start.16 = (bf16[1,144,128]{2,1,0:T(8,128)(2,1)S(1)}, bf16[1,144,128]{2,1,0:T(8,128)(2,1)S(1)}, u32[]{:S(2)}, u32[]{:S(2)}) collective-permute-start(bf16[1,144,128]{2,1,0:T(8,128)(2,1)S(1)} %constant_dynamic-slice_fusion), channel_id=1, source_target_pairs={{0,2},{1,3},{2,0},{3,1},{4,6},{5,7},{6,4},{7,5},{8,10},{9,11},{10,... | collective-permute-start | bytes 110600 | tf_op jit(solution)/shard_map/ppermute | solution.py:313
  86.2 2.2 %collective-permute-done.12 = bf16[1,144,128]{2,1,0:T(8,128)(2,1)S(1)} collective-permute-done((bf16[1,144,128]{2,1,0:T(8,128)(2,1)S(1)}, bf16[1,144,128]{2,1,0:T(8,128)(2,1)S(1)}, u32[]{:S(2)}, u32[]{:S(2)}) %collective-permute-start.12) | collective-permute-done | bytes 36896 | tf_op jit(solution)/shard_map/ppermute | solution.py:313
  (106 shorter events, 19.1 us)
Async XLA Ops:
  0.6 0.9 %copy-start.2 = (bf16[1,4,8,8,256]{4,3,2,1,0:T(8,128)(2,1)S(1)}, bf16[1,4,8,8,256]{4,3,2,1,0:T(8,128)(2,1)}, u32[]{:S(2)}) copy-start(bf16[1,4,8,8,256]{4,3,2,1,0:T(8,128)(2,1)} %param.9) | copy-start | bytes 393220
  4.2 13.8 %collective-permute-start = (bf16[576,128]{1,0:T(8,128)(2,1)}, bf16[576,128]{1,0:T(8,128)(2,1)}, u32[]{:S(2)}, u32[]{:S(2)}) collective-permute-start(bf16[576,128]{1,0:T(8,128)(2,1)} %get-tuple-element.31), channel_id=1, source_target_pairs={{0,1},{1,2},{2,3},{3,4},{4,5},{5,6},{6,7},{7,8},{8,9},{9,10},{10,1... | collective-permute-start | bytes 442376 | tf_op jit(solution)/shard_map/ppermute | solution.py:354
  9.7 8.3 %collective-permute-start.1 = (bf16[576,128]{1,0:T(8,128)(2,1)}, bf16[576,128]{1,0:T(8,128)(2,1)}, u32[]{:S(2)}, u32[]{:S(2)}) collective-permute-start(bf16[576,128]{1,0:T(8,128)(2,1)} %get-tuple-element.32), channel_id=1, source_target_pairs={{1,0},{2,1},{3,2},{4,3},{5,4},{6,5},{7,6},{8,7},{9,8},{10,9},{11,1... | collective-permute-start | bytes 442376 | tf_op jit(solution)/shard_map/ppermute | solution.py:355
  11.0 7.0 %copy-start = (bf16[1,27,128,128]{3,2,1,0:T(8,128)(2,1)S(1)}, bf16[1,27,128,128]{3,2,1,0:T(8,128)(2,1)}, u32[]{:S(2)}) copy-start(bf16[1,27,128,128]{3,2,1,0:T(8,128)(2,1)} %param.12) | copy-start | bytes 2654212
  11.0 7.0 %copy-start.1 = (bf16[1,27,128,128]{3,2,1,0:T(8,128)(2,1)S(1)}, bf16[1,27,128,128]{3,2,1,0:T(8,128)(2,1)}, u32[]{:S(2)}) copy-start(bf16[1,27,128,128]{3,2,1,0:T(8,128)(2,1)} %param.13) | copy-start | bytes 2654212
  18.0 0.9 %copy-start.3 = (bf16[1,4,8,8,256]{4,3,2,1,0:T(8,128)(2,1)S(1)}, bf16[1,4,8,8,256]{4,3,2,1,0:T(8,128)(2,1)}, u32[]{:S(2)}) copy-start(bf16[1,4,8,8,256]{4,3,2,1,0:T(8,128)(2,1)} %param.9) | copy-start | bytes 393220
  18.9 0.9 %copy-start.6 = (bf16[1,4,8,8,256]{4,3,2,1,0:T(8,128)(2,1)S(1)}, bf16[1,4,8,8,256]{4,3,2,1,0:T(8,128)(2,1)}, u32[]{:S(2)}) copy-start(bf16[1,4,8,8,256]{4,3,2,1,0:T(8,128)(2,1)} %param.7) | copy-start | bytes 393220
  19.8 0.9 %copy-start.8 = (bf16[1,4,8,8,256]{4,3,2,1,0:T(8,128)(2,1)S(1)}, bf16[1,4,8,8,256]{4,3,2,1,0:T(8,128)(2,1)}, u32[]{:S(2)}) copy-start(bf16[1,4,8,8,256]{4,3,2,1,0:T(8,128)(2,1)} %param.8) | copy-start | bytes 393220
  20.7 7.5 %copy-start.21 = (bf16[4,8,8,256]{3,2,1,0:T(8,128)(2,1)S(1)}, bf16[4,8,8,256]{3,2,1,0:T(8,128)(2,1)}, u32[]{:S(2)}) copy-start(bf16[4,8,8,256]{3,2,1,0:T(8,128)(2,1)} %param.10) | copy-start | bytes 393220
  20.7 7.5 %copy-start.22 = (bf16[4,8,8,256]{3,2,1,0:T(8,128)(2,1)S(1)}, bf16[4,8,8,256]{3,2,1,0:T(8,128)(2,1)}, u32[]{:S(2)}) copy-start(bf16[4,8,8,256]{3,2,1,0:T(8,128)(2,1)} %param.11) | copy-start | bytes 393220
  20.7 14.2 %copy-start.4 = (bf16[1,4,8,8,256]{4,3,2,1,0:T(8,128)(2,1)S(1)}, bf16[1,4,8,8,256]{4,3,2,1,0:T(8,128)(2,1)}, u32[]{:S(2)}) copy-start(bf16[1,4,8,8,256]{4,3,2,1,0:T(8,128)(2,1)} %param.9) | copy-start | bytes 393220
  26.6 1.6 %collective-permute-start.2 = (bf16[2,256,256]{2,1,0:T(8,128)(2,1)S(1)}, bf16[2,256,256]{2,1,0:T(8,128)(2,1)S(1)}, u32[]{:S(2)}, u32[]{:S(2)}) collective-permute-start(bf16[2,256,256]{2,1,0:T(8,128)(2,1)S(1)} %get-tuple-element.34), channel_id=1, source_target_pairs={{0,16},{16,0},{1,17},{17,1},{2,18},{18,2},{3,19},{19,3},{4,20},{20... | collective-permute-start | bytes 786440 | tf_op jit(solution)/shard_map/ppermute | solution.py:390
  28.9 18.3 %copy-start.9 = (bf16[256,256]{1,0:T(8,128)(2,1)}, bf16[256,256]{1,0:T(8,128)(2,1)S(1)}, u32[]{:S(2)}) copy-start(bf16[256,256]{1,0:T(8,128)(2,1)S(1)} %get-tuple-element.35.state) | copy-start | bytes 393220
  28.9 18.3 %copy-start.11 = (bf16[256,256]{1,0:T(8,128)(2,1)}, bf16[256,256]{1,0:T(8,128)(2,1)S(1)}, u32[]{:S(2)}) copy-start(bf16[256,256]{1,0:T(8,128)(2,1)S(1)} %get-tuple-element.36.act) | copy-start | bytes 393220
  28.9 18.3 %copy-start.13 = (bf16[256,256]{1,0:T(8,128)(2,1)}, bf16[256,256]{1,0:T(8,128)(2,1)S(1)}, u32[]{:S(2)}) copy-start(bf16[256,256]{1,0:T(8,128)(2,1)S(1)} %get-tuple-element.37.grad) | copy-start | bytes 393220
  28.9 7.9 %collective-permute-start.3 = (bf16[576,128]{1,0:T(8,128)(2,1)S(1)}, bf16[576,128]{1,0:T(8,128)(2,1)S(1)}, u32[]{:S(2)}, u32[]{:S(2)}) collective-permute-start(bf16[576,128]{1,0:T(8,128)(2,1)S(1)} %get-tuple-element.38), channel_id=1, source_target_pairs={{0,1},{1,2},{2,3},{3,4},{4,5},{5,6},{6,7},{7,8},{8,9},{9,10},{10,1... | collective-permute-start | bytes 442376 | tf_op jit(solution)/shard_map/ppermute | solution.py:354
  33.5 8.7 %collective-permute-start.4 = (bf16[576,128]{1,0:T(8,128)(2,1)S(1)}, bf16[576,128]{1,0:T(8,128)(2,1)S(1)}, u32[]{:S(2)}, u32[]{:S(2)}) collective-permute-start(bf16[576,128]{1,0:T(8,128)(2,1)S(1)} %get-tuple-element.39), channel_id=1, source_target_pairs={{1,0},{2,1},{3,2},{4,3},{5,4},{6,5},{7,6},{8,7},{9,8},{10,9},{11,1... | collective-permute-start | bytes 442376 | tf_op jit(solution)/shard_map/ppermute | solution.py:355
  54.0 15.7 %collective-permute-start.5 = (bf16[8,144,128]{2,1,0:T(8,128)(2,1)}, bf16[8,144,128]{2,1,0:T(8,128)(2,1)S(1)}, u32[]{:S(2)}, u32[]{:S(2)}) collective-permute-start(bf16[8,144,128]{2,1,0:T(8,128)(2,1)} %get-tuple-element.52), channel_id=1, source_target_pairs={{0,1},{1,0},{2,3},{3,2},{4,5},{5,4},{6,7},{7,6},{8,9},{9,8},{10,11... | collective-permute-start | bytes 884744 | tf_op jit(solution)/shard_map/ppermute | solution.py:313
  55.4 14.5 %collective-permute-start.9 = (bf16[8,144,128]{2,1,0:T(8,128)(2,1)}, bf16[8,144,128]{2,1,0:T(8,128)(2,1)S(1)}, u32[]{:S(2)}, u32[]{:S(2)}) collective-permute-start(bf16[8,144,128]{2,1,0:T(8,128)(2,1)} %copy-done.34), channel_id=1, source_target_pairs={{0,2},{1,3},{2,0},{3,1},{4,6},{5,7},{6,4},{7,5},{8,10},{9,11},{10,... | collective-permute-start | bytes 884744 | tf_op jit(solution)/shard_map/ppermute | solution.py:313
  58.7 11.8 %collective-permute-start.13 = (bf16[8,144,128]{2,1,0:T(8,128)(2,1)}, bf16[8,144,128]{2,1,0:T(8,128)(2,1)S(1)}, u32[]{:S(2)}, u32[]{:S(2)}) collective-permute-start(bf16[8,144,128]{2,1,0:T(8,128)(2,1)} %copy-done.33), channel_id=1, source_target_pairs={{0,4},{1,5},{2,6},{3,7},{4,0},{5,1},{6,2},{7,3},{8,12},{9,13},{10,... | collective-permute-start | bytes 884744 | tf_op jit(solution)/shard_map/ppermute | solution.py:313
  67.3 2.3 %copy-start.20 = (bf16[8,144,128]{2,1,0:T(8,128)(2,1)S(1)}, bf16[8,144,128]{2,1,0:T(8,128)(2,1)}, u32[]{:S(2)}) copy-start(bf16[8,144,128]{2,1,0:T(8,128)(2,1)} %copy-done.19) | copy-start | bytes 884740
  67.3 2.5 %copy-start.18 = (bf16[8,144,128]{2,1,0:T(8,128)(2,1)S(1)}, bf16[8,144,128]{2,1,0:T(8,128)(2,1)}, u32[]{:S(2)}) copy-start(bf16[8,144,128]{2,1,0:T(8,128)(2,1)} %copy-done.17) | copy-start | bytes 884740
  67.3 3.2 %copy-start.16 = (bf16[8,144,128]{2,1,0:T(8,128)(2,1)S(1)}, bf16[8,144,128]{2,1,0:T(8,128)(2,1)}, u32[]{:S(2)}) copy-start(bf16[8,144,128]{2,1,0:T(8,128)(2,1)} %copy-done.15) | copy-start | bytes 884740
  69.8 5.2 %collective-permute-start.6 = (bf16[4,144,128]{2,1,0:T(8,128)(2,1)S(1)}, bf16[4,144,128]{2,1,0:T(8,128)(2,1)S(1)}, u32[]{:S(2)}, u32[]{:S(2)}) collective-permute-start(bf16[4,144,128]{2,1,0:T(8,128)(2,1)S(1)} %dynamic-slice_bitcast_fusion.2), channel_id=1, source_target_pairs={{0,2},{1,3},{2,0},{3,1},{4,6},{5,7},{6,4},{7,5},{8,10},{9,11},{10,... | collective-permute-start | bytes 442376 | tf_op jit(solution)/shard_map/ppermute | solution.py:313
  70.0 7.8 %collective-permute-start.10 = (bf16[4,144,128]{2,1,0:T(8,128)(2,1)S(1)}, bf16[4,144,128]{2,1,0:T(8,128)(2,1)S(1)}, u32[]{:S(2)}, u32[]{:S(2)}) collective-permute-start(bf16[4,144,128]{2,1,0:T(8,128)(2,1)S(1)} %dynamic-slice_bitcast_fusion.1), channel_id=1, source_target_pairs={{0,4},{1,5},{2,6},{3,7},{4,0},{5,1},{6,2},{7,3},{8,12},{9,13},{10,... | collective-permute-start | bytes 442376 | tf_op jit(solution)/shard_map/ppermute | solution.py:313
  70.6 8.3 %collective-permute-start.14 = (bf16[4,144,128]{2,1,0:T(8,128)(2,1)S(1)}, bf16[4,144,128]{2,1,0:T(8,128)(2,1)S(1)}, u32[]{:S(2)}, u32[]{:S(2)}) collective-permute-start(bf16[4,144,128]{2,1,0:T(8,128)(2,1)S(1)} %dynamic-slice_bitcast_fusion), channel_id=1, source_target_pairs={{0,8},{1,9},{2,10},{3,11},{4,12},{5,13},{6,14},{7,15},{8,0},{9,1},... | collective-permute-start | bytes 442376 | tf_op jit(solution)/shard_map/ppermute | solution.py:313
  75.1 4.4 %collective-permute-start.7 = (bf16[2,144,128]{2,1,0:T(8,128)(2,1)S(1)}, bf16[2,144,128]{2,1,0:T(8,128)(2,1)S(1)}, u32[]{:S(2)}, u32[]{:S(2)}) collective-permute-start(bf16[2,144,128]{2,1,0:T(8,128)(2,1)S(1)} %dynamic-slice_bitcast_fusion.5), channel_id=1, source_target_pairs={{0,4},{1,5},{2,6},{3,7},{4,0},{5,1},{6,2},{7,3},{8,12},{9,13},{10,... | collective-permute-start | bytes 221192 | tf_op jit(solution)/shard_map/ppermute | solution.py:313
  77.9 6.5 %collective-permute-start.11 = (bf16[2,144,128]{2,1,0:T(8,128)(2,1)S(1)}, bf16[2,144,128]{2,1,0:T(8,128)(2,1)S(1)}, u32[]{:S(2)}, u32[]{:S(2)}) collective-permute-start(bf16[2,144,128]{2,1,0:T(8,128)(2,1)S(1)} %dynamic-slice_bitcast_fusion.4), channel_id=1, source_target_pairs={{0,8},{1,9},{2,10},{3,11},{4,12},{5,13},{6,14},{7,15},{8,0},{9,1},... | collective-permute-start | bytes 221192 | tf_op jit(solution)/shard_map/ppermute | solution.py:313
  79.0 5.7 %collective-permute-start.15 = (bf16[2,144,128]{2,1,0:T(8,128)(2,1)S(1)}, bf16[2,144,128]{2,1,0:T(8,128)(2,1)S(1)}, u32[]{:S(2)}, u32[]{:S(2)}) collective-permute-start(bf16[2,144,128]{2,1,0:T(8,128)(2,1)S(1)} %dynamic-slice_bitcast_fusion.3), channel_id=1, source_target_pairs={{0,1},{1,0},{2,3},{3,2},{4,5},{5,4},{6,7},{7,6},{8,9},{9,8},{10,11... | collective-permute-start | bytes 221192 | tf_op jit(solution)/shard_map/ppermute | solution.py:313
  79.5 6.7 %collective-permute-start.8 = (bf16[1,144,128]{2,1,0:T(8,128)(2,1)S(1)}, bf16[1,144,128]{2,1,0:T(8,128)(2,1)S(1)}, u32[]{:S(2)}, u32[]{:S(2)}) collective-permute-start(bf16[1,144,128]{2,1,0:T(8,128)(2,1)S(1)} %constant_dynamic-slice_fusion.2), channel_id=1, source_target_pairs={{0,8},{1,9},{2,10},{3,11},{4,12},{5,13},{6,14},{7,15},{8,0},{9,1},... | collective-permute-start | bytes 110600 | tf_op jit(solution)/shard_map/ppermute | solution.py:313
  84.4 4.0 %collective-permute-start.12 = (bf16[1,144,128]{2,1,0:T(8,128)(2,1)S(1)}, bf16[1,144,128]{2,1,0:T(8,128)(2,1)S(1)}, u32[]{:S(2)}, u32[]{:S(2)}) collective-permute-start(bf16[1,144,128]{2,1,0:T(8,128)(2,1)S(1)} %constant_dynamic-slice_fusion.1), channel_id=1, source_target_pairs={{0,1},{1,0},{2,3},{3,2},{4,5},{5,4},{6,7},{7,6},{8,9},{9,8},{10,11... | collective-permute-start | bytes 110600 | tf_op jit(solution)/shard_map/ppermute | solution.py:313
  84.8 4.0 %collective-permute-start.16 = (bf16[1,144,128]{2,1,0:T(8,128)(2,1)S(1)}, bf16[1,144,128]{2,1,0:T(8,128)(2,1)S(1)}, u32[]{:S(2)}, u32[]{:S(2)}) collective-permute-start(bf16[1,144,128]{2,1,0:T(8,128)(2,1)S(1)} %constant_dynamic-slice_fusion), channel_id=1, source_target_pairs={{0,2},{1,3},{2,0},{3,1},{4,6},{5,7},{6,4},{7,5},{8,10},{9,11},{10,... | collective-permute-start | bytes 110600 | tf_op jit(solution)/shard_map/ppermute | solution.py:313
  (20 other events, 15.6 us)

commit v4 on v3

--- a/solution.py
+++ b/solution.py
@@ -8,9 +8,28 @@
 from jax.experimental.pallas import tpu as pltpu
 from jax.sharding import PartitionSpec as P
 
-VMEM = pltpu.CompilerParams(vmem_limit_bytes=20 * 1024 * 1024)
+VMEM = pltpu.CompilerParams(vmem_limit_bytes=65408 * 1024)
 F32 = jnp.float32
 BF16 = jnp.bfloat16
+
+
+class Copies:
+    def __init__(self, sems):
+        self.sems, self.used, self.open = sems, 0, {}
+
+    def start(self, name, source, target):
+        copy = pltpu.make_async_copy(source, target, self.sems.at[self.used])
+        self.used += 1
+        copy.start()
+        self.open[name] = copy
+
+    def need(self, *names):
+        for name in names:
+            if name in self.open:
+                self.open.pop(name).wait()
+
+    def finish(self):
+        self.need(*list(self.open))
 
 
 def half_erf(value):
@@ -95,17 +114,44 @@
         copy.wait()
 
 
-def join_kernel(plane, places, forward, lifted, lowered, fresh, target, state, act, grad, low, high):
+def join_kernel(plane, places, forward_in, lifted_in, lowered_in, fresh_in, target_in, state_out,
+                act_out, grad_out, low_out, high_out, forward, lifted, lowered, fresh, target, state,
+                act, grad, low, high, sems):
+    copies = Copies(sems)
+    copies.start("lifted", lifted_in.at[0], lifted)
+    copies.start("lowered", lowered_in, lowered)
+    copies.start("fresh", fresh_in, fresh)
+    copies.start("forward", forward_in, forward)
+    copies.start("target", target_in, target)
+    copies.finish()
     first_place, last_place = places[0] == 0, places[0] == places[1]
-    state[...] = jnp.where(first_place, fresh[...], lifted[0])
+    state[...] = jnp.where(first_place, fresh[...], lifted[...])
     own = forward[...]
     act[...] = jnp.where(last_place, own, lowered[0])
     error = (own.astype(F32) - target[...].astype(F32)).astype(BF16)
     grad[...] = jnp.where(last_place, error, lowered[1])
     pack_edges(state, act, grad, low, high, plane)
-
-
-def first_kernel(ydim, zdim, flags, state, act, grad, below, above, first, second, second_back,
+    for index, (source, out) in enumerate(
+        ((low, low_out), (high, high_out), (state, state_out), (act, act_out), (grad, grad_out))
+    ):
+        copies.start(index, source, out)
+    copies.finish()
+
+
+def flip_kernel(first_in, second_in, first_out, second_out, source, flipped, sems):
+    copies = Copies(sems)
+    copies.start(0, first_in, source.at[0])
+    copies.start(1, second_in, source.at[1])
+    offsets = source.shape[1]
+    for which, out in enumerate((first_out, second_out)):
+        copies.need(which)
+        for k in range(offsets):
+            flipped[which, offsets - 1 - k] = jnp.transpose(source[which, k])
+        copies.start(2 + which, flipped.at[which], out)
+    copies.finish()
+
+
+def first_kernel(ydim, zdim, copies, made, flags, state, act, grad, below, above, first, second, second_back,
                  new_one, back_two, mid, back, carry, gate, stack):
     plane = ydim * zdim
     cells, double = state.shape
@@ -134,73 +180,131 @@
         ref[plane + cells : inner, :] = (value[plane + cells :].astype(F32) * high_flag).astype(BF16)
 
     core = slice(plane, plane + cells)
+    copies.need("below", "above", "state")
     fill_shifts(stack, smooth_gate(two(state, right, 0)), ydim, zdim)
+    copies.need("first")
     f_one = (one(state, left, 0) + convolve(stack, first, inner, plane)).astype(BF16)
     new_one[...] = f_one[core]
     store_masked(mid, smooth_gate(f_one.astype(F32)).astype(BF16))
 
+    made("new_one", "mid")
+
+    copies.need("act")
     y_one = two(act, left, 1)
     half = half_erf(y_one)
     gated = y_one * half
     gate[...] = gated[plane : plane + inner].astype(BF16)
     fill_shifts(stack, gated, ydim, zdim)
+    copies.need("second")
     r_two = (one(act, right, 1) - convolve(stack, second, inner, plane)).astype(BF16)
     back_two[...] = r_two[core]
     store_masked(back, smooth_gate(r_two.astype(F32)).astype(BF16))
 
+    made("gate", "back_two", "back")
+
+    copies.need("grad")
     fill_shifts(stack, two(grad, right, 2), ydim, zdim)
     slope = gate_slope(y_one[plane : plane + inner], half[plane : plane + inner])
+    copies.need("second_back")
     e_one = (one(grad, left, 2) + slope * convolve(stack, second_back, inner, plane)).astype(BF16)
     store_masked(carry, e_one)
-
-
-def second_kernel(ydim, zdim, state, act, grad, new_one, back_two, mid, back, carry, first, second,
-                  first_back, forward, rebuilt, passed, stack):
+    made("carry")
+
+
+def second_kernel(ydim, zdim, copies, made, state, act, grad, new_one, back_two, mid, back, carry,
+                  first, second, first_back, forward, rebuilt, passed, stack):
     plane = ydim * zdim
     cells, double = state.shape
     width = double // 2
     left, right = slice(0, width), slice(width, double)
-    forward[:, left] = new_one[...]
+
+    copies.need("back", "act", "back_two")
+    fill_shifts(stack, back[...].astype(F32), ydim, zdim)
     rebuilt[:, right] = back_two[...]
-    passed[:, left] = carry[plane : plane + cells, :]
-
-    fill_shifts(stack, back[...].astype(F32), ydim, zdim)
+    copies.need("first")
     rebuilt[:, left] = (
         act[:, left].astype(F32) - convolve(stack, first, cells, plane)
     ).astype(BF16)
+    made("rebuilt")
+    copies.need("carry", "grad")
     fill_shifts(stack, carry[...].astype(F32), ydim, zdim)
+    passed[:, left] = carry[plane : plane + cells, :]
     r_two = back_two[...].astype(F32)
+    copies.need("first_back")
     passed[:, right] = (
         grad[:, right].astype(F32)
         + gate_slope(r_two, half_erf(r_two)) * convolve(stack, first_back, cells, plane)
     ).astype(BF16)
+    made("passed")
+    copies.need("mid", "state", "new_one")
     fill_shifts(stack, mid[...].astype(F32), ydim, zdim)
+    forward[:, left] = new_one[...]
+    copies.need("second")
     forward[:, right] = (
         state[:, right].astype(F32) + convolve(stack, second, cells, plane)
     ).astype(BF16)
-
-
-def tick_kernel(ydim, zdim, paired, places, flags, state_in, act_in, grad_in, below, above, first,
-                second, first_back, second_back, forward, sent, back, carry, gate, state, act, grad,
-                new_one, back_two, mid, rebuilt, stack, sems):
-    copies = [
-        pltpu.make_async_copy(source, target, sems.at[index])
-        for index, (source, target) in enumerate(
-            ((state_in, state), (act_in, act), (grad_in, grad))
-        )
-    ]
-    for copy in copies:
-        copy.start()
-    for copy in copies:
-        copy.wait()
-    first_kernel(ydim, zdim, flags, state, act, grad, below, above, first, second, second_back,
-                 new_one, back_two, mid, back, carry, gate, stack)
-    second_kernel(ydim, zdim, state, act, grad, new_one, back_two, mid, back, carry, first, second,
-                  first_back, forward, rebuilt, sent.at[1], stack)
+    made("forward")
+
+
+def second_alone(ydim, zdim, *refs):
+    names = ("state", "act", "grad", "new_one", "back_two", "mid", "back", "carry", "first", "second",
+             "first_back")
+    sources, outs, local, results = refs[:11], refs[11:14], refs[14:25], refs[25:28]
+    stack, sems = refs[28:]
+    copies = Copies(sems)
+    order = ("back", "act", "back_two", "first", "carry", "grad", "first_back", "mid", "state", "new_one",
+             "second")
+    for name in order:
+        copies.start(name, sources[names.index(name)], local[names.index(name)])
+    where = {"forward": 0, "rebuilt": 1, "passed": 2}
+
+    def made(name):
+        copies.start("out_" + name, results[where[name]], outs[where[name]])
+
+    second_kernel(ydim, zdim, copies, made, *local, *results, stack)
+    copies.finish()
+
+
+def tick_kernel(ydim, zdim, paired, places, flags, state_in, act_in, grad_in, below_in, above_in,
+                first_in, second_in, first_back_in, second_back_in, forward_out, sent_out, back_out,
+                carry_out, gate_out, forward, sent, back, carry, gate, state, act, grad, below, above,
+                first, second, first_back, second_back, new_one, back_two, mid, rebuilt, stack, sems):
+    copies = Copies(sems)
+    for name, source, target in (
+        ("below", below_in, below),
+        ("above", above_in, above),
+        ("state", state_in, state),
+        ("first", first_in, first),
+        ("act", act_in, act),
+        ("second", second_in, second),
+        ("grad", grad_in, grad),
+        ("second_back", second_back_in, second_back),
+        ("first_back", first_back_in, first_back),
+    ):
+        copies.start(name, source, target)
+    stores = {
+        "back": (back, back_out),
+        "carry": (carry, carry_out),
+        "gate": (gate, gate_out),
+        "forward": (forward, forward_out),
+        "passed": (sent.at[1], sent_out.at[1]),
+    }
+
+    def made(*names):
+        for name in names:
+            if name in stores:
+                copies.start("out_" + name, *stores[name])
+
+    first_kernel(ydim, zdim, copies, made, flags, state, act, grad, below, above, first, second,
+                 second_back, new_one, back_two, mid, back, carry, gate, stack)
+    second_kernel(ydim, zdim, copies, made, state, act, grad, new_one, back_two, mid, back, carry, first,
+                  second, first_back, forward, rebuilt, sent.at[1], stack)
     if paired:
         sent[0] = jnp.where(places[0] == 0, forward[...], rebuilt[...])
     else:
         sent[0] = rebuilt[...]
+    copies.start("out_sent", sent.at[0], sent_out.at[0])
+    copies.finish()
 
 
 def correlate(stack, field, cotangent, ydim, zdim, emit):
@@ -231,11 +335,21 @@
     correlate(stack, gate, grad[:, width:].astype(F32), ydim, zdim, store(1))
 
 
-def corr_kernel(ydim, zdim, grad, back, carry, gate, out, stack):
+def corr_kernel(ydim, zdim, grad_in, back_in, carry_in, gate_in, out_ref, grad, back, carry, gate, out,
+                stack, sems):
+    copies = Copies(sems)
+    for name, source, target in (
+        ("carry", carry_in, carry), ("back", back_in, back), ("grad", grad_in, grad), ("gate", gate_in, gate)
+    ):
+        copies.start(name, source, target)
+    copies.finish()
+
     def put(which, at, block):
         out[which, at, :] = block
 
     both_grads(ydim, zdim, grad, back, carry, gate, stack, put)
+    copies.start("out", out, out_ref)
+    copies.finish()
 
 
 def ways_of(count, rows):
@@ -245,11 +359,31 @@
     return [(way * span, span, bits[way % len(bits) :] + bits[: way % len(bits)]) for way in range(ways)]
 
 
-def last_kernel(ydim, zdim, factor, count, direct, spot, flags, state, act, grad, below, above, first,
-                second, second_back, so_far, new_one, back_two, mid, back, carry, *refs):
-    refs, (gate, stack, sums) = refs[:-3], refs[-3:]
-    first_kernel(ydim, zdim, flags, state, act, grad, below, above, first, second, second_back,
-                 new_one, back_two, mid, back, carry, gate, stack)
+def last_kernel(ydim, zdim, factor, count, direct, spot, flags, *args):
+    names = ("state", "act", "grad", "below", "above", "first", "second", "second_back", "so_far")
+    made_names = ("new_one", "back_two", "mid", "back", "carry")
+    n_outs = 6 if direct else 1
+    sources, args = args[:9], args[9:]
+    outs, args = args[:5], args[5:]
+    final_outs, args = args[:n_outs], args[n_outs:]
+    local, args = args[:9], args[9:]
+    results, args = args[:5], args[5:]
+    refs, args = args[:n_outs], args[n_outs:]
+    gate, stack, sums, sems = args
+    copies = Copies(sems)
+    for name in ("below", "above", "state", "first", "act", "second", "grad", "second_back", "so_far"):
+        copies.start(name, sources[names.index(name)], local[names.index(name)])
+
+    def made(*done):
+        for name in done:
+            if name in made_names:
+                index = made_names.index(name)
+                copies.start("out_" + name, results[index], outs[index])
+
+    first_kernel(ydim, zdim, copies, made, flags, *local[:8], *results, gate, stack)
+    back, carry = results[3], results[4]
+    grad, so_far = local[2], local[8]
+    copies.need("so_far")
 
     def put(which, at, block):
         sums[which, at, :] = (block + so_far[which, at, :]) * factor
@@ -257,11 +391,13 @@
     both_grads(ydim, zdim, grad, back, carry, gate, stack, put)
     if not direct:
         refs[0][...] = sums[...].astype(BF16)
+        copies.start("out", refs[0], final_outs[0])
+        copies.finish()
         return
     rows = sums.shape[1] // count
     for index, (start, span, order) in enumerate(ways_of(count, rows)):
         mine = (spot[0] // order[0]) % 2
-        for kept in range(2):
+        for kept in (0, 1):
             side = mine if kept else 1 - mine
             out = refs[2 * index + (0 if kept else 1)]
             for j in range(count // 2):
@@ -278,10 +414,9 @@
                         pieces.append(sums[which, pl.ds(at, upper - lower), :])
                 value = pieces[0] if len(pieces) == 1 else jnp.concatenate(pieces, axis=0)
                 out[j] = value.astype(BF16)
-
-
-def whole(count):
-    return [pl.BlockSpec(memory_space=pltpu.VMEM)] * count
+            at = 2 * index + (0 if kept else 1)
+            copies.start(("half", at), out, final_outs[at])
+    copies.finish()
 
 
 def split_blocks(sums, count):
@@ -334,8 +469,6 @@
     flat = lambda block: block.reshape(cells, 2 * width)
     first = w_first[0].reshape(3, 9 * width, width)
     second = w_second[0].reshape(3, 9 * width, width)
-    first_back = jnp.transpose(w_first[0][::-1], (0, 2, 1)).reshape(3, 9 * width, width)
-    second_back = jnp.transpose(w_second[0][::-1], (0, 2, 1)).reshape(3, 9 * width, width)
     last_section = lax.axis_size("section") - 1
     place = lax.axis_index("section")
     count = lax.axis_size("space")
@@ -358,59 +491,64 @@
     state, act, grad = flat(fwd_in), flat(bwd_act), flat(bwd_grad)
     smem = pl.BlockSpec(memory_space=pltpu.SMEM)
     hbm = pl.BlockSpec(memory_space=pltpu.HBM)
-    scratch = lambda like: pltpu.VMEM(like.shape, like.dtype)
-    inner_stack = pltpu.VMEM((cells + 2 * plane, 9 * width), BF16)
-    outer_stack = pltpu.VMEM((cells + 4 * plane, 9 * width), BF16)
+    inner_stack = array((cells + 2 * plane, 9 * width), BF16)
+    outer_stack = array((cells + 4 * plane, 9 * width), BF16)
+    small_stack = array((cells, 9 * width), BF16)
+    weight = array((3, 9 * width, width), BF16)
+    raw_weight = array((27, width, width), BF16)
+    sums_shape = array((2, offsets, width), F32)
     places = jnp.stack([place, jnp.full_like(place, last_section)]).astype(jnp.int32)
 
-    low, high = pl.pallas_call(
-        functools.partial(edges_kernel, plane),
-        out_shape=(edge, edge),
-        in_specs=[hbm] * 3,
-        out_specs=(hbm, hbm),
-        scratch_shapes=[pltpu.SemaphoreType.DMA((12,))],
-        compiler_params=VMEM,
-        name="edges",
-    )(state, act, grad)
+    def call(kernel, name, scalars, inputs, outs, scratch, copies, flops=0):
+        return pl.pallas_call(
+            kernel,
+            out_shape=tuple(outs),
+            in_specs=[smem] * len(scalars) + [hbm] * len(inputs),
+            out_specs=(hbm,) * len(outs),
+            scratch_shapes=[pltpu.VMEM(like.shape, like.dtype) for like in scratch]
+            + [pltpu.SemaphoreType.DMA((copies,))],
+            compiler_params=VMEM,
+            cost_estimate=pl.CostEstimate(
+                flops=flops, bytes_accessed=sum(x.size * 2 for x in inputs), transcendentals=0
+            ),
+            name=name,
+        )(*scalars, *inputs)
+
+    work = 2 * 27 * cells * width * width
+    low, high = call(functools.partial(edges_kernel, plane), "edges", (), (state, act, grad), (edge,) * 2, (), 12)
     below, above = exchange(low, high)
+    first_back, second_back = call(
+        flip_kernel, "flip", (), (w_first[0], w_second[0]), (raw_weight,) * 2,
+        (array((2,) + raw_weight.shape, BF16),) * 2, 4,
+    )
+    first_back, second_back = first_back.reshape(weight.shape), second_back.reshape(weight.shape)
 
     paired = last_section == 1
-    forward, sent, back, carry, gate = pl.pallas_call(
-        functools.partial(tick_kernel, ydim, zdim, paired),
-        out_shape=(state_shape, array((2, cells, 2 * width), BF16), wide, wide, wide),
-        in_specs=[smem] * 2 + [hbm] * 3 + whole(6),
-        out_specs=tuple(whole(5)),
-        scratch_shapes=[scratch(state_shape)] * 3
-        + [scratch(tile), scratch(tile), scratch(wide), scratch(state_shape), outer_stack]
-        + [pltpu.SemaphoreType.DMA((3,))],
-        compiler_params=VMEM,
-        name="tick_one",
-    )(places, flags, state, act, grad, below, above, first, second, first_back, second_back)
+    pair_shape = array((2, cells, 2 * width), BF16)
+    tick_outs = (state_shape, pair_shape, wide, wide, wide)
+    forward, sent, back, carry, gate = call(
+        functools.partial(tick_kernel, ydim, zdim, paired), "tick_one", (places, flags),
+        (state, act, grad, below, above, first, second, first_back, second_back), tick_outs,
+        tick_outs + (state_shape,) * 3 + (edge,) * 2 + (weight,) * 4
+        + (tile, tile, wide, state_shape, outer_stack), 15, 8 * work,
+    )
     if paired:
         lifted = lowered = lax.ppermute(sent, "section", [(0, 1), (1, 0)])
     else:
         lifted = lax.ppermute(forward[None], "section", [(s, s + 1) for s in range(last_section)])
         lowered = lax.ppermute(sent, "section", [(s + 1, s) for s in range(last_section)])
 
-    state_two, act_two, grad_two, low, high = pl.pallas_call(
-        functools.partial(join_kernel, plane),
-        out_shape=(state_shape,) * 3 + (edge, edge),
-        in_specs=[smem] + whole(5),
-        out_specs=tuple(whole(5)),
-        compiler_params=VMEM,
-        name="join",
-    )(places, forward, lifted, lowered, flat(fresh), flat(target))
+    join_outs = (state_shape,) * 3 + (edge, edge)
+    state_two, act_two, grad_two, low, high = call(
+        functools.partial(join_kernel, plane), "join", (places,),
+        (forward, lifted, lowered, flat(fresh), flat(target)), join_outs,
+        (state_shape, state_shape, pair_shape, state_shape, state_shape) + join_outs, 10,
+    )
     below, above = exchange(low, high)
-
-    so_far = pl.pallas_call(
-        functools.partial(corr_kernel, ydim, zdim),
-        out_shape=array((2, offsets, width), F32),
-        in_specs=whole(4),
-        out_specs=whole(1)[0],
-        scratch_shapes=[pltpu.VMEM((cells, 9 * width), BF16)],
-        compiler_params=VMEM,
-        name="weight_grads",
-    )(grad, back, carry, gate)
+    (so_far,) = call(
+        functools.partial(corr_kernel, ydim, zdim), "weight_grads", (), (grad, back, carry, gate),
+        (sums_shape,), (state_shape, wide, wide, wide, sums_shape, small_stack), 5, 2 * work,
+    )
 
     rows = offsets // count
     direct = rows % 24 == 0
@@ -420,26 +558,19 @@
     else:
         outs = (array((2, offsets, width), BF16),)
     factor = 1.0 / math.sqrt(cells * count)
-    made = pl.pallas_call(
-        functools.partial(last_kernel, ydim, zdim, factor, count, direct),
-        out_shape=(tile, tile, wide, wide, wide) + outs,
-        in_specs=[smem] * 2 + whole(9),
-        out_specs=tuple(whole(5 + len(outs))),
-        scratch_shapes=[scratch(wide), outer_stack, pltpu.VMEM((2, offsets, width), F32)],
-        compiler_params=VMEM,
-        name="tick_two_first",
-    )(spot.astype(jnp.int32).reshape(1), flags, state_two, act_two, grad_two, below, above, first,
-      second, second_back, so_far)
-    forward, rebuilt, passed = pl.pallas_call(
-        functools.partial(second_kernel, ydim, zdim),
-        out_shape=(state_shape,) * 3,
-        in_specs=whole(11),
-        out_specs=tuple(whole(3)),
-        scratch_shapes=[inner_stack],
-        compiler_params=VMEM,
-        cost_estimate=pl.CostEstimate(flops=2 * 81 * cells * width * width, bytes_accessed=4000000, transcendentals=0),
-        name="tick_two_second",
-    )(state_two, act_two, grad_two, *made[:5], first, second, first_back)
+    kept = (tile, tile, wide, wide, wide)
+    made = call(
+        functools.partial(last_kernel, ydim, zdim, factor, count, direct), "tick_two_first",
+        (spot.astype(jnp.int32).reshape(1), flags),
+        (state_two, act_two, grad_two, below, above, first, second, second_back, so_far), kept + outs,
+        (state_shape,) * 3 + (edge,) * 2 + (weight,) * 3 + (sums_shape,) + kept + outs
+        + (wide, outer_stack, sums_shape), 20, 6 * work,
+    )
+    forward, rebuilt, passed = call(
+        functools.partial(second_alone, ydim, zdim), "tick_two_second", (),
+        (state_two, act_two, grad_two, *made[:5], first, second, first_back), (state_shape,) * 3,
+        (state_shape,) * 3 + kept + (weight,) * 3 + (state_shape,) * 3 + (inner_stack,), 14, 3 * work,
+    )
     halves = made[5:] if direct else split_blocks(made[5], count)
     total = reduce_blocks(halves, count, rows)
     return (

time: 90.1 us -> 94.3 us (1.047)
  local copies, waits for them, and re-layouts: 26.2 us -> 0.14 us
  Pallas kernels: 15.5 us -> 40 us
  other arithmetic: 1.32 us -> 5.52 us
  waiting for transfers between devices: 16.9 us -> 18.7 us
    pallas_call x6 -> x7, Pallas kernels: 15.5 us -> 40 us  [call(): pl.pallas_call(kernel, out_shape=tuple(outs), in_specs=[smem] * len(scala...]
    unnamed x70 -> x0, local copies, waits for them, and re-layouts: 19.3 us -> none
    transpose x4 -> x0, local copies, waits for them, and re-layouts: 6.76 us -> none  [the longest x2 4.11 us: shards(): jnp.transpose(w_second[0][::-1], (0, 2, 1)).reshape(3, 9 * width, width)]
    convert_element_type x9, other arithmetic: 0.44 us -> 3.59 us  [reduce_blocks(): total = total.astype(BF16)]
    ppermute x12, waiting for transfers between devices: 9.03 us -> 11.6 us  [reduce_blocks(): got = lax.ppermute(send, 'space', [(i, i ^ bit) for i in range(count)])]
    ppermute x2, waiting for transfers between devices: 1.05 us -> 0.01 us  [exchange(): below = lax.ppermute(high, 'space', up)]
  transfers between devices with their start and end apart: 17 -> 17, of which waited for: 9 -> 8; matrix products, arithmetic and copies ran while one was open for 8% -> 5% of each run, Pallas kernels for 4% -> 11%
where the time goes in v4:
time: 94.3 us; the launch traced here: 94 us
  Pallas kernels  40 us (42%)
  starting transfers between devices  28.7 us (30%)
  waiting for transfers between devices  18.7 us (20%)
  other arithmetic  5.52 us (6%)
    pallas_call x7, Pallas kernels, call(): pl.pallas_call(kernel, out_shape=tuple(outs), in_specs=[smem] * len(scala...  40 us
    ppermute x12, starting transfers between devices, reduce_blocks(): got = lax.ppermute(send, 'space', [(i, i ^ bit) for i in range(count)])  16.3 us
    ppermute x12, waiting for transfers between devices, reduce_blocks(): got = lax.ppermute(send, 'space', [(i, i ^ bit) for i in range(count)])  11.6 us
    ppermute x2, starting transfers between devices, exchange(): below = lax.ppermute(high, 'space', up)  9.56 us
    ppermute x2, waiting for transfers between devices, exchange(): above = lax.ppermute(low, 'space', down)  5.26 us
    convert_element_type x9, other arithmetic, reduce_blocks(): total = total.astype(BF16)  3.59 us
    ppermute x2, starting transfers between devices, exchange(): above = lax.ppermute(low, 'space', down)  2.74 us
  transfers between devices with their start and end apart: 17, of which 8 were waited for; matrix products, arithmetic and copies ran while one was open for 5% of the time, Pallas kernels for 11%

profile of v4, /device:TPU:0, one launch (start us, length us, event | category | flops | bytes accessed | tf_op | source)
XLA Modules:
  0.0 94.0 jit_solution(14287694551737185317)
XLA Ops:
  0.6 10.1 %edges.1 = (bf16[576,128]{1,0:T(8,128)(2,1)}, bf16[576,128]{1,0:T(8,128)(2,1)}) custom-call(bf16[256,256]{1,0:T(8,128)(2,1)} %bitcast.91, bf16[256,256]{1,0:T(8,128)(2,1)} %bitcast.93, bf16[256,256]{1,0:T(8,128)(2,1)} %bitcast.88), custom_call_target="tpu_custom_call" | custom-call | bytes 393216 | tf_op jit(solution)/shard_map/edges/pallas_call | solution.py:503
  10.8 5.5 %collective-permute-start = (bf16[576,128]{1,0:T(8,128)(2,1)}, bf16[576,128]{1,0:T(8,128)(2,1)}, u32[]{:S(2)}, u32[]{:S(2)}) collective-permute-start(bf16[576,128]{1,0:T(8,128)(2,1)} %get-tuple-element.33), channel_id=1, source_target_pairs={{0,1},{1,2},{2,3},{3,4},{4,5},{5,6},{6,7},{7,8},{8,9},{9,10},{10,1... | collective-permute-start | bytes 442376 | tf_op jit(solution)/shard_map/ppermute | solution.py:487
  16.3 1.3 %collective-permute-start.1 = (bf16[576,128]{1,0:T(8,128)(2,1)}, bf16[576,128]{1,0:T(8,128)(2,1)}, u32[]{:S(2)}, u32[]{:S(2)}) collective-permute-start(bf16[576,128]{1,0:T(8,128)(2,1)} %get-tuple-element.34), channel_id=1, source_target_pairs={{1,0},{2,1},{3,2},{4,3},{5,4},{6,5},{7,6},{8,7},{9,8},{10,9},{11,1... | collective-permute-start | bytes 442376 | tf_op jit(solution)/shard_map/ppermute | solution.py:488
  17.6 0.6 add_convert_fusion.3.flags
  18.2 2.7 %flip.1 = (bf16[27,128,128]{2,1,0:T(8,128)(2,1)}, bf16[27,128,128]{2,1,0:T(8,128)(2,1)}) custom-call(bf16[27,128,128]{2,1,0:T(8,128)(2,1)} %bitcast.64, bf16[27,128,128]{2,1,0:T(8,128)(2,1)} %bitcast.68), custom_call_target="tpu_custom_call" | custom-call | bytes 1769472 | tf_op jit(solution)/shard_map/flip/pallas_call | solution.py:503
  21.5 2.6 %collective-permute-done.1.above_in = bf16[576,128]{1,0:T(8,128)(2,1)} collective-permute-done((bf16[576,128]{1,0:T(8,128)(2,1)}, bf16[576,128]{1,0:T(8,128)(2,1)}, u32[]{:S(2)}, u32[]{:S(2)}) %collective-permute-start.1) | collective-permute-done | bytes 147488 | tf_op jit(solution)/shard_map/ppermute | solution.py:488
  24.1 7.9 %tick_one.1 = (bf16[256,256]{1,0:T(8,128)(2,1)}, bf16[2,256,256]{2,1,0:T(8,128)(2,1)}, bf16[384,128]{1,0:T(8,128)(2,1)}, bf16[384,128]{1,0:T(8,128)(2,1)}, bf16[384,128]{1,0:T(8,128)(2,1)}) custom-call(s32[2]{0:T(128)} %pad_add_fusion.places, f32[2]{0:T(128)} %add_convert_fusion.3.flags, bf16[256,256]{1,0:T(8,128)(2,1)} %bitcast.92, ...), custom_call_target="tpu_custom_call" | custom-call | flops 1811939328 | bytes 4227072 | tf_op jit(solution)/shard_map/tick_one/pallas_call | solution.py:503
  32.1 1.9 %collective-permute-done.2.lifted_in.lowered_in = bf16[2,256,256]{2,1,0:T(8,128)(2,1)} collective-permute-done((bf16[2,256,256]{2,1,0:T(8,128)(2,1)}, bf16[2,256,256]{2,1,0:T(8,128)(2,1)}, u32[]{:S(2)}, u32[]{:S(2)}) %collective-permute-start.2) | collective-permute-done | bytes 262176 | tf_op jit(solution)/shard_map/ppermute | solution.py:536
  34.0 2.9 %join.1 = (bf16[256,256]{1,0:T(8,128)(2,1)}, bf16[256,256]{1,0:T(8,128)(2,1)}, bf16[256,256]{1,0:T(8,128)(2,1)}, bf16[576,128]{1,0:T(8,128)(2,1)}, bf16[576,128]{1,0:T(8,128)(2,1)}) custom-call(s32[2]{0:T(128)} %pad_add_fusion.places, bf16[256,256]{1,0:T(8,128)(2,1)} %get-tuple-element.37.forward_in, ...), custom_call_target="tpu_custom_call" | custom-call | bytes 917504 | tf_op jit(solution)/shard_map/join/pallas_call | solution.py:503
  36.9 4.1 %collective-permute-start.3 = (bf16[576,128]{1,0:T(8,128)(2,1)}, bf16[576,128]{1,0:T(8,128)(2,1)}, u32[]{:S(2)}, u32[]{:S(2)}) collective-permute-start(bf16[576,128]{1,0:T(8,128)(2,1)} %get-tuple-element.42), channel_id=1, source_target_pairs={{0,1},{1,2},{2,3},{3,4},{4,5},{5,6},{6,7},{7,8},{8,9},{9,10},{10,1... | collective-permute-start | bytes 442376 | tf_op jit(solution)/shard_map/ppermute | solution.py:487
  40.9 1.5 %collective-permute-start.4 = (bf16[576,128]{1,0:T(8,128)(2,1)}, bf16[576,128]{1,0:T(8,128)(2,1)}, u32[]{:S(2)}, u32[]{:S(2)}) collective-permute-start(bf16[576,128]{1,0:T(8,128)(2,1)} %get-tuple-element.43), channel_id=1, source_target_pairs={{1,0},{2,1},{3,2},{4,3},{5,4},{6,5},{7,6},{8,7},{9,8},{10,9},{11,1... | collective-permute-start | bytes 442376 | tf_op jit(solution)/shard_map/ppermute | solution.py:488
  42.4 3.7 %weight_grads.1.args_8_ = f32[2,3456,128]{2,1,0:T(8,128)} custom-call(bf16[256,256]{1,0:T(8,128)(2,1)} %bitcast.90, bf16[384,128]{1,0:T(8,128)(2,1)} %get-tuple-element.44.back_in, bf16[384,128]{1,0:T(8,128)(2,1)} %get-tuple-element.45.carry_in, bf16[384,128]{1,0:T(8,128)(2,1)} %get-tuple-element.46.gate_in), custom_call_target="tpu_custom_call" | custom-call | flops 452984832 | bytes 425984 | tf_op jit(solution)/shard_map/weight_grads/pallas_call | solution.py:503
  46.1 2.6 %collective-permute-done.4.args_4_ = bf16[576,128]{1,0:T(8,128)(2,1)} collective-permute-done((bf16[576,128]{1,0:T(8,128)(2,1)}, bf16[576,128]{1,0:T(8,128)(2,1)}, u32[]{:S(2)}, u32[]{:S(2)}) %collective-permute-start.4) | collective-permute-done | bytes 147488 | tf_op jit(solution)/shard_map/ppermute | solution.py:488
  48.7 8.3 %tick_two_first.1 = (bf16[256,128]{1,0:T(8,128)(2,1)}, bf16[256,128]{1,0:T(8,128)(2,1)}, bf16[384,128]{1,0:T(8,128)(2,1)}, bf16[384,128]{1,0:T(8,128)(2,1)}, bf1...) custom-call(s32[1]{0:T(128)} %bitcast.14.spot, ...), custom_call_target="tpu_custom_call" | custom-call | flops 1358954496 | bytes 5111808 | tf_op jit(solution)/shard_map/tick_two_first/pallas_call | solution.py:503
  57.1 2.7 %collective-permute-start.5 = (bf16[8,144,128]{2,1,0:T(8,128)(2,1)}, bf16[8,144,128]{2,1,0:T(8,128)(2,1)}, u32[]{:S(2)}, u32[]{:S(2)}) collective-permute-start(bf16[8,144,128]{2,1,0:T(8,128)(2,1)} %get-tuple-element.56), channel_id=1, source_target_pairs={{0,1},{1,0},{2,3},{3,2},{4,5},{5,4},{6,7},{7,6},{8,9},{9,8},{10,11... | collective-permute-start | bytes 884744 | tf_op jit(solution)/shard_map/ppermute | solution.py:448
  59.8 1.5 %collective-permute-start.9 = (bf16[8,144,128]{2,1,0:T(8,128)(2,1)}, bf16[8,144,128]{2,1,0:T(8,128)(2,1)}, u32[]{:S(2)}, u32[]{:S(2)}) collective-permute-start(bf16[8,144,128]{2,1,0:T(8,128)(2,1)} %get-tuple-element.58), channel_id=1, source_target_pairs={{0,2},{1,3},{2,0},{3,1},{4,6},{5,7},{6,4},{7,5},{8,10},{9,11},{10,... | collective-permute-start | bytes 884744 | tf_op jit(solution)/shard_map/ppermute | solution.py:448
  61.3 1.6 %collective-permute-start.13 = (bf16[8,144,128]{2,1,0:T(8,128)(2,1)}, bf16[8,144,128]{2,1,0:T(8,128)(2,1)}, u32[]{:S(2)}, u32[]{:S(2)}) collective-permute-start(bf16[8,144,128]{2,1,0:T(8,128)(2,1)} %get-tuple-element.60), channel_id=1, source_target_pairs={{0,4},{1,5},{2,6},{3,7},{4,0},{5,1},{6,2},{7,3},{8,12},{9,13},{10,... | collective-permute-start | bytes 884744 | tf_op jit(solution)/shard_map/ppermute | solution.py:448
  62.9 4.4 %tick_two_second.1 = (bf16[256,256]{1,0:T(8,128)(2,1)}, bf16[256,256]{1,0:T(8,128)(2,1)}, bf16[256,256]{1,0:T(8,128)(2,1)}) custom-call(bf16[256,256]{1,0:T(8,128)(2,1)} %get-tuple-element.39.args_0_.refs_0_, bf16[256,256]{1,0:T(8,128)(2,1)} %get-tuple-element.40.args_1_.refs_1_, bf16[256,256]{1,0:T(8,128)(2,1)} %get-tuple-element.41.args_2_.refs_2_, ...), custom_call_target="tpu_custom_call" | custom-call | flops 679477248 | bytes 3473408 | tf_op jit(solution)/shard_map/tick_two_second/pallas_call | solution.py:503
  67.2 1.1 %add_convert_fusion.2 = bf16[8,144,128]{2,1,0:T(8,128)(2,1)S(1)} fusion(bf16[8,144,128]{2,1,0:T(8,128)(2,1)} %collective-permute-done.5, bf16[8,144,128]{2,1,0:T(8,128)(2,1)} %get-tuple-element.55), kind=kLoop, calls=%fused_computation.2 | loop fusion | flops 589824 | bytes 884736 | tf_op jit(solution)/shard_map/convert_element_type | solution.py:451
  68.4 0.6 collective-permute-start.6
  69.0 1.1 %add_convert_fusion.1 = bf16[8,144,128]{2,1,0:T(8,128)(2,1)S(1)} fusion(bf16[8,144,128]{2,1,0:T(8,128)(2,1)} %collective-permute-done.9, bf16[8,144,128]{2,1,0:T(8,128)(2,1)} %get-tuple-element.57), kind=kLoop, calls=%fused_computation.1 | loop fusion | flops 589824 | bytes 884736 | tf_op jit(solution)/shard_map/convert_element_type | solution.py:451
  70.2 1.6 %collective-permute-start.10 = (bf16[4,144,128]{2,1,0:T(8,128)(2,1)S(1)}, bf16[4,144,128]{2,1,0:T(8,128)(2,1)S(1)}, u32[]{:S(2)}, u32[]{:S(2)}) collective-permute-start(bf16[4,144,128]{2,1,0:T(8,128)(2,1)S(1)} %dynamic-slice_bitcast_fusion.1), channel_id=1, source_target_pairs={{0,4},{1,5},{2,6},{3,7},{4,0},{5,1},{6,2},{7,3},{8,12},{9,13},{10,... | collective-permute-start | bytes 442376 | tf_op jit(solution)/shard_map/ppermute | solution.py:448
  71.8 1.1 %add_convert_fusion = bf16[8,144,128]{2,1,0:T(8,128)(2,1)S(1)} fusion(bf16[8,144,128]{2,1,0:T(8,128)(2,1)} %collective-permute-done.13, bf16[8,144,128]{2,1,0:T(8,128)(2,1)} %get-tuple-element.59), kind=kLoop, calls=%fused_computation | loop fusion | flops 589824 | bytes 884736 | tf_op jit(solution)/shard_map/convert_element_type | solution.py:451
  73.0 3.0 %collective-permute-start.14 = (bf16[4,144,128]{2,1,0:T(8,128)(2,1)S(1)}, bf16[4,144,128]{2,1,0:T(8,128)(2,1)S(1)}, u32[]{:S(2)}, u32[]{:S(2)}) collective-permute-start(bf16[4,144,128]{2,1,0:T(8,128)(2,1)S(1)} %dynamic-slice_bitcast_fusion), channel_id=1, source_target_pairs={{0,8},{1,9},{2,10},{3,11},{4,12},{5,13},{6,14},{7,15},{8,0},{9,1},... | collective-permute-start | bytes 442376 | tf_op jit(solution)/shard_map/ppermute | solution.py:448
  76.3 3.5 %collective-permute-start.11 = (bf16[2,144,128]{2,1,0:T(8,128)(2,1)S(1)}, bf16[2,144,128]{2,1,0:T(8,128)(2,1)S(1)}, u32[]{:S(2)}, u32[]{:S(2)}) collective-permute-start(bf16[2,144,128]{2,1,0:T(8,128)(2,1)S(1)} %dynamic-slice_bitcast_fusion.4), channel_id=1, source_target_pairs={{0,8},{1,9},{2,10},{3,11},{4,12},{5,13},{6,14},{7,15},{8,0},{9,1},... | collective-permute-start | bytes 221192 | tf_op jit(solution)/shard_map/ppermute | solution.py:448
  79.7 5.0 %collective-permute-done.14 = bf16[4,144,128]{2,1,0:T(8,128)(2,1)S(1)} collective-permute-done((bf16[4,144,128]{2,1,0:T(8,128)(2,1)S(1)}, bf16[4,144,128]{2,1,0:T(8,128)(2,1)S(1)}, u32[]{:S(2)}, u32[]{:S(2)}) %collective-permute-start.14) | collective-permute-done | bytes 147488 | tf_op jit(solution)/shard_map/ppermute | solution.py:448
  85.0 0.7 collective-permute-done.11
  85.8 1.3 %collective-permute-start.12 = (bf16[1,144,128]{2,1,0:T(8,128)(2,1)S(1)}, bf16[1,144,128]{2,1,0:T(8,128)(2,1)S(1)}, u32[]{:S(2)}, u32[]{:S(2)}) collective-permute-start(bf16[1,144,128]{2,1,0:T(8,128)(2,1)S(1)} %constant_dynamic-slice_fusion.1), channel_id=1, source_target_pairs={{0,1},{1,0},{2,3},{3,2},{4,5},{5,4},{6,7},{7,6},{8,9},{9,8},{10,11... | collective-permute-start | bytes 110600 | tf_op jit(solution)/shard_map/ppermute | solution.py:448
  87.1 2.1 %collective-permute-done.15 = bf16[2,144,128]{2,1,0:T(8,128)(2,1)S(1)} collective-permute-done((bf16[2,144,128]{2,1,0:T(8,128)(2,1)S(1)}, bf16[2,144,128]{2,1,0:T(8,128)(2,1)S(1)}, u32[]{:S(2)}, u32[]{:S(2)}) %collective-permute-start.15) | collective-permute-done | bytes 73760 | tf_op jit(solution)/shard_map/ppermute | solution.py:448
  89.3 0.6 collective-permute-done.8
  89.9 3.3 %collective-permute-done.16 = bf16[1,144,128]{2,1,0:T(8,128)(2,1)S(1)} collective-permute-done((bf16[1,144,128]{2,1,0:T(8,128)(2,1)S(1)}, bf16[1,144,128]{2,1,0:T(8,128)(2,1)S(1)}, u32[]{:S(2)}, u32[]{:S(2)}) %collective-permute-start.16) | collective-permute-done | bytes 36896 | tf_op jit(solution)/shard_map/ppermute | solution.py:448
  93.3 0.7 fusion.6
  (33 shorter events, 1.5 us)
Async XLA Ops:
  10.8 10.7 %collective-permute-start = (bf16[576,128]{1,0:T(8,128)(2,1)}, bf16[576,128]{1,0:T(8,128)(2,1)}, u32[]{:S(2)}, u32[]{:S(2)}) collective-permute-start(bf16[576,128]{1,0:T(8,128)(2,1)} %get-tuple-element.33), channel_id=1, source_target_pairs={{0,1},{1,2},{2,3},{3,4},{4,5},{5,6},{6,7},{7,8},{8,9},{9,10},{10,1... | collective-permute-start | bytes 442376 | tf_op jit(solution)/shard_map/ppermute | solution.py:487
  16.3 7.9 %collective-permute-start.1 = (bf16[576,128]{1,0:T(8,128)(2,1)}, bf16[576,128]{1,0:T(8,128)(2,1)}, u32[]{:S(2)}, u32[]{:S(2)}) collective-permute-start(bf16[576,128]{1,0:T(8,128)(2,1)} %get-tuple-element.34), channel_id=1, source_target_pairs={{1,0},{2,1},{3,2},{4,3},{5,4},{6,5},{7,6},{8,7},{9,8},{10,9},{11,1... | collective-permute-start | bytes 442376 | tf_op jit(solution)/shard_map/ppermute | solution.py:488
  32.0 1.9 %collective-permute-start.2 = (bf16[2,256,256]{2,1,0:T(8,128)(2,1)}, bf16[2,256,256]{2,1,0:T(8,128)(2,1)}, u32[]{:S(2)}, u32[]{:S(2)}) collective-permute-start(bf16[2,256,256]{2,1,0:T(8,128)(2,1)} %get-tuple-element.38), channel_id=1, source_target_pairs={{0,16},{16,0},{1,17},{17,1},{2,18},{18,2},{3,19},{19,3},{4,20},{20... | collective-permute-start | bytes 786440 | tf_op jit(solution)/shard_map/ppermute | solution.py:536
  36.9 9.2 %collective-permute-start.3 = (bf16[576,128]{1,0:T(8,128)(2,1)}, bf16[576,128]{1,0:T(8,128)(2,1)}, u32[]{:S(2)}, u32[]{:S(2)}) collective-permute-start(bf16[576,128]{1,0:T(8,128)(2,1)} %get-tuple-element.42), channel_id=1, source_target_pairs={{0,1},{1,2},{2,3},{3,4},{4,5},{5,6},{6,7},{7,8},{8,9},{9,10},{10,1... | collective-permute-start | bytes 442376 | tf_op jit(solution)/shard_map/ppermute | solution.py:487
  40.9 7.8 %collective-permute-start.4 = (bf16[576,128]{1,0:T(8,128)(2,1)}, bf16[576,128]{1,0:T(8,128)(2,1)}, u32[]{:S(2)}, u32[]{:S(2)}) collective-permute-start(bf16[576,128]{1,0:T(8,128)(2,1)} %get-tuple-element.43), channel_id=1, source_target_pairs={{1,0},{2,1},{3,2},{4,3},{5,4},{6,5},{7,6},{8,7},{9,8},{10,9},{11,1... | collective-permute-start | bytes 442376 | tf_op jit(solution)/shard_map/ppermute | solution.py:488
  57.1 10.2 %collective-permute-start.5 = (bf16[8,144,128]{2,1,0:T(8,128)(2,1)}, bf16[8,144,128]{2,1,0:T(8,128)(2,1)}, u32[]{:S(2)}, u32[]{:S(2)}) collective-permute-start(bf16[8,144,128]{2,1,0:T(8,128)(2,1)} %get-tuple-element.56), channel_id=1, source_target_pairs={{0,1},{1,0},{2,3},{3,2},{4,5},{5,4},{6,7},{7,6},{8,9},{9,8},{10,11... | collective-permute-start | bytes 884744 | tf_op jit(solution)/shard_map/ppermute | solution.py:448
  59.8 9.2 %collective-permute-start.9 = (bf16[8,144,128]{2,1,0:T(8,128)(2,1)}, bf16[8,144,128]{2,1,0:T(8,128)(2,1)}, u32[]{:S(2)}, u32[]{:S(2)}) collective-permute-start(bf16[8,144,128]{2,1,0:T(8,128)(2,1)} %get-tuple-element.58), channel_id=1, source_target_pairs={{0,2},{1,3},{2,0},{3,1},{4,6},{5,7},{6,4},{7,5},{8,10},{9,11},{10,... | collective-permute-start | bytes 884744 | tf_op jit(solution)/shard_map/ppermute | solution.py:448
  61.3 10.5 %collective-permute-start.13 = (bf16[8,144,128]{2,1,0:T(8,128)(2,1)}, bf16[8,144,128]{2,1,0:T(8,128)(2,1)}, u32[]{:S(2)}, u32[]{:S(2)}) collective-permute-start(bf16[8,144,128]{2,1,0:T(8,128)(2,1)} %get-tuple-element.60), channel_id=1, source_target_pairs={{0,4},{1,5},{2,6},{3,7},{4,0},{5,1},{6,2},{7,3},{8,12},{9,13},{10,... | collective-permute-start | bytes 884744 | tf_op jit(solution)/shard_map/ppermute | solution.py:448
  68.4 7.6 %collective-permute-start.6 = (bf16[4,144,128]{2,1,0:T(8,128)(2,1)S(1)}, bf16[4,144,128]{2,1,0:T(8,128)(2,1)S(1)}, u32[]{:S(2)}, u32[]{:S(2)}) collective-permute-start(bf16[4,144,128]{2,1,0:T(8,128)(2,1)S(1)} %dynamic-slice_bitcast_fusion.2), channel_id=1, source_target_pairs={{0,2},{1,3},{2,0},{3,1},{4,6},{5,7},{6,4},{7,5},{8,10},{9,11},{10,... | collective-permute-start | bytes 442376 | tf_op jit(solution)/shard_map/ppermute | solution.py:448
  70.2 6.1 %collective-permute-start.10 = (bf16[4,144,128]{2,1,0:T(8,128)(2,1)S(1)}, bf16[4,144,128]{2,1,0:T(8,128)(2,1)S(1)}, u32[]{:S(2)}, u32[]{:S(2)}) collective-permute-start(bf16[4,144,128]{2,1,0:T(8,128)(2,1)S(1)} %dynamic-slice_bitcast_fusion.1), channel_id=1, source_target_pairs={{0,4},{1,5},{2,6},{3,7},{4,0},{5,1},{6,2},{7,3},{8,12},{9,13},{10,... | collective-permute-start | bytes 442376 | tf_op jit(solution)/shard_map/ppermute | solution.py:448
  73.0 11.7 %collective-permute-start.14 = (bf16[4,144,128]{2,1,0:T(8,128)(2,1)S(1)}, bf16[4,144,128]{2,1,0:T(8,128)(2,1)S(1)}, u32[]{:S(2)}, u32[]{:S(2)}) collective-permute-start(bf16[4,144,128]{2,1,0:T(8,128)(2,1)S(1)} %dynamic-slice_bitcast_fusion), channel_id=1, source_target_pairs={{0,8},{1,9},{2,10},{3,11},{4,12},{5,13},{6,14},{7,15},{8,0},{9,1},... | collective-permute-start | bytes 442376 | tf_op jit(solution)/shard_map/ppermute | solution.py:448
  76.0 8.9 %collective-permute-start.7 = (bf16[2,144,128]{2,1,0:T(8,128)(2,1)S(1)}, bf16[2,144,128]{2,1,0:T(8,128)(2,1)S(1)}, u32[]{:S(2)}, u32[]{:S(2)}) collective-permute-start(bf16[2,144,128]{2,1,0:T(8,128)(2,1)S(1)} %dynamic-slice_bitcast_fusion.5), channel_id=1, source_target_pairs={{0,4},{1,5},{2,6},{3,7},{4,0},{5,1},{6,2},{7,3},{8,12},{9,13},{10,... | collective-permute-start | bytes 221192 | tf_op jit(solution)/shard_map/ppermute | solution.py:448
  76.3 9.4 %collective-permute-start.11 = (bf16[2,144,128]{2,1,0:T(8,128)(2,1)S(1)}, bf16[2,144,128]{2,1,0:T(8,128)(2,1)S(1)}, u32[]{:S(2)}, u32[]{:S(2)}) collective-permute-start(bf16[2,144,128]{2,1,0:T(8,128)(2,1)S(1)} %dynamic-slice_bitcast_fusion.4), channel_id=1, source_target_pairs={{0,8},{1,9},{2,10},{3,11},{4,12},{5,13},{6,14},{7,15},{8,0},{9,1},... | collective-permute-start | bytes 221192 | tf_op jit(solution)/shard_map/ppermute | solution.py:448
  84.8 4.4 %collective-permute-start.15 = (bf16[2,144,128]{2,1,0:T(8,128)(2,1)S(1)}, bf16[2,144,128]{2,1,0:T(8,128)(2,1)S(1)}, u32[]{:S(2)}, u32[]{:S(2)}) collective-permute-start(bf16[2,144,128]{2,1,0:T(8,128)(2,1)S(1)} %dynamic-slice_bitcast_fusion.3), channel_id=1, source_target_pairs={{0,1},{1,0},{2,3},{3,2},{4,5},{5,4},{6,7},{7,6},{8,9},{9,8},{10,11... | collective-permute-start | bytes 221192 | tf_op jit(solution)/shard_map/ppermute | solution.py:448
  85.0 4.9 %collective-permute-start.8 = (bf16[1,144,128]{2,1,0:T(8,128)(2,1)S(1)}, bf16[1,144,128]{2,1,0:T(8,128)(2,1)S(1)}, u32[]{:S(2)}, u32[]{:S(2)}) collective-permute-start(bf16[1,144,128]{2,1,0:T(8,128)(2,1)S(1)} %constant_dynamic-slice_fusion.2), channel_id=1, source_target_pairs={{0,8},{1,9},{2,10},{3,11},{4,12},{5,13},{6,14},{7,15},{8,0},{9,1},... | collective-permute-start | bytes 110600 | tf_op jit(solution)/shard_map/ppermute | solution.py:448
  85.8 4.1 %collective-permute-start.12 = (bf16[1,144,128]{2,1,0:T(8,128)(2,1)S(1)}, bf16[1,144,128]{2,1,0:T(8,128)(2,1)S(1)}, u32[]{:S(2)}, u32[]{:S(2)}) collective-permute-start(bf16[1,144,128]{2,1,0:T(8,128)(2,1)S(1)} %constant_dynamic-slice_fusion.1), channel_id=1, source_target_pairs={{0,1},{1,0},{2,3},{3,2},{4,5},{5,4},{6,7},{7,6},{8,9},{9,8},{10,11... | collective-permute-start | bytes 110600 | tf_op jit(solution)/shard_map/ppermute | solution.py:448
  89.2 4.0 %collective-permute-start.16 = (bf16[1,144,128]{2,1,0:T(8,128)(2,1)S(1)}, bf16[1,144,128]{2,1,0:T(8,128)(2,1)S(1)}, u32[]{:S(2)}, u32[]{:S(2)}) collective-permute-start(bf16[1,144,128]{2,1,0:T(8,128)(2,1)S(1)} %constant_dynamic-slice_fusion), channel_id=1, source_target_pairs={{0,2},{1,3},{2,0},{3,1},{4,6},{5,7},{6,4},{7,5},{8,10},{9,11},{10,... | collective-permute-start | bytes 110600 | tf_op jit(solution)/shard_map/ppermute | solution.py:448

commit v5 on v4

--- a/solution.py
+++ b/solution.py
@@ -8,7 +8,6 @@
 from jax.experimental.pallas import tpu as pltpu
 from jax.sharding import PartitionSpec as P
 
-VMEM = pltpu.CompilerParams(vmem_limit_bytes=65408 * 1024)
 F32 = jnp.float32
 BF16 = jnp.bfloat16
 
@@ -89,7 +88,7 @@
         high[at : at + plane, :] = source[cells - plane : cells, half]
 
 
-def edges_kernel(plane, state, act, grad, low, high, sems):
+def edges_kernel(plane, state, act, grad, low_out, high_out, low, high, sems):
     width = state.shape[1] // 2
     cells = state.shape[0]
     left, right = pl.ds(0, width), pl.ds(width, width)
@@ -98,57 +97,35 @@
         moves.append((source, half, 2 * plane, index * 2 * plane))
     for index, (source, half) in enumerate(((state, left), (act, right), (grad, left))):
         moves.append((source, half, plane, (6 + index) * plane))
-    copies = []
-    for source, half, size, at in moves:
-        for start, out in ((0, low), (cells - size, high)):
-            copies.append(
-                pltpu.make_async_copy(
-                    source.at[pl.ds(start, size), half],
-                    out.at[pl.ds(at, size), :],
-                    sems.at[len(copies)],
-                )
-            )
-    for copy in copies:
-        copy.start()
-    for copy in copies:
-        copy.wait()
-
-
-def join_kernel(plane, places, forward_in, lifted_in, lowered_in, fresh_in, target_in, state_out,
-                act_out, grad_out, low_out, high_out, forward, lifted, lowered, fresh, target, state,
-                act, grad, low, high, sems):
     copies = Copies(sems)
-    copies.start("lifted", lifted_in.at[0], lifted)
-    copies.start("lowered", lowered_in, lowered)
-    copies.start("fresh", fresh_in, fresh)
-    copies.start("forward", forward_in, forward)
-    copies.start("target", target_in, target)
+    for side, (out, result) in enumerate(((high, high_out), (low, low_out))):
+        for index, (source, half, size, at) in enumerate(moves):
+            start = 0 if side else cells - size
+            copies.start((side, index), source.at[pl.ds(start, size), half], out.at[pl.ds(at, size), :])
+    for side, (out, result) in enumerate(((high, high_out), (low, low_out))):
+        copies.need(*[(side, index) for index in range(len(moves))])
+        copies.start(side, out, result)
     copies.finish()
+
+
+def join_kernel(plane, places, forward, lifted, lowered, fresh, target, state, act, grad, low, high):
     first_place, last_place = places[0] == 0, places[0] == places[1]
-    state[...] = jnp.where(first_place, fresh[...], lifted[...])
+    state[...] = jnp.where(first_place, fresh[...], lifted[0])
     own = forward[...]
     act[...] = jnp.where(last_place, own, lowered[0])
     error = (own.astype(F32) - target[...].astype(F32)).astype(BF16)
     grad[...] = jnp.where(last_place, error, lowered[1])
     pack_edges(state, act, grad, low, high, plane)
-    for index, (source, out) in enumerate(
-        ((low, low_out), (high, high_out), (state, state_out), (act, act_out), (grad, grad_out))
-    ):
-        copies.start(index, source, out)
-    copies.finish()
-
-
-def flip_kernel(first_in, second_in, first_out, second_out, source, flipped, sems):
-    copies = Copies(sems)
-    copies.start(0, first_in, source.at[0])
-    copies.start(1, second_in, source.at[1])
-    offsets = source.shape[1]
-    for which, out in enumerate((first_out, second_out)):
-        copies.need(which)
+
+
+def flip_kernel(first, second, state_in, act_in, grad_in, first_back, second_back, state, act, grad):
+    state[...] = state_in[...]
+    act[...] = act_in[...]
+    grad[...] = grad_in[...]
+    offsets = first.shape[0]
+    for source, out in ((first, first_back), (second, second_back)):
         for k in range(offsets):
-            flipped[which, offsets - 1 - k] = jnp.transpose(source[which, k])
-        copies.start(2 + which, flipped.at[which], out)
-    copies.finish()
+            out[offsets - 1 - k] = jnp.transpose(source[k])
 
 
 def first_kernel(ydim, zdim, copies, made, flags, state, act, grad, below, above, first, second, second_back,
@@ -246,65 +223,19 @@
     made("forward")
 
 
-def second_alone(ydim, zdim, *refs):
-    names = ("state", "act", "grad", "new_one", "back_two", "mid", "back", "carry", "first", "second",
-             "first_back")
-    sources, outs, local, results = refs[:11], refs[11:14], refs[14:25], refs[25:28]
-    stack, sems = refs[28:]
-    copies = Copies(sems)
-    order = ("back", "act", "back_two", "first", "carry", "grad", "first_back", "mid", "state", "new_one",
-             "second")
-    for name in order:
-        copies.start(name, sources[names.index(name)], local[names.index(name)])
-    where = {"forward": 0, "rebuilt": 1, "passed": 2}
-
-    def made(name):
-        copies.start("out_" + name, results[where[name]], outs[where[name]])
-
-    second_kernel(ydim, zdim, copies, made, *local, *results, stack)
-    copies.finish()
-
-
-def tick_kernel(ydim, zdim, paired, places, flags, state_in, act_in, grad_in, below_in, above_in,
-                first_in, second_in, first_back_in, second_back_in, forward_out, sent_out, back_out,
-                carry_out, gate_out, forward, sent, back, carry, gate, state, act, grad, below, above,
-                first, second, first_back, second_back, new_one, back_two, mid, rebuilt, stack, sems):
-    copies = Copies(sems)
-    for name, source, target in (
-        ("below", below_in, below),
-        ("above", above_in, above),
-        ("state", state_in, state),
-        ("first", first_in, first),
-        ("act", act_in, act),
-        ("second", second_in, second),
-        ("grad", grad_in, grad),
-        ("second_back", second_back_in, second_back),
-        ("first_back", first_back_in, first_back),
-    ):
-        copies.start(name, source, target)
-    stores = {
-        "back": (back, back_out),
-        "carry": (carry, carry_out),
-        "gate": (gate, gate_out),
-        "forward": (forward, forward_out),
-        "passed": (sent.at[1], sent_out.at[1]),
-    }
-
-    def made(*names):
-        for name in names:
-            if name in stores:
-                copies.start("out_" + name, *stores[name])
-
-    first_kernel(ydim, zdim, copies, made, flags, state, act, grad, below, above, first, second,
+def tick_kernel(ydim, zdim, paired, places, flags, state, act, grad, below, above, first, second,
+                first_back, second_back, forward, sent, back, carry, gate, new_one, back_two, mid,
+                rebuilt, stack):
+    copies = Copies(None)
+    ignore = lambda *names: None
+    first_kernel(ydim, zdim, copies, ignore, flags, state, act, grad, below, above, first, second,
                  second_back, new_one, back_two, mid, back, carry, gate, stack)
-    second_kernel(ydim, zdim, copies, made, state, act, grad, new_one, back_two, mid, back, carry, first,
-                  second, first_back, forward, rebuilt, sent.at[1], stack)
+    second_kernel(ydim, zdim, copies, ignore, state, act, grad, new_one, back_two, mid, back, carry,
+                  first, second, first_back, forward, rebuilt, sent.at[1], stack)
     if paired:
         sent[0] = jnp.where(places[0] == 0, forward[...], rebuilt[...])
     else:
         sent[0] = rebuilt[...]
-    copies.start("out_sent", sent.at[0], sent_out.at[0])
-    copies.finish()
 
 
 def correlate(stack, field, cotangent, ydim, zdim, emit):
@@ -335,21 +266,11 @@
     correlate(stack, gate, grad[:, width:].astype(F32), ydim, zdim, store(1))
 
 
-def corr_kernel(ydim, zdim, grad_in, back_in, carry_in, gate_in, out_ref, grad, back, carry, gate, out,
-                stack, sems):
-    copies = Copies(sems)
-    for name, source, target in (
-        ("carry", carry_in, carry), ("back", back_in, back), ("grad", grad_in, grad), ("gate", gate_in, gate)
-    ):
-        copies.start(name, source, target)
-    copies.finish()
-
+def corr_kernel(ydim, zdim, grad, back, carry, gate, out, stack):
     def put(which, at, block):
         out[which, at, :] = block
 
     both_grads(ydim, zdim, grad, back, carry, gate, stack, put)
-    copies.start("out", out, out_ref)
-    copies.finish()
 
 
 def ways_of(count, rows):
@@ -359,31 +280,18 @@
     return [(way * span, span, bits[way % len(bits) :] + bits[: way % len(bits)]) for way in range(ways)]
 
 
-def last_kernel(ydim, zdim, factor, count, direct, spot, flags, *args):
-    names = ("state", "act", "grad", "below", "above", "first", "second", "second_back", "so_far")
-    made_names = ("new_one", "back_two", "mid", "back", "carry")
+def last_kernel(ydim, zdim, factor, count, direct, spot, flags, state, act, grad, below, above, first,
+                second, first_back, second_back, so_far, *args):
     n_outs = 6 if direct else 1
-    sources, args = args[:9], args[9:]
-    outs, args = args[:5], args[5:]
+    results_out, args = args[:3], args[3:]
     final_outs, args = args[:n_outs], args[n_outs:]
-    local, args = args[:9], args[9:]
-    results, args = args[:5], args[5:]
+    results, args = args[:3], args[3:]
     refs, args = args[:n_outs], args[n_outs:]
-    gate, stack, sums, sems = args
+    new_one, back_two, mid, back, carry, gate, stack, sums, sems = args
     copies = Copies(sems)
-    for name in ("below", "above", "state", "first", "act", "second", "grad", "second_back", "so_far"):
-        copies.start(name, sources[names.index(name)], local[names.index(name)])
-
-    def made(*done):
-        for name in done:
-            if name in made_names:
-                index = made_names.index(name)
-                copies.start("out_" + name, results[index], outs[index])
-
-    first_kernel(ydim, zdim, copies, made, flags, *local[:8], *results, gate, stack)
-    back, carry = results[3], results[4]
-    grad, so_far = local[2], local[8]
-    copies.need("so_far")
+    ignore = lambda *names: None
+    first_kernel(ydim, zdim, copies, ignore, flags, state, act, grad, below, above, first, second,
+                 second_back, new_one, back_two, mid, back, carry, gate, stack)
 
     def put(which, at, block):
         sums[which, at, :] = (block + so_far[which, at, :]) * factor
@@ -392,10 +300,8 @@
     if not direct:
         refs[0][...] = sums[...].astype(BF16)
         copies.start("out", refs[0], final_outs[0])
-        copies.finish()
-        return
     rows = sums.shape[1] // count
-    for index, (start, span, order) in enumerate(ways_of(count, rows)):
+    for index, (start, span, order) in enumerate(ways_of(count, rows) if direct else ()):
         mine = (spot[0] // order[0]) % 2
         for kept in (0, 1):
             side = mine if kept else 1 - mine
@@ -416,6 +322,14 @@
                 out[j] = value.astype(BF16)
             at = 2 * index + (0 if kept else 1)
             copies.start(("half", at), out, final_outs[at])
+
+    where = {"forward": 0, "rebuilt": 1, "passed": 2}
+
+    def made(name):
+        copies.start("out_" + name, results[where[name]], results_out[where[name]])
+
+    second_kernel(ydim, zdim, copies, made, state, act, grad, new_one, back_two, mid, back, carry, first,
+                  second, first_back, *results, stack)
     copies.finish()
 
 
@@ -491,7 +405,6 @@
     state, act, grad = flat(fwd_in), flat(bwd_act), flat(bwd_grad)
     smem = pl.BlockSpec(memory_space=pltpu.SMEM)
     hbm = pl.BlockSpec(memory_space=pltpu.HBM)
-    inner_stack = array((cells + 2 * plane, 9 * width), BF16)
     outer_stack = array((cells + 4 * plane, 9 * width), BF16)
     small_stack = array((cells, 9 * width), BF16)
     weight = array((3, 9 * width, width), BF16)
@@ -499,15 +412,17 @@
     sums_shape = array((2, offsets, width), F32)
     places = jnp.stack([place, jnp.full_like(place, last_section)]).astype(jnp.int32)
 
-    def call(kernel, name, scalars, inputs, outs, scratch, copies, flops=0):
+    vmem = pl.BlockSpec(memory_space=pltpu.VMEM)
+
+    def call(kernel, name, scalars, inputs, outs, scratch, grant, copies=0, places=(vmem, vmem), flops=0):
+        semaphores = [pltpu.SemaphoreType.DMA((copies,))] if copies else []
         return pl.pallas_call(
             kernel,
             out_shape=tuple(outs),
-            in_specs=[smem] * len(scalars) + [hbm] * len(inputs),
-            out_specs=(hbm,) * len(outs),
-            scratch_shapes=[pltpu.VMEM(like.shape, like.dtype) for like in scratch]
-            + [pltpu.SemaphoreType.DMA((copies,))],
-            compiler_params=VMEM,
+            in_specs=[smem] * len(scalars) + [places[0]] * len(inputs),
+            out_specs=(places[1],) * len(outs),
+            scratch_shapes=[pltpu.VMEM(like.shape, like.dtype) for like in scratch] + semaphores,
+            compiler_params=pltpu.CompilerParams(vmem_limit_bytes=grant),
             cost_estimate=pl.CostEstimate(
                 flops=flops, bytes_accessed=sum(x.size * 2 for x in inputs), transcendentals=0
             ),
@@ -515,11 +430,14 @@
         )(*scalars, *inputs)
 
     work = 2 * 27 * cells * width * width
-    low, high = call(functools.partial(edges_kernel, plane), "edges", (), (state, act, grad), (edge,) * 2, (), 12)
+    low, high = call(
+        functools.partial(edges_kernel, plane), "edges", (), (state, act, grad), (edge,) * 2,
+        (edge,) * 2, 65408 * 1024, 14, (hbm, hbm),
+    )
     below, above = exchange(low, high)
-    first_back, second_back = call(
-        flip_kernel, "flip", (), (w_first[0], w_second[0]), (raw_weight,) * 2,
-        (array((2,) + raw_weight.shape, BF16),) * 2, 4,
+    first_back, second_back, state, act, grad = call(
+        flip_kernel, "flip", (), (w_first[0], w_second[0], state, act, grad),
+        (raw_weight,) * 2 + (state_shape,) * 3, (), 16 * 1024 * 1024,
     )
     first_back, second_back = first_back.reshape(weight.shape), second_back.reshape(weight.shape)
 
@@ -529,8 +447,7 @@
     forward, sent, back, carry, gate = call(
         functools.partial(tick_kernel, ydim, zdim, paired), "tick_one", (places, flags),
         (state, act, grad, below, above, first, second, first_back, second_back), tick_outs,
-        tick_outs + (state_shape,) * 3 + (edge,) * 2 + (weight,) * 4
-        + (tile, tile, wide, state_shape, outer_stack), 15, 8 * work,
+        (tile, tile, wide, state_shape, outer_stack), 16 * 1024 * 1024, flops=8 * work,
     )
     if paired:
         lifted = lowered = lax.ppermute(sent, "section", [(0, 1), (1, 0)])
@@ -542,12 +459,12 @@
     state_two, act_two, grad_two, low, high = call(
         functools.partial(join_kernel, plane), "join", (places,),
         (forward, lifted, lowered, flat(fresh), flat(target)), join_outs,
-        (state_shape, state_shape, pair_shape, state_shape, state_shape) + join_outs, 10,
+        (), 16 * 1024 * 1024,
     )
     below, above = exchange(low, high)
     (so_far,) = call(
-        functools.partial(corr_kernel, ydim, zdim), "weight_grads", (), (grad, back, carry, gate),
-        (sums_shape,), (state_shape, wide, wide, wide, sums_shape, small_stack), 5, 2 * work,
+        functools.partial(corr_kernel, ydim, zdim), "weight_grads", (), (flat(bwd_grad), back, carry, gate),
+        (sums_shape,), (small_stack,), 16 * 1024 * 1024, flops=2 * work,
     )
 
     rows = offsets // count
@@ -558,20 +475,17 @@
     else:
         outs = (array((2, offsets, width), BF16),)
     factor = 1.0 / math.sqrt(cells * count)
-    kept = (tile, tile, wide, wide, wide)
+    results = (state_shape,) * 3
     made = call(
-        functools.partial(last_kernel, ydim, zdim, factor, count, direct), "tick_two_first",
+        functools.partial(last_kernel, ydim, zdim, factor, count, direct), "tick_two",
         (spot.astype(jnp.int32).reshape(1), flags),
-        (state_two, act_two, grad_two, below, above, first, second, second_back, so_far), kept + outs,
-        (state_shape,) * 3 + (edge,) * 2 + (weight,) * 3 + (sums_shape,) + kept + outs
-        + (wide, outer_stack, sums_shape), 20, 6 * work,
-    )
-    forward, rebuilt, passed = call(
-        functools.partial(second_alone, ydim, zdim), "tick_two_second", (),
-        (state_two, act_two, grad_two, *made[:5], first, second, first_back), (state_shape,) * 3,
-        (state_shape,) * 3 + kept + (weight,) * 3 + (state_shape,) * 3 + (inner_stack,), 14, 3 * work,
-    )
-    halves = made[5:] if direct else split_blocks(made[5], count)
+        (state_two, act_two, grad_two, below, above, first, second, first_back, second_back, so_far),
+        results + outs,
+        results + outs + (tile, tile, wide, wide, wide, wide, outer_stack, sums_shape),
+        48 * 1024 * 1024, 9, (vmem, hbm), 9 * work,
+    )
+    forward, rebuilt, passed = made[:3]
+    halves = made[3:] if direct else split_blocks(made[3], count)
     total = reduce_blocks(halves, count, rows)
     return (
         forward.reshape((1,) + shape),

time: 94.3 us -> 77.3 us (0.82)
  Pallas kernels: 40 us -> 17.3 us
  local copies, waits for them, and re-layouts: 0.14 us -> 6.95 us
  starting transfers between devices: 28.7 us -> 33.4 us
  other arithmetic: 5.52 us -> 1.36 us
  waiting for transfers between devices: 18.7 us -> 17 us
    pallas_call x7 -> x6, Pallas kernels: 40 us -> 17.3 us  [call(): pl.pallas_call(kernel, out_shape=tuple(outs), in_specs=[smem] * len(scala...]
    unnamed x0 -> x22, local copies, waits for them, and re-layouts: none -> 6.81 us
    ppermute x12, starting transfers between devices: 16.3 us -> 22.3 us  [reduce_blocks(): got = lax.ppermute(send, 'space', [(i, i ^ bit) for i in range(count)])]
    convert_element_type x9, other arithmetic: 3.59 us -> 0.47 us  [reduce_blocks(): total = total.astype(BF16)]
    ppermute x12, waiting for transfers between devices: 11.6 us -> 9.02 us  [reduce_blocks(): got = lax.ppermute(send, 'space', [(i, i ^ bit) for i in range(count)])]
    ppermute x2, starting transfers between devices: 9.56 us -> 8.26 us  [exchange(): below = lax.ppermute(high, 'space', up)]
    ppermute x2, waiting for transfers between devices: 5.26 us -> 6.46 us  [exchange(): above = lax.ppermute(low, 'space', down)]
  transfers between devices with their start and end apart: 17 -> 17, of which waited for: 8 -> 10; matrix products, arithmetic and copies ran while one was open for 5% -> 1% of each run, Pallas kernels for 11% -> 2%
where the time goes in v5:
time: 77.3 us; the launch traced here: 76.9 us
  starting transfers between devices  33.4 us (43%)
  Pallas kernels  17.3 us (22%)
  waiting for transfers between devices  17 us (22%)
  local copies, waits for them, and re-layouts  6.95 us (9%)
  other arithmetic  1.36 us (2%)
  between operations  0.91 us (1%)
    ppermute x12, starting transfers between devices, reduce_blocks(): got = lax.ppermute(send, 'space', [(i, i ^ bit) for i in range(count)])  22.3 us
    pallas_call x6, Pallas kernels, call(): pl.pallas_call(kernel, out_shape=tuple(outs), in_specs=[smem] * len(scala...  17.3 us
    ppermute x12, waiting for transfers between devices, reduce_blocks(): got = lax.ppermute(send, 'space', [(i, i ^ bit) for i in range(count)])  9.02 us
    ppermute x2, starting transfers between devices, exchange(): below = lax.ppermute(high, 'space', up)  8.26 us
    unnamed x22, local copies, waits for them, and re-layouts  6.81 us
    ppermute x2, waiting for transfers between devices, exchange(): above = lax.ppermute(low, 'space', down)  6.46 us
    ppermute x2, starting transfers between devices, exchange(): above = lax.ppermute(low, 'space', down)  2.76 us
  transfers between devices with their start and end apart: 17, of which 10 were waited for; matrix products, arithmetic and copies ran while one was open for 1% of the time, Pallas kernels for 2%

profile of v5, /device:TPU:0, one launch (start us, length us, event | category | flops | bytes accessed | tf_op | source)
XLA Modules:
  0.0 76.9 jit_solution(793695078053329528)
XLA Ops:
  0.6 1.7 %edges.1 = (bf16[576,128]{1,0:T(8,128)(2,1)}, bf16[576,128]{1,0:T(8,128)(2,1)}) custom-call(bf16[256,256]{1,0:T(8,128)(2,1)} %bitcast.77, bf16[256,256]{1,0:T(8,128)(2,1)} %bitcast.79, bf16[256,256]{1,0:T(8,128)(2,1)} %bitcast.70), custom_call_target="tpu_custom_call" | custom-call | bytes 393216 | tf_op jit(solution)/shard_map/edges/pallas_call | solution.py:419
  2.3 4.9 %collective-permute-start = (bf16[576,128]{1,0:T(8,128)(2,1)}, bf16[576,128]{1,0:T(8,128)(2,1)S(1)}, u32[]{:S(2)}, u32[]{:S(2)}) collective-permute-start(bf16[576,128]{1,0:T(8,128)(2,1)} %get-tuple-element.34), channel_id=1, source_target_pairs={{0,1},{1,2},{2,3},{3,4},{4,5},{5,6},{6,7},{7,8},{8,9},{9,10},{10,1... | collective-permute-start | bytes 442376 | tf_op jit(solution)/shard_map/ppermute | solution.py:401
  7.2 1.3 %collective-permute-start.1 = (bf16[576,128]{1,0:T(8,128)(2,1)}, bf16[576,128]{1,0:T(8,128)(2,1)S(1)}, u32[]{:S(2)}, u32[]{:S(2)}) collective-permute-start(bf16[576,128]{1,0:T(8,128)(2,1)} %get-tuple-element.35), channel_id=1, source_target_pairs={{1,0},{2,1},{3,2},{4,3},{5,4},{6,5},{7,6},{8,7},{9,8},{10,9},{11,1... | collective-permute-start | bytes 442376 | tf_op jit(solution)/shard_map/ppermute | solution.py:402
  8.6 1.2 %copy-done.1 = bf16[1,27,128,128]{3,2,1,0:T(8,128)(2,1)S(1)} copy-done((bf16[1,27,128,128]{3,2,1,0:T(8,128)(2,1)S(1)}, bf16[1,27,128,128]{3,2,1,0:T(8,128)(2,1)}, u32[]{:S(2)}) %copy-start.1) | copy-done | bytes 884760
  9.7 1.2 %copy-done.3 = bf16[1,27,128,128]{3,2,1,0:T(8,128)(2,1)S(1)} copy-done((bf16[1,27,128,128]{3,2,1,0:T(8,128)(2,1)S(1)}, bf16[1,27,128,128]{3,2,1,0:T(8,128)(2,1)}, u32[]{:S(2)}) %copy-start.3) | copy-done | bytes 884760
  10.9 0.9 %copy-done.5 = bf16[1,4,8,8,256]{4,3,2,1,0:T(8,128)(2,1)S(1)} copy-done((bf16[1,4,8,8,256]{4,3,2,1,0:T(8,128)(2,1)S(1)}, bf16[1,4,8,8,256]{4,3,2,1,0:T(8,128)(2,1)}, u32[]{:S(2)}) %copy-start.5) | copy-done | bytes 131096
  11.8 0.9 %copy-done.7 = bf16[1,4,8,8,256]{4,3,2,1,0:T(8,128)(2,1)S(1)} copy-done((bf16[1,4,8,8,256]{4,3,2,1,0:T(8,128)(2,1)S(1)}, bf16[1,4,8,8,256]{4,3,2,1,0:T(8,128)(2,1)}, u32[]{:S(2)}) %copy-start.7) | copy-done | bytes 131096
  12.7 0.9 %copy-done.8 = bf16[1,4,8,8,256]{4,3,2,1,0:T(8,128)(2,1)S(1)} copy-done((bf16[1,4,8,8,256]{4,3,2,1,0:T(8,128)(2,1)S(1)}, bf16[1,4,8,8,256]{4,3,2,1,0:T(8,128)(2,1)}, u32[]{:S(2)}) %copy-start.8) | copy-done | bytes 131096
  14.2 1.3 %collective-permute-done.1.above = bf16[576,128]{1,0:T(8,128)(2,1)S(1)} collective-permute-done((bf16[576,128]{1,0:T(8,128)(2,1)}, bf16[576,128]{1,0:T(8,128)(2,1)S(1)}, u32[]{:S(2)}, u32[]{:S(2)}) %collective-permute-start.1) | collective-permute-done | bytes 147488 | tf_op jit(solution)/shard_map/ppermute | solution.py:402
  15.6 4.9 %tick_one.1 = (bf16[256,256]{1,0:T(8,128)(2,1)S(1)}, bf16[2,256,256]{2,1,0:T(8,128)(2,1)S(1)}, bf16[384,128]{1,0:T(8,128)(2,1)S(1)}, bf16[384,128]{1,0:T(8,128)(2,1)S(1)}, bf16[384,128]{1,0:T(8,128)(2,1)S(1)}) custom-call(s32[2]{0:T(128)S(1)} %pad_add_fusion.places, f32[2]{0:T(128)S(1)} %add_convert_fusion.3.flags, ...), custom_call_target="tpu_custom_call" | custom-call | flops 1811939328 | bytes 4227072 | tf_op jit(solution)/shard_map/tick_one/pallas_call | solution.py:419
  20.5 1.5 %collective-permute-done.2.lifted.lowered = bf16[2,256,256]{2,1,0:T(8,128)(2,1)S(1)} collective-permute-done((bf16[2,256,256]{2,1,0:T(8,128)(2,1)S(1)}, bf16[2,256,256]{2,1,0:T(8,128)(2,1)S(1)}, u32[]{:S(2)}, u32[]{:S(2)}) %collective-permute-start.2) | collective-permute-done | bytes 262176 | tf_op jit(solution)/shard_map/ppermute | solution.py:453
  22.7 3.4 %collective-permute-start.3 = (bf16[576,128]{1,0:T(8,128)(2,1)S(1)}, bf16[576,128]{1,0:T(8,128)(2,1)S(1)}, u32[]{:S(2)}, u32[]{:S(2)}) collective-permute-start(bf16[576,128]{1,0:T(8,128)(2,1)S(1)} %get-tuple-element.43), channel_id=1, source_target_pairs={{0,1},{1,2},{2,3},{3,4},{4,5},{5,6},{6,7},{7,8},{8,9},{9,10},{10,1... | collective-permute-start | bytes 442376 | tf_op jit(solution)/shard_map/ppermute | solution.py:401
  26.2 1.5 %collective-permute-start.4 = (bf16[576,128]{1,0:T(8,128)(2,1)S(1)}, bf16[576,128]{1,0:T(8,128)(2,1)S(1)}, u32[]{:S(2)}, u32[]{:S(2)}) collective-permute-start(bf16[576,128]{1,0:T(8,128)(2,1)S(1)} %get-tuple-element.44), channel_id=1, source_target_pairs={{1,0},{2,1},{3,2},{4,3},{5,4},{6,5},{7,6},{8,7},{9,8},{10,9},{11,1... | collective-permute-start | bytes 442376 | tf_op jit(solution)/shard_map/ppermute | solution.py:402
  27.6 0.8 %weight_grads.1.so_far = f32[2,3456,128]{2,1,0:T(8,128)S(1)} custom-call(bf16[256,256]{1,0:T(8,128)(2,1)S(1)} %bitcast.72, bf16[384,128]{1,0:T(8,128)(2,1)S(1)} %get-tuple-element.45.back, bf16[384,128]{1,0:T(8,128)(2,1)S(1)} %get-tuple-element.46.carry, bf16[384,128]{1,0:T(8,128)(2,1)S(1)} %get-tuple-element.47.gate), custom_call_target="tpu_custom_call" | custom-call | flops 452984832 | bytes 425984 | tf_op jit(solution)/shard_map/weight_grads/pallas_call | solution.py:419
  28.5 1.7 %copy-done = f32[2,3456,128]{2,1,0:T(8,128)} copy-done((f32[2,3456,128]{2,1,0:T(8,128)}, f32[2,3456,128]{2,1,0:T(8,128)S(1)}, u32[]{:S(2)}) %copy-start) | copy-done | bytes 3538968
  30.2 5.1 %collective-permute-done.4.above = bf16[576,128]{1,0:T(8,128)(2,1)S(1)} collective-permute-done((bf16[576,128]{1,0:T(8,128)(2,1)S(1)}, bf16[576,128]{1,0:T(8,128)(2,1)S(1)}, u32[]{:S(2)}, u32[]{:S(2)}) %collective-permute-start.4) | collective-permute-done | bytes 147488 | tf_op jit(solution)/shard_map/ppermute | solution.py:402
  35.4 8.8 %tick_two.1 = (bf16[256,256]{1,0:T(8,128)(2,1)}, bf16[256,256]{1,0:T(8,128)(2,1)}, bf16[256,256]{1,0:T(8,128)(2,1)}, bf16[8,144,128]{2,1,0:T(8,128)(2,1)S(1)}, b...) custom-call(s32[1]{0:T(128)} %bitcast.spot, ...), custom_call_target="tpu_custom_call" | custom-call | flops 2038431744 | bytes 5996544 | tf_op jit(solution)/shard_map/tick_two/pallas_call | solution.py:419
  44.1 1.7 %collective-permute-start.5 = (bf16[8,144,128]{2,1,0:T(8,128)(2,1)S(1)}, bf16[8,144,128]{2,1,0:T(8,128)(2,1)S(1)}, u32[]{:S(2)}, u32[]{:S(2)}) collective-permute-start(bf16[8,144,128]{2,1,0:T(8,128)(2,1)S(1)} %get-tuple-element.52), channel_id=1, source_target_pairs={{0,1},{1,0},{2,3},{3,2},{4,5},{5,4},{6,7},{7,6},{8,9},{9,8},{10,11... | collective-permute-start | bytes 884744 | tf_op jit(solution)/shard_map/ppermute | solution.py:362
  45.8 3.1 %collective-permute-start.9 = (bf16[8,144,128]{2,1,0:T(8,128)(2,1)S(1)}, bf16[8,144,128]{2,1,0:T(8,128)(2,1)S(1)}, u32[]{:S(2)}, u32[]{:S(2)}) collective-permute-start(bf16[8,144,128]{2,1,0:T(8,128)(2,1)S(1)} %get-tuple-element.54), channel_id=1, source_target_pairs={{0,2},{1,3},{2,0},{3,1},{4,6},{5,7},{6,4},{7,5},{8,10},{9,11},{10,... | collective-permute-start | bytes 884744 | tf_op jit(solution)/shard_map/ppermute | solution.py:362
  48.9 1.6 %collective-permute-start.13 = (bf16[8,144,128]{2,1,0:T(8,128)(2,1)S(1)}, bf16[8,144,128]{2,1,0:T(8,128)(2,1)S(1)}, u32[]{:S(2)}, u32[]{:S(2)}) collective-permute-start(bf16[8,144,128]{2,1,0:T(8,128)(2,1)S(1)} %get-tuple-element.56), channel_id=1, source_target_pairs={{0,4},{1,5},{2,6},{3,7},{4,0},{5,1},{6,2},{7,3},{8,12},{9,13},{10,... | collective-permute-start | bytes 884744 | tf_op jit(solution)/shard_map/ppermute | solution.py:362
  50.5 1.9 %collective-permute-done.5 = bf16[8,144,128]{2,1,0:T(8,128)(2,1)S(1)} collective-permute-done((bf16[8,144,128]{2,1,0:T(8,128)(2,1)S(1)}, bf16[8,144,128]{2,1,0:T(8,128)(2,1)S(1)}, u32[]{:S(2)}, u32[]{:S(2)}) %collective-permute-start.5) | collective-permute-done | bytes 294944 | tf_op jit(solution)/shard_map/ppermute | solution.py:362
  52.5 2.7 %collective-permute-start.6 = (bf16[4,144,128]{2,1,0:T(8,128)(2,1)S(1)}, bf16[4,144,128]{2,1,0:T(8,128)(2,1)S(1)}, u32[]{:S(2)}, u32[]{:S(2)}) collective-permute-start(bf16[4,144,128]{2,1,0:T(8,128)(2,1)S(1)} %dynamic-slice_bitcast_fusion.2), channel_id=1, source_target_pairs={{0,2},{1,3},{2,0},{3,1},{4,6},{5,7},{6,4},{7,5},{8,10},{9,11},{10,... | collective-permute-start | bytes 442376 | tf_op jit(solution)/shard_map/ppermute | solution.py:362
  55.4 2.0 %collective-permute-start.10 = (bf16[4,144,128]{2,1,0:T(8,128)(2,1)S(1)}, bf16[4,144,128]{2,1,0:T(8,128)(2,1)S(1)}, u32[]{:S(2)}, u32[]{:S(2)}) collective-permute-start(bf16[4,144,128]{2,1,0:T(8,128)(2,1)S(1)} %dynamic-slice_bitcast_fusion.1), channel_id=1, source_target_pairs={{0,4},{1,5},{2,6},{3,7},{4,0},{5,1},{6,2},{7,3},{8,12},{9,13},{10,... | collective-permute-start | bytes 442376 | tf_op jit(solution)/shard_map/ppermute | solution.py:362
  57.5 2.6 %collective-permute-start.14 = (bf16[4,144,128]{2,1,0:T(8,128)(2,1)S(1)}, bf16[4,144,128]{2,1,0:T(8,128)(2,1)S(1)}, u32[]{:S(2)}, u32[]{:S(2)}) collective-permute-start(bf16[4,144,128]{2,1,0:T(8,128)(2,1)S(1)} %dynamic-slice_bitcast_fusion), channel_id=1, source_target_pairs={{0,8},{1,9},{2,10},{3,11},{4,12},{5,13},{6,14},{7,15},{8,0},{9,1},... | collective-permute-start | bytes 442376 | tf_op jit(solution)/shard_map/ppermute | solution.py:362
  60.8 2.0 %collective-permute-done.10 = bf16[4,144,128]{2,1,0:T(8,128)(2,1)S(1)} collective-permute-done((bf16[4,144,128]{2,1,0:T(8,128)(2,1)S(1)}, bf16[4,144,128]{2,1,0:T(8,128)(2,1)S(1)}, u32[]{:S(2)}, u32[]{:S(2)}) %collective-permute-start.10) | collective-permute-done | bytes 147488 | tf_op jit(solution)/shard_map/ppermute | solution.py:362
  62.8 2.9 %collective-permute-start.11 = (bf16[2,144,128]{2,1,0:T(8,128)(2,1)S(1)}, bf16[2,144,128]{2,1,0:T(8,128)(2,1)S(1)}, u32[]{:S(2)}, u32[]{:S(2)}) collective-permute-start(bf16[2,144,128]{2,1,0:T(8,128)(2,1)S(1)} %dynamic-slice_bitcast_fusion.4), channel_id=1, source_target_pairs={{0,8},{1,9},{2,10},{3,11},{4,12},{5,13},{6,14},{7,15},{8,0},{9,1},... | collective-permute-start | bytes 221192 | tf_op jit(solution)/shard_map/ppermute | solution.py:362
  65.8 1.8 %collective-permute-done.14 = bf16[4,144,128]{2,1,0:T(8,128)(2,1)S(1)} collective-permute-done((bf16[4,144,128]{2,1,0:T(8,128)(2,1)S(1)}, bf16[4,144,128]{2,1,0:T(8,128)(2,1)S(1)}, u32[]{:S(2)}, u32[]{:S(2)}) %collective-permute-start.14) | collective-permute-done | bytes 147488 | tf_op jit(solution)/shard_map/ppermute | solution.py:362
  68.4 1.2 %collective-permute-start.8 = (bf16[1,144,128]{2,1,0:T(8,128)(2,1)S(1)}, bf16[1,144,128]{2,1,0:T(8,128)(2,1)S(1)}, u32[]{:S(2)}, u32[]{:S(2)}) collective-permute-start(bf16[1,144,128]{2,1,0:T(8,128)(2,1)S(1)} %constant_dynamic-slice_fusion.2), channel_id=1, source_target_pairs={{0,8},{1,9},{2,10},{3,11},{4,12},{5,13},{6,14},{7,15},{8,0},{9,1},... | collective-permute-start | bytes 110600 | tf_op jit(solution)/shard_map/ppermute | solution.py:362
  69.6 2.4 %collective-permute-start.12 = (bf16[1,144,128]{2,1,0:T(8,128)(2,1)S(1)}, bf16[1,144,128]{2,1,0:T(8,128)(2,1)S(1)}, u32[]{:S(2)}, u32[]{:S(2)}) collective-permute-start(bf16[1,144,128]{2,1,0:T(8,128)(2,1)S(1)} %constant_dynamic-slice_fusion.1), channel_id=1, source_target_pairs={{0,1},{1,0},{2,3},{3,2},{4,5},{5,4},{6,7},{7,6},{8,9},{9,8},{10,11... | collective-permute-start | bytes 110600 | tf_op jit(solution)/shard_map/ppermute | solution.py:362
  72.1 0.9 %collective-permute-start.16 = (bf16[1,144,128]{2,1,0:T(8,128)(2,1)S(1)}, bf16[1,144,128]{2,1,0:T(8,128)(2,1)S(1)}, u32[]{:S(2)}, u32[]{:S(2)}) collective-permute-start(bf16[1,144,128]{2,1,0:T(8,128)(2,1)S(1)} %constant_dynamic-slice_fusion), channel_id=1, source_target_pairs={{0,2},{1,3},{2,0},{3,1},{4,6},{5,7},{6,4},{7,5},{8,10},{9,11},{10,... | collective-permute-start | bytes 110600 | tf_op jit(solution)/shard_map/ppermute | solution.py:362
  73.9 2.2 %collective-permute-done.16 = bf16[1,144,128]{2,1,0:T(8,128)(2,1)S(1)} collective-permute-done((bf16[1,144,128]{2,1,0:T(8,128)(2,1)S(1)}, bf16[1,144,128]{2,1,0:T(8,128)(2,1)S(1)}, u32[]{:S(2)}, u32[]{:S(2)}) %collective-permute-start.16) | collective-permute-done | bytes 36896 | tf_op jit(solution)/shard_map/ppermute | solution.py:362
  76.2 0.7 fusion.6
  (54 shorter events, 4.3 us)
Async XLA Ops:
  2.3 11.9 %collective-permute-start = (bf16[576,128]{1,0:T(8,128)(2,1)}, bf16[576,128]{1,0:T(8,128)(2,1)S(1)}, u32[]{:S(2)}, u32[]{:S(2)}) collective-permute-start(bf16[576,128]{1,0:T(8,128)(2,1)} %get-tuple-element.34), channel_id=1, source_target_pairs={{0,1},{1,2},{2,3},{3,4},{4,5},{5,6},{6,7},{7,8},{8,9},{9,10},{10,1... | collective-permute-start | bytes 442376 | tf_op jit(solution)/shard_map/ppermute | solution.py:401
  7.2 8.4 %collective-permute-start.1 = (bf16[576,128]{1,0:T(8,128)(2,1)}, bf16[576,128]{1,0:T(8,128)(2,1)S(1)}, u32[]{:S(2)}, u32[]{:S(2)}) collective-permute-start(bf16[576,128]{1,0:T(8,128)(2,1)} %get-tuple-element.35), channel_id=1, source_target_pairs={{1,0},{2,1},{3,2},{4,3},{5,4},{6,5},{7,6},{8,7},{9,8},{10,9},{11,1... | collective-permute-start | bytes 442376 | tf_op jit(solution)/shard_map/ppermute | solution.py:402
  8.6 1.2 %copy-start.1 = (bf16[1,27,128,128]{3,2,1,0:T(8,128)(2,1)S(1)}, bf16[1,27,128,128]{3,2,1,0:T(8,128)(2,1)}, u32[]{:S(2)}) copy-start(bf16[1,27,128,128]{3,2,1,0:T(8,128)(2,1)} %param.12) | copy-start | bytes 2654212
  9.7 1.2 %copy-start.3 = (bf16[1,27,128,128]{3,2,1,0:T(8,128)(2,1)S(1)}, bf16[1,27,128,128]{3,2,1,0:T(8,128)(2,1)}, u32[]{:S(2)}) copy-start(bf16[1,27,128,128]{3,2,1,0:T(8,128)(2,1)} %param.13) | copy-start | bytes 2654212
  10.9 0.9 %copy-start.5 = (bf16[1,4,8,8,256]{4,3,2,1,0:T(8,128)(2,1)S(1)}, bf16[1,4,8,8,256]{4,3,2,1,0:T(8,128)(2,1)}, u32[]{:S(2)}) copy-start(bf16[1,4,8,8,256]{4,3,2,1,0:T(8,128)(2,1)} %param.9) | copy-start | bytes 393220
  11.8 0.9 %copy-start.7 = (bf16[1,4,8,8,256]{4,3,2,1,0:T(8,128)(2,1)S(1)}, bf16[1,4,8,8,256]{4,3,2,1,0:T(8,128)(2,1)}, u32[]{:S(2)}) copy-start(bf16[1,4,8,8,256]{4,3,2,1,0:T(8,128)(2,1)} %param.7) | copy-start | bytes 393220
  12.7 0.9 %copy-start.8 = (bf16[1,4,8,8,256]{4,3,2,1,0:T(8,128)(2,1)S(1)}, bf16[1,4,8,8,256]{4,3,2,1,0:T(8,128)(2,1)}, u32[]{:S(2)}) copy-start(bf16[1,4,8,8,256]{4,3,2,1,0:T(8,128)(2,1)} %param.8) | copy-start | bytes 393220
  14.1 7.9 %copy-start.9 = (bf16[4,8,8,256]{3,2,1,0:T(8,128)(2,1)S(1)}, bf16[4,8,8,256]{3,2,1,0:T(8,128)(2,1)}, u32[]{:S(2)}) copy-start(bf16[4,8,8,256]{3,2,1,0:T(8,128)(2,1)} %param.10) | copy-start | bytes 393220
  14.1 7.9 %copy-start.10 = (bf16[4,8,8,256]{3,2,1,0:T(8,128)(2,1)S(1)}, bf16[4,8,8,256]{3,2,1,0:T(8,128)(2,1)}, u32[]{:S(2)}) copy-start(bf16[4,8,8,256]{3,2,1,0:T(8,128)(2,1)} %param.11) | copy-start | bytes 393220
  15.6 12.1 %copy-start.6 = (bf16[1,4,8,8,256]{4,3,2,1,0:T(8,128)(2,1)S(1)}, bf16[1,4,8,8,256]{4,3,2,1,0:T(8,128)(2,1)}, u32[]{:S(2)}) copy-start(bf16[1,4,8,8,256]{4,3,2,1,0:T(8,128)(2,1)} %param.9) | copy-start | bytes 393220
  20.4 14.9 %copy-start.2 = (bf16[1,27,128,128]{3,2,1,0:T(8,128)(2,1)S(1)}, bf16[1,27,128,128]{3,2,1,0:T(8,128)(2,1)}, u32[]{:S(2)}) copy-start(bf16[1,27,128,128]{3,2,1,0:T(8,128)(2,1)} %param.12) | copy-start | bytes 2654212
  20.5 14.9 %copy-start.4 = (bf16[1,27,128,128]{3,2,1,0:T(8,128)(2,1)S(1)}, bf16[1,27,128,128]{3,2,1,0:T(8,128)(2,1)}, u32[]{:S(2)}) copy-start(bf16[1,27,128,128]{3,2,1,0:T(8,128)(2,1)} %param.13) | copy-start | bytes 2654212
  20.5 1.6 %collective-permute-start.2 = (bf16[2,256,256]{2,1,0:T(8,128)(2,1)S(1)}, bf16[2,256,256]{2,1,0:T(8,128)(2,1)S(1)}, u32[]{:S(2)}, u32[]{:S(2)}) collective-permute-start(bf16[2,256,256]{2,1,0:T(8,128)(2,1)S(1)} %get-tuple-element.39), channel_id=1, source_target_pairs={{0,16},{16,0},{1,17},{17,1},{2,18},{18,2},{3,19},{19,3},{4,20},{20... | collective-permute-start | bytes 786440 | tf_op jit(solution)/shard_map/ppermute | solution.py:453
  22.7 7.5 %collective-permute-start.3 = (bf16[576,128]{1,0:T(8,128)(2,1)S(1)}, bf16[576,128]{1,0:T(8,128)(2,1)S(1)}, u32[]{:S(2)}, u32[]{:S(2)}) collective-permute-start(bf16[576,128]{1,0:T(8,128)(2,1)S(1)} %get-tuple-element.43), channel_id=1, source_target_pairs={{0,1},{1,2},{2,3},{3,4},{4,5},{5,6},{6,7},{7,8},{8,9},{9,10},{10,1... | collective-permute-start | bytes 442376 | tf_op jit(solution)/shard_map/ppermute | solution.py:401
  26.2 9.2 %collective-permute-start.4 = (bf16[576,128]{1,0:T(8,128)(2,1)S(1)}, bf16[576,128]{1,0:T(8,128)(2,1)S(1)}, u32[]{:S(2)}, u32[]{:S(2)}) collective-permute-start(bf16[576,128]{1,0:T(8,128)(2,1)S(1)} %get-tuple-element.44), channel_id=1, source_target_pairs={{1,0},{2,1},{3,2},{4,3},{5,4},{6,5},{7,6},{8,7},{9,8},{10,9},{11,1... | collective-permute-start | bytes 442376 | tf_op jit(solution)/shard_map/ppermute | solution.py:402
  28.5 1.7 %copy-start = (f32[2,3456,128]{2,1,0:T(8,128)}, f32[2,3456,128]{2,1,0:T(8,128)S(1)}, u32[]{:S(2)}) copy-start(f32[2,3456,128]{2,1,0:T(8,128)S(1)} %weight_grads.1.so_far) | copy-start | bytes 10616836
  44.1 8.3 %collective-permute-start.5 = (bf16[8,144,128]{2,1,0:T(8,128)(2,1)S(1)}, bf16[8,144,128]{2,1,0:T(8,128)(2,1)S(1)}, u32[]{:S(2)}, u32[]{:S(2)}) collective-permute-start(bf16[8,144,128]{2,1,0:T(8,128)(2,1)S(1)} %get-tuple-element.52), channel_id=1, source_target_pairs={{0,1},{1,0},{2,3},{3,2},{4,5},{5,4},{6,7},{7,6},{8,9},{9,8},{10,11... | collective-permute-start | bytes 884744 | tf_op jit(solution)/shard_map/ppermute | solution.py:362
  45.8 9.5 %collective-permute-start.9 = (bf16[8,144,128]{2,1,0:T(8,128)(2,1)S(1)}, bf16[8,144,128]{2,1,0:T(8,128)(2,1)S(1)}, u32[]{:S(2)}, u32[]{:S(2)}) collective-permute-start(bf16[8,144,128]{2,1,0:T(8,128)(2,1)S(1)} %get-tuple-element.54), channel_id=1, source_target_pairs={{0,2},{1,3},{2,0},{3,1},{4,6},{5,7},{6,4},{7,5},{8,10},{9,11},{10,... | collective-permute-start | bytes 884744 | tf_op jit(solution)/shard_map/ppermute | solution.py:362
  48.9 8.5 %collective-permute-start.13 = (bf16[8,144,128]{2,1,0:T(8,128)(2,1)S(1)}, bf16[8,144,128]{2,1,0:T(8,128)(2,1)S(1)}, u32[]{:S(2)}, u32[]{:S(2)}) collective-permute-start(bf16[8,144,128]{2,1,0:T(8,128)(2,1)S(1)} %get-tuple-element.56), channel_id=1, source_target_pairs={{0,4},{1,5},{2,6},{3,7},{4,0},{5,1},{6,2},{7,3},{8,12},{9,13},{10,... | collective-permute-start | bytes 884744 | tf_op jit(solution)/shard_map/ppermute | solution.py:362
  52.5 7.6 %collective-permute-start.6 = (bf16[4,144,128]{2,1,0:T(8,128)(2,1)S(1)}, bf16[4,144,128]{2,1,0:T(8,128)(2,1)S(1)}, u32[]{:S(2)}, u32[]{:S(2)}) collective-permute-start(bf16[4,144,128]{2,1,0:T(8,128)(2,1)S(1)} %dynamic-slice_bitcast_fusion.2), channel_id=1, source_target_pairs={{0,2},{1,3},{2,0},{3,1},{4,6},{5,7},{6,4},{7,5},{8,10},{9,11},{10,... | collective-permute-start | bytes 442376 | tf_op jit(solution)/shard_map/ppermute | solution.py:362
  55.4 7.4 %collective-permute-start.10 = (bf16[4,144,128]{2,1,0:T(8,128)(2,1)S(1)}, bf16[4,144,128]{2,1,0:T(8,128)(2,1)S(1)}, u32[]{:S(2)}, u32[]{:S(2)}) collective-permute-start(bf16[4,144,128]{2,1,0:T(8,128)(2,1)S(1)} %dynamic-slice_bitcast_fusion.1), channel_id=1, source_target_pairs={{0,4},{1,5},{2,6},{3,7},{4,0},{5,1},{6,2},{7,3},{8,12},{9,13},{10,... | collective-permute-start | bytes 442376 | tf_op jit(solution)/shard_map/ppermute | solution.py:362
  57.5 10.1 %collective-permute-start.14 = (bf16[4,144,128]{2,1,0:T(8,128)(2,1)S(1)}, bf16[4,144,128]{2,1,0:T(8,128)(2,1)S(1)}, u32[]{:S(2)}, u32[]{:S(2)}) collective-permute-start(bf16[4,144,128]{2,1,0:T(8,128)(2,1)S(1)} %dynamic-slice_bitcast_fusion), channel_id=1, source_target_pairs={{0,8},{1,9},{2,10},{3,11},{4,12},{5,13},{6,14},{7,15},{8,0},{9,1},... | collective-permute-start | bytes 442376 | tf_op jit(solution)/shard_map/ppermute | solution.py:362
  60.2 8.1 %collective-permute-start.7 = (bf16[2,144,128]{2,1,0:T(8,128)(2,1)S(1)}, bf16[2,144,128]{2,1,0:T(8,128)(2,1)S(1)}, u32[]{:S(2)}, u32[]{:S(2)}) collective-permute-start(bf16[2,144,128]{2,1,0:T(8,128)(2,1)S(1)} %dynamic-slice_bitcast_fusion.5), channel_id=1, source_target_pairs={{0,4},{1,5},{2,6},{3,7},{4,0},{5,1},{6,2},{7,3},{8,12},{9,13},{10,... | collective-permute-start | bytes 221192 | tf_op jit(solution)/shard_map/ppermute | solution.py:362
  62.8 6.7 %collective-permute-start.11 = (bf16[2,144,128]{2,1,0:T(8,128)(2,1)S(1)}, bf16[2,144,128]{2,1,0:T(8,128)(2,1)S(1)}, u32[]{:S(2)}, u32[]{:S(2)}) collective-permute-start(bf16[2,144,128]{2,1,0:T(8,128)(2,1)S(1)} %dynamic-slice_bitcast_fusion.4), channel_id=1, source_target_pairs={{0,8},{1,9},{2,10},{3,11},{4,12},{5,13},{6,14},{7,15},{8,0},{9,1},... | collective-permute-start | bytes 221192 | tf_op jit(solution)/shard_map/ppermute | solution.py:362
  67.7 4.4 %collective-permute-start.15 = (bf16[2,144,128]{2,1,0:T(8,128)(2,1)S(1)}, bf16[2,144,128]{2,1,0:T(8,128)(2,1)S(1)}, u32[]{:S(2)}, u32[]{:S(2)}) collective-permute-start(bf16[2,144,128]{2,1,0:T(8,128)(2,1)S(1)} %dynamic-slice_bitcast_fusion.3), channel_id=1, source_target_pairs={{0,1},{1,0},{2,3},{3,2},{4,5},{5,4},{6,7},{7,6},{8,9},{9,8},{10,11... | collective-permute-start | bytes 221192 | tf_op jit(solution)/shard_map/ppermute | solution.py:362
  68.4 4.9 %collective-permute-start.8 = (bf16[1,144,128]{2,1,0:T(8,128)(2,1)S(1)}, bf16[1,144,128]{2,1,0:T(8,128)(2,1)S(1)}, u32[]{:S(2)}, u32[]{:S(2)}) collective-permute-start(bf16[1,144,128]{2,1,0:T(8,128)(2,1)S(1)} %constant_dynamic-slice_fusion.2), channel_id=1, source_target_pairs={{0,8},{1,9},{2,10},{3,11},{4,12},{5,13},{6,14},{7,15},{8,0},{9,1},... | collective-permute-start | bytes 110600 | tf_op jit(solution)/shard_map/ppermute | solution.py:362
  69.6 4.3 %collective-permute-start.12 = (bf16[1,144,128]{2,1,0:T(8,128)(2,1)S(1)}, bf16[1,144,128]{2,1,0:T(8,128)(2,1)S(1)}, u32[]{:S(2)}, u32[]{:S(2)}) collective-permute-start(bf16[1,144,128]{2,1,0:T(8,128)(2,1)S(1)} %constant_dynamic-slice_fusion.1), channel_id=1, source_target_pairs={{0,1},{1,0},{2,3},{3,2},{4,5},{5,4},{6,7},{7,6},{8,9},{9,8},{10,11... | collective-permute-start | bytes 110600 | tf_op jit(solution)/shard_map/ppermute | solution.py:362
  72.1 4.0 %collective-permute-start.16 = (bf16[1,144,128]{2,1,0:T(8,128)(2,1)S(1)}, bf16[1,144,128]{2,1,0:T(8,128)(2,1)S(1)}, u32[]{:S(2)}, u32[]{:S(2)}) collective-permute-start(bf16[1,144,128]{2,1,0:T(8,128)(2,1)S(1)} %constant_dynamic-slice_fusion), channel_id=1, source_target_pairs={{0,2},{1,3},{2,0},{3,1},{4,6},{5,7},{6,4},{7,5},{8,10},{9,11},{10,... | collective-permute-start | bytes 110600 | tf_op jit(solution)/shard_map/ppermute | solution.py:362

commit v6 on v5

--- a/solution.py
+++ b/solution.py
@@ -275,9 +275,11 @@
 
 def ways_of(count, rows):
     bits = [1 << level for level in range(count.bit_length() - 1)]
+    turning, last = bits[:-1], bits[-1:]
     ways = 3
     span = 2 * rows // ways
-    return [(way * span, span, bits[way % len(bits) :] + bits[: way % len(bits)]) for way in range(ways)]
+    orders = [turning[way % len(turning) :] + turning[: way % len(turning)] + last for way in range(ways)]
+    return [(way * span, span, order) for way, order in enumerate(orders)]
 
 
 def last_kernel(ydim, zdim, factor, count, direct, spot, flags, state, act, grad, below, above, first,
@@ -289,12 +291,14 @@
     refs, args = args[:n_outs], args[n_outs:]
     new_one, back_two, mid, back, carry, gate, stack, sums, sems = args
     copies = Copies(sems)
+    copies.start("so_far", so_far, sums)
     ignore = lambda *names: None
     first_kernel(ydim, zdim, copies, ignore, flags, state, act, grad, below, above, first, second,
                  second_back, new_one, back_two, mid, back, carry, gate, stack)
+    copies.need("so_far")
 
     def put(which, at, block):
-        sums[which, at, :] = (block + so_far[which, at, :]) * factor
+        sums[which, at, :] = (block + sums[which, at, :]) * factor
 
     both_grads(ydim, zdim, grad, back, carry, gate, stack, put)
     if not direct:
@@ -355,23 +359,26 @@
         (halves[2 * way], halves[2 * way + 1], order)
         for way, (_, _, order) in enumerate(ways_of(count, rows))
     ]
-    for step in range(count.bit_length() - 1):
+    def halved(total, bit):
+        total = total.astype(BF16)
+        total = total.reshape((2, total.shape[0] // 2) + total.shape[1:])
+        mine = (spot // bit) % 2
+        keep = lax.dynamic_index_in_dim(total, mine, 0, keepdims=False)
+        return keep, lax.dynamic_index_in_dim(total, 1 - mine, 0, keepdims=False)
+
+    def swapped(send, bit):
+        return lax.ppermute(send, "space", [(i, i ^ bit) for i in range(count)]).astype(F32)
+
+    depth = count.bit_length() - 1
+    for step in range(depth - 1):
         later = []
         for keep, send, order in ways:
-            bit = order[step]
-            got = lax.ppermute(send, "space", [(i, i ^ bit) for i in range(count)])
-            total = keep.astype(F32) + got.astype(F32)
-            if step + 1 < len(order):
-                total = total.astype(BF16)
-                total = total.reshape((2, total.shape[0] // 2) + total.shape[1:])
-                mine = (spot // order[step + 1]) % 2
-                keep = lax.dynamic_index_in_dim(total, mine, 0, keepdims=False)
-                send = lax.dynamic_index_in_dim(total, 1 - mine, 0, keepdims=False)
-            else:
-                keep, send = total[0], None
-            later.append((keep, send, order))
+            total = keep.astype(F32) + swapped(send, order[step])
+            later.append((*halved(total, order[step + 1]), order))
         ways = later
-    return jnp.concatenate([keep for keep, _, _ in ways], axis=0)
+    keep = jnp.concatenate([keep[0] for keep, _, _ in ways], axis=0)
+    send = jnp.concatenate([send[0] for _, send, _ in ways], axis=0)
+    return keep.astype(F32) + swapped(send, ways[0][2][-1])
 
 
 def shards(fwd_in, bwd_act, bwd_grad, fresh, target, w_first, w_second):
@@ -414,12 +421,13 @@
 
     vmem = pl.BlockSpec(memory_space=pltpu.VMEM)
 
-    def call(kernel, name, scalars, inputs, outs, scratch, grant, copies=0, places=(vmem, vmem), flops=0):
+    def call(kernel, name, scalars, inputs, outs, scratch, grant, copies=0, places=(vmem, vmem), flops=0,
+             far=0):
         semaphores = [pltpu.SemaphoreType.DMA((copies,))] if copies else []
         return pl.pallas_call(
             kernel,
             out_shape=tuple(outs),
-            in_specs=[smem] * len(scalars) + [places[0]] * len(inputs),
+            in_specs=[smem] * len(scalars) + [places[0]] * (len(inputs) - far) + [hbm] * far,
             out_specs=(places[1],) * len(outs),
             scratch_shapes=[pltpu.VMEM(like.shape, like.dtype) for like in scratch] + semaphores,
             compiler_params=pltpu.CompilerParams(vmem_limit_bytes=grant),
@@ -482,7 +490,7 @@
         (state_two, act_two, grad_two, below, above, first, second, first_back, second_back, so_far),
         results + outs,
         results + outs + (tile, tile, wide, wide, wide, wide, outer_stack, sums_shape),
-        48 * 1024 * 1024, 9, (vmem, hbm), 9 * work,
+        48 * 1024 * 1024, 10, (vmem, hbm), 9 * work, 1,
     )
     forward, rebuilt, passed = made[:3]
     halves = made[3:] if direct else split_blocks(made[3], count)

time: 77.3 us -> 75.2 us (0.973)
  starting transfers between devices: 33.4 us -> 30 us
  waiting for transfers between devices: 17 us -> 19.1 us
  Pallas kernels: 17.3 us -> 16.4 us
    ppermute x12 -> x10, starting transfers between devices: 22.3 us -> 18.9 us  [swapped(): lax.ppermute(send, 'space', [(i, i ^ bit) for i in range(count)])]
    ppermute x12 -> x10, waiting for transfers between devices: 9.02 us -> 11.2 us  [swapped(): lax.ppermute(send, 'space', [(i, i ^ bit) for i in range(count)])]
    pallas_call x6, Pallas kernels: 17.3 us -> 16.4 us  [call(): pl.pallas_call(kernel, out_shape=tuple(outs), in_specs=[smem] * len(scala...]
  transfers between devices with their start and end apart: 17 -> 15, of which waited for: 10 -> 9; matrix products, arithmetic and copies ran while one was open for 1% -> 1% of each run, Pallas kernels for 2% -> 2%
where the time goes in v6:
time: 75.2 us; the launch traced here: 74.7 us
  starting transfers between devices  30 us (40%)
  waiting for transfers between devices  19.1 us (25%)
  Pallas kernels  16.4 us (22%)
  local copies, waits for them, and re-layouts  7.68 us (10%)
  between operations  0.89 us (1%)
    ppermute x10, starting transfers between devices, swapped(): lax.ppermute(send, 'space', [(i, i ^ bit) for i in range(count)])  18.9 us
    pallas_call x6, Pallas kernels, call(): pl.pallas_call(kernel, out_shape=tuple(outs), in_specs=[smem] * len(scala...  16.4 us
    ppermute x10, waiting for transfers between devices, swapped(): lax.ppermute(send, 'space', [(i, i ^ bit) for i in range(count)])  11.2 us
    ppermute x2, starting transfers between devices, exchange(): below = lax.ppermute(high, 'space', up)  8.25 us
    unnamed x22, local copies, waits for them, and re-layouts  6.82 us
    ppermute x2, waiting for transfers between devices, exchange(): above = lax.ppermute(low, 'space', down)  6.45 us
    ppermute x2, starting transfers between devices, exchange(): above = lax.ppermute(low, 'space', down)  2.76 us
    ppermute x1, waiting for transfers between devices, shards(): lifted = lowered = lax.ppermute(sent, 'section', [(0, 1), (1, 0)])  1.52 us
  transfers between devices with their start and end apart: 15, of which 9 were waited for; matrix products, arithmetic and copies ran while one was open for 1% of the time, Pallas kernels for 2%

profile of v6, /device:TPU:0, one launch (start us, length us, event | category | flops | bytes accessed | tf_op | source)
XLA Modules:
  0.0 74.7 jit_solution(15344145422624354941)
XLA Ops:
  0.6 1.7 %edges.1 = (bf16[576,128]{1,0:T(8,128)(2,1)}, bf16[576,128]{1,0:T(8,128)(2,1)}) custom-call(bf16[256,256]{1,0:T(8,128)(2,1)} %bitcast.83, bf16[256,256]{1,0:T(8,128)(2,1)} %bitcast.85, bf16[256,256]{1,0:T(8,128)(2,1)} %bitcast.76), custom_call_target="tpu_custom_call" | custom-call | bytes 393216 | tf_op jit(solution)/shard_map/edges/pallas_call | solution.py:427
  2.3 4.9 %collective-permute-start = (bf16[576,128]{1,0:T(8,128)(2,1)}, bf16[576,128]{1,0:T(8,128)(2,1)S(1)}, u32[]{:S(2)}, u32[]{:S(2)}) collective-permute-start(bf16[576,128]{1,0:T(8,128)(2,1)} %get-tuple-element.34), channel_id=1, source_target_pairs={{0,1},{1,2},{2,3},{3,4},{4,5},{5,6},{6,7},{7,8},{8,9},{9,10},{10,1... | collective-permute-start | bytes 442376 | tf_op jit(solution)/shard_map/ppermute | solution.py:408
  7.2 1.3 %collective-permute-start.1 = (bf16[576,128]{1,0:T(8,128)(2,1)}, bf16[576,128]{1,0:T(8,128)(2,1)S(1)}, u32[]{:S(2)}, u32[]{:S(2)}) collective-permute-start(bf16[576,128]{1,0:T(8,128)(2,1)} %get-tuple-element.35), channel_id=1, source_target_pairs={{1,0},{2,1},{3,2},{4,3},{5,4},{6,5},{7,6},{8,7},{9,8},{10,9},{11,1... | collective-permute-start | bytes 442376 | tf_op jit(solution)/shard_map/ppermute | solution.py:409
  8.6 1.2 %copy-done.1 = bf16[1,27,128,128]{3,2,1,0:T(8,128)(2,1)S(1)} copy-done((bf16[1,27,128,128]{3,2,1,0:T(8,128)(2,1)S(1)}, bf16[1,27,128,128]{3,2,1,0:T(8,128)(2,1)}, u32[]{:S(2)}) %copy-start.1) | copy-done | bytes 884760
  9.7 1.2 %copy-done.3 = bf16[1,27,128,128]{3,2,1,0:T(8,128)(2,1)S(1)} copy-done((bf16[1,27,128,128]{3,2,1,0:T(8,128)(2,1)S(1)}, bf16[1,27,128,128]{3,2,1,0:T(8,128)(2,1)}, u32[]{:S(2)}) %copy-start.3) | copy-done | bytes 884760
  10.9 0.9 %copy-done.5 = bf16[1,4,8,8,256]{4,3,2,1,0:T(8,128)(2,1)S(1)} copy-done((bf16[1,4,8,8,256]{4,3,2,1,0:T(8,128)(2,1)S(1)}, bf16[1,4,8,8,256]{4,3,2,1,0:T(8,128)(2,1)}, u32[]{:S(2)}) %copy-start.5) | copy-done | bytes 131096
  11.8 0.9 %copy-done.7 = bf16[1,4,8,8,256]{4,3,2,1,0:T(8,128)(2,1)S(1)} copy-done((bf16[1,4,8,8,256]{4,3,2,1,0:T(8,128)(2,1)S(1)}, bf16[1,4,8,8,256]{4,3,2,1,0:T(8,128)(2,1)}, u32[]{:S(2)}) %copy-start.7) | copy-done | bytes 131096
  12.7 0.9 %copy-done.8 = bf16[1,4,8,8,256]{4,3,2,1,0:T(8,128)(2,1)S(1)} copy-done((bf16[1,4,8,8,256]{4,3,2,1,0:T(8,128)(2,1)S(1)}, bf16[1,4,8,8,256]{4,3,2,1,0:T(8,128)(2,1)}, u32[]{:S(2)}) %copy-start.8) | copy-done | bytes 131096
  14.2 1.3 %collective-permute-done.1.above = bf16[576,128]{1,0:T(8,128)(2,1)S(1)} collective-permute-done((bf16[576,128]{1,0:T(8,128)(2,1)}, bf16[576,128]{1,0:T(8,128)(2,1)S(1)}, u32[]{:S(2)}, u32[]{:S(2)}) %collective-permute-start.1) | collective-permute-done | bytes 147488 | tf_op jit(solution)/shard_map/ppermute | solution.py:409
  15.6 4.9 %tick_one.1 = (bf16[256,256]{1,0:T(8,128)(2,1)S(1)}, bf16[2,256,256]{2,1,0:T(8,128)(2,1)S(1)}, bf16[384,128]{1,0:T(8,128)(2,1)S(1)}, bf16[384,128]{1,0:T(8,128)(2,1)S(1)}, bf16[384,128]{1,0:T(8,128)(2,1)S(1)}) custom-call(s32[2]{0:T(128)S(1)} %pad_add_fusion.places, f32[2]{0:T(128)S(1)} %add_convert_fusion.3.flags, ...), custom_call_target="tpu_custom_call" | custom-call | flops 1811939328 | bytes 4227072 | tf_op jit(solution)/shard_map/tick_one/pallas_call | solution.py:427
  20.5 1.5 %collective-permute-done.2.lifted.lowered = bf16[2,256,256]{2,1,0:T(8,128)(2,1)S(1)} collective-permute-done((bf16[2,256,256]{2,1,0:T(8,128)(2,1)S(1)}, bf16[2,256,256]{2,1,0:T(8,128)(2,1)S(1)}, u32[]{:S(2)}, u32[]{:S(2)}) %collective-permute-start.2) | collective-permute-done | bytes 262176 | tf_op jit(solution)/shard_map/ppermute | solution.py:461
  22.7 3.4 %collective-permute-start.3 = (bf16[576,128]{1,0:T(8,128)(2,1)S(1)}, bf16[576,128]{1,0:T(8,128)(2,1)S(1)}, u32[]{:S(2)}, u32[]{:S(2)}) collective-permute-start(bf16[576,128]{1,0:T(8,128)(2,1)S(1)} %get-tuple-element.43), channel_id=1, source_target_pairs={{0,1},{1,2},{2,3},{3,4},{4,5},{5,6},{6,7},{7,8},{8,9},{9,10},{10,1... | collective-permute-start | bytes 442376 | tf_op jit(solution)/shard_map/ppermute | solution.py:408
  26.2 1.5 %collective-permute-start.4 = (bf16[576,128]{1,0:T(8,128)(2,1)S(1)}, bf16[576,128]{1,0:T(8,128)(2,1)S(1)}, u32[]{:S(2)}, u32[]{:S(2)}) collective-permute-start(bf16[576,128]{1,0:T(8,128)(2,1)S(1)} %get-tuple-element.44), channel_id=1, source_target_pairs={{1,0},{2,1},{3,2},{4,3},{5,4},{6,5},{7,6},{8,7},{9,8},{10,9},{11,1... | collective-permute-start | bytes 442376 | tf_op jit(solution)/shard_map/ppermute | solution.py:409
  27.6 0.8 %weight_grads.1.so_far = f32[2,3456,128]{2,1,0:T(8,128)S(1)} custom-call(bf16[256,256]{1,0:T(8,128)(2,1)S(1)} %bitcast.78, bf16[384,128]{1,0:T(8,128)(2,1)S(1)} %get-tuple-element.45.back, bf16[384,128]{1,0:T(8,128)(2,1)S(1)} %get-tuple-element.46.carry, bf16[384,128]{1,0:T(8,128)(2,1)S(1)} %get-tuple-element.47.gate), custom_call_target="tpu_custom_call" | custom-call | flops 452984832 | bytes 425984 | tf_op jit(solution)/shard_map/weight_grads/pallas_call | solution.py:427
  28.5 1.7 %copy-done = f32[2,3456,128]{2,1,0:T(8,128)} copy-done((f32[2,3456,128]{2,1,0:T(8,128)}, f32[2,3456,128]{2,1,0:T(8,128)S(1)}, u32[]{:S(2)}) %copy-start) | copy-done | bytes 3538968
  30.2 5.1 %collective-permute-done.4.above = bf16[576,128]{1,0:T(8,128)(2,1)S(1)} collective-permute-done((bf16[576,128]{1,0:T(8,128)(2,1)S(1)}, bf16[576,128]{1,0:T(8,128)(2,1)S(1)}, u32[]{:S(2)}, u32[]{:S(2)}) %collective-permute-start.4) | collective-permute-done | bytes 147488 | tf_op jit(solution)/shard_map/ppermute | solution.py:409
  35.4 7.8 %tick_two.1 = (bf16[256,256]{1,0:T(8,128)(2,1)}, bf16[256,256]{1,0:T(8,128)(2,1)}, bf16[256,256]{1,0:T(8,128)(2,1)}, bf16[8,144,128]{2,1,0:T(8,128)(2,1)S(1)}, b...) custom-call(s32[1]{0:T(128)} %bitcast.spot, ...), custom_call_target="tpu_custom_call" | custom-call | flops 2038431744 | bytes 5996544 | tf_op jit(solution)/shard_map/tick_two/pallas_call | solution.py:427
  43.2 1.6 %collective-permute-start.5 = (bf16[8,144,128]{2,1,0:T(8,128)(2,1)S(1)}, bf16[8,144,128]{2,1,0:T(8,128)(2,1)S(1)}, u32[]{:S(2)}, u32[]{:S(2)}) collective-permute-start(bf16[8,144,128]{2,1,0:T(8,128)(2,1)S(1)} %get-tuple-element.52), channel_id=1, source_target_pairs={{0,1},{1,0},{2,3},{3,2},{4,5},{5,4},{6,7},{7,6},{8,9},{9,8},{10,11... | collective-permute-start | bytes 884744 | tf_op jit(solution)/shard_map/ppermute | solution.py:370
  44.8 3.1 %collective-permute-start.8 = (bf16[8,144,128]{2,1,0:T(8,128)(2,1)S(1)}, bf16[8,144,128]{2,1,0:T(8,128)(2,1)S(1)}, u32[]{:S(2)}, u32[]{:S(2)}) collective-permute-start(bf16[8,144,128]{2,1,0:T(8,128)(2,1)S(1)} %get-tuple-element.54), channel_id=1, source_target_pairs={{0,2},{1,3},{2,0},{3,1},{4,6},{5,7},{6,4},{7,5},{8,10},{9,11},{10,... | collective-permute-start | bytes 884744 | tf_op jit(solution)/shard_map/ppermute | solution.py:370
  48.0 1.6 %collective-permute-start.11 = (bf16[8,144,128]{2,1,0:T(8,128)(2,1)S(1)}, bf16[8,144,128]{2,1,0:T(8,128)(2,1)S(1)}, u32[]{:S(2)}, u32[]{:S(2)}) collective-permute-start(bf16[8,144,128]{2,1,0:T(8,128)(2,1)S(1)} %get-tuple-element.56), channel_id=1, source_target_pairs={{0,4},{1,5},{2,6},{3,7},{4,0},{5,1},{6,2},{7,3},{8,12},{9,13},{10,... | collective-permute-start | bytes 884744 | tf_op jit(solution)/shard_map/ppermute | solution.py:370
  49.5 1.9 %collective-permute-done.5 = bf16[8,144,128]{2,1,0:T(8,128)(2,1)S(1)} collective-permute-done((bf16[8,144,128]{2,1,0:T(8,128)(2,1)S(1)}, bf16[8,144,128]{2,1,0:T(8,128)(2,1)S(1)}, u32[]{:S(2)}, u32[]{:S(2)}) %collective-permute-start.5) | collective-permute-done | bytes 294944 | tf_op jit(solution)/shard_map/ppermute | solution.py:370
  51.6 2.7 %collective-permute-start.6 = (bf16[4,144,128]{2,1,0:T(8,128)(2,1)S(1)}, bf16[4,144,128]{2,1,0:T(8,128)(2,1)S(1)}, u32[]{:S(2)}, u32[]{:S(2)}) collective-permute-start(bf16[4,144,128]{2,1,0:T(8,128)(2,1)S(1)} %dynamic-slice_bitcast_fusion.2), channel_id=1, source_target_pairs={{0,2},{1,3},{2,0},{3,1},{4,6},{5,7},{6,4},{7,5},{8,10},{9,11},{10,... | collective-permute-start | bytes 442376 | tf_op jit(solution)/shard_map/ppermute | solution.py:370
  54.4 2.0 %collective-permute-start.9 = (bf16[4,144,128]{2,1,0:T(8,128)(2,1)S(1)}, bf16[4,144,128]{2,1,0:T(8,128)(2,1)S(1)}, u32[]{:S(2)}, u32[]{:S(2)}) collective-permute-start(bf16[4,144,128]{2,1,0:T(8,128)(2,1)S(1)} %dynamic-slice_bitcast_fusion.1), channel_id=1, source_target_pairs={{0,4},{1,5},{2,6},{3,7},{4,0},{5,1},{6,2},{7,3},{8,12},{9,13},{10,... | collective-permute-start | bytes 442376 | tf_op jit(solution)/shard_map/ppermute | solution.py:370
  56.6 1.4 %collective-permute-start.12 = (bf16[4,144,128]{2,1,0:T(8,128)(2,1)S(1)}, bf16[4,144,128]{2,1,0:T(8,128)(2,1)S(1)}, u32[]{:S(2)}, u32[]{:S(2)}) collective-permute-start(bf16[4,144,128]{2,1,0:T(8,128)(2,1)S(1)} %dynamic-slice_bitcast_fusion), channel_id=1, source_target_pairs={{0,1},{1,0},{2,3},{3,2},{4,5},{5,4},{6,7},{7,6},{8,9},{9,8},{10,11... | collective-permute-start | bytes 442376 | tf_op jit(solution)/shard_map/ppermute | solution.py:370
  58.1 1.4 %collective-permute-start.7 = (bf16[2,144,128]{2,1,0:T(8,128)(2,1)S(1)}, bf16[2,144,128]{2,1,0:T(8,128)(2,1)S(1)}, u32[]{:S(2)}, u32[]{:S(2)}) collective-permute-start(bf16[2,144,128]{2,1,0:T(8,128)(2,1)S(1)} %dynamic-slice_bitcast_fusion.5), channel_id=1, source_target_pairs={{0,4},{1,5},{2,6},{3,7},{4,0},{5,1},{6,2},{7,3},{8,12},{9,13},{10,... | collective-permute-start | bytes 221192 | tf_op jit(solution)/shard_map/ppermute | solution.py:370
  59.5 0.9 %collective-permute-done.9 = bf16[4,144,128]{2,1,0:T(8,128)(2,1)S(1)} collective-permute-done((bf16[4,144,128]{2,1,0:T(8,128)(2,1)S(1)}, bf16[4,144,128]{2,1,0:T(8,128)(2,1)S(1)}, u32[]{:S(2)}, u32[]{:S(2)}) %collective-permute-start.9) | collective-permute-done | bytes 147488 | tf_op jit(solution)/shard_map/ppermute | solution.py:370
  60.5 1.3 %collective-permute-start.10 = (bf16[2,144,128]{2,1,0:T(8,128)(2,1)S(1)}, bf16[2,144,128]{2,1,0:T(8,128)(2,1)S(1)}, u32[]{:S(2)}, u32[]{:S(2)}) collective-permute-start(bf16[2,144,128]{2,1,0:T(8,128)(2,1)S(1)} %dynamic-slice_bitcast_fusion.4), channel_id=1, source_target_pairs={{0,1},{1,0},{2,3},{3,2},{4,5},{5,4},{6,7},{7,6},{8,9},{9,8},{10,11... | collective-permute-start | bytes 221192 | tf_op jit(solution)/shard_map/ppermute | solution.py:370
  62.6 1.0 %collective-permute-start.13 = (bf16[2,144,128]{2,1,0:T(8,128)(2,1)S(1)}, bf16[2,144,128]{2,1,0:T(8,128)(2,1)S(1)}, u32[]{:S(2)}, u32[]{:S(2)}) collective-permute-start(bf16[2,144,128]{2,1,0:T(8,128)(2,1)S(1)} %dynamic-slice_bitcast_fusion.3), channel_id=1, source_target_pairs={{0,2},{1,3},{2,0},{3,1},{4,6},{5,7},{6,4},{7,5},{8,10},{9,11},{10,... | collective-permute-start | bytes 221192 | tf_op jit(solution)/shard_map/ppermute | solution.py:370
  63.7 1.3 %collective-permute-done.10 = bf16[2,144,128]{2,1,0:T(8,128)(2,1)S(1)} collective-permute-done((bf16[2,144,128]{2,1,0:T(8,128)(2,1)S(1)}, bf16[2,144,128]{2,1,0:T(8,128)(2,1)S(1)}, u32[]{:S(2)}, u32[]{:S(2)}) %collective-permute-start.10) | collective-permute-done | bytes 73760 | tf_op jit(solution)/shard_map/ppermute | solution.py:370
  65.0 2.1 %collective-permute-done.13 = bf16[2,144,128]{2,1,0:T(8,128)(2,1)S(1)} collective-permute-done((bf16[2,144,128]{2,1,0:T(8,128)(2,1)S(1)}, bf16[2,144,128]{2,1,0:T(8,128)(2,1)S(1)}, u32[]{:S(2)}, u32[]{:S(2)}) %collective-permute-start.13) | collective-permute-done | bytes 73760 | tf_op jit(solution)/shard_map/ppermute | solution.py:370
  67.1 2.6 %collective-permute-start.14 = (bf16[432,128]{1,0:T(8,128)(2,1)S(1)}, bf16[432,128]{1,0:T(8,128)(2,1)S(1)}, u32[]{:S(2)}, u32[]{:S(2)}) collective-permute-start(bf16[432,128]{1,0:T(8,128)(2,1)S(1)} %pad_maximum_fusion), channel_id=1, source_target_pairs={{0,8},{1,9},{2,10},{3,11},{4,12},{5,13},{6,14},{7,15},{8,0},{9,1},... | collective-permute-start | bytes 331784 | tf_op jit(solution)/shard_map/ppermute | solution.py:370
  69.8 4.2 %collective-permute-done.14 = bf16[432,128]{1,0:T(8,128)(2,1)S(1)} collective-permute-done((bf16[432,128]{1,0:T(8,128)(2,1)S(1)}, bf16[432,128]{1,0:T(8,128)(2,1)S(1)}, u32[]{:S(2)}, u32[]{:S(2)}) %collective-permute-start.14) | collective-permute-done | bytes 110624 | tf_op jit(solution)/shard_map/ppermute | solution.py:370
  (49 shorter events, 3.6 us)
Async XLA Ops:
  2.3 11.9 %collective-permute-start = (bf16[576,128]{1,0:T(8,128)(2,1)}, bf16[576,128]{1,0:T(8,128)(2,1)S(1)}, u32[]{:S(2)}, u32[]{:S(2)}) collective-permute-start(bf16[576,128]{1,0:T(8,128)(2,1)} %get-tuple-element.34), channel_id=1, source_target_pairs={{0,1},{1,2},{2,3},{3,4},{4,5},{5,6},{6,7},{7,8},{8,9},{9,10},{10,1... | collective-permute-start | bytes 442376 | tf_op jit(solution)/shard_map/ppermute | solution.py:408
  7.2 8.4 %collective-permute-start.1 = (bf16[576,128]{1,0:T(8,128)(2,1)}, bf16[576,128]{1,0:T(8,128)(2,1)S(1)}, u32[]{:S(2)}, u32[]{:S(2)}) collective-permute-start(bf16[576,128]{1,0:T(8,128)(2,1)} %get-tuple-element.35), channel_id=1, source_target_pairs={{1,0},{2,1},{3,2},{4,3},{5,4},{6,5},{7,6},{8,7},{9,8},{10,9},{11,1... | collective-permute-start | bytes 442376 | tf_op jit(solution)/shard_map/ppermute | solution.py:409
  8.6 1.2 %copy-start.1 = (bf16[1,27,128,128]{3,2,1,0:T(8,128)(2,1)S(1)}, bf16[1,27,128,128]{3,2,1,0:T(8,128)(2,1)}, u32[]{:S(2)}) copy-start(bf16[1,27,128,128]{3,2,1,0:T(8,128)(2,1)} %param.12) | copy-start | bytes 2654212
  9.7 1.2 %copy-start.3 = (bf16[1,27,128,128]{3,2,1,0:T(8,128)(2,1)S(1)}, bf16[1,27,128,128]{3,2,1,0:T(8,128)(2,1)}, u32[]{:S(2)}) copy-start(bf16[1,27,128,128]{3,2,1,0:T(8,128)(2,1)} %param.13) | copy-start | bytes 2654212
  10.9 0.9 %copy-start.5 = (bf16[1,4,8,8,256]{4,3,2,1,0:T(8,128)(2,1)S(1)}, bf16[1,4,8,8,256]{4,3,2,1,0:T(8,128)(2,1)}, u32[]{:S(2)}) copy-start(bf16[1,4,8,8,256]{4,3,2,1,0:T(8,128)(2,1)} %param.9) | copy-start | bytes 393220
  11.8 0.9 %copy-start.7 = (bf16[1,4,8,8,256]{4,3,2,1,0:T(8,128)(2,1)S(1)}, bf16[1,4,8,8,256]{4,3,2,1,0:T(8,128)(2,1)}, u32[]{:S(2)}) copy-start(bf16[1,4,8,8,256]{4,3,2,1,0:T(8,128)(2,1)} %param.7) | copy-start | bytes 393220
  12.7 0.9 %copy-start.8 = (bf16[1,4,8,8,256]{4,3,2,1,0:T(8,128)(2,1)S(1)}, bf16[1,4,8,8,256]{4,3,2,1,0:T(8,128)(2,1)}, u32[]{:S(2)}) copy-start(bf16[1,4,8,8,256]{4,3,2,1,0:T(8,128)(2,1)} %param.8) | copy-start | bytes 393220
  14.1 8.0 %copy-start.9 = (bf16[4,8,8,256]{3,2,1,0:T(8,128)(2,1)S(1)}, bf16[4,8,8,256]{3,2,1,0:T(8,128)(2,1)}, u32[]{:S(2)}) copy-start(bf16[4,8,8,256]{3,2,1,0:T(8,128)(2,1)} %param.10) | copy-start | bytes 393220
  14.1 7.9 %copy-start.10 = (bf16[4,8,8,256]{3,2,1,0:T(8,128)(2,1)S(1)}, bf16[4,8,8,256]{3,2,1,0:T(8,128)(2,1)}, u32[]{:S(2)}) copy-start(bf16[4,8,8,256]{3,2,1,0:T(8,128)(2,1)} %param.11) | copy-start | bytes 393220
  15.6 12.1 %copy-start.6 = (bf16[1,4,8,8,256]{4,3,2,1,0:T(8,128)(2,1)S(1)}, bf16[1,4,8,8,256]{4,3,2,1,0:T(8,128)(2,1)}, u32[]{:S(2)}) copy-start(bf16[1,4,8,8,256]{4,3,2,1,0:T(8,128)(2,1)} %param.9) | copy-start | bytes 393220
  20.4 14.9 %copy-start.2 = (bf16[1,27,128,128]{3,2,1,0:T(8,128)(2,1)S(1)}, bf16[1,27,128,128]{3,2,1,0:T(8,128)(2,1)}, u32[]{:S(2)}) copy-start(bf16[1,27,128,128]{3,2,1,0:T(8,128)(2,1)} %param.12) | copy-start | bytes 2654212
  20.5 14.9 %copy-start.4 = (bf16[1,27,128,128]{3,2,1,0:T(8,128)(2,1)S(1)}, bf16[1,27,128,128]{3,2,1,0:T(8,128)(2,1)}, u32[]{:S(2)}) copy-start(bf16[1,27,128,128]{3,2,1,0:T(8,128)(2,1)} %param.13) | copy-start | bytes 2654212
  20.5 1.6 %collective-permute-start.2 = (bf16[2,256,256]{2,1,0:T(8,128)(2,1)S(1)}, bf16[2,256,256]{2,1,0:T(8,128)(2,1)S(1)}, u32[]{:S(2)}, u32[]{:S(2)}) collective-permute-start(bf16[2,256,256]{2,1,0:T(8,128)(2,1)S(1)} %get-tuple-element.39), channel_id=1, source_target_pairs={{0,16},{16,0},{1,17},{17,1},{2,18},{18,2},{3,19},{19,3},{4,20},{20... | collective-permute-start | bytes 786440 | tf_op jit(solution)/shard_map/ppermute | solution.py:461
  22.7 7.5 %collective-permute-start.3 = (bf16[576,128]{1,0:T(8,128)(2,1)S(1)}, bf16[576,128]{1,0:T(8,128)(2,1)S(1)}, u32[]{:S(2)}, u32[]{:S(2)}) collective-permute-start(bf16[576,128]{1,0:T(8,128)(2,1)S(1)} %get-tuple-element.43), channel_id=1, source_target_pairs={{0,1},{1,2},{2,3},{3,4},{4,5},{5,6},{6,7},{7,8},{8,9},{9,10},{10,1... | collective-permute-start | bytes 442376 | tf_op jit(solution)/shard_map/ppermute | solution.py:408
  26.2 9.2 %collective-permute-start.4 = (bf16[576,128]{1,0:T(8,128)(2,1)S(1)}, bf16[576,128]{1,0:T(8,128)(2,1)S(1)}, u32[]{:S(2)}, u32[]{:S(2)}) collective-permute-start(bf16[576,128]{1,0:T(8,128)(2,1)S(1)} %get-tuple-element.44), channel_id=1, source_target_pairs={{1,0},{2,1},{3,2},{4,3},{5,4},{6,5},{7,6},{8,7},{9,8},{10,9},{11,1... | collective-permute-start | bytes 442376 | tf_op jit(solution)/shard_map/ppermute | solution.py:409
  28.5 1.8 %copy-start = (f32[2,3456,128]{2,1,0:T(8,128)}, f32[2,3456,128]{2,1,0:T(8,128)S(1)}, u32[]{:S(2)}) copy-start(f32[2,3456,128]{2,1,0:T(8,128)S(1)} %weight_grads.1.so_far) | copy-start | bytes 10616836
  43.2 8.3 %collective-permute-start.5 = (bf16[8,144,128]{2,1,0:T(8,128)(2,1)S(1)}, bf16[8,144,128]{2,1,0:T(8,128)(2,1)S(1)}, u32[]{:S(2)}, u32[]{:S(2)}) collective-permute-start(bf16[8,144,128]{2,1,0:T(8,128)(2,1)S(1)} %get-tuple-element.52), channel_id=1, source_target_pairs={{0,1},{1,0},{2,3},{3,2},{4,5},{5,4},{6,7},{7,6},{8,9},{9,8},{10,11... | collective-permute-start | bytes 884744 | tf_op jit(solution)/shard_map/ppermute | solution.py:370
  44.8 9.5 %collective-permute-start.8 = (bf16[8,144,128]{2,1,0:T(8,128)(2,1)S(1)}, bf16[8,144,128]{2,1,0:T(8,128)(2,1)S(1)}, u32[]{:S(2)}, u32[]{:S(2)}) collective-permute-start(bf16[8,144,128]{2,1,0:T(8,128)(2,1)S(1)} %get-tuple-element.54), channel_id=1, source_target_pairs={{0,2},{1,3},{2,0},{3,1},{4,6},{5,7},{6,4},{7,5},{8,10},{9,11},{10,... | collective-permute-start | bytes 884744 | tf_op jit(solution)/shard_map/ppermute | solution.py:370
  48.0 8.5 %collective-permute-start.11 = (bf16[8,144,128]{2,1,0:T(8,128)(2,1)S(1)}, bf16[8,144,128]{2,1,0:T(8,128)(2,1)S(1)}, u32[]{:S(2)}, u32[]{:S(2)}) collective-permute-start(bf16[8,144,128]{2,1,0:T(8,128)(2,1)S(1)} %get-tuple-element.56), channel_id=1, source_target_pairs={{0,4},{1,5},{2,6},{3,7},{4,0},{5,1},{6,2},{7,3},{8,12},{9,13},{10,... | collective-permute-start | bytes 884744 | tf_op jit(solution)/shard_map/ppermute | solution.py:370
  51.6 6.4 %collective-permute-start.6 = (bf16[4,144,128]{2,1,0:T(8,128)(2,1)S(1)}, bf16[4,144,128]{2,1,0:T(8,128)(2,1)S(1)}, u32[]{:S(2)}, u32[]{:S(2)}) collective-permute-start(bf16[4,144,128]{2,1,0:T(8,128)(2,1)S(1)} %dynamic-slice_bitcast_fusion.2), channel_id=1, source_target_pairs={{0,2},{1,3},{2,0},{3,1},{4,6},{5,7},{6,4},{7,5},{8,10},{9,11},{10,... | collective-permute-start | bytes 442376 | tf_op jit(solution)/shard_map/ppermute | solution.py:370
  54.4 6.0 %collective-permute-start.9 = (bf16[4,144,128]{2,1,0:T(8,128)(2,1)S(1)}, bf16[4,144,128]{2,1,0:T(8,128)(2,1)S(1)}, u32[]{:S(2)}, u32[]{:S(2)}) collective-permute-start(bf16[4,144,128]{2,1,0:T(8,128)(2,1)S(1)} %dynamic-slice_bitcast_fusion.1), channel_id=1, source_target_pairs={{0,4},{1,5},{2,6},{3,7},{4,0},{5,1},{6,2},{7,3},{8,12},{9,13},{10,... | collective-permute-start | bytes 442376 | tf_op jit(solution)/shard_map/ppermute | solution.py:370
  56.6 6.0 %collective-permute-start.12 = (bf16[4,144,128]{2,1,0:T(8,128)(2,1)S(1)}, bf16[4,144,128]{2,1,0:T(8,128)(2,1)S(1)}, u32[]{:S(2)}, u32[]{:S(2)}) collective-permute-start(bf16[4,144,128]{2,1,0:T(8,128)(2,1)S(1)} %dynamic-slice_bitcast_fusion), channel_id=1, source_target_pairs={{0,1},{1,0},{2,3},{3,2},{4,5},{5,4},{6,7},{7,6},{8,9},{9,8},{10,11... | collective-permute-start | bytes 442376 | tf_op jit(solution)/shard_map/ppermute | solution.py:370
  58.1 5.5 %collective-permute-start.7 = (bf16[2,144,128]{2,1,0:T(8,128)(2,1)S(1)}, bf16[2,144,128]{2,1,0:T(8,128)(2,1)S(1)}, u32[]{:S(2)}, u32[]{:S(2)}) collective-permute-start(bf16[2,144,128]{2,1,0:T(8,128)(2,1)S(1)} %dynamic-slice_bitcast_fusion.5), channel_id=1, source_target_pairs={{0,4},{1,5},{2,6},{3,7},{4,0},{5,1},{6,2},{7,3},{8,12},{9,13},{10,... | collective-permute-start | bytes 221192 | tf_op jit(solution)/shard_map/ppermute | solution.py:370
  60.5 4.4 %collective-permute-start.10 = (bf16[2,144,128]{2,1,0:T(8,128)(2,1)S(1)}, bf16[2,144,128]{2,1,0:T(8,128)(2,1)S(1)}, u32[]{:S(2)}, u32[]{:S(2)}) collective-permute-start(bf16[2,144,128]{2,1,0:T(8,128)(2,1)S(1)} %dynamic-slice_bitcast_fusion.4), channel_id=1, source_target_pairs={{0,1},{1,0},{2,3},{3,2},{4,5},{5,4},{6,7},{7,6},{8,9},{9,8},{10,11... | collective-permute-start | bytes 221192 | tf_op jit(solution)/shard_map/ppermute | solution.py:370
  62.6 4.4 %collective-permute-start.13 = (bf16[2,144,128]{2,1,0:T(8,128)(2,1)S(1)}, bf16[2,144,128]{2,1,0:T(8,128)(2,1)S(1)}, u32[]{:S(2)}, u32[]{:S(2)}) collective-permute-start(bf16[2,144,128]{2,1,0:T(8,128)(2,1)S(1)} %dynamic-slice_bitcast_fusion.3), channel_id=1, source_target_pairs={{0,2},{1,3},{2,0},{3,1},{4,6},{5,7},{6,4},{7,5},{8,10},{9,11},{10,... | collective-permute-start | bytes 221192 | tf_op jit(solution)/shard_map/ppermute | solution.py:370
  67.1 6.9 %collective-permute-start.14 = (bf16[432,128]{1,0:T(8,128)(2,1)S(1)}, bf16[432,128]{1,0:T(8,128)(2,1)S(1)}, u32[]{:S(2)}, u32[]{:S(2)}) collective-permute-start(bf16[432,128]{1,0:T(8,128)(2,1)S(1)} %pad_maximum_fusion), channel_id=1, source_target_pairs={{0,8},{1,9},{2,10},{3,11},{4,12},{5,13},{6,14},{7,15},{8,0},{9,1},... | collective-permute-start | bytes 331784 | tf_op jit(solution)/shard_map/ppermute | solution.py:370

commit v7 on v6

--- a/solution.py
+++ b/solution.py
@@ -74,21 +74,24 @@
     return total
 
 
-def pack_edges(state, act, grad, low, high, plane):
+def pack_edges(odd, state, act, grad, near, far, plane):
     width = state.shape[1] // 2
     cells = state.shape[0]
     left, right = slice(0, width), slice(width, 2 * width)
+
+    def put(at, size, source, half):
+        low = source[0:size, half]
+        high = source[cells - size : cells, half]
+        near[at : at + size, :] = jnp.where(odd, low, high)
+        far[at : at + size, :] = jnp.where(odd, high, low)
+
     for index, (source, half) in enumerate(((state, right), (act, left), (grad, right))):
-        at = index * 2 * plane
-        low[at : at + 2 * plane, :] = source[0 : 2 * plane, half]
-        high[at : at + 2 * plane, :] = source[cells - 2 * plane : cells, half]
+        put(index * 2 * plane, 2 * plane, source, half)
     for index, (source, half) in enumerate(((state, left), (act, right), (grad, left))):
-        at = (6 + index) * plane
-        low[at : at + plane, :] = source[0:plane, half]
-        high[at : at + plane, :] = source[cells - plane : cells, half]
-
-
-def edges_kernel(plane, state, act, grad, low_out, high_out, low, high, sems):
+        put((6 + index) * plane, plane, source, half)
+
+
+def edges_kernel(plane, state, act, grad, near_out, far_out, near, far, sems):
     width = state.shape[1] // 2
     cells = state.shape[0]
     left, right = pl.ds(0, width), pl.ds(width, width)
@@ -98,24 +101,26 @@
     for index, (source, half) in enumerate(((state, left), (act, right), (grad, left))):
         moves.append((source, half, plane, (6 + index) * plane))
     copies = Copies(sems)
-    for side, (out, result) in enumerate(((high, high_out), (low, low_out))):
+    odd = lax.rem(lax.axis_index("space"), 2)
+    for side, (out, high) in enumerate(((near, 1 - odd), (far, odd))):
         for index, (source, half, size, at) in enumerate(moves):
-            start = 0 if side else cells - size
+            start = pl.multiple_of(high * (cells - size), plane)
             copies.start((side, index), source.at[pl.ds(start, size), half], out.at[pl.ds(at, size), :])
-    for side, (out, result) in enumerate(((high, high_out), (low, low_out))):
+    for side, (out, result) in enumerate(((near, near_out), (far, far_out))):
         copies.need(*[(side, index) for index in range(len(moves))])
         copies.start(side, out, result)
     copies.finish()
 
 
-def join_kernel(plane, places, forward, lifted, lowered, fresh, target, state, act, grad, low, high):
-    first_place, last_place = places[0] == 0, places[0] == places[1]
+def join_kernel(plane, forward, lifted, lowered, fresh, target, state, act, grad, near, far):
+    place = lax.axis_index("section")
+    first_place, last_place = place == 0, place == lax.axis_size("section") - 1
     state[...] = jnp.where(first_place, fresh[...], lifted[0])
     own = forward[...]
     act[...] = jnp.where(last_place, own, lowered[0])
     error = (own.astype(F32) - target[...].astype(F32)).astype(BF16)
     grad[...] = jnp.where(last_place, error, lowered[1])
-    pack_edges(state, act, grad, low, high, plane)
+    pack_edges(lax.rem(lax.axis_index("space"), 2) == 1, state, act, grad, near, far, plane)
 
 
 def flip_kernel(first, second, state_in, act_in, grad_in, first_back, second_back, state, act, grad):
@@ -128,7 +133,7 @@
             out[offsets - 1 - k] = jnp.transpose(source[k])
 
 
-def first_kernel(ydim, zdim, copies, made, flags, state, act, grad, below, above, first, second, second_back,
+def first_kernel(ydim, zdim, copies, made, state, act, grad, near, far, first, second, second_back,
                  new_one, back_two, mid, back, carry, gate, stack):
     plane = ydim * zdim
     cells, double = state.shape
@@ -137,27 +142,31 @@
     outer = cells + 4 * plane
     left, right = slice(0, width), slice(width, double)
 
+    spot = lax.axis_index("space")
+    odd = lax.rem(spot, 2) == 1
+
+    def around(source, half, at, size):
+        one_side, other_side = near[at : at + size, :], far[at : at + size, :]
+        below = jnp.where(odd, one_side, other_side)
+        above = jnp.where(odd, other_side, one_side)
+        return jnp.concatenate([below, source[:, half], above], axis=0).astype(F32)
+
     def two(source, half, index):
-        at = index * 2 * plane
-        return jnp.concatenate(
-            [below[at : at + 2 * plane, :], source[:, half], above[at : at + 2 * plane, :]], axis=0
-        ).astype(F32)
+        return around(source, half, index * 2 * plane, 2 * plane)
 
     def one(source, half, index):
-        at = (6 + index) * plane
-        return jnp.concatenate(
-            [below[at : at + plane, :], source[:, half], above[at : at + plane, :]], axis=0
-        ).astype(F32)
-
-    low_flag, high_flag = flags[0], flags[1]
+        return around(source, half, (6 + index) * plane, plane)
+
+    inside_low, inside_high = spot > 0, spot < lax.axis_size("space") - 1
 
     def store_masked(ref, value):
-        ref[0:plane, :] = (value[0:plane].astype(F32) * low_flag).astype(BF16)
+        blank = jnp.zeros((plane, width), BF16)
+        ref[0:plane, :] = jnp.where(inside_low, value[0:plane], blank)
         ref[plane : plane + cells, :] = value[plane : plane + cells]
-        ref[plane + cells : inner, :] = (value[plane + cells :].astype(F32) * high_flag).astype(BF16)
+        ref[plane + cells : inner, :] = jnp.where(inside_high, value[plane + cells :], blank)
 
     core = slice(plane, plane + cells)
-    copies.need("below", "above", "state")
+    copies.need("near", "far", "state")
     fill_shifts(stack, smooth_gate(two(state, right, 0)), ydim, zdim)
     copies.need("first")
     f_one = (one(state, left, 0) + convolve(stack, first, inner, plane)).astype(BF16)
@@ -223,17 +232,17 @@
     made("forward")
 
 
-def tick_kernel(ydim, zdim, paired, places, flags, state, act, grad, below, above, first, second,
+def tick_kernel(ydim, zdim, paired, state, act, grad, near, far, first, second,
                 first_back, second_back, forward, sent, back, carry, gate, new_one, back_two, mid,
                 rebuilt, stack):
     copies = Copies(None)
     ignore = lambda *names: None
-    first_kernel(ydim, zdim, copies, ignore, flags, state, act, grad, below, above, first, second,
+    first_kernel(ydim, zdim, copies, ignore, state, act, grad, near, far, first, second,
                  second_back, new_one, back_two, mid, back, carry, gate, stack)
     second_kernel(ydim, zdim, copies, ignore, state, act, grad, new_one, back_two, mid, back, carry,
                   first, second, first_back, forward, rebuilt, sent.at[1], stack)
     if paired:
-        sent[0] = jnp.where(places[0] == 0, forward[...], rebuilt[...])
+        sent[0] = jnp.where(lax.axis_index("section") == 0, forward[...], rebuilt[...])
     else:
         sent[0] = rebuilt[...]
 
@@ -282,7 +291,7 @@
     return [(way * span, span, order) for way, order in enumerate(orders)]
 
 
-def last_kernel(ydim, zdim, factor, count, direct, spot, flags, state, act, grad, below, above, first,
+def last_kernel(ydim, zdim, factor, count, direct, state, act, grad, near, far, first,
                 second, first_back, second_back, so_far, *args):
     n_outs = 6 if direct else 1
     results_out, args = args[:3], args[3:]
@@ -293,7 +302,7 @@
     copies = Copies(sems)
     copies.start("so_far", so_far, sums)
     ignore = lambda *names: None
-    first_kernel(ydim, zdim, copies, ignore, flags, state, act, grad, below, above, first, second,
+    first_kernel(ydim, zdim, copies, ignore, state, act, grad, near, far, first, second,
                  second_back, new_one, back_two, mid, back, carry, gate, stack)
     copies.need("so_far")
 
@@ -306,7 +315,7 @@
         copies.start("out", refs[0], final_outs[0])
     rows = sums.shape[1] // count
     for index, (start, span, order) in enumerate(ways_of(count, rows) if direct else ()):
-        mine = (spot[0] // order[0]) % 2
+        mine = lax.rem(lax.div(lax.axis_index("space"), order[0]), 2)
         for kept in (0, 1):
             side = mine if kept else 1 - mine
             out = refs[2 * index + (0 if kept else 1)]
@@ -393,10 +402,8 @@
     last_section = lax.axis_size("section") - 1
     place = lax.axis_index("section")
     count = lax.axis_size("space")
-    spot = lax.axis_index("space")
-    flags = jnp.stack([spot > 0, spot < count - 1]).astype(F32)
-    up = [(i, i + 1) for i in range(count - 1)]
-    down = [(i + 1, i) for i in range(count - 1)]
+    beside = [(i, i ^ 1) for i in range(count) if i ^ 1 < count]
+    across = [pair for i in range(1, count - 1, 2) for pair in ((i, i + 1), (i + 1, i))]
     array = jax.ShapeDtypeStruct
     edge = array((9 * plane, width), BF16)
     tile = array((cells, width), BF16)
@@ -404,30 +411,28 @@
     state_shape = array((cells, 2 * width), BF16)
     offsets = 27 * width
 
-    def exchange(low, high):
-        below = lax.ppermute(high, "space", up)
-        above = lax.ppermute(low, "space", down)
-        return below, above
+    def exchange(near, far):
+        far = lax.ppermute(far, "space", across)
+        near = lax.ppermute(near, "space", beside)
+        return near, far
 
     state, act, grad = flat(fwd_in), flat(bwd_act), flat(bwd_grad)
-    smem = pl.BlockSpec(memory_space=pltpu.SMEM)
     hbm = pl.BlockSpec(memory_space=pltpu.HBM)
     outer_stack = array((cells + 4 * plane, 9 * width), BF16)
     small_stack = array((cells, 9 * width), BF16)
     weight = array((3, 9 * width, width), BF16)
     raw_weight = array((27, width, width), BF16)
     sums_shape = array((2, offsets, width), F32)
-    places = jnp.stack([place, jnp.full_like(place, last_section)]).astype(jnp.int32)
 
     vmem = pl.BlockSpec(memory_space=pltpu.VMEM)
 
-    def call(kernel, name, scalars, inputs, outs, scratch, grant, copies=0, places=(vmem, vmem), flops=0,
+    def call(kernel, name, inputs, outs, scratch, grant, copies=0, places=(vmem, vmem), flops=0,
              far=0):
         semaphores = [pltpu.SemaphoreType.DMA((copies,))] if copies else []
         return pl.pallas_call(
             kernel,
             out_shape=tuple(outs),
-            in_specs=[smem] * len(scalars) + [places[0]] * (len(inputs) - far) + [hbm] * far,
+            in_specs=[places[0]] * (len(inputs) - far) + [hbm] * far,
             out_specs=(places[1],) * len(outs),
             scratch_shapes=[pltpu.VMEM(like.shape, like.dtype) for like in scratch] + semaphores,
             compiler_params=pltpu.CompilerParams(vmem_limit_bytes=grant),
@@ -435,16 +440,16 @@
                 flops=flops, bytes_accessed=sum(x.size * 2 for x in inputs), transcendentals=0
             ),
             name=name,
-        )(*scalars, *inputs)
+        )(*inputs)
 
     work = 2 * 27 * cells * width * width
-    low, high = call(
-        functools.partial(edges_kernel, plane), "edges", (), (state, act, grad), (edge,) * 2,
+    near, far = call(
+        functools.partial(edges_kernel, plane), "edges", (state, act, grad), (edge,) * 2,
         (edge,) * 2, 65408 * 1024, 14, (hbm, hbm),
     )
-    below, above = exchange(low, high)
+    near, far = exchange(near, far)
     first_back, second_back, state, act, grad = call(
-        flip_kernel, "flip", (), (w_first[0], w_second[0], state, act, grad),
+        flip_kernel, "flip", (w_first[0], w_second[0], state, act, grad),
         (raw_weight,) * 2 + (state_shape,) * 3, (), 16 * 1024 * 1024,
     )
     first_back, second_back = first_back.reshape(weight.shape), second_back.reshape(weight.shape)
@@ -453,8 +458,8 @@
     pair_shape = array((2, cells, 2 * width), BF16)
     tick_outs = (state_shape, pair_shape, wide, wide, wide)
     forward, sent, back, carry, gate = call(
-        functools.partial(tick_kernel, ydim, zdim, paired), "tick_one", (places, flags),
-        (state, act, grad, below, above, first, second, first_back, second_back), tick_outs,
+        functools.partial(tick_kernel, ydim, zdim, paired), "tick_one",
+        (state, act, grad, near, far, first, second, first_back, second_back), tick_outs,
         (tile, tile, wide, state_shape, outer_stack), 16 * 1024 * 1024, flops=8 * work,
     )
     if paired:
@@ -464,14 +469,14 @@
         lowered = lax.ppermute(sent, "section", [(s + 1, s) for s in range(last_section)])
 
     join_outs = (state_shape,) * 3 + (edge, edge)
-    state_two, act_two, grad_two, low, high = call(
-        functools.partial(join_kernel, plane), "join", (places,),
+    state_two, act_two, grad_two, near, far = call(
+        functools.partial(join_kernel, plane), "join",
         (forward, lifted, lowered, flat(fresh), flat(target)), join_outs,
         (), 16 * 1024 * 1024,
     )
-    below, above = exchange(low, high)
+    near, far = exchange(near, far)
     (so_far,) = call(
-        functools.partial(corr_kernel, ydim, zdim), "weight_grads", (), (flat(bwd_grad), back, carry, gate),
+        functools.partial(corr_kernel, ydim, zdim), "weight_grads", (flat(bwd_grad), back, carry, gate),
         (sums_shape,), (small_stack,), 16 * 1024 * 1024, flops=2 * work,
     )
 
@@ -486,8 +491,7 @@
     results = (state_shape,) * 3
     made = call(
         functools.partial(last_kernel, ydim, zdim, factor, count, direct), "tick_two",
-        (spot.astype(jnp.int32).reshape(1), flags),
-        (state_two, act_two, grad_two, below, above, first, second, first_back, second_back, so_far),
+        (state_two, act_two, grad_two, near, far, first, second, first_back, second_back, so_far),
         results + outs,
         results + outs + (tile, tile, wide, wide, wide, wide, outer_stack, sums_shape),
         48 * 1024 * 1024, 10, (vmem, hbm), 9 * work, 1,

time: 75.2 us -> 67.8 us (0.902)
  waiting for transfers between devices: 19.1 us -> 13.9 us
  Pallas kernels: 16.4 us -> 14.7 us
    ppermute x4, waiting for transfers between devices: 6.45 us -> 0.71 us  [the longest x2 0.71 us: exchange(): near = lax.ppermute(near, 'space', beside)]
    ppermute x4, starting transfers between devices: 11 us -> 8.78 us  [the longest x2 7.29 us: exchange(): near = lax.ppermute(near, 'space', beside)]
    ppermute x10, starting transfers between devices: 18.9 us -> 20.8 us  [swapped(): lax.ppermute(send, 'space', [(i, i ^ bit) for i in range(count)])]
    pallas_call x6, Pallas kernels: 16.4 us -> 14.7 us  [call(): pl.pallas_call(kernel, out_shape=tuple(outs), in_specs=[places[0]] * (len...]
  transfers between devices with their start and end apart: 15 -> 15, of which waited for: 9 -> 8; matrix products, arithmetic and copies ran while one was open for 1% -> 1% of each run, Pallas kernels for 2% -> 2%
where the time goes in v7:
time: 67.8 us; the launch traced here: 67.4 us
  starting transfers between devices  29.7 us (44%)
  Pallas kernels  14.7 us (22%)
  waiting for transfers between devices  13.9 us (21%)
  local copies, waits for them, and re-layouts  7.67 us (11%)
  between operations  0.9 us (1%)
    ppermute x10, starting transfers between devices, swapped(): lax.ppermute(send, 'space', [(i, i ^ bit) for i in range(count)])  20.8 us
    pallas_call x6, Pallas kernels, call(): pl.pallas_call(kernel, out_shape=tuple(outs), in_specs=[places[0]] * (len...  14.7 us
    ppermute x10, waiting for transfers between devices, swapped(): lax.ppermute(send, 'space', [(i, i ^ bit) for i in range(count)])  11.7 us
    ppermute x2, starting transfers between devices, exchange(): near = lax.ppermute(near, 'space', beside)  7.29 us
    unnamed x22, local copies, waits for them, and re-layouts  6.82 us
    ppermute x1, waiting for transfers between devices, shards(): lifted = lowered = lax.ppermute(sent, 'section', [(0, 1), (1, 0)])  1.52 us
    ppermute x2, starting transfers between devices, exchange(): far = lax.ppermute(far, 'space', across)  1.5 us
  transfers between devices with their start and end apart: 15, of which 8 were waited for; matrix products, arithmetic and copies ran while one was open for 1% of the time, Pallas kernels for 2%

profile of v7, /device:TPU:0, one launch (start us, length us, event | category | flops | bytes accessed | tf_op | source)
XLA Modules:
  0.0 67.4 jit_solution(17502010970654378641)
XLA Ops:
  0.6 1.7 %edges.1 = (bf16[576,128]{1,0:T(8,128)(2,1)}, bf16[576,128]{1,0:T(8,128)(2,1)}) custom-call(bf16[256,256]{1,0:T(8,128)(2,1)} %bitcast.79, bf16[256,256]{1,0:T(8,128)(2,1)} %bitcast.81, bf16[256,256]{1,0:T(8,128)(2,1)} %bitcast.72), custom_call_target="tpu_custom_call" | custom-call | bytes 393216 | tf_op jit(solution)/shard_map/edges/pallas_call | solution.py:432
  2.3 3.0 %collective-permute-start = (bf16[576,128]{1,0:T(8,128)(2,1)}, bf16[576,128]{1,0:T(8,128)(2,1)S(1)}, u32[]{:S(2)}, u32[]{:S(2)}) collective-permute-start(bf16[576,128]{1,0:T(8,128)(2,1)} %get-tuple-element.34), channel_id=1, source_target_pairs={{0,1},{1,0},{2,3},{3,2},{4,5},{5,4},{6,7},{7,6},{8,9},{9,8},{10,11... | collective-permute-start | bytes 442376 | tf_op jit(solution)/shard_map/ppermute | solution.py:416
  5.3 0.7 collective-permute-start.1
  6.0 1.2 %copy-done.1 = bf16[1,27,128,128]{3,2,1,0:T(8,128)(2,1)S(1)} copy-done((bf16[1,27,128,128]{3,2,1,0:T(8,128)(2,1)S(1)}, bf16[1,27,128,128]{3,2,1,0:T(8,128)(2,1)}, u32[]{:S(2)}) %copy-start.1) | copy-done | bytes 884760
  7.2 1.2 %copy-done.3 = bf16[1,27,128,128]{3,2,1,0:T(8,128)(2,1)S(1)} copy-done((bf16[1,27,128,128]{3,2,1,0:T(8,128)(2,1)S(1)}, bf16[1,27,128,128]{3,2,1,0:T(8,128)(2,1)}, u32[]{:S(2)}) %copy-start.3) | copy-done | bytes 884760
  8.3 0.9 %copy-done.5 = bf16[1,4,8,8,256]{4,3,2,1,0:T(8,128)(2,1)S(1)} copy-done((bf16[1,4,8,8,256]{4,3,2,1,0:T(8,128)(2,1)S(1)}, bf16[1,4,8,8,256]{4,3,2,1,0:T(8,128)(2,1)}, u32[]{:S(2)}) %copy-start.5) | copy-done | bytes 131096
  9.2 0.9 %copy-done.7 = bf16[1,4,8,8,256]{4,3,2,1,0:T(8,128)(2,1)S(1)} copy-done((bf16[1,4,8,8,256]{4,3,2,1,0:T(8,128)(2,1)S(1)}, bf16[1,4,8,8,256]{4,3,2,1,0:T(8,128)(2,1)}, u32[]{:S(2)}) %copy-start.7) | copy-done | bytes 131096
  10.1 0.9 %copy-done.8 = bf16[1,4,8,8,256]{4,3,2,1,0:T(8,128)(2,1)S(1)} copy-done((bf16[1,4,8,8,256]{4,3,2,1,0:T(8,128)(2,1)S(1)}, bf16[1,4,8,8,256]{4,3,2,1,0:T(8,128)(2,1)}, u32[]{:S(2)}) %copy-start.8) | copy-done | bytes 131096
  11.0 0.5 flip.1
  11.6 4.4 %tick_one.1 = (bf16[256,256]{1,0:T(8,128)(2,1)S(1)}, bf16[2,256,256]{2,1,0:T(8,128)(2,1)S(1)}, bf16[384,128]{1,0:T(8,128)(2,1)S(1)}, bf16[384,128]{1,0:T(8,128)(2,1)S(1)}, bf16[384,128]{1,0:T(8,128)(2,1)S(1)}) custom-call(bf16[256,256]{1,0:T(8,128)(2,1)S(1)} %get-tuple-element.31.state, bf16[256,256]{1,0:T(8,128)(2,1)S(1)} %get-tuple-element.32.act, ...), custom_call_target="tpu_custom_call" | custom-call | flops 1811939328 | bytes 4227072 | tf_op jit(solution)/shard_map/tick_one/pallas_call | solution.py:432
  16.1 1.5 %collective-permute-done.2.lifted.lowered = bf16[2,256,256]{2,1,0:T(8,128)(2,1)S(1)} collective-permute-done((bf16[2,256,256]{2,1,0:T(8,128)(2,1)S(1)}, bf16[2,256,256]{2,1,0:T(8,128)(2,1)S(1)}, u32[]{:S(2)}, u32[]{:S(2)}) %collective-permute-start.2) | collective-permute-done | bytes 262176 | tf_op jit(solution)/shard_map/ppermute | solution.py:466
  17.8 4.3 %collective-permute-start.3 = (bf16[576,128]{1,0:T(8,128)(2,1)S(1)}, bf16[576,128]{1,0:T(8,128)(2,1)S(1)}, u32[]{:S(2)}, u32[]{:S(2)}) collective-permute-start(bf16[576,128]{1,0:T(8,128)(2,1)S(1)} %get-tuple-element.43), channel_id=1, source_target_pairs={{0,1},{1,0},{2,3},{3,2},{4,5},{5,4},{6,7},{7,6},{8,9},{9,8},{10,11... | collective-permute-start | bytes 442376 | tf_op jit(solution)/shard_map/ppermute | solution.py:416
  22.0 0.8 %collective-permute-start.4 = (bf16[576,128]{1,0:T(8,128)(2,1)S(1)}, bf16[576,128]{1,0:T(8,128)(2,1)S(1)}, u32[]{:S(2)}, u32[]{:S(2)}) collective-permute-start(bf16[576,128]{1,0:T(8,128)(2,1)S(1)} %get-tuple-element.44), channel_id=1, source_target_pairs={{1,2},{2,1},{3,4},{4,3},{5,6},{6,5},{7,8},{8,7},{9,10},{10,9},{11,... | collective-permute-start | bytes 442376 | tf_op jit(solution)/shard_map/ppermute | solution.py:415
  22.9 0.8 %weight_grads.1.so_far = f32[2,3456,128]{2,1,0:T(8,128)S(1)} custom-call(bf16[256,256]{1,0:T(8,128)(2,1)S(1)} %bitcast.74, bf16[384,128]{1,0:T(8,128)(2,1)S(1)} %get-tuple-element.45.back, bf16[384,128]{1,0:T(8,128)(2,1)S(1)} %get-tuple-element.46.carry, bf16[384,128]{1,0:T(8,128)(2,1)S(1)} %get-tuple-element.47.gate), custom_call_target="tpu_custom_call" | custom-call | flops 452984832 | bytes 425984 | tf_op jit(solution)/shard_map/weight_grads/pallas_call | solution.py:432
  23.7 1.7 %copy-done = f32[2,3456,128]{2,1,0:T(8,128)} copy-done((f32[2,3456,128]{2,1,0:T(8,128)}, f32[2,3456,128]{2,1,0:T(8,128)S(1)}, u32[]{:S(2)}) %copy-start) | copy-done | bytes 3538968
  25.5 0.7 %collective-permute-done.3.near = bf16[576,128]{1,0:T(8,128)(2,1)S(1)} collective-permute-done((bf16[576,128]{1,0:T(8,128)(2,1)S(1)}, bf16[576,128]{1,0:T(8,128)(2,1)S(1)}, u32[]{:S(2)}, u32[]{:S(2)}) %collective-permute-start.3) | collective-permute-done | bytes 147488 | tf_op jit(solution)/shard_map/ppermute | solution.py:416
  26.2 7.2 %tick_two.1 = (bf16[256,256]{1,0:T(8,128)(2,1)}, bf16[256,256]{1,0:T(8,128)(2,1)}, bf16[256,256]{1,0:T(8,128)(2,1)}, bf16[8,144,128]{2,1,0:T(8,128)(2,1)S(1)}, b...) custom-call(bf16[256,256]{1,0:T(8,128)(2,1)S(1)} %get-tuple-element., ...), custom_call_target="tpu_custom_call" | custom-call | flops 2038431744 | bytes 5996544 | tf_op jit(solution)/shard_map/tick_two/pallas_call | solution.py:432
  33.4 5.9 %collective-permute-start.5 = (bf16[8,144,128]{2,1,0:T(8,128)(2,1)S(1)}, bf16[8,144,128]{2,1,0:T(8,128)(2,1)S(1)}, u32[]{:S(2)}, u32[]{:S(2)}) collective-permute-start(bf16[8,144,128]{2,1,0:T(8,128)(2,1)S(1)} %get-tuple-element.52), channel_id=1, source_target_pairs={{0,1},{1,0},{2,3},{3,2},{4,5},{5,4},{6,7},{7,6},{8,9},{9,8},{10,11... | collective-permute-start | bytes 884744 | tf_op jit(solution)/shard_map/ppermute | solution.py:379
  39.3 1.1 %collective-permute-start.8 = (bf16[8,144,128]{2,1,0:T(8,128)(2,1)S(1)}, bf16[8,144,128]{2,1,0:T(8,128)(2,1)S(1)}, u32[]{:S(2)}, u32[]{:S(2)}) collective-permute-start(bf16[8,144,128]{2,1,0:T(8,128)(2,1)S(1)} %get-tuple-element.54), channel_id=1, source_target_pairs={{0,2},{1,3},{2,0},{3,1},{4,6},{5,7},{6,4},{7,5},{8,10},{9,11},{10,... | collective-permute-start | bytes 884744 | tf_op jit(solution)/shard_map/ppermute | solution.py:379
  40.4 1.6 %collective-permute-start.11 = (bf16[8,144,128]{2,1,0:T(8,128)(2,1)S(1)}, bf16[8,144,128]{2,1,0:T(8,128)(2,1)S(1)}, u32[]{:S(2)}, u32[]{:S(2)}) collective-permute-start(bf16[8,144,128]{2,1,0:T(8,128)(2,1)S(1)} %get-tuple-element.56), channel_id=1, source_target_pairs={{0,4},{1,5},{2,6},{3,7},{4,0},{5,1},{6,2},{7,3},{8,12},{9,13},{10,... | collective-permute-start | bytes 884744 | tf_op jit(solution)/shard_map/ppermute | solution.py:379
  42.0 3.8 %collective-permute-done.5 = bf16[8,144,128]{2,1,0:T(8,128)(2,1)S(1)} collective-permute-done((bf16[8,144,128]{2,1,0:T(8,128)(2,1)S(1)}, bf16[8,144,128]{2,1,0:T(8,128)(2,1)S(1)}, u32[]{:S(2)}, u32[]{:S(2)}) %collective-permute-start.5) | collective-permute-done | bytes 294944 | tf_op jit(solution)/shard_map/ppermute | solution.py:379
  45.9 1.4 %collective-permute-start.6 = (bf16[4,144,128]{2,1,0:T(8,128)(2,1)S(1)}, bf16[4,144,128]{2,1,0:T(8,128)(2,1)S(1)}, u32[]{:S(2)}, u32[]{:S(2)}) collective-permute-start(bf16[4,144,128]{2,1,0:T(8,128)(2,1)S(1)} %dynamic-slice_bitcast_fusion.2), channel_id=1, source_target_pairs={{0,2},{1,3},{2,0},{3,1},{4,6},{5,7},{6,4},{7,5},{8,10},{9,11},{10,... | collective-permute-start | bytes 442376 | tf_op jit(solution)/shard_map/ppermute | solution.py:379
  47.4 1.6 %collective-permute-start.9 = (bf16[4,144,128]{2,1,0:T(8,128)(2,1)S(1)}, bf16[4,144,128]{2,1,0:T(8,128)(2,1)S(1)}, u32[]{:S(2)}, u32[]{:S(2)}) collective-permute-start(bf16[4,144,128]{2,1,0:T(8,128)(2,1)S(1)} %dynamic-slice_bitcast_fusion.1), channel_id=1, source_target_pairs={{0,4},{1,5},{2,6},{3,7},{4,0},{5,1},{6,2},{7,3},{8,12},{9,13},{10,... | collective-permute-start | bytes 442376 | tf_op jit(solution)/shard_map/ppermute | solution.py:379
  49.2 1.6 %collective-permute-start.12 = (bf16[4,144,128]{2,1,0:T(8,128)(2,1)S(1)}, bf16[4,144,128]{2,1,0:T(8,128)(2,1)S(1)}, u32[]{:S(2)}, u32[]{:S(2)}) collective-permute-start(bf16[4,144,128]{2,1,0:T(8,128)(2,1)S(1)} %dynamic-slice_bitcast_fusion), channel_id=1, source_target_pairs={{0,1},{1,0},{2,3},{3,2},{4,5},{5,4},{6,7},{7,6},{8,9},{9,8},{10,11... | collective-permute-start | bytes 442376 | tf_op jit(solution)/shard_map/ppermute | solution.py:379
  51.2 2.3 %collective-permute-start.7 = (bf16[2,144,128]{2,1,0:T(8,128)(2,1)S(1)}, bf16[2,144,128]{2,1,0:T(8,128)(2,1)S(1)}, u32[]{:S(2)}, u32[]{:S(2)}) collective-permute-start(bf16[2,144,128]{2,1,0:T(8,128)(2,1)S(1)} %dynamic-slice_bitcast_fusion.5), channel_id=1, source_target_pairs={{0,4},{1,5},{2,6},{3,7},{4,0},{5,1},{6,2},{7,3},{8,12},{9,13},{10,... | collective-permute-start | bytes 221192 | tf_op jit(solution)/shard_map/ppermute | solution.py:379
  53.6 1.5 %collective-permute-start.10 = (bf16[2,144,128]{2,1,0:T(8,128)(2,1)S(1)}, bf16[2,144,128]{2,1,0:T(8,128)(2,1)S(1)}, u32[]{:S(2)}, u32[]{:S(2)}) collective-permute-start(bf16[2,144,128]{2,1,0:T(8,128)(2,1)S(1)} %dynamic-slice_bitcast_fusion.4), channel_id=1, source_target_pairs={{0,1},{1,0},{2,3},{3,2},{4,5},{5,4},{6,7},{7,6},{8,9},{9,8},{10,11... | collective-permute-start | bytes 221192 | tf_op jit(solution)/shard_map/ppermute | solution.py:379
  55.3 1.2 %collective-permute-start.13 = (bf16[2,144,128]{2,1,0:T(8,128)(2,1)S(1)}, bf16[2,144,128]{2,1,0:T(8,128)(2,1)S(1)}, u32[]{:S(2)}, u32[]{:S(2)}) collective-permute-start(bf16[2,144,128]{2,1,0:T(8,128)(2,1)S(1)} %dynamic-slice_bitcast_fusion.3), channel_id=1, source_target_pairs={{0,2},{1,3},{2,0},{3,1},{4,6},{5,7},{6,4},{7,5},{8,10},{9,11},{10,... | collective-permute-start | bytes 221192 | tf_op jit(solution)/shard_map/ppermute | solution.py:379
  56.5 1.5 %collective-permute-done.10 = bf16[2,144,128]{2,1,0:T(8,128)(2,1)S(1)} collective-permute-done((bf16[2,144,128]{2,1,0:T(8,128)(2,1)S(1)}, bf16[2,144,128]{2,1,0:T(8,128)(2,1)S(1)}, u32[]{:S(2)}, u32[]{:S(2)}) %collective-permute-start.10) | collective-permute-done | bytes 73760 | tf_op jit(solution)/shard_map/ppermute | solution.py:379
  58.1 1.6 %collective-permute-done.13 = bf16[2,144,128]{2,1,0:T(8,128)(2,1)S(1)} collective-permute-done((bf16[2,144,128]{2,1,0:T(8,128)(2,1)S(1)}, bf16[2,144,128]{2,1,0:T(8,128)(2,1)S(1)}, u32[]{:S(2)}, u32[]{:S(2)}) %collective-permute-start.13) | collective-permute-done | bytes 73760 | tf_op jit(solution)/shard_map/ppermute | solution.py:379
  59.8 2.6 %collective-permute-start.14 = (bf16[432,128]{1,0:T(8,128)(2,1)S(1)}, bf16[432,128]{1,0:T(8,128)(2,1)S(1)}, u32[]{:S(2)}, u32[]{:S(2)}) collective-permute-start(bf16[432,128]{1,0:T(8,128)(2,1)S(1)} %pad_maximum_fusion), channel_id=1, source_target_pairs={{0,8},{1,9},{2,10},{3,11},{4,12},{5,13},{6,14},{7,15},{8,0},{9,1},... | collective-permute-start | bytes 331784 | tf_op jit(solution)/shard_map/ppermute | solution.py:379
  62.3 4.3 %collective-permute-done.14 = bf16[432,128]{1,0:T(8,128)(2,1)S(1)} collective-permute-done((bf16[432,128]{1,0:T(8,128)(2,1)S(1)}, bf16[432,128]{1,0:T(8,128)(2,1)S(1)}, u32[]{:S(2)}, u32[]{:S(2)}) %collective-permute-start.14) | collective-permute-done | bytes 110624 | tf_op jit(solution)/shard_map/ppermute | solution.py:379
  66.7 0.7 %slice_bitcast_fusion = (f32[1,216,128]{2,1,0:T(8,128)}, f32[1,216,128]{2,1,0:T(8,128)}) fusion(f32[432,128]{1,0:T(8,128)S(1)} %convert_add_fusion.3), kind=kLoop, calls=%fused_computation.19 | loop fusion | bytes 442368 | tf_op jit(solution)/shard_map/broadcast_in_dim | solution.py:507
  (47 shorter events, 1.3 us)
Async XLA Ops:
  2.3 9.3 %collective-permute-start = (bf16[576,128]{1,0:T(8,128)(2,1)}, bf16[576,128]{1,0:T(8,128)(2,1)S(1)}, u32[]{:S(2)}, u32[]{:S(2)}) collective-permute-start(bf16[576,128]{1,0:T(8,128)(2,1)} %get-tuple-element.34), channel_id=1, source_target_pairs={{0,1},{1,0},{2,3},{3,2},{4,5},{5,4},{6,7},{7,6},{8,9},{9,8},{10,11... | collective-permute-start | bytes 442376 | tf_op jit(solution)/shard_map/ppermute | solution.py:416
  5.3 6.3 %collective-permute-start.1 = (bf16[576,128]{1,0:T(8,128)(2,1)}, bf16[576,128]{1,0:T(8,128)(2,1)S(1)}, u32[]{:S(2)}, u32[]{:S(2)}) collective-permute-start(bf16[576,128]{1,0:T(8,128)(2,1)} %get-tuple-element.35), channel_id=1, source_target_pairs={{1,2},{2,1},{3,4},{4,3},{5,6},{6,5},{7,8},{8,7},{9,10},{10,9},{11,... | collective-permute-start | bytes 442376 | tf_op jit(solution)/shard_map/ppermute | solution.py:415
  6.0 1.2 %copy-start.1 = (bf16[1,27,128,128]{3,2,1,0:T(8,128)(2,1)S(1)}, bf16[1,27,128,128]{3,2,1,0:T(8,128)(2,1)}, u32[]{:S(2)}) copy-start(bf16[1,27,128,128]{3,2,1,0:T(8,128)(2,1)} %param.12) | copy-start | bytes 2654212
  7.2 1.2 %copy-start.3 = (bf16[1,27,128,128]{3,2,1,0:T(8,128)(2,1)S(1)}, bf16[1,27,128,128]{3,2,1,0:T(8,128)(2,1)}, u32[]{:S(2)}) copy-start(bf16[1,27,128,128]{3,2,1,0:T(8,128)(2,1)} %param.13) | copy-start | bytes 2654212
  8.3 0.9 %copy-start.5 = (bf16[1,4,8,8,256]{4,3,2,1,0:T(8,128)(2,1)S(1)}, bf16[1,4,8,8,256]{4,3,2,1,0:T(8,128)(2,1)}, u32[]{:S(2)}) copy-start(bf16[1,4,8,8,256]{4,3,2,1,0:T(8,128)(2,1)} %param.9) | copy-start | bytes 393220
  9.2 0.9 %copy-start.7 = (bf16[1,4,8,8,256]{4,3,2,1,0:T(8,128)(2,1)S(1)}, bf16[1,4,8,8,256]{4,3,2,1,0:T(8,128)(2,1)}, u32[]{:S(2)}) copy-start(bf16[1,4,8,8,256]{4,3,2,1,0:T(8,128)(2,1)} %param.7) | copy-start | bytes 393220
  10.1 0.9 %copy-start.8 = (bf16[1,4,8,8,256]{4,3,2,1,0:T(8,128)(2,1)S(1)}, bf16[1,4,8,8,256]{4,3,2,1,0:T(8,128)(2,1)}, u32[]{:S(2)}) copy-start(bf16[1,4,8,8,256]{4,3,2,1,0:T(8,128)(2,1)} %param.8) | copy-start | bytes 393220
  11.6 6.1 %copy-start.9 = (bf16[4,8,8,256]{3,2,1,0:T(8,128)(2,1)S(1)}, bf16[4,8,8,256]{3,2,1,0:T(8,128)(2,1)}, u32[]{:S(2)}) copy-start(bf16[4,8,8,256]{3,2,1,0:T(8,128)(2,1)} %param.10) | copy-start | bytes 393220
  11.6 6.1 %copy-start.10 = (bf16[4,8,8,256]{3,2,1,0:T(8,128)(2,1)S(1)}, bf16[4,8,8,256]{3,2,1,0:T(8,128)(2,1)}, u32[]{:S(2)}) copy-start(bf16[4,8,8,256]{3,2,1,0:T(8,128)(2,1)} %param.11) | copy-start | bytes 393220
  11.6 11.3 %copy-start.6 = (bf16[1,4,8,8,256]{4,3,2,1,0:T(8,128)(2,1)S(1)}, bf16[1,4,8,8,256]{4,3,2,1,0:T(8,128)(2,1)}, u32[]{:S(2)}) copy-start(bf16[1,4,8,8,256]{4,3,2,1,0:T(8,128)(2,1)} %param.9) | copy-start | bytes 393220
  16.0 10.2 %copy-start.2 = (bf16[1,27,128,128]{3,2,1,0:T(8,128)(2,1)S(1)}, bf16[1,27,128,128]{3,2,1,0:T(8,128)(2,1)}, u32[]{:S(2)}) copy-start(bf16[1,27,128,128]{3,2,1,0:T(8,128)(2,1)} %param.12) | copy-start | bytes 2654212
  16.0 10.2 %copy-start.4 = (bf16[1,27,128,128]{3,2,1,0:T(8,128)(2,1)S(1)}, bf16[1,27,128,128]{3,2,1,0:T(8,128)(2,1)}, u32[]{:S(2)}) copy-start(bf16[1,27,128,128]{3,2,1,0:T(8,128)(2,1)} %param.13) | copy-start | bytes 2654212
  16.0 1.6 %collective-permute-start.2 = (bf16[2,256,256]{2,1,0:T(8,128)(2,1)S(1)}, bf16[2,256,256]{2,1,0:T(8,128)(2,1)S(1)}, u32[]{:S(2)}, u32[]{:S(2)}) collective-permute-start(bf16[2,256,256]{2,1,0:T(8,128)(2,1)S(1)} %get-tuple-element.39), channel_id=1, source_target_pairs={{0,16},{16,0},{1,17},{17,1},{2,18},{18,2},{3,19},{19,3},{4,20},{20... | collective-permute-start | bytes 786440 | tf_op jit(solution)/shard_map/ppermute | solution.py:466
  17.8 8.4 %collective-permute-start.3 = (bf16[576,128]{1,0:T(8,128)(2,1)S(1)}, bf16[576,128]{1,0:T(8,128)(2,1)S(1)}, u32[]{:S(2)}, u32[]{:S(2)}) collective-permute-start(bf16[576,128]{1,0:T(8,128)(2,1)S(1)} %get-tuple-element.43), channel_id=1, source_target_pairs={{0,1},{1,0},{2,3},{3,2},{4,5},{5,4},{6,7},{7,6},{8,9},{9,8},{10,11... | collective-permute-start | bytes 442376 | tf_op jit(solution)/shard_map/ppermute | solution.py:416
  22.0 4.2 %collective-permute-start.4 = (bf16[576,128]{1,0:T(8,128)(2,1)S(1)}, bf16[576,128]{1,0:T(8,128)(2,1)S(1)}, u32[]{:S(2)}, u32[]{:S(2)}) collective-permute-start(bf16[576,128]{1,0:T(8,128)(2,1)S(1)} %get-tuple-element.44), channel_id=1, source_target_pairs={{1,2},{2,1},{3,4},{4,3},{5,6},{6,5},{7,8},{8,7},{9,10},{10,9},{11,... | collective-permute-start | bytes 442376 | tf_op jit(solution)/shard_map/ppermute | solution.py:415
  23.7 1.8 %copy-start = (f32[2,3456,128]{2,1,0:T(8,128)}, f32[2,3456,128]{2,1,0:T(8,128)S(1)}, u32[]{:S(2)}) copy-start(f32[2,3456,128]{2,1,0:T(8,128)S(1)} %weight_grads.1.so_far) | copy-start | bytes 10616836
  33.4 12.4 %collective-permute-start.5 = (bf16[8,144,128]{2,1,0:T(8,128)(2,1)S(1)}, bf16[8,144,128]{2,1,0:T(8,128)(2,1)S(1)}, u32[]{:S(2)}, u32[]{:S(2)}) collective-permute-start(bf16[8,144,128]{2,1,0:T(8,128)(2,1)S(1)} %get-tuple-element.52), channel_id=1, source_target_pairs={{0,1},{1,0},{2,3},{3,2},{4,5},{5,4},{6,7},{7,6},{8,9},{9,8},{10,11... | collective-permute-start | bytes 884744 | tf_op jit(solution)/shard_map/ppermute | solution.py:379
  39.3 8.0 %collective-permute-start.8 = (bf16[8,144,128]{2,1,0:T(8,128)(2,1)S(1)}, bf16[8,144,128]{2,1,0:T(8,128)(2,1)S(1)}, u32[]{:S(2)}, u32[]{:S(2)}) collective-permute-start(bf16[8,144,128]{2,1,0:T(8,128)(2,1)S(1)} %get-tuple-element.54), channel_id=1, source_target_pairs={{0,2},{1,3},{2,0},{3,1},{4,6},{5,7},{6,4},{7,5},{8,10},{9,11},{10,... | collective-permute-start | bytes 884744 | tf_op jit(solution)/shard_map/ppermute | solution.py:379
  40.4 8.6 %collective-permute-start.11 = (bf16[8,144,128]{2,1,0:T(8,128)(2,1)S(1)}, bf16[8,144,128]{2,1,0:T(8,128)(2,1)S(1)}, u32[]{:S(2)}, u32[]{:S(2)}) collective-permute-start(bf16[8,144,128]{2,1,0:T(8,128)(2,1)S(1)} %get-tuple-element.56), channel_id=1, source_target_pairs={{0,4},{1,5},{2,6},{3,7},{4,0},{5,1},{6,2},{7,3},{8,12},{9,13},{10,... | collective-permute-start | bytes 884744 | tf_op jit(solution)/shard_map/ppermute | solution.py:379
  45.9 5.2 %collective-permute-start.6 = (bf16[4,144,128]{2,1,0:T(8,128)(2,1)S(1)}, bf16[4,144,128]{2,1,0:T(8,128)(2,1)S(1)}, u32[]{:S(2)}, u32[]{:S(2)}) collective-permute-start(bf16[4,144,128]{2,1,0:T(8,128)(2,1)S(1)} %dynamic-slice_bitcast_fusion.2), channel_id=1, source_target_pairs={{0,2},{1,3},{2,0},{3,1},{4,6},{5,7},{6,4},{7,5},{8,10},{9,11},{10,... | collective-permute-start | bytes 442376 | tf_op jit(solution)/shard_map/ppermute | solution.py:379
  47.4 6.1 %collective-permute-start.9 = (bf16[4,144,128]{2,1,0:T(8,128)(2,1)S(1)}, bf16[4,144,128]{2,1,0:T(8,128)(2,1)S(1)}, u32[]{:S(2)}, u32[]{:S(2)}) collective-permute-start(bf16[4,144,128]{2,1,0:T(8,128)(2,1)S(1)} %dynamic-slice_bitcast_fusion.1), channel_id=1, source_target_pairs={{0,4},{1,5},{2,6},{3,7},{4,0},{5,1},{6,2},{7,3},{8,12},{9,13},{10,... | collective-permute-start | bytes 442376 | tf_op jit(solution)/shard_map/ppermute | solution.py:379
  49.2 6.0 %collective-permute-start.12 = (bf16[4,144,128]{2,1,0:T(8,128)(2,1)S(1)}, bf16[4,144,128]{2,1,0:T(8,128)(2,1)S(1)}, u32[]{:S(2)}, u32[]{:S(2)}) collective-permute-start(bf16[4,144,128]{2,1,0:T(8,128)(2,1)S(1)} %dynamic-slice_bitcast_fusion), channel_id=1, source_target_pairs={{0,1},{1,0},{2,3},{3,2},{4,5},{5,4},{6,7},{7,6},{8,9},{9,8},{10,11... | collective-permute-start | bytes 442376 | tf_op jit(solution)/shard_map/ppermute | solution.py:379
  51.2 5.3 %collective-permute-start.7 = (bf16[2,144,128]{2,1,0:T(8,128)(2,1)S(1)}, bf16[2,144,128]{2,1,0:T(8,128)(2,1)S(1)}, u32[]{:S(2)}, u32[]{:S(2)}) collective-permute-start(bf16[2,144,128]{2,1,0:T(8,128)(2,1)S(1)} %dynamic-slice_bitcast_fusion.5), channel_id=1, source_target_pairs={{0,4},{1,5},{2,6},{3,7},{4,0},{5,1},{6,2},{7,3},{8,12},{9,13},{10,... | collective-permute-start | bytes 221192 | tf_op jit(solution)/shard_map/ppermute | solution.py:379
  53.6 4.4 %collective-permute-start.10 = (bf16[2,144,128]{2,1,0:T(8,128)(2,1)S(1)}, bf16[2,144,128]{2,1,0:T(8,128)(2,1)S(1)}, u32[]{:S(2)}, u32[]{:S(2)}) collective-permute-start(bf16[2,144,128]{2,1,0:T(8,128)(2,1)S(1)} %dynamic-slice_bitcast_fusion.4), channel_id=1, source_target_pairs={{0,1},{1,0},{2,3},{3,2},{4,5},{5,4},{6,7},{7,6},{8,9},{9,8},{10,11... | collective-permute-start | bytes 221192 | tf_op jit(solution)/shard_map/ppermute | solution.py:379
  55.3 4.4 %collective-permute-start.13 = (bf16[2,144,128]{2,1,0:T(8,128)(2,1)S(1)}, bf16[2,144,128]{2,1,0:T(8,128)(2,1)S(1)}, u32[]{:S(2)}, u32[]{:S(2)}) collective-permute-start(bf16[2,144,128]{2,1,0:T(8,128)(2,1)S(1)} %dynamic-slice_bitcast_fusion.3), channel_id=1, source_target_pairs={{0,2},{1,3},{2,0},{3,1},{4,6},{5,7},{6,4},{7,5},{8,10},{9,11},{10,... | collective-permute-start | bytes 221192 | tf_op jit(solution)/shard_map/ppermute | solution.py:379
  59.8 6.9 %collective-permute-start.14 = (bf16[432,128]{1,0:T(8,128)(2,1)S(1)}, bf16[432,128]{1,0:T(8,128)(2,1)S(1)}, u32[]{:S(2)}, u32[]{:S(2)}) collective-permute-start(bf16[432,128]{1,0:T(8,128)(2,1)S(1)} %pad_maximum_fusion), channel_id=1, source_target_pairs={{0,8},{1,9},{2,10},{3,11},{4,12},{5,13},{6,14},{7,15},{8,0},{9,1},... | collective-permute-start | bytes 331784 | tf_op jit(solution)/shard_map/ppermute | solution.py:379

commit v8 on v7

--- a/solution.py
+++ b/solution.py
@@ -123,6 +123,10 @@
     pack_edges(lax.rem(lax.axis_index("space"), 2) == 1, state, act, grad, near, far, plane)
 
 
+def own_kernel(ydim, zdim, state, act, grad, first, second, second_back, partial, stack):
+    own_sums(ydim, zdim, gated_fields(state, act, grad), (first, second, second_back), partial, stack)
+
+
 def flip_kernel(first, second, state_in, act_in, grad_in, first_back, second_back, state, act, grad):
     state[...] = state_in[...]
     act[...] = act_in[...]
@@ -133,7 +137,47 @@
             out[offsets - 1 - k] = jnp.transpose(source[k])
 
 
-def first_kernel(ydim, zdim, copies, made, state, act, grad, near, far, first, second, second_back,
+def own_sums(ydim, zdim, fields, weights, partial, stack):
+    plane = ydim * zdim
+    for index, (field, weight) in enumerate(zip(fields, weights)):
+        fill_shifts(stack, field, ydim, zdim)
+        cells = field.shape[0]
+        partial[index] = jnp.zeros(partial.shape[1:], F32)
+        for step in range(3):
+            at = (2 - step) * plane
+            partial[index, at : at + cells, :] += jnp.dot(
+                stack[0:cells, :], weight[step], preferred_element_type=F32
+            )
+
+
+def gated_fields(state, act, grad):
+    width = state.shape[1] // 2
+    return (
+        smooth_gate(state[:, width:].astype(F32)),
+        smooth_gate(act[:, :width].astype(F32)),
+        grad[:, width:].astype(F32),
+    )
+
+
+def halo_sums(index, partial, stack, weights, plane):
+    total = partial[index]
+    inner = total.shape[0]
+    low = jnp.dot(stack[0 : 2 * plane, :], weights[0], preferred_element_type=F32)
+    both = jnp.dot(stack[plane : 3 * plane, :], weights[1], preferred_element_type=F32)
+    high = jnp.dot(stack[2 * plane : 4 * plane, :], weights[2], preferred_element_type=F32)
+    return jnp.concatenate(
+        [
+            total[0:plane] + low[0:plane] + both[0:plane],
+            total[plane : 2 * plane] + low[plane:],
+            total[2 * plane : inner - 2 * plane],
+            total[inner - 2 * plane : inner - plane] + high[0:plane],
+            total[inner - plane :] + high[plane:] + both[plane:],
+        ],
+        axis=0,
+    )
+
+
+def first_kernel(ydim, zdim, copies, made, state, act, grad, near, far, first, second, second_back, partial,
                  new_one, back_two, mid, back, carry, gate, stack):
     plane = ydim * zdim
     cells, double = state.shape
@@ -154,6 +198,9 @@
     def two(source, half, index):
         return around(source, half, index * 2 * plane, 2 * plane)
 
+    def outside(field):
+        return jnp.concatenate([field[0 : 2 * plane], field[2 * plane + cells :]], axis=0)
+
     def one(source, half, index):
         return around(source, half, (6 + index) * plane, plane)
 
@@ -167,9 +214,9 @@
 
     core = slice(plane, plane + cells)
     copies.need("near", "far", "state")
-    fill_shifts(stack, smooth_gate(two(state, right, 0)), ydim, zdim)
+    fill_shifts(stack, smooth_gate(outside(two(state, right, 0))), ydim, zdim)
     copies.need("first")
-    f_one = (one(state, left, 0) + convolve(stack, first, inner, plane)).astype(BF16)
+    f_one = (one(state, left, 0) + halo_sums(0, partial, stack, first, plane)).astype(BF16)
     new_one[...] = f_one[core]
     store_masked(mid, smooth_gate(f_one.astype(F32)).astype(BF16))
 
@@ -180,19 +227,19 @@
     half = half_erf(y_one)
     gated = y_one * half
     gate[...] = gated[plane : plane + inner].astype(BF16)
-    fill_shifts(stack, gated, ydim, zdim)
+    fill_shifts(stack, outside(gated), ydim, zdim)
     copies.need("second")
-    r_two = (one(act, right, 1) - convolve(stack, second, inner, plane)).astype(BF16)
+    r_two = (one(act, right, 1) - halo_sums(1, partial, stack, second, plane)).astype(BF16)
     back_two[...] = r_two[core]
     store_masked(back, smooth_gate(r_two.astype(F32)).astype(BF16))
 
     made("gate", "back_two", "back")
 
     copies.need("grad")
-    fill_shifts(stack, two(grad, right, 2), ydim, zdim)
+    fill_shifts(stack, outside(two(grad, right, 2)), ydim, zdim)
     slope = gate_slope(y_one[plane : plane + inner], half[plane : plane + inner])
     copies.need("second_back")
-    e_one = (one(grad, left, 2) + slope * convolve(stack, second_back, inner, plane)).astype(BF16)
+    e_one = (one(grad, left, 2) + slope * halo_sums(2, partial, stack, second_back, plane)).astype(BF16)
     store_masked(carry, e_one)
     made("carry")
 
@@ -233,12 +280,12 @@
 
 
 def tick_kernel(ydim, zdim, paired, state, act, grad, near, far, first, second,
-                first_back, second_back, forward, sent, back, carry, gate, new_one, back_two, mid,
+                first_back, second_back, partial, forward, sent, back, carry, gate, new_one, back_two, mid,
                 rebuilt, stack):
     copies = Copies(None)
     ignore = lambda *names: None
     first_kernel(ydim, zdim, copies, ignore, state, act, grad, near, far, first, second,
-                 second_back, new_one, back_two, mid, back, carry, gate, stack)
+                 second_back, partial, new_one, back_two, mid, back, carry, gate, stack)
     second_kernel(ydim, zdim, copies, ignore, state, act, grad, new_one, back_two, mid, back, carry,
                   first, second, first_back, forward, rebuilt, sent.at[1], stack)
     if paired:
@@ -292,7 +339,7 @@
 
 
 def last_kernel(ydim, zdim, factor, count, direct, state, act, grad, near, far, first,
-                second, first_back, second_back, so_far, *args):
+                second, first_back, second_back, partial, so_far, *args):
     n_outs = 6 if direct else 1
     results_out, args = args[:3], args[3:]
     final_outs, args = args[:n_outs], args[n_outs:]
@@ -303,7 +350,7 @@
     copies.start("so_far", so_far, sums)
     ignore = lambda *names: None
     first_kernel(ydim, zdim, copies, ignore, state, act, grad, near, far, first, second,
-                 second_back, new_one, back_two, mid, back, carry, gate, stack)
+                 second_back, partial, new_one, back_two, mid, back, carry, gate, stack)
     copies.need("so_far")
 
     def put(which, at, block):
@@ -454,12 +501,23 @@
     )
     first_back, second_back = first_back.reshape(weight.shape), second_back.reshape(weight.shape)
 
+    partial_shape = array((3, cells + 2 * plane, width), F32)
+
+    def own(state, act, grad):
+        (partial,) = call(
+            functools.partial(own_kernel, ydim, zdim), "own_sums",
+            (state, act, grad, first, second, second_back), (partial_shape,), (small_stack,),
+            16 * 1024 * 1024, flops=2 * work,
+        )
+        return partial
+
+    partial = own(state, act, grad)
     paired = last_section == 1
     pair_shape = array((2, cells, 2 * width), BF16)
     tick_outs = (state_shape, pair_shape, wide, wide, wide)
     forward, sent, back, carry, gate = call(
         functools.partial(tick_kernel, ydim, zdim, paired), "tick_one",
-        (state, act, grad, near, far, first, second, first_back, second_back), tick_outs,
+        (state, act, grad, near, far, first, second, first_back, second_back, partial), tick_outs,
         (tile, tile, wide, state_shape, outer_stack), 16 * 1024 * 1024, flops=8 * work,
     )
     if paired:
@@ -480,6 +538,7 @@
         (sums_shape,), (small_stack,), 16 * 1024 * 1024, flops=2 * work,
     )
 
+    partial = own(state_two, act_two, grad_two)
     rows = offsets // count
     direct = rows % 24 == 0
     if direct:
@@ -491,7 +550,8 @@
     results = (state_shape,) * 3
     made = call(
         functools.partial(last_kernel, ydim, zdim, factor, count, direct), "tick_two",
-        (state_two, act_two, grad_two, near, far, first, second, first_back, second_back, so_far),
+        (state_two, act_two, grad_two, near, far, first, second, first_back, second_back, partial,
+         so_far),
         results + outs,
         results + outs + (tile, tile, wide, wide, wide, wide, outer_stack, sums_shape),
         48 * 1024 * 1024, 10, (vmem, hbm), 9 * work, 1,

time: 67.8 us -> 68.5 us (1.010)
  Pallas kernels: 14.7 us -> 17 us
  starting transfers between devices: 29.7 us -> 28.7 us
    pallas_call x6 -> x8, Pallas kernels: 14.7 us -> 17 us  [call(): pl.pallas_call(kernel, out_shape=tuple(outs), in_specs=[places[0]] * (len...]
    ppermute x10, starting transfers between devices: 20.8 us -> 19.8 us  [swapped(): lax.ppermute(send, 'space', [(i, i ^ bit) for i in range(count)])]
    ppermute x2, waiting for transfers between devices: 0.71 us -> 0.01 us  [exchange(): near = lax.ppermute(near, 'space', beside)]
    unnamed x22 -> x24, local copies, waits for them, and re-layouts: 6.82 us -> 6.82 us
  transfers between devices with their start and end apart: 15 -> 15, of which waited for: 8 -> 7; matrix products, arithmetic and copies ran while one was open for 1% -> 1% of each run, Pallas kernels for 2% -> 7%
where the time goes in v8:
time: 68.5 us; the launch traced here: 68.1 us
  starting transfers between devices  28.7 us (42%)
  Pallas kernels  17 us (25%)
  waiting for transfers between devices  13.3 us (19%)
  local copies, waits for them, and re-layouts  7.67 us (11%)
  between operations  0.94 us (1%)
    ppermute x10, starting transfers between devices, swapped(): lax.ppermute(send, 'space', [(i, i ^ bit) for i in range(count)])  19.8 us
    pallas_call x8, Pallas kernels, call(): pl.pallas_call(kernel, out_shape=tuple(outs), in_specs=[places[0]] * (len...  17 us
    ppermute x10, waiting for transfers between devices, swapped(): lax.ppermute(send, 'space', [(i, i ^ bit) for i in range(count)])  11.8 us
    ppermute x2, starting transfers between devices, exchange(): near = lax.ppermute(near, 'space', beside)  7.29 us
    unnamed x24, local copies, waits for them, and re-layouts  6.82 us
    ppermute x1, waiting for transfers between devices, shards(): lifted = lowered = lax.ppermute(sent, 'section', [(0, 1), (1, 0)])  1.52 us
    ppermute x2, starting transfers between devices, exchange(): far = lax.ppermute(far, 'space', across)  1.5 us
  transfers between devices with their start and end apart: 15, of which 7 were waited for; matrix products, arithmetic and copies ran while one was open for 1% of the time, Pallas kernels for 7%

profile of v8, /device:TPU:0, one launch (start us, length us, event | category | flops | bytes accessed | tf_op | source)
XLA Modules:
  0.0 68.1 jit_solution(16162419583645237086)
XLA Ops:
  0.6 1.7 %edges.1 = (bf16[576,128]{1,0:T(8,128)(2,1)}, bf16[576,128]{1,0:T(8,128)(2,1)}) custom-call(bf16[256,256]{1,0:T(8,128)(2,1)} %bitcast.85, bf16[256,256]{1,0:T(8,128)(2,1)} %bitcast.87, bf16[256,256]{1,0:T(8,128)(2,1)} %bitcast.80), custom_call_target="tpu_custom_call" | custom-call | bytes 393216 | tf_op jit(solution)/shard_map/edges/pallas_call | solution.py:479
  2.3 3.0 %collective-permute-start = (bf16[576,128]{1,0:T(8,128)(2,1)}, bf16[576,128]{1,0:T(8,128)(2,1)S(1)}, u32[]{:S(2)}, u32[]{:S(2)}) collective-permute-start(bf16[576,128]{1,0:T(8,128)(2,1)} %get-tuple-element.34), channel_id=1, source_target_pairs={{0,1},{1,0},{2,3},{3,2},{4,5},{5,4},{6,7},{7,6},{8,9},{9,8},{10,11... | collective-permute-start | bytes 442376 | tf_op jit(solution)/shard_map/ppermute | solution.py:463
  5.3 0.7 collective-permute-start.1
  6.0 1.2 %copy-done = bf16[1,27,128,128]{3,2,1,0:T(8,128)(2,1)S(1)} copy-done((bf16[1,27,128,128]{3,2,1,0:T(8,128)(2,1)S(1)}, bf16[1,27,128,128]{3,2,1,0:T(8,128)(2,1)}, u32[]{:S(2)}) %copy-start) | copy-done | bytes 884760
  7.2 1.2 %copy-done.2 = bf16[1,27,128,128]{3,2,1,0:T(8,128)(2,1)S(1)} copy-done((bf16[1,27,128,128]{3,2,1,0:T(8,128)(2,1)S(1)}, bf16[1,27,128,128]{3,2,1,0:T(8,128)(2,1)}, u32[]{:S(2)}) %copy-start.2) | copy-done | bytes 884760
  8.3 0.9 %copy-done.6 = bf16[1,4,8,8,256]{4,3,2,1,0:T(8,128)(2,1)S(1)} copy-done((bf16[1,4,8,8,256]{4,3,2,1,0:T(8,128)(2,1)S(1)}, bf16[1,4,8,8,256]{4,3,2,1,0:T(8,128)(2,1)}, u32[]{:S(2)}) %copy-start.6) | copy-done | bytes 131096
  9.2 0.9 %copy-done.8 = bf16[1,4,8,8,256]{4,3,2,1,0:T(8,128)(2,1)S(1)} copy-done((bf16[1,4,8,8,256]{4,3,2,1,0:T(8,128)(2,1)S(1)}, bf16[1,4,8,8,256]{4,3,2,1,0:T(8,128)(2,1)}, u32[]{:S(2)}) %copy-start.8) | copy-done | bytes 131096
  10.1 0.9 %copy-done.9 = bf16[1,4,8,8,256]{4,3,2,1,0:T(8,128)(2,1)S(1)} copy-done((bf16[1,4,8,8,256]{4,3,2,1,0:T(8,128)(2,1)S(1)}, bf16[1,4,8,8,256]{4,3,2,1,0:T(8,128)(2,1)}, u32[]{:S(2)}) %copy-start.9) | copy-done | bytes 131096
  11.6 1.6 %own_sums.2.partial = f32[3,384,128]{2,1,0:T(8,128)S(1)} custom-call(bf16[256,256]{1,0:T(8,128)(2,1)S(1)} %get-tuple-element.31.state, bf16[256,256]{1,0:T(8,128)(2,1)S(1)} %get-tuple-element.32.act, bf16[256,256]{1,0:T(8,128)(2,1)S(1)} %get-tuple-element.33.grad, bf16[3,1152,128]{2,1,0:T(8,128)(2,1)S(1)} %bitcast.67, bf16[3,1152,128]{2,1,0:T(8,128)(2,1)S(1)} %bitcast.72, ...), custom_call_target="tpu_custom_call" | custom-call | flops 452984832 | bytes 3047424 | tf_op jit(solution)/shard_map/own_sums/pallas_call | solution.py:479
  13.2 2.6 %tick_one.1 = (bf16[256,256]{1,0:T(8,128)(2,1)S(1)}, bf16[2,256,256]{2,1,0:T(8,128)(2,1)S(1)}, bf16[384,128]{1,0:T(8,128)(2,1)S(1)}, bf16[384,128]{1,0:T(8,128)(2,1)S(1)}, bf16[384,128]{1,0:T(8,128)(2,1)S(1)}) custom-call(bf16[256,256]{1,0:T(8,128)(2,1)S(1)} %get-tuple-element.31.state, bf16[256,256]{1,0:T(8,128)(2,1)S(1)} %get-tuple-element.32.act, ...), custom_call_target="tpu_custom_call" | custom-call | flops 1811939328 | bytes 4521984 | tf_op jit(solution)/shard_map/tick_one/pallas_call | solution.py:479
  15.9 1.5 %collective-permute-done.2.lifted.lowered = bf16[2,256,256]{2,1,0:T(8,128)(2,1)S(1)} collective-permute-done((bf16[2,256,256]{2,1,0:T(8,128)(2,1)S(1)}, bf16[2,256,256]{2,1,0:T(8,128)(2,1)S(1)}, u32[]{:S(2)}, u32[]{:S(2)}) %collective-permute-start.2) | collective-permute-done | bytes 262176 | tf_op jit(solution)/shard_map/ppermute | solution.py:524
  17.5 4.3 %collective-permute-start.3 = (bf16[576,128]{1,0:T(8,128)(2,1)S(1)}, bf16[576,128]{1,0:T(8,128)(2,1)S(1)}, u32[]{:S(2)}, u32[]{:S(2)}) collective-permute-start(bf16[576,128]{1,0:T(8,128)(2,1)S(1)} %get-tuple-element.43), channel_id=1, source_target_pairs={{0,1},{1,0},{2,3},{3,2},{4,5},{5,4},{6,7},{7,6},{8,9},{9,8},{10,11... | collective-permute-start | bytes 442376 | tf_op jit(solution)/shard_map/ppermute | solution.py:463
  21.8 0.8 %collective-permute-start.4 = (bf16[576,128]{1,0:T(8,128)(2,1)S(1)}, bf16[576,128]{1,0:T(8,128)(2,1)S(1)}, u32[]{:S(2)}, u32[]{:S(2)}) collective-permute-start(bf16[576,128]{1,0:T(8,128)(2,1)S(1)} %get-tuple-element.44), channel_id=1, source_target_pairs={{1,2},{2,1},{3,4},{4,3},{5,6},{6,5},{7,8},{8,7},{9,10},{10,9},{11,... | collective-permute-start | bytes 442376 | tf_op jit(solution)/shard_map/ppermute | solution.py:462
  22.7 0.8 %weight_grads.1.so_far = f32[2,3456,128]{2,1,0:T(8,128)S(1)} custom-call(bf16[256,256]{1,0:T(8,128)(2,1)S(1)} %bitcast.82, bf16[384,128]{1,0:T(8,128)(2,1)S(1)} %get-tuple-element.45.back, bf16[384,128]{1,0:T(8,128)(2,1)S(1)} %get-tuple-element.46.carry, bf16[384,128]{1,0:T(8,128)(2,1)S(1)} %get-tuple-element.47.gate), custom_call_target="tpu_custom_call" | custom-call | flops 452984832 | bytes 425984 | tf_op jit(solution)/shard_map/weight_grads/pallas_call | solution.py:479
  23.5 1.7 %copy-done.4 = f32[2,3456,128]{2,1,0:T(8,128)} copy-done((f32[2,3456,128]{2,1,0:T(8,128)}, f32[2,3456,128]{2,1,0:T(8,128)S(1)}, u32[]{:S(2)}) %copy-start.4) | copy-done | bytes 3538968
  25.3 1.6 %own_sums.3.partial = f32[3,384,128]{2,1,0:T(8,128)S(1)} custom-call(bf16[256,256]{1,0:T(8,128)(2,1)S(1)} %get-tuple-element.40.state, bf16[256,256]{1,0:T(8,128)(2,1)S(1)} %get-tuple-element.41.act, bf16[256,256]{1,0:T(8,128)(2,1)S(1)} %get-tuple-element.42.grad, bf16[3,1152,128]{2,1,0:T(8,128)(2,1)S(1)} %bitcast.69, bf16[3,1152,128]{2,1,0:T(8,128)(2,1)S(1)} %bitcast.74, ...), custom_call_target="tpu_custom_call" | custom-call | flops 452984832 | bytes 3047424 | tf_op jit(solution)/shard_map/own_sums/pallas_call | solution.py:479
  26.9 8.1 %tick_two.1 = (bf16[256,256]{1,0:T(8,128)(2,1)}, bf16[256,256]{1,0:T(8,128)(2,1)}, bf16[256,256]{1,0:T(8,128)(2,1)}, bf16[8,144,128]{2,1,0:T(8,128)(2,1)S(1)}, b...) custom-call(bf16[256,256]{1,0:T(8,128)(2,1)S(1)} %get-tuple-element., ...), custom_call_target="tpu_custom_call" | custom-call | flops 2038431744 | bytes 6291456 | tf_op jit(solution)/shard_map/tick_two/pallas_call | solution.py:479
  35.0 5.0 %collective-permute-start.5 = (bf16[8,144,128]{2,1,0:T(8,128)(2,1)S(1)}, bf16[8,144,128]{2,1,0:T(8,128)(2,1)S(1)}, u32[]{:S(2)}, u32[]{:S(2)}) collective-permute-start(bf16[8,144,128]{2,1,0:T(8,128)(2,1)S(1)} %get-tuple-element.52), channel_id=1, source_target_pairs={{0,1},{1,0},{2,3},{3,2},{4,5},{5,4},{6,7},{7,6},{8,9},{9,8},{10,11... | collective-permute-start | bytes 884744 | tf_op jit(solution)/shard_map/ppermute | solution.py:426
  40.0 1.1 %collective-permute-start.8 = (bf16[8,144,128]{2,1,0:T(8,128)(2,1)S(1)}, bf16[8,144,128]{2,1,0:T(8,128)(2,1)S(1)}, u32[]{:S(2)}, u32[]{:S(2)}) collective-permute-start(bf16[8,144,128]{2,1,0:T(8,128)(2,1)S(1)} %get-tuple-element.54), channel_id=1, source_target_pairs={{0,2},{1,3},{2,0},{3,1},{4,6},{5,7},{6,4},{7,5},{8,10},{9,11},{10,... | collective-permute-start | bytes 884744 | tf_op jit(solution)/shard_map/ppermute | solution.py:426
  41.1 1.6 %collective-permute-start.11 = (bf16[8,144,128]{2,1,0:T(8,128)(2,1)S(1)}, bf16[8,144,128]{2,1,0:T(8,128)(2,1)S(1)}, u32[]{:S(2)}, u32[]{:S(2)}) collective-permute-start(bf16[8,144,128]{2,1,0:T(8,128)(2,1)S(1)} %get-tuple-element.56), channel_id=1, source_target_pairs={{0,4},{1,5},{2,6},{3,7},{4,0},{5,1},{6,2},{7,3},{8,12},{9,13},{10,... | collective-permute-start | bytes 884744 | tf_op jit(solution)/shard_map/ppermute | solution.py:426
  42.7 3.8 %collective-permute-done.5 = bf16[8,144,128]{2,1,0:T(8,128)(2,1)S(1)} collective-permute-done((bf16[8,144,128]{2,1,0:T(8,128)(2,1)S(1)}, bf16[8,144,128]{2,1,0:T(8,128)(2,1)S(1)}, u32[]{:S(2)}, u32[]{:S(2)}) %collective-permute-start.5) | collective-permute-done | bytes 294944 | tf_op jit(solution)/shard_map/ppermute | solution.py:426
  46.6 1.4 %collective-permute-start.6 = (bf16[4,144,128]{2,1,0:T(8,128)(2,1)S(1)}, bf16[4,144,128]{2,1,0:T(8,128)(2,1)S(1)}, u32[]{:S(2)}, u32[]{:S(2)}) collective-permute-start(bf16[4,144,128]{2,1,0:T(8,128)(2,1)S(1)} %dynamic-slice_bitcast_fusion.2), channel_id=1, source_target_pairs={{0,2},{1,3},{2,0},{3,1},{4,6},{5,7},{6,4},{7,5},{8,10},{9,11},{10,... | collective-permute-start | bytes 442376 | tf_op jit(solution)/shard_map/ppermute | solution.py:426
  48.1 1.6 %collective-permute-start.9 = (bf16[4,144,128]{2,1,0:T(8,128)(2,1)S(1)}, bf16[4,144,128]{2,1,0:T(8,128)(2,1)S(1)}, u32[]{:S(2)}, u32[]{:S(2)}) collective-permute-start(bf16[4,144,128]{2,1,0:T(8,128)(2,1)S(1)} %dynamic-slice_bitcast_fusion.1), channel_id=1, source_target_pairs={{0,4},{1,5},{2,6},{3,7},{4,0},{5,1},{6,2},{7,3},{8,12},{9,13},{10,... | collective-permute-start | bytes 442376 | tf_op jit(solution)/shard_map/ppermute | solution.py:426
  49.9 1.6 %collective-permute-start.12 = (bf16[4,144,128]{2,1,0:T(8,128)(2,1)S(1)}, bf16[4,144,128]{2,1,0:T(8,128)(2,1)S(1)}, u32[]{:S(2)}, u32[]{:S(2)}) collective-permute-start(bf16[4,144,128]{2,1,0:T(8,128)(2,1)S(1)} %dynamic-slice_bitcast_fusion), channel_id=1, source_target_pairs={{0,1},{1,0},{2,3},{3,2},{4,5},{5,4},{6,7},{7,6},{8,9},{9,8},{10,11... | collective-permute-start | bytes 442376 | tf_op jit(solution)/shard_map/ppermute | solution.py:426
  51.9 2.3 %collective-permute-start.7 = (bf16[2,144,128]{2,1,0:T(8,128)(2,1)S(1)}, bf16[2,144,128]{2,1,0:T(8,128)(2,1)S(1)}, u32[]{:S(2)}, u32[]{:S(2)}) collective-permute-start(bf16[2,144,128]{2,1,0:T(8,128)(2,1)S(1)} %dynamic-slice_bitcast_fusion.5), channel_id=1, source_target_pairs={{0,4},{1,5},{2,6},{3,7},{4,0},{5,1},{6,2},{7,3},{8,12},{9,13},{10,... | collective-permute-start | bytes 221192 | tf_op jit(solution)/shard_map/ppermute | solution.py:426
  54.3 1.5 %collective-permute-start.10 = (bf16[2,144,128]{2,1,0:T(8,128)(2,1)S(1)}, bf16[2,144,128]{2,1,0:T(8,128)(2,1)S(1)}, u32[]{:S(2)}, u32[]{:S(2)}) collective-permute-start(bf16[2,144,128]{2,1,0:T(8,128)(2,1)S(1)} %dynamic-slice_bitcast_fusion.4), channel_id=1, source_target_pairs={{0,1},{1,0},{2,3},{3,2},{4,5},{5,4},{6,7},{7,6},{8,9},{9,8},{10,11... | collective-permute-start | bytes 221192 | tf_op jit(solution)/shard_map/ppermute | solution.py:426
  56.0 1.2 %collective-permute-start.13 = (bf16[2,144,128]{2,1,0:T(8,128)(2,1)S(1)}, bf16[2,144,128]{2,1,0:T(8,128)(2,1)S(1)}, u32[]{:S(2)}, u32[]{:S(2)}) collective-permute-start(bf16[2,144,128]{2,1,0:T(8,128)(2,1)S(1)} %dynamic-slice_bitcast_fusion.3), channel_id=1, source_target_pairs={{0,2},{1,3},{2,0},{3,1},{4,6},{5,7},{6,4},{7,5},{8,10},{9,11},{10,... | collective-permute-start | bytes 221192 | tf_op jit(solution)/shard_map/ppermute | solution.py:426
  57.2 1.5 %collective-permute-done.10 = bf16[2,144,128]{2,1,0:T(8,128)(2,1)S(1)} collective-permute-done((bf16[2,144,128]{2,1,0:T(8,128)(2,1)S(1)}, bf16[2,144,128]{2,1,0:T(8,128)(2,1)S(1)}, u32[]{:S(2)}, u32[]{:S(2)}) %collective-permute-start.10) | collective-permute-done | bytes 73760 | tf_op jit(solution)/shard_map/ppermute | solution.py:426
  58.8 1.6 %collective-permute-done.13 = bf16[2,144,128]{2,1,0:T(8,128)(2,1)S(1)} collective-permute-done((bf16[2,144,128]{2,1,0:T(8,128)(2,1)S(1)}, bf16[2,144,128]{2,1,0:T(8,128)(2,1)S(1)}, u32[]{:S(2)}, u32[]{:S(2)}) %collective-permute-start.13) | collective-permute-done | bytes 73760 | tf_op jit(solution)/shard_map/ppermute | solution.py:426
  60.5 2.5 %collective-permute-start.14 = (bf16[432,128]{1,0:T(8,128)(2,1)S(1)}, bf16[432,128]{1,0:T(8,128)(2,1)S(1)}, u32[]{:S(2)}, u32[]{:S(2)}) collective-permute-start(bf16[432,128]{1,0:T(8,128)(2,1)S(1)} %pad_maximum_fusion), channel_id=1, source_target_pairs={{0,8},{1,9},{2,10},{3,11},{4,12},{5,13},{6,14},{7,15},{8,0},{9,1},... | collective-permute-start | bytes 331784 | tf_op jit(solution)/shard_map/ppermute | solution.py:426
  63.0 4.4 %collective-permute-done.14 = bf16[432,128]{1,0:T(8,128)(2,1)S(1)} collective-permute-done((bf16[432,128]{1,0:T(8,128)(2,1)S(1)}, bf16[432,128]{1,0:T(8,128)(2,1)S(1)}, u32[]{:S(2)}, u32[]{:S(2)}) %collective-permute-start.14) | collective-permute-done | bytes 110624 | tf_op jit(solution)/shard_map/ppermute | solution.py:426
  67.4 0.7 %slice_bitcast_fusion = (f32[1,216,128]{2,1,0:T(8,128)}, f32[1,216,128]{2,1,0:T(8,128)}) fusion(f32[432,128]{1,0:T(8,128)S(1)} %convert_add_fusion.3), kind=kLoop, calls=%fused_computation.19 | loop fusion | bytes 442368 | tf_op jit(solution)/shard_map/broadcast_in_dim | solution.py:567
  (51 shorter events, 1.9 us)
Async XLA Ops:
  2.3 10.9 %collective-permute-start = (bf16[576,128]{1,0:T(8,128)(2,1)}, bf16[576,128]{1,0:T(8,128)(2,1)S(1)}, u32[]{:S(2)}, u32[]{:S(2)}) collective-permute-start(bf16[576,128]{1,0:T(8,128)(2,1)} %get-tuple-element.34), channel_id=1, source_target_pairs={{0,1},{1,0},{2,3},{3,2},{4,5},{5,4},{6,7},{7,6},{8,9},{9,8},{10,11... | collective-permute-start | bytes 442376 | tf_op jit(solution)/shard_map/ppermute | solution.py:463
  5.3 7.9 %collective-permute-start.1 = (bf16[576,128]{1,0:T(8,128)(2,1)}, bf16[576,128]{1,0:T(8,128)(2,1)S(1)}, u32[]{:S(2)}, u32[]{:S(2)}) collective-permute-start(bf16[576,128]{1,0:T(8,128)(2,1)} %get-tuple-element.35), channel_id=1, source_target_pairs={{1,2},{2,1},{3,4},{4,3},{5,6},{6,5},{7,8},{8,7},{9,10},{10,9},{11,... | collective-permute-start | bytes 442376 | tf_op jit(solution)/shard_map/ppermute | solution.py:462
  6.0 1.2 %copy-start = (bf16[1,27,128,128]{3,2,1,0:T(8,128)(2,1)S(1)}, bf16[1,27,128,128]{3,2,1,0:T(8,128)(2,1)}, u32[]{:S(2)}) copy-start(bf16[1,27,128,128]{3,2,1,0:T(8,128)(2,1)} %param.12) | copy-start | bytes 2654212
  7.2 1.2 %copy-start.2 = (bf16[1,27,128,128]{3,2,1,0:T(8,128)(2,1)S(1)}, bf16[1,27,128,128]{3,2,1,0:T(8,128)(2,1)}, u32[]{:S(2)}) copy-start(bf16[1,27,128,128]{3,2,1,0:T(8,128)(2,1)} %param.13) | copy-start | bytes 2654212
  8.3 0.9 %copy-start.6 = (bf16[1,4,8,8,256]{4,3,2,1,0:T(8,128)(2,1)S(1)}, bf16[1,4,8,8,256]{4,3,2,1,0:T(8,128)(2,1)}, u32[]{:S(2)}) copy-start(bf16[1,4,8,8,256]{4,3,2,1,0:T(8,128)(2,1)} %param.9) | copy-start | bytes 393220
  9.2 0.9 %copy-start.8 = (bf16[1,4,8,8,256]{4,3,2,1,0:T(8,128)(2,1)S(1)}, bf16[1,4,8,8,256]{4,3,2,1,0:T(8,128)(2,1)}, u32[]{:S(2)}) copy-start(bf16[1,4,8,8,256]{4,3,2,1,0:T(8,128)(2,1)} %param.7) | copy-start | bytes 393220
  10.1 0.9 %copy-start.9 = (bf16[1,4,8,8,256]{4,3,2,1,0:T(8,128)(2,1)S(1)}, bf16[1,4,8,8,256]{4,3,2,1,0:T(8,128)(2,1)}, u32[]{:S(2)}) copy-start(bf16[1,4,8,8,256]{4,3,2,1,0:T(8,128)(2,1)} %param.8) | copy-start | bytes 393220
  11.6 13.7 %copy-start.5 = (bf16[27,128,128]{2,1,0:T(8,128)(2,1)}, bf16[27,128,128]{2,1,0:T(8,128)(2,1)S(1)}, u32[]{:S(2)}) copy-start(bf16[27,128,128]{2,1,0:T(8,128)(2,1)S(1)} %get-tuple-element.37) | copy-start | bytes 2654212
  13.2 4.2 %copy-start.10 = (bf16[4,8,8,256]{3,2,1,0:T(8,128)(2,1)S(1)}, bf16[4,8,8,256]{3,2,1,0:T(8,128)(2,1)}, u32[]{:S(2)}) copy-start(bf16[4,8,8,256]{3,2,1,0:T(8,128)(2,1)} %param.10) | copy-start | bytes 393220
  13.2 4.2 %copy-start.11 = (bf16[4,8,8,256]{3,2,1,0:T(8,128)(2,1)S(1)}, bf16[4,8,8,256]{3,2,1,0:T(8,128)(2,1)}, u32[]{:S(2)}) copy-start(bf16[4,8,8,256]{3,2,1,0:T(8,128)(2,1)} %param.11) | copy-start | bytes 393220
  13.2 9.5 %copy-start.7 = (bf16[1,4,8,8,256]{4,3,2,1,0:T(8,128)(2,1)S(1)}, bf16[1,4,8,8,256]{4,3,2,1,0:T(8,128)(2,1)}, u32[]{:S(2)}) copy-start(bf16[1,4,8,8,256]{4,3,2,1,0:T(8,128)(2,1)} %param.9) | copy-start | bytes 393220
  15.8 9.5 %copy-start.1 = (bf16[1,27,128,128]{3,2,1,0:T(8,128)(2,1)S(1)}, bf16[1,27,128,128]{3,2,1,0:T(8,128)(2,1)}, u32[]{:S(2)}) copy-start(bf16[1,27,128,128]{3,2,1,0:T(8,128)(2,1)} %param.12) | copy-start | bytes 2654212
  15.8 9.5 %copy-start.3 = (bf16[1,27,128,128]{3,2,1,0:T(8,128)(2,1)S(1)}, bf16[1,27,128,128]{3,2,1,0:T(8,128)(2,1)}, u32[]{:S(2)}) copy-start(bf16[1,27,128,128]{3,2,1,0:T(8,128)(2,1)} %param.13) | copy-start | bytes 2654212
  15.8 1.6 %collective-permute-start.2 = (bf16[2,256,256]{2,1,0:T(8,128)(2,1)S(1)}, bf16[2,256,256]{2,1,0:T(8,128)(2,1)S(1)}, u32[]{:S(2)}, u32[]{:S(2)}) collective-permute-start(bf16[2,256,256]{2,1,0:T(8,128)(2,1)S(1)} %get-tuple-element.39), channel_id=1, source_target_pairs={{0,16},{16,0},{1,17},{17,1},{2,18},{18,2},{3,19},{19,3},{4,20},{20... | collective-permute-start | bytes 786440 | tf_op jit(solution)/shard_map/ppermute | solution.py:524
  17.5 9.3 %collective-permute-start.3 = (bf16[576,128]{1,0:T(8,128)(2,1)S(1)}, bf16[576,128]{1,0:T(8,128)(2,1)S(1)}, u32[]{:S(2)}, u32[]{:S(2)}) collective-permute-start(bf16[576,128]{1,0:T(8,128)(2,1)S(1)} %get-tuple-element.43), channel_id=1, source_target_pairs={{0,1},{1,0},{2,3},{3,2},{4,5},{5,4},{6,7},{7,6},{8,9},{9,8},{10,11... | collective-permute-start | bytes 442376 | tf_op jit(solution)/shard_map/ppermute | solution.py:463
  21.8 5.1 %collective-permute-start.4 = (bf16[576,128]{1,0:T(8,128)(2,1)S(1)}, bf16[576,128]{1,0:T(8,128)(2,1)S(1)}, u32[]{:S(2)}, u32[]{:S(2)}) collective-permute-start(bf16[576,128]{1,0:T(8,128)(2,1)S(1)} %get-tuple-element.44), channel_id=1, source_target_pairs={{1,2},{2,1},{3,4},{4,3},{5,6},{6,5},{7,8},{8,7},{9,10},{10,9},{11,... | collective-permute-start | bytes 442376 | tf_op jit(solution)/shard_map/ppermute | solution.py:462
  23.5 1.7 %copy-start.4 = (f32[2,3456,128]{2,1,0:T(8,128)}, f32[2,3456,128]{2,1,0:T(8,128)S(1)}, u32[]{:S(2)}) copy-start(f32[2,3456,128]{2,1,0:T(8,128)S(1)} %weight_grads.1.so_far) | copy-start | bytes 10616836
  35.0 11.5 %collective-permute-start.5 = (bf16[8,144,128]{2,1,0:T(8,128)(2,1)S(1)}, bf16[8,144,128]{2,1,0:T(8,128)(2,1)S(1)}, u32[]{:S(2)}, u32[]{:S(2)}) collective-permute-start(bf16[8,144,128]{2,1,0:T(8,128)(2,1)S(1)} %get-tuple-element.52), channel_id=1, source_target_pairs={{0,1},{1,0},{2,3},{3,2},{4,5},{5,4},{6,7},{7,6},{8,9},{9,8},{10,11... | collective-permute-start | bytes 884744 | tf_op jit(solution)/shard_map/ppermute | solution.py:426
  40.0 8.0 %collective-permute-start.8 = (bf16[8,144,128]{2,1,0:T(8,128)(2,1)S(1)}, bf16[8,144,128]{2,1,0:T(8,128)(2,1)S(1)}, u32[]{:S(2)}, u32[]{:S(2)}) collective-permute-start(bf16[8,144,128]{2,1,0:T(8,128)(2,1)S(1)} %get-tuple-element.54), channel_id=1, source_target_pairs={{0,2},{1,3},{2,0},{3,1},{4,6},{5,7},{6,4},{7,5},{8,10},{9,11},{10,... | collective-permute-start | bytes 884744 | tf_op jit(solution)/shard_map/ppermute | solution.py:426
  41.1 8.7 %collective-permute-start.11 = (bf16[8,144,128]{2,1,0:T(8,128)(2,1)S(1)}, bf16[8,144,128]{2,1,0:T(8,128)(2,1)S(1)}, u32[]{:S(2)}, u32[]{:S(2)}) collective-permute-start(bf16[8,144,128]{2,1,0:T(8,128)(2,1)S(1)} %get-tuple-element.56), channel_id=1, source_target_pairs={{0,4},{1,5},{2,6},{3,7},{4,0},{5,1},{6,2},{7,3},{8,12},{9,13},{10,... | collective-permute-start | bytes 884744 | tf_op jit(solution)/shard_map/ppermute | solution.py:426
  46.6 5.2 %collective-permute-start.6 = (bf16[4,144,128]{2,1,0:T(8,128)(2,1)S(1)}, bf16[4,144,128]{2,1,0:T(8,128)(2,1)S(1)}, u32[]{:S(2)}, u32[]{:S(2)}) collective-permute-start(bf16[4,144,128]{2,1,0:T(8,128)(2,1)S(1)} %dynamic-slice_bitcast_fusion.2), channel_id=1, source_target_pairs={{0,2},{1,3},{2,0},{3,1},{4,6},{5,7},{6,4},{7,5},{8,10},{9,11},{10,... | collective-permute-start | bytes 442376 | tf_op jit(solution)/shard_map/ppermute | solution.py:426
  48.1 6.1 %collective-permute-start.9 = (bf16[4,144,128]{2,1,0:T(8,128)(2,1)S(1)}, bf16[4,144,128]{2,1,0:T(8,128)(2,1)S(1)}, u32[]{:S(2)}, u32[]{:S(2)}) collective-permute-start(bf16[4,144,128]{2,1,0:T(8,128)(2,1)S(1)} %dynamic-slice_bitcast_fusion.1), channel_id=1, source_target_pairs={{0,4},{1,5},{2,6},{3,7},{4,0},{5,1},{6,2},{7,3},{8,12},{9,13},{10,... | collective-permute-start | bytes 442376 | tf_op jit(solution)/shard_map/ppermute | solution.py:426
  49.9 6.0 %collective-permute-start.12 = (bf16[4,144,128]{2,1,0:T(8,128)(2,1)S(1)}, bf16[4,144,128]{2,1,0:T(8,128)(2,1)S(1)}, u32[]{:S(2)}, u32[]{:S(2)}) collective-permute-start(bf16[4,144,128]{2,1,0:T(8,128)(2,1)S(1)} %dynamic-slice_bitcast_fusion), channel_id=1, source_target_pairs={{0,1},{1,0},{2,3},{3,2},{4,5},{5,4},{6,7},{7,6},{8,9},{9,8},{10,11... | collective-permute-start | bytes 442376 | tf_op jit(solution)/shard_map/ppermute | solution.py:426
  51.9 5.3 %collective-permute-start.7 = (bf16[2,144,128]{2,1,0:T(8,128)(2,1)S(1)}, bf16[2,144,128]{2,1,0:T(8,128)(2,1)S(1)}, u32[]{:S(2)}, u32[]{:S(2)}) collective-permute-start(bf16[2,144,128]{2,1,0:T(8,128)(2,1)S(1)} %dynamic-slice_bitcast_fusion.5), channel_id=1, source_target_pairs={{0,4},{1,5},{2,6},{3,7},{4,0},{5,1},{6,2},{7,3},{8,12},{9,13},{10,... | collective-permute-start | bytes 221192 | tf_op jit(solution)/shard_map/ppermute | solution.py:426
  54.3 4.4 %collective-permute-start.10 = (bf16[2,144,128]{2,1,0:T(8,128)(2,1)S(1)}, bf16[2,144,128]{2,1,0:T(8,128)(2,1)S(1)}, u32[]{:S(2)}, u32[]{:S(2)}) collective-permute-start(bf16[2,144,128]{2,1,0:T(8,128)(2,1)S(1)} %dynamic-slice_bitcast_fusion.4), channel_id=1, source_target_pairs={{0,1},{1,0},{2,3},{3,2},{4,5},{5,4},{6,7},{7,6},{8,9},{9,8},{10,11... | collective-permute-start | bytes 221192 | tf_op jit(solution)/shard_map/ppermute | solution.py:426
  56.0 4.4 %collective-permute-start.13 = (bf16[2,144,128]{2,1,0:T(8,128)(2,1)S(1)}, bf16[2,144,128]{2,1,0:T(8,128)(2,1)S(1)}, u32[]{:S(2)}, u32[]{:S(2)}) collective-permute-start(bf16[2,144,128]{2,1,0:T(8,128)(2,1)S(1)} %dynamic-slice_bitcast_fusion.3), channel_id=1, source_target_pairs={{0,2},{1,3},{2,0},{3,1},{4,6},{5,7},{6,4},{7,5},{8,10},{9,11},{10,... | collective-permute-start | bytes 221192 | tf_op jit(solution)/shard_map/ppermute | solution.py:426
  60.5 6.9 %collective-permute-start.14 = (bf16[432,128]{1,0:T(8,128)(2,1)S(1)}, bf16[432,128]{1,0:T(8,128)(2,1)S(1)}, u32[]{:S(2)}, u32[]{:S(2)}) collective-permute-start(bf16[432,128]{1,0:T(8,128)(2,1)S(1)} %pad_maximum_fusion), channel_id=1, source_target_pairs={{0,8},{1,9},{2,10},{3,11},{4,12},{5,13},{6,14},{7,15},{8,0},{9,1},... | collective-permute-start | bytes 331784 | tf_op jit(solution)/shard_map/ppermute | solution.py:426

commit v9 on v8

--- a/solution.py
+++ b/solution.py
@@ -347,14 +347,12 @@
     refs, args = args[:n_outs], args[n_outs:]
     new_one, back_two, mid, back, carry, gate, stack, sums, sems = args
     copies = Copies(sems)
-    copies.start("so_far", so_far, sums)
     ignore = lambda *names: None
     first_kernel(ydim, zdim, copies, ignore, state, act, grad, near, far, first, second,
                  second_back, partial, new_one, back_two, mid, back, carry, gate, stack)
-    copies.need("so_far")
 
     def put(which, at, block):
-        sums[which, at, :] = (block + sums[which, at, :]) * factor
+        sums[which, at, :] = (block + so_far[which, at, :]) * factor
 
     both_grads(ydim, zdim, grad, back, carry, gate, stack, put)
     if not direct:
@@ -554,7 +552,7 @@
          so_far),
         results + outs,
         results + outs + (tile, tile, wide, wide, wide, wide, outer_stack, sums_shape),
-        48 * 1024 * 1024, 10, (vmem, hbm), 9 * work, 1,
+        32 * 1024 * 1024, 10, (vmem, hbm), 9 * work,
     )
     forward, rebuilt, passed = made[:3]
     halves = made[3:] if direct else split_blocks(made[3], count)

time: 68.5 us -> 65.3 us (0.953)
  Pallas kernels: 17 us -> 13.9 us
  local copies, waits for them, and re-layouts: 7.67 us -> 5.93 us
  starting transfers between devices: 28.7 us -> 29.6 us
  waiting for transfers between devices: 13.3 us -> 14.1 us
    pallas_call x8, Pallas kernels: 17 us -> 13.9 us  [call(): pl.pallas_call(kernel, out_shape=tuple(outs), in_specs=[places[0]] * (len...]
    unnamed x24 -> x20, local copies, waits for them, and re-layouts: 6.82 us -> 5.07 us
    ppermute x10, starting transfers between devices: 19.8 us -> 20.8 us  [swapped(): lax.ppermute(send, 'space', [(i, i ^ bit) for i in range(count)])]
    ppermute x2, waiting for transfers between devices: 0.01 us -> 0.85 us  [exchange(): near = lax.ppermute(near, 'space', beside)]
  transfers between devices with their start and end apart: 15 -> 15, of which waited for: 7 -> 8; matrix products, arithmetic and copies ran while one was open for 1% -> 1% of each run, Pallas kernels for 7% -> 7%
where the time goes in v9:
time: 65.3 us; the launch traced here: 65 us
  starting transfers between devices  29.6 us (45%)
  waiting for transfers between devices  14.1 us (22%)
  Pallas kernels  13.9 us (21%)
  local copies, waits for them, and re-layouts  5.93 us (9%)
  between operations  0.92 us (1%)
    ppermute x10, starting transfers between devices, swapped(): lax.ppermute(send, 'space', [(i, i ^ bit) for i in range(count)])  20.8 us
    pallas_call x8, Pallas kernels, call(): pl.pallas_call(kernel, out_shape=tuple(outs), in_specs=[places[0]] * (len...  13.9 us
    ppermute x10, waiting for transfers between devices, swapped(): lax.ppermute(send, 'space', [(i, i ^ bit) for i in range(count)])  11.7 us
    ppermute x2, starting transfers between devices, exchange(): near = lax.ppermute(near, 'space', beside)  7.29 us
    unnamed x20, local copies, waits for them, and re-layouts  5.07 us
    ppermute x1, waiting for transfers between devices, shards(): lifted = lowered = lax.ppermute(sent, 'section', [(0, 1), (1, 0)])  1.52 us
    ppermute x2, starting transfers between devices, exchange(): far = lax.ppermute(far, 'space', across)  1.5 us
  transfers between devices with their start and end apart: 15, of which 8 were waited for; matrix products, arithmetic and copies ran while one was open for 1% of the time, Pallas kernels for 7%

profile of v9, /device:TPU:0, one launch (start us, length us, event | category | flops | bytes accessed | tf_op | source)
XLA Modules:
  0.0 65.0 jit_solution(9765314523960623966)
XLA Ops:
  0.6 1.7 %edges.1 = (bf16[576,128]{1,0:T(8,128)(2,1)}, bf16[576,128]{1,0:T(8,128)(2,1)}) custom-call(bf16[256,256]{1,0:T(8,128)(2,1)} %bitcast.85, bf16[256,256]{1,0:T(8,128)(2,1)} %bitcast.87, bf16[256,256]{1,0:T(8,128)(2,1)} %bitcast.80), custom_call_target="tpu_custom_call" | custom-call | bytes 393216 | tf_op jit(solution)/shard_map/edges/pallas_call | solution.py:477
  2.3 3.0 %collective-permute-start = (bf16[576,128]{1,0:T(8,128)(2,1)}, bf16[576,128]{1,0:T(8,128)(2,1)S(1)}, u32[]{:S(2)}, u32[]{:S(2)}) collective-permute-start(bf16[576,128]{1,0:T(8,128)(2,1)} %get-tuple-element.34), channel_id=1, source_target_pairs={{0,1},{1,0},{2,3},{3,2},{4,5},{5,4},{6,7},{7,6},{8,9},{9,8},{10,11... | collective-permute-start | bytes 442376 | tf_op jit(solution)/shard_map/ppermute | solution.py:461
  5.3 0.7 %collective-permute-start.1 = (bf16[576,128]{1,0:T(8,128)(2,1)}, bf16[576,128]{1,0:T(8,128)(2,1)S(1)}, u32[]{:S(2)}, u32[]{:S(2)}) collective-permute-start(bf16[576,128]{1,0:T(8,128)(2,1)} %get-tuple-element.35), channel_id=1, source_target_pairs={{1,2},{2,1},{3,4},{4,3},{5,6},{6,5},{7,8},{8,7},{9,10},{10,9},{11,... | collective-permute-start | bytes 442376 | tf_op jit(solution)/shard_map/ppermute | solution.py:460
  6.0 1.2 %copy-done = bf16[1,27,128,128]{3,2,1,0:T(8,128)(2,1)S(1)} copy-done((bf16[1,27,128,128]{3,2,1,0:T(8,128)(2,1)S(1)}, bf16[1,27,128,128]{3,2,1,0:T(8,128)(2,1)}, u32[]{:S(2)}) %copy-start) | copy-done | bytes 884760
  7.2 1.2 %copy-done.2 = bf16[1,27,128,128]{3,2,1,0:T(8,128)(2,1)S(1)} copy-done((bf16[1,27,128,128]{3,2,1,0:T(8,128)(2,1)S(1)}, bf16[1,27,128,128]{3,2,1,0:T(8,128)(2,1)}, u32[]{:S(2)}) %copy-start.2) | copy-done | bytes 884760
  8.3 0.9 %copy-done.4 = bf16[1,4,8,8,256]{4,3,2,1,0:T(8,128)(2,1)S(1)} copy-done((bf16[1,4,8,8,256]{4,3,2,1,0:T(8,128)(2,1)S(1)}, bf16[1,4,8,8,256]{4,3,2,1,0:T(8,128)(2,1)}, u32[]{:S(2)}) %copy-start.4) | copy-done | bytes 131096
  9.2 0.9 %copy-done.6 = bf16[1,4,8,8,256]{4,3,2,1,0:T(8,128)(2,1)S(1)} copy-done((bf16[1,4,8,8,256]{4,3,2,1,0:T(8,128)(2,1)S(1)}, bf16[1,4,8,8,256]{4,3,2,1,0:T(8,128)(2,1)}, u32[]{:S(2)}) %copy-start.6) | copy-done | bytes 131096
  10.1 0.9 %copy-done.7 = bf16[1,4,8,8,256]{4,3,2,1,0:T(8,128)(2,1)S(1)} copy-done((bf16[1,4,8,8,256]{4,3,2,1,0:T(8,128)(2,1)S(1)}, bf16[1,4,8,8,256]{4,3,2,1,0:T(8,128)(2,1)}, u32[]{:S(2)}) %copy-start.7) | copy-done | bytes 131096
  11.6 1.6 %own_sums.2.partial = f32[3,384,128]{2,1,0:T(8,128)S(1)} custom-call(bf16[256,256]{1,0:T(8,128)(2,1)S(1)} %get-tuple-element.31.state, bf16[256,256]{1,0:T(8,128)(2,1)S(1)} %get-tuple-element.32.act, bf16[256,256]{1,0:T(8,128)(2,1)S(1)} %get-tuple-element.33.grad, bf16[3,1152,128]{2,1,0:T(8,128)(2,1)S(1)} %bitcast.67, bf16[3,1152,128]{2,1,0:T(8,128)(2,1)S(1)} %bitcast.72, ...), custom_call_target="tpu_custom_call" | custom-call | flops 452984832 | bytes 3047424 | tf_op jit(solution)/shard_map/own_sums/pallas_call | solution.py:477
  13.2 2.6 %tick_one.1 = (bf16[256,256]{1,0:T(8,128)(2,1)S(1)}, bf16[2,256,256]{2,1,0:T(8,128)(2,1)S(1)}, bf16[384,128]{1,0:T(8,128)(2,1)S(1)}, bf16[384,128]{1,0:T(8,128)(2,1)S(1)}, bf16[384,128]{1,0:T(8,128)(2,1)S(1)}) custom-call(bf16[256,256]{1,0:T(8,128)(2,1)S(1)} %get-tuple-element.31.state, bf16[256,256]{1,0:T(8,128)(2,1)S(1)} %get-tuple-element.32.act, ...), custom_call_target="tpu_custom_call" | custom-call | flops 1811939328 | bytes 4521984 | tf_op jit(solution)/shard_map/tick_one/pallas_call | solution.py:477
  15.9 1.5 %collective-permute-done.2.lifted.lowered = bf16[2,256,256]{2,1,0:T(8,128)(2,1)S(1)} collective-permute-done((bf16[2,256,256]{2,1,0:T(8,128)(2,1)S(1)}, bf16[2,256,256]{2,1,0:T(8,128)(2,1)S(1)}, u32[]{:S(2)}, u32[]{:S(2)}) %collective-permute-start.2) | collective-permute-done | bytes 262176 | tf_op jit(solution)/shard_map/ppermute | solution.py:522
  17.5 4.3 %collective-permute-start.3 = (bf16[576,128]{1,0:T(8,128)(2,1)S(1)}, bf16[576,128]{1,0:T(8,128)(2,1)S(1)}, u32[]{:S(2)}, u32[]{:S(2)}) collective-permute-start(bf16[576,128]{1,0:T(8,128)(2,1)S(1)} %get-tuple-element.43), channel_id=1, source_target_pairs={{0,1},{1,0},{2,3},{3,2},{4,5},{5,4},{6,7},{7,6},{8,9},{9,8},{10,11... | collective-permute-start | bytes 442376 | tf_op jit(solution)/shard_map/ppermute | solution.py:461
  21.8 0.8 %collective-permute-start.4 = (bf16[576,128]{1,0:T(8,128)(2,1)S(1)}, bf16[576,128]{1,0:T(8,128)(2,1)S(1)}, u32[]{:S(2)}, u32[]{:S(2)}) collective-permute-start(bf16[576,128]{1,0:T(8,128)(2,1)S(1)} %get-tuple-element.44), channel_id=1, source_target_pairs={{1,2},{2,1},{3,4},{4,3},{5,6},{6,5},{7,8},{8,7},{9,10},{10,9},{11,... | collective-permute-start | bytes 442376 | tf_op jit(solution)/shard_map/ppermute | solution.py:460
  22.7 0.8 %weight_grads.1.so_far = f32[2,3456,128]{2,1,0:T(8,128)S(1)} custom-call(bf16[256,256]{1,0:T(8,128)(2,1)S(1)} %bitcast.82, bf16[384,128]{1,0:T(8,128)(2,1)S(1)} %get-tuple-element.45.back, bf16[384,128]{1,0:T(8,128)(2,1)S(1)} %get-tuple-element.46.carry, bf16[384,128]{1,0:T(8,128)(2,1)S(1)} %get-tuple-element.47.gate), custom_call_target="tpu_custom_call" | custom-call | flops 452984832 | bytes 425984 | tf_op jit(solution)/shard_map/weight_grads/pallas_call | solution.py:477
  23.5 1.6 %own_sums.3.partial = f32[3,384,128]{2,1,0:T(8,128)S(1)} custom-call(bf16[256,256]{1,0:T(8,128)(2,1)S(1)} %get-tuple-element.40.state, bf16[256,256]{1,0:T(8,128)(2,1)S(1)} %get-tuple-element.41.act, bf16[256,256]{1,0:T(8,128)(2,1)S(1)} %get-tuple-element.42.grad, bf16[3,1152,128]{2,1,0:T(8,128)(2,1)S(1)} %bitcast.69, bf16[3,1152,128]{2,1,0:T(8,128)(2,1)S(1)} %bitcast.74, ...), custom_call_target="tpu_custom_call" | custom-call | flops 452984832 | bytes 3047424 | tf_op jit(solution)/shard_map/own_sums/pallas_call | solution.py:477
  25.1 0.8 %collective-permute-done.3.near = bf16[576,128]{1,0:T(8,128)(2,1)S(1)} collective-permute-done((bf16[576,128]{1,0:T(8,128)(2,1)S(1)}, bf16[576,128]{1,0:T(8,128)(2,1)S(1)}, u32[]{:S(2)}, u32[]{:S(2)}) %collective-permute-start.3) | collective-permute-done | bytes 147488 | tf_op jit(solution)/shard_map/ppermute | solution.py:461
  26.0 5.0 %tick_two.1 = (bf16[256,256]{1,0:T(8,128)(2,1)}, bf16[256,256]{1,0:T(8,128)(2,1)}, bf16[256,256]{1,0:T(8,128)(2,1)}, bf16[8,144,128]{2,1,0:T(8,128)(2,1)S(1)}, b...) custom-call(bf16[256,256]{1,0:T(8,128)(2,1)S(1)} %get-tuple-element., ...), custom_call_target="tpu_custom_call" | custom-call | flops 2038431744 | bytes 6291456 | tf_op jit(solution)/shard_map/tick_two/pallas_call | solution.py:477
  31.0 5.9 %collective-permute-start.5 = (bf16[8,144,128]{2,1,0:T(8,128)(2,1)S(1)}, bf16[8,144,128]{2,1,0:T(8,128)(2,1)S(1)}, u32[]{:S(2)}, u32[]{:S(2)}) collective-permute-start(bf16[8,144,128]{2,1,0:T(8,128)(2,1)S(1)} %get-tuple-element.52), channel_id=1, source_target_pairs={{0,1},{1,0},{2,3},{3,2},{4,5},{5,4},{6,7},{7,6},{8,9},{9,8},{10,11... | collective-permute-start | bytes 884744 | tf_op jit(solution)/shard_map/ppermute | solution.py:424
  36.9 1.1 %collective-permute-start.8 = (bf16[8,144,128]{2,1,0:T(8,128)(2,1)S(1)}, bf16[8,144,128]{2,1,0:T(8,128)(2,1)S(1)}, u32[]{:S(2)}, u32[]{:S(2)}) collective-permute-start(bf16[8,144,128]{2,1,0:T(8,128)(2,1)S(1)} %get-tuple-element.54), channel_id=1, source_target_pairs={{0,2},{1,3},{2,0},{3,1},{4,6},{5,7},{6,4},{7,5},{8,10},{9,11},{10,... | collective-permute-start | bytes 884744 | tf_op jit(solution)/shard_map/ppermute | solution.py:424
  38.0 1.6 %collective-permute-start.11 = (bf16[8,144,128]{2,1,0:T(8,128)(2,1)S(1)}, bf16[8,144,128]{2,1,0:T(8,128)(2,1)S(1)}, u32[]{:S(2)}, u32[]{:S(2)}) collective-permute-start(bf16[8,144,128]{2,1,0:T(8,128)(2,1)S(1)} %get-tuple-element.56), channel_id=1, source_target_pairs={{0,4},{1,5},{2,6},{3,7},{4,0},{5,1},{6,2},{7,3},{8,12},{9,13},{10,... | collective-permute-start | bytes 884744 | tf_op jit(solution)/shard_map/ppermute | solution.py:424
  39.6 3.8 %collective-permute-done.5 = bf16[8,144,128]{2,1,0:T(8,128)(2,1)S(1)} collective-permute-done((bf16[8,144,128]{2,1,0:T(8,128)(2,1)S(1)}, bf16[8,144,128]{2,1,0:T(8,128)(2,1)S(1)}, u32[]{:S(2)}, u32[]{:S(2)}) %collective-permute-start.5) | collective-permute-done | bytes 294944 | tf_op jit(solution)/shard_map/ppermute | solution.py:424
  43.5 1.4 %collective-permute-start.6 = (bf16[4,144,128]{2,1,0:T(8,128)(2,1)S(1)}, bf16[4,144,128]{2,1,0:T(8,128)(2,1)S(1)}, u32[]{:S(2)}, u32[]{:S(2)}) collective-permute-start(bf16[4,144,128]{2,1,0:T(8,128)(2,1)S(1)} %dynamic-slice_bitcast_fusion.2), channel_id=1, source_target_pairs={{0,2},{1,3},{2,0},{3,1},{4,6},{5,7},{6,4},{7,5},{8,10},{9,11},{10,... | collective-permute-start | bytes 442376 | tf_op jit(solution)/shard_map/ppermute | solution.py:424
  45.0 1.6 %collective-permute-start.9 = (bf16[4,144,128]{2,1,0:T(8,128)(2,1)S(1)}, bf16[4,144,128]{2,1,0:T(8,128)(2,1)S(1)}, u32[]{:S(2)}, u32[]{:S(2)}) collective-permute-start(bf16[4,144,128]{2,1,0:T(8,128)(2,1)S(1)} %dynamic-slice_bitcast_fusion.1), channel_id=1, source_target_pairs={{0,4},{1,5},{2,6},{3,7},{4,0},{5,1},{6,2},{7,3},{8,12},{9,13},{10,... | collective-permute-start | bytes 442376 | tf_op jit(solution)/shard_map/ppermute | solution.py:424
  46.8 1.6 %collective-permute-start.12 = (bf16[4,144,128]{2,1,0:T(8,128)(2,1)S(1)}, bf16[4,144,128]{2,1,0:T(8,128)(2,1)S(1)}, u32[]{:S(2)}, u32[]{:S(2)}) collective-permute-start(bf16[4,144,128]{2,1,0:T(8,128)(2,1)S(1)} %dynamic-slice_bitcast_fusion), channel_id=1, source_target_pairs={{0,1},{1,0},{2,3},{3,2},{4,5},{5,4},{6,7},{7,6},{8,9},{9,8},{10,11... | collective-permute-start | bytes 442376 | tf_op jit(solution)/shard_map/ppermute | solution.py:424
  48.8 2.3 %collective-permute-start.7 = (bf16[2,144,128]{2,1,0:T(8,128)(2,1)S(1)}, bf16[2,144,128]{2,1,0:T(8,128)(2,1)S(1)}, u32[]{:S(2)}, u32[]{:S(2)}) collective-permute-start(bf16[2,144,128]{2,1,0:T(8,128)(2,1)S(1)} %dynamic-slice_bitcast_fusion.5), channel_id=1, source_target_pairs={{0,4},{1,5},{2,6},{3,7},{4,0},{5,1},{6,2},{7,3},{8,12},{9,13},{10,... | collective-permute-start | bytes 221192 | tf_op jit(solution)/shard_map/ppermute | solution.py:424
  51.2 1.5 %collective-permute-start.10 = (bf16[2,144,128]{2,1,0:T(8,128)(2,1)S(1)}, bf16[2,144,128]{2,1,0:T(8,128)(2,1)S(1)}, u32[]{:S(2)}, u32[]{:S(2)}) collective-permute-start(bf16[2,144,128]{2,1,0:T(8,128)(2,1)S(1)} %dynamic-slice_bitcast_fusion.4), channel_id=1, source_target_pairs={{0,1},{1,0},{2,3},{3,2},{4,5},{5,4},{6,7},{7,6},{8,9},{9,8},{10,11... | collective-permute-start | bytes 221192 | tf_op jit(solution)/shard_map/ppermute | solution.py:424
  52.9 1.2 %collective-permute-start.13 = (bf16[2,144,128]{2,1,0:T(8,128)(2,1)S(1)}, bf16[2,144,128]{2,1,0:T(8,128)(2,1)S(1)}, u32[]{:S(2)}, u32[]{:S(2)}) collective-permute-start(bf16[2,144,128]{2,1,0:T(8,128)(2,1)S(1)} %dynamic-slice_bitcast_fusion.3), channel_id=1, source_target_pairs={{0,2},{1,3},{2,0},{3,1},{4,6},{5,7},{6,4},{7,5},{8,10},{9,11},{10,... | collective-permute-start | bytes 221192 | tf_op jit(solution)/shard_map/ppermute | solution.py:424
  54.1 1.5 %collective-permute-done.10 = bf16[2,144,128]{2,1,0:T(8,128)(2,1)S(1)} collective-permute-done((bf16[2,144,128]{2,1,0:T(8,128)(2,1)S(1)}, bf16[2,144,128]{2,1,0:T(8,128)(2,1)S(1)}, u32[]{:S(2)}, u32[]{:S(2)}) %collective-permute-start.10) | collective-permute-done | bytes 73760 | tf_op jit(solution)/shard_map/ppermute | solution.py:424
  55.7 1.6 %collective-permute-done.13 = bf16[2,144,128]{2,1,0:T(8,128)(2,1)S(1)} collective-permute-done((bf16[2,144,128]{2,1,0:T(8,128)(2,1)S(1)}, bf16[2,144,128]{2,1,0:T(8,128)(2,1)S(1)}, u32[]{:S(2)}, u32[]{:S(2)}) %collective-permute-start.13) | collective-permute-done | bytes 73760 | tf_op jit(solution)/shard_map/ppermute | solution.py:424
  57.3 2.6 %collective-permute-start.14 = (bf16[432,128]{1,0:T(8,128)(2,1)S(1)}, bf16[432,128]{1,0:T(8,128)(2,1)S(1)}, u32[]{:S(2)}, u32[]{:S(2)}) collective-permute-start(bf16[432,128]{1,0:T(8,128)(2,1)S(1)} %pad_maximum_fusion), channel_id=1, source_target_pairs={{0,8},{1,9},{2,10},{3,11},{4,12},{5,13},{6,14},{7,15},{8,0},{9,1},... | collective-permute-start | bytes 331784 | tf_op jit(solution)/shard_map/ppermute | solution.py:424
  59.9 4.3 %collective-permute-done.14 = bf16[432,128]{1,0:T(8,128)(2,1)S(1)} collective-permute-done((bf16[432,128]{1,0:T(8,128)(2,1)S(1)}, bf16[432,128]{1,0:T(8,128)(2,1)S(1)}, u32[]{:S(2)}, u32[]{:S(2)}) %collective-permute-start.14) | collective-permute-done | bytes 110624 | tf_op jit(solution)/shard_map/ppermute | solution.py:424
  64.3 0.7 %slice_bitcast_fusion = (f32[1,216,128]{2,1,0:T(8,128)}, f32[1,216,128]{2,1,0:T(8,128)}) fusion(f32[432,128]{1,0:T(8,128)S(1)} %convert_add_fusion.3), kind=kLoop, calls=%fused_computation.19 | loop fusion | bytes 442368 | tf_op jit(solution)/shard_map/broadcast_in_dim | solution.py:565
  (47 shorter events, 1.9 us)
Async XLA Ops:
  2.3 10.9 %collective-permute-start = (bf16[576,128]{1,0:T(8,128)(2,1)}, bf16[576,128]{1,0:T(8,128)(2,1)S(1)}, u32[]{:S(2)}, u32[]{:S(2)}) collective-permute-start(bf16[576,128]{1,0:T(8,128)(2,1)} %get-tuple-element.34), channel_id=1, source_target_pairs={{0,1},{1,0},{2,3},{3,2},{4,5},{5,4},{6,7},{7,6},{8,9},{9,8},{10,11... | collective-permute-start | bytes 442376 | tf_op jit(solution)/shard_map/ppermute | solution.py:461
  5.3 7.9 %collective-permute-start.1 = (bf16[576,128]{1,0:T(8,128)(2,1)}, bf16[576,128]{1,0:T(8,128)(2,1)S(1)}, u32[]{:S(2)}, u32[]{:S(2)}) collective-permute-start(bf16[576,128]{1,0:T(8,128)(2,1)} %get-tuple-element.35), channel_id=1, source_target_pairs={{1,2},{2,1},{3,4},{4,3},{5,6},{6,5},{7,8},{8,7},{9,10},{10,9},{11,... | collective-permute-start | bytes 442376 | tf_op jit(solution)/shard_map/ppermute | solution.py:460
  6.0 1.2 %copy-start = (bf16[1,27,128,128]{3,2,1,0:T(8,128)(2,1)S(1)}, bf16[1,27,128,128]{3,2,1,0:T(8,128)(2,1)}, u32[]{:S(2)}) copy-start(bf16[1,27,128,128]{3,2,1,0:T(8,128)(2,1)} %param.12) | copy-start | bytes 2654212
  7.2 1.2 %copy-start.2 = (bf16[1,27,128,128]{3,2,1,0:T(8,128)(2,1)S(1)}, bf16[1,27,128,128]{3,2,1,0:T(8,128)(2,1)}, u32[]{:S(2)}) copy-start(bf16[1,27,128,128]{3,2,1,0:T(8,128)(2,1)} %param.13) | copy-start | bytes 2654212
  8.3 0.9 %copy-start.4 = (bf16[1,4,8,8,256]{4,3,2,1,0:T(8,128)(2,1)S(1)}, bf16[1,4,8,8,256]{4,3,2,1,0:T(8,128)(2,1)}, u32[]{:S(2)}) copy-start(bf16[1,4,8,8,256]{4,3,2,1,0:T(8,128)(2,1)} %param.9) | copy-start | bytes 393220
  9.2 0.9 %copy-start.6 = (bf16[1,4,8,8,256]{4,3,2,1,0:T(8,128)(2,1)S(1)}, bf16[1,4,8,8,256]{4,3,2,1,0:T(8,128)(2,1)}, u32[]{:S(2)}) copy-start(bf16[1,4,8,8,256]{4,3,2,1,0:T(8,128)(2,1)} %param.7) | copy-start | bytes 393220
  10.1 0.9 %copy-start.7 = (bf16[1,4,8,8,256]{4,3,2,1,0:T(8,128)(2,1)S(1)}, bf16[1,4,8,8,256]{4,3,2,1,0:T(8,128)(2,1)}, u32[]{:S(2)}) copy-start(bf16[1,4,8,8,256]{4,3,2,1,0:T(8,128)(2,1)} %param.8) | copy-start | bytes 393220
  13.1 4.2 %copy-start.8 = (bf16[4,8,8,256]{3,2,1,0:T(8,128)(2,1)S(1)}, bf16[4,8,8,256]{3,2,1,0:T(8,128)(2,1)}, u32[]{:S(2)}) copy-start(bf16[4,8,8,256]{3,2,1,0:T(8,128)(2,1)} %param.10) | copy-start | bytes 393220
  13.2 4.2 %copy-start.9 = (bf16[4,8,8,256]{3,2,1,0:T(8,128)(2,1)S(1)}, bf16[4,8,8,256]{3,2,1,0:T(8,128)(2,1)}, u32[]{:S(2)}) copy-start(bf16[4,8,8,256]{3,2,1,0:T(8,128)(2,1)} %param.11) | copy-start | bytes 393220
  13.2 9.5 %copy-start.5 = (bf16[1,4,8,8,256]{4,3,2,1,0:T(8,128)(2,1)S(1)}, bf16[1,4,8,8,256]{4,3,2,1,0:T(8,128)(2,1)}, u32[]{:S(2)}) copy-start(bf16[1,4,8,8,256]{4,3,2,1,0:T(8,128)(2,1)} %param.9) | copy-start | bytes 393220
  15.8 7.7 %copy-start.1 = (bf16[1,27,128,128]{3,2,1,0:T(8,128)(2,1)S(1)}, bf16[1,27,128,128]{3,2,1,0:T(8,128)(2,1)}, u32[]{:S(2)}) copy-start(bf16[1,27,128,128]{3,2,1,0:T(8,128)(2,1)} %param.12) | copy-start | bytes 2654212
  15.8 7.7 %copy-start.3 = (bf16[1,27,128,128]{3,2,1,0:T(8,128)(2,1)S(1)}, bf16[1,27,128,128]{3,2,1,0:T(8,128)(2,1)}, u32[]{:S(2)}) copy-start(bf16[1,27,128,128]{3,2,1,0:T(8,128)(2,1)} %param.13) | copy-start | bytes 2654212
  15.8 1.6 %collective-permute-start.2 = (bf16[2,256,256]{2,1,0:T(8,128)(2,1)S(1)}, bf16[2,256,256]{2,1,0:T(8,128)(2,1)S(1)}, u32[]{:S(2)}, u32[]{:S(2)}) collective-permute-start(bf16[2,256,256]{2,1,0:T(8,128)(2,1)S(1)} %get-tuple-element.39), channel_id=1, source_target_pairs={{0,16},{16,0},{1,17},{17,1},{2,18},{18,2},{3,19},{19,3},{4,20},{20... | collective-permute-start | bytes 786440 | tf_op jit(solution)/shard_map/ppermute | solution.py:522
  17.5 8.4 %collective-permute-start.3 = (bf16[576,128]{1,0:T(8,128)(2,1)S(1)}, bf16[576,128]{1,0:T(8,128)(2,1)S(1)}, u32[]{:S(2)}, u32[]{:S(2)}) collective-permute-start(bf16[576,128]{1,0:T(8,128)(2,1)S(1)} %get-tuple-element.43), channel_id=1, source_target_pairs={{0,1},{1,0},{2,3},{3,2},{4,5},{5,4},{6,7},{7,6},{8,9},{9,8},{10,11... | collective-permute-start | bytes 442376 | tf_op jit(solution)/shard_map/ppermute | solution.py:461
  21.8 4.2 %collective-permute-start.4 = (bf16[576,128]{1,0:T(8,128)(2,1)S(1)}, bf16[576,128]{1,0:T(8,128)(2,1)S(1)}, u32[]{:S(2)}, u32[]{:S(2)}) collective-permute-start(bf16[576,128]{1,0:T(8,128)(2,1)S(1)} %get-tuple-element.44), channel_id=1, source_target_pairs={{1,2},{2,1},{3,4},{4,3},{5,6},{6,5},{7,8},{8,7},{9,10},{10,9},{11,... | collective-permute-start | bytes 442376 | tf_op jit(solution)/shard_map/ppermute | solution.py:460
  31.0 12.4 %collective-permute-start.5 = (bf16[8,144,128]{2,1,0:T(8,128)(2,1)S(1)}, bf16[8,144,128]{2,1,0:T(8,128)(2,1)S(1)}, u32[]{:S(2)}, u32[]{:S(2)}) collective-permute-start(bf16[8,144,128]{2,1,0:T(8,128)(2,1)S(1)} %get-tuple-element.52), channel_id=1, source_target_pairs={{0,1},{1,0},{2,3},{3,2},{4,5},{5,4},{6,7},{7,6},{8,9},{9,8},{10,11... | collective-permute-start | bytes 884744 | tf_op jit(solution)/shard_map/ppermute | solution.py:424
  36.9 8.0 %collective-permute-start.8 = (bf16[8,144,128]{2,1,0:T(8,128)(2,1)S(1)}, bf16[8,144,128]{2,1,0:T(8,128)(2,1)S(1)}, u32[]{:S(2)}, u32[]{:S(2)}) collective-permute-start(bf16[8,144,128]{2,1,0:T(8,128)(2,1)S(1)} %get-tuple-element.54), channel_id=1, source_target_pairs={{0,2},{1,3},{2,0},{3,1},{4,6},{5,7},{6,4},{7,5},{8,10},{9,11},{10,... | collective-permute-start | bytes 884744 | tf_op jit(solution)/shard_map/ppermute | solution.py:424
  38.0 8.6 %collective-permute-start.11 = (bf16[8,144,128]{2,1,0:T(8,128)(2,1)S(1)}, bf16[8,144,128]{2,1,0:T(8,128)(2,1)S(1)}, u32[]{:S(2)}, u32[]{:S(2)}) collective-permute-start(bf16[8,144,128]{2,1,0:T(8,128)(2,1)S(1)} %get-tuple-element.56), channel_id=1, source_target_pairs={{0,4},{1,5},{2,6},{3,7},{4,0},{5,1},{6,2},{7,3},{8,12},{9,13},{10,... | collective-permute-start | bytes 884744 | tf_op jit(solution)/shard_map/ppermute | solution.py:424
  43.5 5.2 %collective-permute-start.6 = (bf16[4,144,128]{2,1,0:T(8,128)(2,1)S(1)}, bf16[4,144,128]{2,1,0:T(8,128)(2,1)S(1)}, u32[]{:S(2)}, u32[]{:S(2)}) collective-permute-start(bf16[4,144,128]{2,1,0:T(8,128)(2,1)S(1)} %dynamic-slice_bitcast_fusion.2), channel_id=1, source_target_pairs={{0,2},{1,3},{2,0},{3,1},{4,6},{5,7},{6,4},{7,5},{8,10},{9,11},{10,... | collective-permute-start | bytes 442376 | tf_op jit(solution)/shard_map/ppermute | solution.py:424
  45.0 6.1 %collective-permute-start.9 = (bf16[4,144,128]{2,1,0:T(8,128)(2,1)S(1)}, bf16[4,144,128]{2,1,0:T(8,128)(2,1)S(1)}, u32[]{:S(2)}, u32[]{:S(2)}) collective-permute-start(bf16[4,144,128]{2,1,0:T(8,128)(2,1)S(1)} %dynamic-slice_bitcast_fusion.1), channel_id=1, source_target_pairs={{0,4},{1,5},{2,6},{3,7},{4,0},{5,1},{6,2},{7,3},{8,12},{9,13},{10,... | collective-permute-start | bytes 442376 | tf_op jit(solution)/shard_map/ppermute | solution.py:424
  46.8 6.0 %collective-permute-start.12 = (bf16[4,144,128]{2,1,0:T(8,128)(2,1)S(1)}, bf16[4,144,128]{2,1,0:T(8,128)(2,1)S(1)}, u32[]{:S(2)}, u32[]{:S(2)}) collective-permute-start(bf16[4,144,128]{2,1,0:T(8,128)(2,1)S(1)} %dynamic-slice_bitcast_fusion), channel_id=1, source_target_pairs={{0,1},{1,0},{2,3},{3,2},{4,5},{5,4},{6,7},{7,6},{8,9},{9,8},{10,11... | collective-permute-start | bytes 442376 | tf_op jit(solution)/shard_map/ppermute | solution.py:424
  48.8 5.2 %collective-permute-start.7 = (bf16[2,144,128]{2,1,0:T(8,128)(2,1)S(1)}, bf16[2,144,128]{2,1,0:T(8,128)(2,1)S(1)}, u32[]{:S(2)}, u32[]{:S(2)}) collective-permute-start(bf16[2,144,128]{2,1,0:T(8,128)(2,1)S(1)} %dynamic-slice_bitcast_fusion.5), channel_id=1, source_target_pairs={{0,4},{1,5},{2,6},{3,7},{4,0},{5,1},{6,2},{7,3},{8,12},{9,13},{10,... | collective-permute-start | bytes 221192 | tf_op jit(solution)/shard_map/ppermute | solution.py:424
  51.2 4.4 %collective-permute-start.10 = (bf16[2,144,128]{2,1,0:T(8,128)(2,1)S(1)}, bf16[2,144,128]{2,1,0:T(8,128)(2,1)S(1)}, u32[]{:S(2)}, u32[]{:S(2)}) collective-permute-start(bf16[2,144,128]{2,1,0:T(8,128)(2,1)S(1)} %dynamic-slice_bitcast_fusion.4), channel_id=1, source_target_pairs={{0,1},{1,0},{2,3},{3,2},{4,5},{5,4},{6,7},{7,6},{8,9},{9,8},{10,11... | collective-permute-start | bytes 221192 | tf_op jit(solution)/shard_map/ppermute | solution.py:424
  52.9 4.4 %collective-permute-start.13 = (bf16[2,144,128]{2,1,0:T(8,128)(2,1)S(1)}, bf16[2,144,128]{2,1,0:T(8,128)(2,1)S(1)}, u32[]{:S(2)}, u32[]{:S(2)}) collective-permute-start(bf16[2,144,128]{2,1,0:T(8,128)(2,1)S(1)} %dynamic-slice_bitcast_fusion.3), channel_id=1, source_target_pairs={{0,2},{1,3},{2,0},{3,1},{4,6},{5,7},{6,4},{7,5},{8,10},{9,11},{10,... | collective-permute-start | bytes 221192 | tf_op jit(solution)/shard_map/ppermute | solution.py:424
  57.3 6.9 %collective-permute-start.14 = (bf16[432,128]{1,0:T(8,128)(2,1)S(1)}, bf16[432,128]{1,0:T(8,128)(2,1)S(1)}, u32[]{:S(2)}, u32[]{:S(2)}) collective-permute-start(bf16[432,128]{1,0:T(8,128)(2,1)S(1)} %pad_maximum_fusion), channel_id=1, source_target_pairs={{0,8},{1,9},{2,10},{3,11},{4,12},{5,13},{6,14},{7,15},{8,0},{9,1},... | collective-permute-start | bytes 331784 | tf_op jit(solution)/shard_map/ppermute | solution.py:424

commit v10 on v9

--- a/solution.py
+++ b/solution.py
@@ -91,7 +91,8 @@
         put((6 + index) * plane, plane, source, half)
 
 
-def edges_kernel(plane, state, act, grad, near_out, far_out, near, far, sems):
+def edges_kernel(plane, state, act, grad, near_out, far_out, fields_out, near, far, fields,
+                 sems):
     width = state.shape[1] // 2
     cells = state.shape[0]
     left, right = pl.ds(0, width), pl.ds(width, width)
@@ -106,9 +107,13 @@
         for index, (source, half, size, at) in enumerate(moves):
             start = pl.multiple_of(high * (cells - size), plane)
             copies.start((side, index), source.at[pl.ds(start, size), half], out.at[pl.ds(at, size), :])
+    for index, source in enumerate((state, act, grad)):
+        copies.start(("field", index), source, fields.at[index])
     for side, (out, result) in enumerate(((near, near_out), (far, far_out))):
         copies.need(*[(side, index) for index in range(len(moves))])
         copies.start(side, out, result)
+    copies.need(*[("field", index) for index in range(3)])
+    copies.start("fields", fields, fields_out)
     copies.finish()
 
 
@@ -127,10 +132,11 @@
     own_sums(ydim, zdim, gated_fields(state, act, grad), (first, second, second_back), partial, stack)
 
 
-def flip_kernel(first, second, state_in, act_in, grad_in, first_back, second_back, state, act, grad):
-    state[...] = state_in[...]
-    act[...] = act_in[...]
-    grad[...] = grad_in[...]
+def flip_kernel(first, second, fields, first_out, second_out, first_back, second_back, state, act, grad):
+    for index, out in enumerate((state, act, grad)):
+        out[...] = fields[index]
+    first_out[...] = first[...]
+    second_out[...] = second[...]
     offsets = first.shape[0]
     for source, out in ((first, first_back), (second, second_back)):
         for k in range(offsets):
@@ -279,7 +285,7 @@
     made("forward")
 
 
-def tick_kernel(ydim, zdim, paired, state, act, grad, near, far, first, second,
+def tick_kernel(ydim, zdim, paired, state, act, grad, far, near, first, second,
                 first_back, second_back, partial, forward, sent, back, carry, gate, new_one, back_two, mid,
                 rebuilt, stack):
     copies = Copies(None)
@@ -338,7 +344,7 @@
     return [(way * span, span, order) for way, order in enumerate(orders)]
 
 
-def last_kernel(ydim, zdim, factor, count, direct, state, act, grad, near, far, first,
+def last_kernel(ydim, zdim, factor, count, direct, state, act, grad, far, near, first,
                 second, first_back, second_back, partial, so_far, *args):
     n_outs = 6 if direct else 1
     results_out, args = args[:3], args[3:]
@@ -488,20 +494,22 @@
         )(*inputs)
 
     work = 2 * 27 * cells * width * width
-    near, far = call(
-        functools.partial(edges_kernel, plane), "edges", (state, act, grad), (edge,) * 2,
-        (edge,) * 2, 65408 * 1024, 14, (hbm, hbm),
+    fields_shape = array((3, cells, 2 * width), BF16)
+    near, far, fields = call(
+        functools.partial(edges_kernel, plane), "edges", (state, act, grad), (edge, edge, fields_shape),
+        (edge, edge, fields_shape), 65408 * 1024, 18, (hbm, hbm),
     )
     near, far = exchange(near, far)
-    first_back, second_back, state, act, grad = call(
-        flip_kernel, "flip", (w_first[0], w_second[0], state, act, grad),
-        (raw_weight,) * 2 + (state_shape,) * 3, (), 16 * 1024 * 1024,
-    )
-    first_back, second_back = first_back.reshape(weight.shape), second_back.reshape(weight.shape)
+    held = call(
+        flip_kernel, "flip", (w_first[0], w_second[0], fields),
+        (raw_weight,) * 4 + (state_shape,) * 3, (), 16 * 1024 * 1024,
+    )
+    first_held, second_held, first_back, second_back = (part.reshape(weight.shape) for part in held[:4])
+    state, act, grad = held[4:]
 
     partial_shape = array((3, cells + 2 * plane, width), F32)
 
-    def own(state, act, grad):
+    def own(state, act, grad, first, second):
         (partial,) = call(
             functools.partial(own_kernel, ydim, zdim), "own_sums",
             (state, act, grad, first, second, second_back), (partial_shape,), (small_stack,),
@@ -509,13 +517,14 @@
         )
         return partial
 
-    partial = own(state, act, grad)
+    partial = own(state, act, grad, first_held, second_held)
     paired = last_section == 1
     pair_shape = array((2, cells, 2 * width), BF16)
     tick_outs = (state_shape, pair_shape, wide, wide, wide)
     forward, sent, back, carry, gate = call(
         functools.partial(tick_kernel, ydim, zdim, paired), "tick_one",
-        (state, act, grad, near, far, first, second, first_back, second_back, partial), tick_outs,
+        (state, act, grad, far, near, first_held, second_held, first_back, second_back, partial),
+        tick_outs,
         (tile, tile, wide, state_shape, outer_stack), 16 * 1024 * 1024, flops=8 * work,
     )
     if paired:
@@ -536,7 +545,7 @@
         (sums_shape,), (small_stack,), 16 * 1024 * 1024, flops=2 * work,
     )
 
-    partial = own(state_two, act_two, grad_two)
+    partial = own(state_two, act_two, grad_two, first, second)
     rows = offsets // count
     direct = rows % 24 == 0
     if direct:
@@ -548,7 +557,7 @@
     results = (state_shape,) * 3
     made = call(
         functools.partial(last_kernel, ydim, zdim, factor, count, direct), "tick_two",
-        (state_two, act_two, grad_two, near, far, first, second, first_back, second_back, partial,
+        (state_two, act_two, grad_two, far, near, first, second, first_back, second_back, partial,
          so_far),
         results + outs,
         results + outs + (tile, tile, wide, wide, wide, wide, outer_stack, sums_shape),

time: 65.3 us -> 67.8 us (1.038)
  waiting for transfers between devices: 14.1 us -> 24 us
  starting transfers between devices: 29.6 us -> 23.4 us
  local copies, waits for them, and re-layouts: 5.93 us -> 4.21 us
    ppermute x10, starting transfers between devices: 20.8 us -> 12.9 us  [swapped(): lax.ppermute(send, 'space', [(i, i ^ bit) for i in range(count)])]
    ppermute x2, waiting for transfers between devices: 0.85 us -> 5.85 us  [exchange(): near = lax.ppermute(near, 'space', beside)]
    ppermute x10, waiting for transfers between devices: 11.7 us -> 16.7 us  [swapped(): lax.ppermute(send, 'space', [(i, i ^ bit) for i in range(count)])]
    unnamed x20 -> x16, local copies, waits for them, and re-layouts: 5.07 us -> 3.36 us
    ppermute x2, starting transfers between devices: 7.29 us -> 8.88 us  [exchange(): near = lax.ppermute(near, 'space', beside)]
  transfers between devices with their start and end apart: 15 -> 15, of which waited for: 8 -> 11; matrix products, arithmetic and copies ran while one was open for 1% -> 1% of each run, Pallas kernels for 7% -> 7%
where the time goes in v10:
time: 67.8 us; the launch traced here: 67.5 us
  waiting for transfers between devices  24 us (35%)
  starting transfers between devices  23.4 us (35%)
  Pallas kernels  14.5 us (21%)
  local copies, waits for them, and re-layouts  4.21 us (6%)
  between operations  0.91 us (1%)
    ppermute x10, waiting for transfers between devices, swapped(): lax.ppermute(send, 'space', [(i, i ^ bit) for i in range(count)])  16.7 us
    pallas_call x8, Pallas kernels, call(): pl.pallas_call(kernel, out_shape=tuple(outs), in_specs=[places[0]] * (len...  14.5 us
    ppermute x10, starting transfers between devices, swapped(): lax.ppermute(send, 'space', [(i, i ^ bit) for i in range(count)])  12.9 us
    ppermute x2, starting transfers between devices, exchange(): near = lax.ppermute(near, 'space', beside)  8.88 us
    ppermute x2, waiting for transfers between devices, exchange(): near = lax.ppermute(near, 'space', beside)  5.85 us
    unnamed x16, local copies, waits for them, and re-layouts  3.36 us
    ppermute x1, waiting for transfers between devices, shards(): lifted = lowered = lax.ppermute(sent, 'section', [(0, 1), (1, 0)])  1.52 us
    ppermute x2, starting transfers between devices, exchange(): far = lax.ppermute(far, 'space', across)  1.52 us
  transfers between devices with their start and end apart: 15, of which 11 were waited for; matrix products, arithmetic and copies ran while one was open for 1% of the time, Pallas kernels for 7%

profile of v10, /device:TPU:0, one launch (start us, length us, event | category | flops | bytes accessed | tf_op | source)
XLA Modules:
  0.0 67.5 jit_solution(18245276792710412723)
XLA Ops:
  0.6 2.1 %edges.1 = (bf16[576,128]{1,0:T(8,128)(2,1)}, bf16[576,128]{1,0:T(8,128)(2,1)}, bf16[3,256,256]{2,1,0:T(8,128)(2,1)}) custom-call(bf16[256,256]{1,0:T(8,128)(2,1)} %bitcast.100, bf16[256,256]{1,0:T(8,128)(2,1)} %bitcast.101, bf16[256,256]{1,0:T(8,128)(2,1)} %bitcast.84), custom_call_target="tpu_custom_call" | custom-call | bytes 393216 | tf_op jit(solution)/shard_map/edges/pallas_call | solution.py:483
  2.8 0.7 collective-permute-start
  3.5 5.7 %collective-permute-start.1 = (bf16[576,128]{1,0:T(8,128)(2,1)}, bf16[576,128]{1,0:T(8,128)(2,1)S(1)}, u32[]{:S(2)}, u32[]{:S(2)}) collective-permute-start(bf16[576,128]{1,0:T(8,128)(2,1)} %get-tuple-element.39), channel_id=1, source_target_pairs={{0,1},{1,0},{2,3},{3,2},{4,5},{5,4},{6,7},{7,6},{8,9},{9,8},{10,11... | collective-permute-start | bytes 442376 | tf_op jit(solution)/shard_map/ppermute | solution.py:467
  9.2 1.2 %copy-done = bf16[1,27,128,128]{3,2,1,0:T(8,128)(2,1)S(1)} copy-done((bf16[1,27,128,128]{3,2,1,0:T(8,128)(2,1)S(1)}, bf16[1,27,128,128]{3,2,1,0:T(8,128)(2,1)}, u32[]{:S(2)}) %copy-start) | copy-done | bytes 884760
  10.4 1.2 %copy-done.2 = bf16[1,27,128,128]{3,2,1,0:T(8,128)(2,1)S(1)} copy-done((bf16[1,27,128,128]{3,2,1,0:T(8,128)(2,1)S(1)}, bf16[1,27,128,128]{3,2,1,0:T(8,128)(2,1)}, u32[]{:S(2)}) %copy-start.2) | copy-done | bytes 884760
  11.5 1.0 %copy-done.5 = bf16[3,256,256]{2,1,0:T(8,128)(2,1)S(1)} copy-done((bf16[3,256,256]{2,1,0:T(8,128)(2,1)S(1)}, bf16[3,256,256]{2,1,0:T(8,128)(2,1)}, u32[]{:S(2)}) %copy-start.5) | copy-done | bytes 393240
  13.1 1.6 %own_sums.2.partial = f32[3,384,128]{2,1,0:T(8,128)S(1)} custom-call(bf16[256,256]{1,0:T(8,128)(2,1)S(1)} %get-tuple-element.35.state, bf16[256,256]{1,0:T(8,128)(2,1)S(1)} %get-tuple-element.36.act, bf16[256,256]{1,0:T(8,128)(2,1)S(1)} %get-tuple-element.37.grad, bf16[3,1152,128]{2,1,0:T(8,128)(2,1)S(1)} %bitcast.78, bf16[3,1152,128]{2,1,0:T(8,128)(2,1)S(1)} %bitcast.80, ...), custom_call_target="tpu_custom_call" | custom-call | flops 452984832 | bytes 3047424 | tf_op jit(solution)/shard_map/own_sums/pallas_call | solution.py:483
  14.8 1.3 %collective-permute-done.1.near = bf16[576,128]{1,0:T(8,128)(2,1)S(1)} collective-permute-done((bf16[576,128]{1,0:T(8,128)(2,1)}, bf16[576,128]{1,0:T(8,128)(2,1)S(1)}, u32[]{:S(2)}, u32[]{:S(2)}) %collective-permute-start.1) | collective-permute-done | bytes 147488 | tf_op jit(solution)/shard_map/ppermute | solution.py:467
  16.0 2.6 %tick_one.1 = (bf16[256,256]{1,0:T(8,128)(2,1)S(1)}, bf16[2,256,256]{2,1,0:T(8,128)(2,1)S(1)}, bf16[384,128]{1,0:T(8,128)(2,1)S(1)}, bf16[384,128]{1,0:T(8,128)(2,1)S(1)}, bf16[384,128]{1,0:T(8,128)(2,1)S(1)}) custom-call(bf16[256,256]{1,0:T(8,128)(2,1)S(1)} %get-tuple-element.35.state, bf16[256,256]{1,0:T(8,128)(2,1)S(1)} %get-tuple-element.36.act, ...), custom_call_target="tpu_custom_call" | custom-call | flops 1811939328 | bytes 4521984 | tf_op jit(solution)/shard_map/tick_one/pallas_call | solution.py:483
  18.7 1.5 %collective-permute-done.2.lifted.lowered = bf16[2,256,256]{2,1,0:T(8,128)(2,1)S(1)} collective-permute-done((bf16[2,256,256]{2,1,0:T(8,128)(2,1)S(1)}, bf16[2,256,256]{2,1,0:T(8,128)(2,1)S(1)}, u32[]{:S(2)}, u32[]{:S(2)}) %collective-permute-start.2) | collective-permute-done | bytes 262176 | tf_op jit(solution)/shard_map/ppermute | solution.py:531
  20.4 0.9 %collective-permute-start.3 = (bf16[576,128]{1,0:T(8,128)(2,1)S(1)}, bf16[576,128]{1,0:T(8,128)(2,1)S(1)}, u32[]{:S(2)}, u32[]{:S(2)}) collective-permute-start(bf16[576,128]{1,0:T(8,128)(2,1)S(1)} %get-tuple-element.49), channel_id=1, source_target_pairs={{1,2},{2,1},{3,4},{4,3},{5,6},{6,5},{7,8},{8,7},{9,10},{10,9},{11,... | collective-permute-start | bytes 442376 | tf_op jit(solution)/shard_map/ppermute | solution.py:466
  21.2 3.1 %collective-permute-start.4 = (bf16[576,128]{1,0:T(8,128)(2,1)S(1)}, bf16[576,128]{1,0:T(8,128)(2,1)S(1)}, u32[]{:S(2)}, u32[]{:S(2)}) collective-permute-start(bf16[576,128]{1,0:T(8,128)(2,1)S(1)} %get-tuple-element.50), channel_id=1, source_target_pairs={{0,1},{1,0},{2,3},{3,2},{4,5},{5,4},{6,7},{7,6},{8,9},{9,8},{10,11... | collective-permute-start | bytes 442376 | tf_op jit(solution)/shard_map/ppermute | solution.py:467
  24.4 0.8 %weight_grads.1.so_far = f32[2,3456,128]{2,1,0:T(8,128)S(1)} custom-call(bf16[256,256]{1,0:T(8,128)(2,1)S(1)} %bitcast.85, bf16[384,128]{1,0:T(8,128)(2,1)S(1)} %get-tuple-element.51.back, bf16[384,128]{1,0:T(8,128)(2,1)S(1)} %get-tuple-element.52.carry, bf16[384,128]{1,0:T(8,128)(2,1)S(1)} %get-tuple-element.53.gate), custom_call_target="tpu_custom_call" | custom-call | flops 452984832 | bytes 425984 | tf_op jit(solution)/shard_map/weight_grads/pallas_call | solution.py:483
  25.2 1.6 %own_sums.3.partial = f32[3,384,128]{2,1,0:T(8,128)S(1)} custom-call(bf16[256,256]{1,0:T(8,128)(2,1)S(1)} %get-tuple-element.46.state, bf16[256,256]{1,0:T(8,128)(2,1)S(1)} %get-tuple-element.47.act, bf16[256,256]{1,0:T(8,128)(2,1)S(1)} %get-tuple-element.48.grad, bf16[3,1152,128]{2,1,0:T(8,128)(2,1)S(1)} %bitcast.73, bf16[3,1152,128]{2,1,0:T(8,128)(2,1)S(1)} %bitcast.76, ...), custom_call_target="tpu_custom_call" | custom-call | flops 452984832 | bytes 3047424 | tf_op jit(solution)/shard_map/own_sums/pallas_call | solution.py:483
  26.8 4.6 %collective-permute-done.4.near = bf16[576,128]{1,0:T(8,128)(2,1)S(1)} collective-permute-done((bf16[576,128]{1,0:T(8,128)(2,1)S(1)}, bf16[576,128]{1,0:T(8,128)(2,1)S(1)}, u32[]{:S(2)}, u32[]{:S(2)}) %collective-permute-start.4) | collective-permute-done | bytes 147488 | tf_op jit(solution)/shard_map/ppermute | solution.py:467
  31.4 5.0 %tick_two.1 = (bf16[256,256]{1,0:T(8,128)(2,1)}, bf16[256,256]{1,0:T(8,128)(2,1)}, bf16[256,256]{1,0:T(8,128)(2,1)}, bf16[8,144,128]{2,1,0:T(8,128)(2,1)S(1)}, b...) custom-call(bf16[256,256]{1,0:T(8,128)(2,1)S(1)} %get-tuple-element., ...), custom_call_target="tpu_custom_call" | custom-call | flops 2038431744 | bytes 6291456 | tf_op jit(solution)/shard_map/tick_two/pallas_call | solution.py:483
  36.4 2.1 %collective-permute-start.5 = (bf16[8,144,128]{2,1,0:T(8,128)(2,1)S(1)}, bf16[8,144,128]{2,1,0:T(8,128)(2,1)S(1)}, u32[]{:S(2)}, u32[]{:S(2)}) collective-permute-start(bf16[8,144,128]{2,1,0:T(8,128)(2,1)S(1)} %get-tuple-element.58), channel_id=1, source_target_pairs={{0,1},{1,0},{2,3},{3,2},{4,5},{5,4},{6,7},{7,6},{8,9},{9,8},{10,11... | collective-permute-start | bytes 884744 | tf_op jit(solution)/shard_map/ppermute | solution.py:430
  38.5 1.2 %collective-permute-start.8 = (bf16[8,144,128]{2,1,0:T(8,128)(2,1)S(1)}, bf16[8,144,128]{2,1,0:T(8,128)(2,1)S(1)}, u32[]{:S(2)}, u32[]{:S(2)}) collective-permute-start(bf16[8,144,128]{2,1,0:T(8,128)(2,1)S(1)} %get-tuple-element.60), channel_id=1, source_target_pairs={{0,2},{1,3},{2,0},{3,1},{4,6},{5,7},{6,4},{7,5},{8,10},{9,11},{10,... | collective-permute-start | bytes 884744 | tf_op jit(solution)/shard_map/ppermute | solution.py:430
  39.7 1.6 %collective-permute-start.11 = (bf16[8,144,128]{2,1,0:T(8,128)(2,1)S(1)}, bf16[8,144,128]{2,1,0:T(8,128)(2,1)S(1)}, u32[]{:S(2)}, u32[]{:S(2)}) collective-permute-start(bf16[8,144,128]{2,1,0:T(8,128)(2,1)S(1)} %get-tuple-element.62), channel_id=1, source_target_pairs={{0,4},{1,5},{2,6},{3,7},{4,0},{5,1},{6,2},{7,3},{8,12},{9,13},{10,... | collective-permute-start | bytes 884744 | tf_op jit(solution)/shard_map/ppermute | solution.py:430
  41.3 4.2 %collective-permute-done.5 = bf16[8,144,128]{2,1,0:T(8,128)(2,1)S(1)} collective-permute-done((bf16[8,144,128]{2,1,0:T(8,128)(2,1)S(1)}, bf16[8,144,128]{2,1,0:T(8,128)(2,1)S(1)}, u32[]{:S(2)}, u32[]{:S(2)}) %collective-permute-start.5) | collective-permute-done | bytes 294944 | tf_op jit(solution)/shard_map/ppermute | solution.py:430
  45.6 0.8 %collective-permute-start.6 = (bf16[4,144,128]{2,1,0:T(8,128)(2,1)S(1)}, bf16[4,144,128]{2,1,0:T(8,128)(2,1)S(1)}, u32[]{:S(2)}, u32[]{:S(2)}) collective-permute-start(bf16[4,144,128]{2,1,0:T(8,128)(2,1)S(1)} %dynamic-slice_bitcast_fusion.2), channel_id=1, source_target_pairs={{0,2},{1,3},{2,0},{3,1},{4,6},{5,7},{6,4},{7,5},{8,10},{9,11},{10,... | collective-permute-start | bytes 442376 | tf_op jit(solution)/shard_map/ppermute | solution.py:430
  47.1 2.6 %collective-permute-start.9 = (bf16[4,144,128]{2,1,0:T(8,128)(2,1)S(1)}, bf16[4,144,128]{2,1,0:T(8,128)(2,1)S(1)}, u32[]{:S(2)}, u32[]{:S(2)}) collective-permute-start(bf16[4,144,128]{2,1,0:T(8,128)(2,1)S(1)} %dynamic-slice_bitcast_fusion.1), channel_id=1, source_target_pairs={{0,4},{1,5},{2,6},{3,7},{4,0},{5,1},{6,2},{7,3},{8,12},{9,13},{10,... | collective-permute-start | bytes 442376 | tf_op jit(solution)/shard_map/ppermute | solution.py:430
  50.1 0.7 %collective-permute-done.6 = bf16[4,144,128]{2,1,0:T(8,128)(2,1)S(1)} collective-permute-done((bf16[4,144,128]{2,1,0:T(8,128)(2,1)S(1)}, bf16[4,144,128]{2,1,0:T(8,128)(2,1)S(1)}, u32[]{:S(2)}, u32[]{:S(2)}) %collective-permute-start.6) | collective-permute-done | bytes 147488 | tf_op jit(solution)/shard_map/ppermute | solution.py:430
  50.9 2.1 %collective-permute-start.7 = (bf16[2,144,128]{2,1,0:T(8,128)(2,1)S(1)}, bf16[2,144,128]{2,1,0:T(8,128)(2,1)S(1)}, u32[]{:S(2)}, u32[]{:S(2)}) collective-permute-start(bf16[2,144,128]{2,1,0:T(8,128)(2,1)S(1)} %dynamic-slice_bitcast_fusion.5), channel_id=1, source_target_pairs={{0,4},{1,5},{2,6},{3,7},{4,0},{5,1},{6,2},{7,3},{8,12},{9,13},{10,... | collective-permute-start | bytes 221192 | tf_op jit(solution)/shard_map/ppermute | solution.py:430
  53.0 0.6 collective-permute-done.9
  53.6 1.2 %collective-permute-start.10 = (bf16[2,144,128]{2,1,0:T(8,128)(2,1)S(1)}, bf16[2,144,128]{2,1,0:T(8,128)(2,1)S(1)}, u32[]{:S(2)}, u32[]{:S(2)}) collective-permute-start(bf16[2,144,128]{2,1,0:T(8,128)(2,1)S(1)} %dynamic-slice_bitcast_fusion.4), channel_id=1, source_target_pairs={{0,1},{1,0},{2,3},{3,2},{4,5},{5,4},{6,7},{7,6},{8,9},{9,8},{10,11... | collective-permute-start | bytes 221192 | tf_op jit(solution)/shard_map/ppermute | solution.py:430
  54.8 0.9 %collective-permute-done.12 = bf16[4,144,128]{2,1,0:T(8,128)(2,1)S(1)} collective-permute-done((bf16[4,144,128]{2,1,0:T(8,128)(2,1)S(1)}, bf16[4,144,128]{2,1,0:T(8,128)(2,1)S(1)}, u32[]{:S(2)}, u32[]{:S(2)}) %collective-permute-start.12) | collective-permute-done | bytes 147488 | tf_op jit(solution)/shard_map/ppermute | solution.py:430
  56.0 2.1 %collective-permute-done.10 = bf16[2,144,128]{2,1,0:T(8,128)(2,1)S(1)} collective-permute-done((bf16[2,144,128]{2,1,0:T(8,128)(2,1)S(1)}, bf16[2,144,128]{2,1,0:T(8,128)(2,1)S(1)}, u32[]{:S(2)}, u32[]{:S(2)}) %collective-permute-start.10) | collective-permute-done | bytes 73760 | tf_op jit(solution)/shard_map/ppermute | solution.py:430
  58.1 2.2 %collective-permute-done.13 = bf16[2,144,128]{2,1,0:T(8,128)(2,1)S(1)} collective-permute-done((bf16[2,144,128]{2,1,0:T(8,128)(2,1)S(1)}, bf16[2,144,128]{2,1,0:T(8,128)(2,1)S(1)}, u32[]{:S(2)}, u32[]{:S(2)}) %collective-permute-start.13) | collective-permute-done | bytes 73760 | tf_op jit(solution)/shard_map/ppermute | solution.py:430
  60.3 1.0 %collective-permute-start.14 = (bf16[432,128]{1,0:T(8,128)(2,1)S(1)}, bf16[432,128]{1,0:T(8,128)(2,1)S(1)}, u32[]{:S(2)}, u32[]{:S(2)}) collective-permute-start(bf16[432,128]{1,0:T(8,128)(2,1)S(1)} %pad_maximum_fusion), channel_id=1, source_target_pairs={{0,8},{1,9},{2,10},{3,11},{4,12},{5,13},{6,14},{7,15},{8,0},{9,1},... | collective-permute-start | bytes 331784 | tf_op jit(solution)/shard_map/ppermute | solution.py:430
  61.4 5.4 %collective-permute-done.14 = bf16[432,128]{1,0:T(8,128)(2,1)S(1)} collective-permute-done((bf16[432,128]{1,0:T(8,128)(2,1)S(1)}, bf16[432,128]{1,0:T(8,128)(2,1)S(1)}, u32[]{:S(2)}, u32[]{:S(2)}) %collective-permute-start.14) | collective-permute-done | bytes 110624 | tf_op jit(solution)/shard_map/ppermute | solution.py:430
  66.8 0.7 %slice_bitcast_fusion = (f32[1,216,128]{2,1,0:T(8,128)}, f32[1,216,128]{2,1,0:T(8,128)}) fusion(f32[432,128]{1,0:T(8,128)S(1)} %convert_add_fusion.3), kind=kLoop, calls=%fused_computation.19 | loop fusion | bytes 442368 | tf_op jit(solution)/shard_map/broadcast_in_dim | solution.py:574
  (43 shorter events, 2.5 us)
Async XLA Ops:
  2.8 12.0 %collective-permute-start = (bf16[576,128]{1,0:T(8,128)(2,1)}, bf16[576,128]{1,0:T(8,128)(2,1)S(1)}, u32[]{:S(2)}, u32[]{:S(2)}) collective-permute-start(bf16[576,128]{1,0:T(8,128)(2,1)} %get-tuple-element.38), channel_id=1, source_target_pairs={{1,2},{2,1},{3,4},{4,3},{5,6},{6,5},{7,8},{8,7},{9,10},{10,9},{11,... | collective-permute-start | bytes 442376 | tf_op jit(solution)/shard_map/ppermute | solution.py:466
  3.5 12.6 %collective-permute-start.1 = (bf16[576,128]{1,0:T(8,128)(2,1)}, bf16[576,128]{1,0:T(8,128)(2,1)S(1)}, u32[]{:S(2)}, u32[]{:S(2)}) collective-permute-start(bf16[576,128]{1,0:T(8,128)(2,1)} %get-tuple-element.39), channel_id=1, source_target_pairs={{0,1},{1,0},{2,3},{3,2},{4,5},{5,4},{6,7},{7,6},{8,9},{9,8},{10,11... | collective-permute-start | bytes 442376 | tf_op jit(solution)/shard_map/ppermute | solution.py:467
  9.2 1.2 %copy-start = (bf16[1,27,128,128]{3,2,1,0:T(8,128)(2,1)S(1)}, bf16[1,27,128,128]{3,2,1,0:T(8,128)(2,1)}, u32[]{:S(2)}) copy-start(bf16[1,27,128,128]{3,2,1,0:T(8,128)(2,1)} %param.12) | copy-start | bytes 2654212
  10.4 1.2 %copy-start.2 = (bf16[1,27,128,128]{3,2,1,0:T(8,128)(2,1)S(1)}, bf16[1,27,128,128]{3,2,1,0:T(8,128)(2,1)}, u32[]{:S(2)}) copy-start(bf16[1,27,128,128]{3,2,1,0:T(8,128)(2,1)} %param.13) | copy-start | bytes 2654212
  11.5 1.0 %copy-start.5 = (bf16[3,256,256]{2,1,0:T(8,128)(2,1)S(1)}, bf16[3,256,256]{2,1,0:T(8,128)(2,1)}, u32[]{:S(2)}) copy-start(bf16[3,256,256]{2,1,0:T(8,128)(2,1)} %get-tuple-element.34.fields) | copy-start | bytes 1179652
  14.7 5.5 %copy-start.6 = (bf16[4,8,8,256]{3,2,1,0:T(8,128)(2,1)S(1)}, bf16[4,8,8,256]{3,2,1,0:T(8,128)(2,1)}, u32[]{:S(2)}) copy-start(bf16[4,8,8,256]{3,2,1,0:T(8,128)(2,1)} %param.10) | copy-start | bytes 393220
  14.7 5.5 %copy-start.7 = (bf16[4,8,8,256]{3,2,1,0:T(8,128)(2,1)S(1)}, bf16[4,8,8,256]{3,2,1,0:T(8,128)(2,1)}, u32[]{:S(2)}) copy-start(bf16[4,8,8,256]{3,2,1,0:T(8,128)(2,1)} %param.11) | copy-start | bytes 393220
  16.0 8.3 %copy-start.4 = (bf16[1,4,8,8,256]{4,3,2,1,0:T(8,128)(2,1)S(1)}, bf16[1,4,8,8,256]{4,3,2,1,0:T(8,128)(2,1)}, u32[]{:S(2)}) copy-start(bf16[1,4,8,8,256]{4,3,2,1,0:T(8,128)(2,1)} %param.9) | copy-start | bytes 393220
  18.6 6.6 %copy-start.1 = (bf16[1,27,128,128]{3,2,1,0:T(8,128)(2,1)S(1)}, bf16[1,27,128,128]{3,2,1,0:T(8,128)(2,1)}, u32[]{:S(2)}) copy-start(bf16[1,27,128,128]{3,2,1,0:T(8,128)(2,1)} %param.12) | copy-start | bytes 2654212
  18.6 6.6 %copy-start.3 = (bf16[1,27,128,128]{3,2,1,0:T(8,128)(2,1)S(1)}, bf16[1,27,128,128]{3,2,1,0:T(8,128)(2,1)}, u32[]{:S(2)}) copy-start(bf16[1,27,128,128]{3,2,1,0:T(8,128)(2,1)} %param.13) | copy-start | bytes 2654212
  18.6 1.6 %collective-permute-start.2 = (bf16[2,256,256]{2,1,0:T(8,128)(2,1)S(1)}, bf16[2,256,256]{2,1,0:T(8,128)(2,1)S(1)}, u32[]{:S(2)}, u32[]{:S(2)}) collective-permute-start(bf16[2,256,256]{2,1,0:T(8,128)(2,1)S(1)} %get-tuple-element.45), channel_id=1, source_target_pairs={{0,16},{16,0},{1,17},{17,1},{2,18},{18,2},{3,19},{19,3},{4,20},{20... | collective-permute-start | bytes 786440 | tf_op jit(solution)/shard_map/ppermute | solution.py:531
  20.4 6.5 %collective-permute-start.3 = (bf16[576,128]{1,0:T(8,128)(2,1)S(1)}, bf16[576,128]{1,0:T(8,128)(2,1)S(1)}, u32[]{:S(2)}, u32[]{:S(2)}) collective-permute-start(bf16[576,128]{1,0:T(8,128)(2,1)S(1)} %get-tuple-element.49), channel_id=1, source_target_pairs={{1,2},{2,1},{3,4},{4,3},{5,6},{6,5},{7,8},{8,7},{9,10},{10,9},{11,... | collective-permute-start | bytes 442376 | tf_op jit(solution)/shard_map/ppermute | solution.py:466
  21.2 10.2 %collective-permute-start.4 = (bf16[576,128]{1,0:T(8,128)(2,1)S(1)}, bf16[576,128]{1,0:T(8,128)(2,1)S(1)}, u32[]{:S(2)}, u32[]{:S(2)}) collective-permute-start(bf16[576,128]{1,0:T(8,128)(2,1)S(1)} %get-tuple-element.50), channel_id=1, source_target_pairs={{0,1},{1,0},{2,3},{3,2},{4,5},{5,4},{6,7},{7,6},{8,9},{9,8},{10,11... | collective-permute-start | bytes 442376 | tf_op jit(solution)/shard_map/ppermute | solution.py:467
  36.4 9.1 %collective-permute-start.5 = (bf16[8,144,128]{2,1,0:T(8,128)(2,1)S(1)}, bf16[8,144,128]{2,1,0:T(8,128)(2,1)S(1)}, u32[]{:S(2)}, u32[]{:S(2)}) collective-permute-start(bf16[8,144,128]{2,1,0:T(8,128)(2,1)S(1)} %get-tuple-element.58), channel_id=1, source_target_pairs={{0,1},{1,0},{2,3},{3,2},{4,5},{5,4},{6,7},{7,6},{8,9},{9,8},{10,11... | collective-permute-start | bytes 884744 | tf_op jit(solution)/shard_map/ppermute | solution.py:430
  38.5 8.4 %collective-permute-start.8 = (bf16[8,144,128]{2,1,0:T(8,128)(2,1)S(1)}, bf16[8,144,128]{2,1,0:T(8,128)(2,1)S(1)}, u32[]{:S(2)}, u32[]{:S(2)}) collective-permute-start(bf16[8,144,128]{2,1,0:T(8,128)(2,1)S(1)} %get-tuple-element.60), channel_id=1, source_target_pairs={{0,2},{1,3},{2,0},{3,1},{4,6},{5,7},{6,4},{7,5},{8,10},{9,11},{10,... | collective-permute-start | bytes 884744 | tf_op jit(solution)/shard_map/ppermute | solution.py:430
  39.7 10.0 %collective-permute-start.11 = (bf16[8,144,128]{2,1,0:T(8,128)(2,1)S(1)}, bf16[8,144,128]{2,1,0:T(8,128)(2,1)S(1)}, u32[]{:S(2)}, u32[]{:S(2)}) collective-permute-start(bf16[8,144,128]{2,1,0:T(8,128)(2,1)S(1)} %get-tuple-element.62), channel_id=1, source_target_pairs={{0,4},{1,5},{2,6},{3,7},{4,0},{5,1},{6,2},{7,3},{8,12},{9,13},{10,... | collective-permute-start | bytes 884744 | tf_op jit(solution)/shard_map/ppermute | solution.py:430
  45.6 5.2 %collective-permute-start.6 = (bf16[4,144,128]{2,1,0:T(8,128)(2,1)S(1)}, bf16[4,144,128]{2,1,0:T(8,128)(2,1)S(1)}, u32[]{:S(2)}, u32[]{:S(2)}) collective-permute-start(bf16[4,144,128]{2,1,0:T(8,128)(2,1)S(1)} %dynamic-slice_bitcast_fusion.2), channel_id=1, source_target_pairs={{0,2},{1,3},{2,0},{3,1},{4,6},{5,7},{6,4},{7,5},{8,10},{9,11},{10,... | collective-permute-start | bytes 442376 | tf_op jit(solution)/shard_map/ppermute | solution.py:430
  47.1 6.5 %collective-permute-start.9 = (bf16[4,144,128]{2,1,0:T(8,128)(2,1)S(1)}, bf16[4,144,128]{2,1,0:T(8,128)(2,1)S(1)}, u32[]{:S(2)}, u32[]{:S(2)}) collective-permute-start(bf16[4,144,128]{2,1,0:T(8,128)(2,1)S(1)} %dynamic-slice_bitcast_fusion.1), channel_id=1, source_target_pairs={{0,4},{1,5},{2,6},{3,7},{4,0},{5,1},{6,2},{7,3},{8,12},{9,13},{10,... | collective-permute-start | bytes 442376 | tf_op jit(solution)/shard_map/ppermute | solution.py:430
  49.8 6.0 %collective-permute-start.12 = (bf16[4,144,128]{2,1,0:T(8,128)(2,1)S(1)}, bf16[4,144,128]{2,1,0:T(8,128)(2,1)S(1)}, u32[]{:S(2)}, u32[]{:S(2)}) collective-permute-start(bf16[4,144,128]{2,1,0:T(8,128)(2,1)S(1)} %dynamic-slice_bitcast_fusion), channel_id=1, source_target_pairs={{0,1},{1,0},{2,3},{3,2},{4,5},{5,4},{6,7},{7,6},{8,9},{9,8},{10,11... | collective-permute-start | bytes 442376 | tf_op jit(solution)/shard_map/ppermute | solution.py:430
  50.9 5.0 %collective-permute-start.7 = (bf16[2,144,128]{2,1,0:T(8,128)(2,1)S(1)}, bf16[2,144,128]{2,1,0:T(8,128)(2,1)S(1)}, u32[]{:S(2)}, u32[]{:S(2)}) collective-permute-start(bf16[2,144,128]{2,1,0:T(8,128)(2,1)S(1)} %dynamic-slice_bitcast_fusion.5), channel_id=1, source_target_pairs={{0,4},{1,5},{2,6},{3,7},{4,0},{5,1},{6,2},{7,3},{8,12},{9,13},{10,... | collective-permute-start | bytes 221192 | tf_op jit(solution)/shard_map/ppermute | solution.py:430
  53.6 4.4 %collective-permute-start.10 = (bf16[2,144,128]{2,1,0:T(8,128)(2,1)S(1)}, bf16[2,144,128]{2,1,0:T(8,128)(2,1)S(1)}, u32[]{:S(2)}, u32[]{:S(2)}) collective-permute-start(bf16[2,144,128]{2,1,0:T(8,128)(2,1)S(1)} %dynamic-slice_bitcast_fusion.4), channel_id=1, source_target_pairs={{0,1},{1,0},{2,3},{3,2},{4,5},{5,4},{6,7},{7,6},{8,9},{9,8},{10,11... | collective-permute-start | bytes 221192 | tf_op jit(solution)/shard_map/ppermute | solution.py:430
  55.8 4.4 %collective-permute-start.13 = (bf16[2,144,128]{2,1,0:T(8,128)(2,1)S(1)}, bf16[2,144,128]{2,1,0:T(8,128)(2,1)S(1)}, u32[]{:S(2)}, u32[]{:S(2)}) collective-permute-start(bf16[2,144,128]{2,1,0:T(8,128)(2,1)S(1)} %dynamic-slice_bitcast_fusion.3), channel_id=1, source_target_pairs={{0,2},{1,3},{2,0},{3,1},{4,6},{5,7},{6,4},{7,5},{8,10},{9,11},{10,... | collective-permute-start | bytes 221192 | tf_op jit(solution)/shard_map/ppermute | solution.py:430
  60.3 6.4 %collective-permute-start.14 = (bf16[432,128]{1,0:T(8,128)(2,1)S(1)}, bf16[432,128]{1,0:T(8,128)(2,1)S(1)}, u32[]{:S(2)}, u32[]{:S(2)}) collective-permute-start(bf16[432,128]{1,0:T(8,128)(2,1)S(1)} %pad_maximum_fusion), channel_id=1, source_target_pairs={{0,8},{1,9},{2,10},{3,11},{4,12},{5,13},{6,14},{7,15},{8,0},{9,1},... | collective-permute-start | bytes 331784 | tf_op jit(solution)/shard_map/ppermute | solution.py:430

commit v11 on v10

--- a/solution.py
+++ b/solution.py
@@ -285,7 +285,7 @@
     made("forward")
 
 
-def tick_kernel(ydim, zdim, paired, state, act, grad, far, near, first, second,
+def tick_kernel(ydim, zdim, paired, state, act, grad, near, far, first, second,
                 first_back, second_back, partial, forward, sent, back, carry, gate, new_one, back_two, mid,
                 rebuilt, stack):
     copies = Copies(None)
@@ -344,7 +344,7 @@
     return [(way * span, span, order) for way, order in enumerate(orders)]
 
 
-def last_kernel(ydim, zdim, factor, count, direct, state, act, grad, far, near, first,
+def last_kernel(ydim, zdim, factor, count, direct, state, act, grad, near, far, first,
                 second, first_back, second_back, partial, so_far, *args):
     n_outs = 6 if direct else 1
     results_out, args = args[:3], args[3:]
@@ -523,7 +523,7 @@
     tick_outs = (state_shape, pair_shape, wide, wide, wide)
     forward, sent, back, carry, gate = call(
         functools.partial(tick_kernel, ydim, zdim, paired), "tick_one",
-        (state, act, grad, far, near, first_held, second_held, first_back, second_back, partial),
+        (state, act, grad, near, far, first_held, second_held, first_back, second_back, partial),
         tick_outs,
         (tile, tile, wide, state_shape, outer_stack), 16 * 1024 * 1024, flops=8 * work,
     )
@@ -557,7 +557,7 @@
     results = (state_shape,) * 3
     made = call(
         functools.partial(last_kernel, ydim, zdim, factor, count, direct), "tick_two",
-        (state_two, act_two, grad_two, far, near, first, second, first_back, second_back, partial,
+        (state_two, act_two, grad_two, near, far, first, second, first_back, second_back, partial,
          so_far),
         results + outs,
         results + outs + (tile, tile, wide, wide, wide, wide, outer_stack, sums_shape),

time: 67.8 us -> 64.1 us (0.945)
  waiting for transfers between devices: 24 us -> 14.1 us
  starting transfers between devices: 23.4 us -> 29.6 us
    ppermute x10, starting transfers between devices: 12.9 us -> 20.8 us  [swapped(): lax.ppermute(send, 'space', [(i, i ^ bit) for i in range(count)])]
    ppermute x2, waiting for transfers between devices: 5.85 us -> 0.85 us  [exchange(): near = lax.ppermute(near, 'space', beside)]
    ppermute x10, waiting for transfers between devices: 16.7 us -> 11.7 us  [swapped(): lax.ppermute(send, 'space', [(i, i ^ bit) for i in range(count)])]
    ppermute x2, starting transfers between devices: 8.88 us -> 7.29 us  [exchange(): near = lax.ppermute(near, 'space', beside)]
  transfers between devices with their start and end apart: 15 -> 15, of which waited for: 11 -> 8; matrix products, arithmetic and copies ran while one was open for 1% -> 1% of each run, Pallas kernels for 7% -> 7%
where the time goes in v11:
time: 64.1 us; the launch traced here: 63.8 us
  starting transfers between devices  29.6 us (46%)
  Pallas kernels  14.5 us (23%)
  waiting for transfers between devices  14.1 us (22%)
  local copies, waits for them, and re-layouts  4.21 us (7%)
  between operations  0.92 us (1%)
    ppermute x10, starting transfers between devices, swapped(): lax.ppermute(send, 'space', [(i, i ^ bit) for i in range(count)])  20.8 us
    pallas_call x8, Pallas kernels, call(): pl.pallas_call(kernel, out_shape=tuple(outs), in_specs=[places[0]] * (len...  14.5 us
    ppermute x10, waiting for transfers between devices, swapped(): lax.ppermute(send, 'space', [(i, i ^ bit) for i in range(count)])  11.7 us
    ppermute x2, starting transfers between devices, exchange(): near = lax.ppermute(near, 'space', beside)  7.29 us
    unnamed x16, local copies, waits for them, and re-layouts  3.36 us
    ppermute x1, waiting for transfers between devices, shards(): lifted = lowered = lax.ppermute(sent, 'section', [(0, 1), (1, 0)])  1.52 us
    ppermute x2, starting transfers between devices, exchange(): far = lax.ppermute(far, 'space', across)  1.5 us
  transfers between devices with their start and end apart: 15, of which 8 were waited for; matrix products, arithmetic and copies ran while one was open for 1% of the time, Pallas kernels for 7%

profile of v11, /device:TPU:0, one launch (start us, length us, event | category | flops | bytes accessed | tf_op | source)
XLA Modules:
  0.0 63.8 jit_solution(9832690645208670538)
XLA Ops:
  0.6 2.1 %edges.1 = (bf16[576,128]{1,0:T(8,128)(2,1)}, bf16[576,128]{1,0:T(8,128)(2,1)}, bf16[3,256,256]{2,1,0:T(8,128)(2,1)}) custom-call(bf16[256,256]{1,0:T(8,128)(2,1)} %bitcast.100, bf16[256,256]{1,0:T(8,128)(2,1)} %bitcast.101, bf16[256,256]{1,0:T(8,128)(2,1)} %bitcast.84), custom_call_target="tpu_custom_call" | custom-call | bytes 393216 | tf_op jit(solution)/shard_map/edges/pallas_call | solution.py:483
  2.8 3.0 %collective-permute-start = (bf16[576,128]{1,0:T(8,128)(2,1)}, bf16[576,128]{1,0:T(8,128)(2,1)S(1)}, u32[]{:S(2)}, u32[]{:S(2)}) collective-permute-start(bf16[576,128]{1,0:T(8,128)(2,1)} %get-tuple-element.38), channel_id=1, source_target_pairs={{0,1},{1,0},{2,3},{3,2},{4,5},{5,4},{6,7},{7,6},{8,9},{9,8},{10,11... | collective-permute-start | bytes 442376 | tf_op jit(solution)/shard_map/ppermute | solution.py:467
  5.8 0.7 %collective-permute-start.1 = (bf16[576,128]{1,0:T(8,128)(2,1)}, bf16[576,128]{1,0:T(8,128)(2,1)S(1)}, u32[]{:S(2)}, u32[]{:S(2)}) collective-permute-start(bf16[576,128]{1,0:T(8,128)(2,1)} %get-tuple-element.39), channel_id=1, source_target_pairs={{1,2},{2,1},{3,4},{4,3},{5,6},{6,5},{7,8},{8,7},{9,10},{10,9},{11,... | collective-permute-start | bytes 442376 | tf_op jit(solution)/shard_map/ppermute | solution.py:466
  6.5 1.2 %copy-done = bf16[1,27,128,128]{3,2,1,0:T(8,128)(2,1)S(1)} copy-done((bf16[1,27,128,128]{3,2,1,0:T(8,128)(2,1)S(1)}, bf16[1,27,128,128]{3,2,1,0:T(8,128)(2,1)}, u32[]{:S(2)}) %copy-start) | copy-done | bytes 884760
  7.6 1.2 %copy-done.2 = bf16[1,27,128,128]{3,2,1,0:T(8,128)(2,1)S(1)} copy-done((bf16[1,27,128,128]{3,2,1,0:T(8,128)(2,1)S(1)}, bf16[1,27,128,128]{3,2,1,0:T(8,128)(2,1)}, u32[]{:S(2)}) %copy-start.2) | copy-done | bytes 884760
  8.8 1.0 %copy-done.5 = bf16[3,256,256]{2,1,0:T(8,128)(2,1)S(1)} copy-done((bf16[3,256,256]{2,1,0:T(8,128)(2,1)S(1)}, bf16[3,256,256]{2,1,0:T(8,128)(2,1)}, u32[]{:S(2)}) %copy-start.5) | copy-done | bytes 393240
  9.8 0.6 flip.1
  10.4 1.6 %own_sums.2.partial = f32[3,384,128]{2,1,0:T(8,128)S(1)} custom-call(bf16[256,256]{1,0:T(8,128)(2,1)S(1)} %get-tuple-element.35.state, bf16[256,256]{1,0:T(8,128)(2,1)S(1)} %get-tuple-element.36.act, bf16[256,256]{1,0:T(8,128)(2,1)S(1)} %get-tuple-element.37.grad, bf16[3,1152,128]{2,1,0:T(8,128)(2,1)S(1)} %bitcast.78, bf16[3,1152,128]{2,1,0:T(8,128)(2,1)S(1)} %bitcast.80, ...), custom_call_target="tpu_custom_call" | custom-call | flops 452984832 | bytes 3047424 | tf_op jit(solution)/shard_map/own_sums/pallas_call | solution.py:483
  12.0 2.6 %tick_one.1 = (bf16[256,256]{1,0:T(8,128)(2,1)S(1)}, bf16[2,256,256]{2,1,0:T(8,128)(2,1)S(1)}, bf16[384,128]{1,0:T(8,128)(2,1)S(1)}, bf16[384,128]{1,0:T(8,128)(2,1)S(1)}, bf16[384,128]{1,0:T(8,128)(2,1)S(1)}) custom-call(bf16[256,256]{1,0:T(8,128)(2,1)S(1)} %get-tuple-element.35.state, bf16[256,256]{1,0:T(8,128)(2,1)S(1)} %get-tuple-element.36.act, ...), custom_call_target="tpu_custom_call" | custom-call | flops 1811939328 | bytes 4521984 | tf_op jit(solution)/shard_map/tick_one/pallas_call | solution.py:483
  14.7 1.5 %collective-permute-done.2.lifted.lowered = bf16[2,256,256]{2,1,0:T(8,128)(2,1)S(1)} collective-permute-done((bf16[2,256,256]{2,1,0:T(8,128)(2,1)S(1)}, bf16[2,256,256]{2,1,0:T(8,128)(2,1)S(1)}, u32[]{:S(2)}, u32[]{:S(2)}) %collective-permute-start.2) | collective-permute-done | bytes 262176 | tf_op jit(solution)/shard_map/ppermute | solution.py:531
  16.4 4.3 %collective-permute-start.3 = (bf16[576,128]{1,0:T(8,128)(2,1)S(1)}, bf16[576,128]{1,0:T(8,128)(2,1)S(1)}, u32[]{:S(2)}, u32[]{:S(2)}) collective-permute-start(bf16[576,128]{1,0:T(8,128)(2,1)S(1)} %get-tuple-element.49), channel_id=1, source_target_pairs={{0,1},{1,0},{2,3},{3,2},{4,5},{5,4},{6,7},{7,6},{8,9},{9,8},{10,11... | collective-permute-start | bytes 442376 | tf_op jit(solution)/shard_map/ppermute | solution.py:467
  20.7 0.8 %collective-permute-start.4 = (bf16[576,128]{1,0:T(8,128)(2,1)S(1)}, bf16[576,128]{1,0:T(8,128)(2,1)S(1)}, u32[]{:S(2)}, u32[]{:S(2)}) collective-permute-start(bf16[576,128]{1,0:T(8,128)(2,1)S(1)} %get-tuple-element.50), channel_id=1, source_target_pairs={{1,2},{2,1},{3,4},{4,3},{5,6},{6,5},{7,8},{8,7},{9,10},{10,9},{11,... | collective-permute-start | bytes 442376 | tf_op jit(solution)/shard_map/ppermute | solution.py:466
  21.5 0.8 %weight_grads.1.so_far = f32[2,3456,128]{2,1,0:T(8,128)S(1)} custom-call(bf16[256,256]{1,0:T(8,128)(2,1)S(1)} %bitcast.85, bf16[384,128]{1,0:T(8,128)(2,1)S(1)} %get-tuple-element.51.back, bf16[384,128]{1,0:T(8,128)(2,1)S(1)} %get-tuple-element.52.carry, bf16[384,128]{1,0:T(8,128)(2,1)S(1)} %get-tuple-element.53.gate), custom_call_target="tpu_custom_call" | custom-call | flops 452984832 | bytes 425984 | tf_op jit(solution)/shard_map/weight_grads/pallas_call | solution.py:483
  22.4 1.6 %own_sums.3.partial = f32[3,384,128]{2,1,0:T(8,128)S(1)} custom-call(bf16[256,256]{1,0:T(8,128)(2,1)S(1)} %get-tuple-element.46.state, bf16[256,256]{1,0:T(8,128)(2,1)S(1)} %get-tuple-element.47.act, bf16[256,256]{1,0:T(8,128)(2,1)S(1)} %get-tuple-element.48.grad, bf16[3,1152,128]{2,1,0:T(8,128)(2,1)S(1)} %bitcast.73, bf16[3,1152,128]{2,1,0:T(8,128)(2,1)S(1)} %bitcast.76, ...), custom_call_target="tpu_custom_call" | custom-call | flops 452984832 | bytes 3047424 | tf_op jit(solution)/shard_map/own_sums/pallas_call | solution.py:483
  24.0 0.8 %collective-permute-done.3.near = bf16[576,128]{1,0:T(8,128)(2,1)S(1)} collective-permute-done((bf16[576,128]{1,0:T(8,128)(2,1)S(1)}, bf16[576,128]{1,0:T(8,128)(2,1)S(1)}, u32[]{:S(2)}, u32[]{:S(2)}) %collective-permute-start.3) | collective-permute-done | bytes 147488 | tf_op jit(solution)/shard_map/ppermute | solution.py:467
  24.8 5.0 %tick_two.1 = (bf16[256,256]{1,0:T(8,128)(2,1)}, bf16[256,256]{1,0:T(8,128)(2,1)}, bf16[256,256]{1,0:T(8,128)(2,1)}, bf16[8,144,128]{2,1,0:T(8,128)(2,1)S(1)}, b...) custom-call(bf16[256,256]{1,0:T(8,128)(2,1)S(1)} %get-tuple-element., ...), custom_call_target="tpu_custom_call" | custom-call | flops 2038431744 | bytes 6291456 | tf_op jit(solution)/shard_map/tick_two/pallas_call | solution.py:483
  29.8 5.9 %collective-permute-start.5 = (bf16[8,144,128]{2,1,0:T(8,128)(2,1)S(1)}, bf16[8,144,128]{2,1,0:T(8,128)(2,1)S(1)}, u32[]{:S(2)}, u32[]{:S(2)}) collective-permute-start(bf16[8,144,128]{2,1,0:T(8,128)(2,1)S(1)} %get-tuple-element.58), channel_id=1, source_target_pairs={{0,1},{1,0},{2,3},{3,2},{4,5},{5,4},{6,7},{7,6},{8,9},{9,8},{10,11... | collective-permute-start | bytes 884744 | tf_op jit(solution)/shard_map/ppermute | solution.py:430
  35.8 1.1 %collective-permute-start.8 = (bf16[8,144,128]{2,1,0:T(8,128)(2,1)S(1)}, bf16[8,144,128]{2,1,0:T(8,128)(2,1)S(1)}, u32[]{:S(2)}, u32[]{:S(2)}) collective-permute-start(bf16[8,144,128]{2,1,0:T(8,128)(2,1)S(1)} %get-tuple-element.60), channel_id=1, source_target_pairs={{0,2},{1,3},{2,0},{3,1},{4,6},{5,7},{6,4},{7,5},{8,10},{9,11},{10,... | collective-permute-start | bytes 884744 | tf_op jit(solution)/shard_map/ppermute | solution.py:430
  36.9 1.6 %collective-permute-start.11 = (bf16[8,144,128]{2,1,0:T(8,128)(2,1)S(1)}, bf16[8,144,128]{2,1,0:T(8,128)(2,1)S(1)}, u32[]{:S(2)}, u32[]{:S(2)}) collective-permute-start(bf16[8,144,128]{2,1,0:T(8,128)(2,1)S(1)} %get-tuple-element.62), channel_id=1, source_target_pairs={{0,4},{1,5},{2,6},{3,7},{4,0},{5,1},{6,2},{7,3},{8,12},{9,13},{10,... | collective-permute-start | bytes 884744 | tf_op jit(solution)/shard_map/ppermute | solution.py:430
  38.4 3.8 %collective-permute-done.5 = bf16[8,144,128]{2,1,0:T(8,128)(2,1)S(1)} collective-permute-done((bf16[8,144,128]{2,1,0:T(8,128)(2,1)S(1)}, bf16[8,144,128]{2,1,0:T(8,128)(2,1)S(1)}, u32[]{:S(2)}, u32[]{:S(2)}) %collective-permute-start.5) | collective-permute-done | bytes 294944 | tf_op jit(solution)/shard_map/ppermute | solution.py:430
  42.4 1.4 %collective-permute-start.6 = (bf16[4,144,128]{2,1,0:T(8,128)(2,1)S(1)}, bf16[4,144,128]{2,1,0:T(8,128)(2,1)S(1)}, u32[]{:S(2)}, u32[]{:S(2)}) collective-permute-start(bf16[4,144,128]{2,1,0:T(8,128)(2,1)S(1)} %dynamic-slice_bitcast_fusion.2), channel_id=1, source_target_pairs={{0,2},{1,3},{2,0},{3,1},{4,6},{5,7},{6,4},{7,5},{8,10},{9,11},{10,... | collective-permute-start | bytes 442376 | tf_op jit(solution)/shard_map/ppermute | solution.py:430
  43.9 1.6 %collective-permute-start.9 = (bf16[4,144,128]{2,1,0:T(8,128)(2,1)S(1)}, bf16[4,144,128]{2,1,0:T(8,128)(2,1)S(1)}, u32[]{:S(2)}, u32[]{:S(2)}) collective-permute-start(bf16[4,144,128]{2,1,0:T(8,128)(2,1)S(1)} %dynamic-slice_bitcast_fusion.1), channel_id=1, source_target_pairs={{0,4},{1,5},{2,6},{3,7},{4,0},{5,1},{6,2},{7,3},{8,12},{9,13},{10,... | collective-permute-start | bytes 442376 | tf_op jit(solution)/shard_map/ppermute | solution.py:430
  45.6 1.6 %collective-permute-start.12 = (bf16[4,144,128]{2,1,0:T(8,128)(2,1)S(1)}, bf16[4,144,128]{2,1,0:T(8,128)(2,1)S(1)}, u32[]{:S(2)}, u32[]{:S(2)}) collective-permute-start(bf16[4,144,128]{2,1,0:T(8,128)(2,1)S(1)} %dynamic-slice_bitcast_fusion), channel_id=1, source_target_pairs={{0,1},{1,0},{2,3},{3,2},{4,5},{5,4},{6,7},{7,6},{8,9},{9,8},{10,11... | collective-permute-start | bytes 442376 | tf_op jit(solution)/shard_map/ppermute | solution.py:430
  47.2 0.3 collective-permute-done.6
  47.6 2.3 %collective-permute-start.7 = (bf16[2,144,128]{2,1,0:T(8,128)(2,1)S(1)}, bf16[2,144,128]{2,1,0:T(8,128)(2,1)S(1)}, u32[]{:S(2)}, u32[]{:S(2)}) collective-permute-start(bf16[2,144,128]{2,1,0:T(8,128)(2,1)S(1)} %dynamic-slice_bitcast_fusion.5), channel_id=1, source_target_pairs={{0,4},{1,5},{2,6},{3,7},{4,0},{5,1},{6,2},{7,3},{8,12},{9,13},{10,... | collective-permute-start | bytes 221192 | tf_op jit(solution)/shard_map/ppermute | solution.py:430
  50.1 1.5 %collective-permute-start.10 = (bf16[2,144,128]{2,1,0:T(8,128)(2,1)S(1)}, bf16[2,144,128]{2,1,0:T(8,128)(2,1)S(1)}, u32[]{:S(2)}, u32[]{:S(2)}) collective-permute-start(bf16[2,144,128]{2,1,0:T(8,128)(2,1)S(1)} %dynamic-slice_bitcast_fusion.4), channel_id=1, source_target_pairs={{0,1},{1,0},{2,3},{3,2},{4,5},{5,4},{6,7},{7,6},{8,9},{9,8},{10,11... | collective-permute-start | bytes 221192 | tf_op jit(solution)/shard_map/ppermute | solution.py:430
  51.7 1.2 %collective-permute-start.13 = (bf16[2,144,128]{2,1,0:T(8,128)(2,1)S(1)}, bf16[2,144,128]{2,1,0:T(8,128)(2,1)S(1)}, u32[]{:S(2)}, u32[]{:S(2)}) collective-permute-start(bf16[2,144,128]{2,1,0:T(8,128)(2,1)S(1)} %dynamic-slice_bitcast_fusion.3), channel_id=1, source_target_pairs={{0,2},{1,3},{2,0},{3,1},{4,6},{5,7},{6,4},{7,5},{8,10},{9,11},{10,... | collective-permute-start | bytes 221192 | tf_op jit(solution)/shard_map/ppermute | solution.py:430
  52.9 1.5 %collective-permute-done.10 = bf16[2,144,128]{2,1,0:T(8,128)(2,1)S(1)} collective-permute-done((bf16[2,144,128]{2,1,0:T(8,128)(2,1)S(1)}, bf16[2,144,128]{2,1,0:T(8,128)(2,1)S(1)}, u32[]{:S(2)}, u32[]{:S(2)}) %collective-permute-start.10) | collective-permute-done | bytes 73760 | tf_op jit(solution)/shard_map/ppermute | solution.py:430
  54.5 1.6 %collective-permute-done.13 = bf16[2,144,128]{2,1,0:T(8,128)(2,1)S(1)} collective-permute-done((bf16[2,144,128]{2,1,0:T(8,128)(2,1)S(1)}, bf16[2,144,128]{2,1,0:T(8,128)(2,1)S(1)}, u32[]{:S(2)}, u32[]{:S(2)}) %collective-permute-start.13) | collective-permute-done | bytes 73760 | tf_op jit(solution)/shard_map/ppermute | solution.py:430
  56.2 2.6 %collective-permute-start.14 = (bf16[432,128]{1,0:T(8,128)(2,1)S(1)}, bf16[432,128]{1,0:T(8,128)(2,1)S(1)}, u32[]{:S(2)}, u32[]{:S(2)}) collective-permute-start(bf16[432,128]{1,0:T(8,128)(2,1)S(1)} %pad_maximum_fusion), channel_id=1, source_target_pairs={{0,8},{1,9},{2,10},{3,11},{4,12},{5,13},{6,14},{7,15},{8,0},{9,1},... | collective-permute-start | bytes 331784 | tf_op jit(solution)/shard_map/ppermute | solution.py:430
  58.7 4.3 %collective-permute-done.14 = bf16[432,128]{1,0:T(8,128)(2,1)S(1)} collective-permute-done((bf16[432,128]{1,0:T(8,128)(2,1)S(1)}, bf16[432,128]{1,0:T(8,128)(2,1)S(1)}, u32[]{:S(2)}, u32[]{:S(2)}) %collective-permute-start.14) | collective-permute-done | bytes 110624 | tf_op jit(solution)/shard_map/ppermute | solution.py:430
  63.1 0.7 %slice_bitcast_fusion = (f32[1,216,128]{2,1,0:T(8,128)}, f32[1,216,128]{2,1,0:T(8,128)}) fusion(f32[432,128]{1,0:T(8,128)S(1)} %convert_add_fusion.3), kind=kLoop, calls=%fused_computation.19 | loop fusion | bytes 442368 | tf_op jit(solution)/shard_map/broadcast_in_dim | solution.py:574
  (43 shorter events, 1.0 us)
Async XLA Ops:
  2.8 9.2 %collective-permute-start = (bf16[576,128]{1,0:T(8,128)(2,1)}, bf16[576,128]{1,0:T(8,128)(2,1)S(1)}, u32[]{:S(2)}, u32[]{:S(2)}) collective-permute-start(bf16[576,128]{1,0:T(8,128)(2,1)} %get-tuple-element.38), channel_id=1, source_target_pairs={{0,1},{1,0},{2,3},{3,2},{4,5},{5,4},{6,7},{7,6},{8,9},{9,8},{10,11... | collective-permute-start | bytes 442376 | tf_op jit(solution)/shard_map/ppermute | solution.py:467
  5.8 6.2 %collective-permute-start.1 = (bf16[576,128]{1,0:T(8,128)(2,1)}, bf16[576,128]{1,0:T(8,128)(2,1)S(1)}, u32[]{:S(2)}, u32[]{:S(2)}) collective-permute-start(bf16[576,128]{1,0:T(8,128)(2,1)} %get-tuple-element.39), channel_id=1, source_target_pairs={{1,2},{2,1},{3,4},{4,3},{5,6},{6,5},{7,8},{8,7},{9,10},{10,9},{11,... | collective-permute-start | bytes 442376 | tf_op jit(solution)/shard_map/ppermute | solution.py:466
  6.5 1.2 %copy-start = (bf16[1,27,128,128]{3,2,1,0:T(8,128)(2,1)S(1)}, bf16[1,27,128,128]{3,2,1,0:T(8,128)(2,1)}, u32[]{:S(2)}) copy-start(bf16[1,27,128,128]{3,2,1,0:T(8,128)(2,1)} %param.12) | copy-start | bytes 2654212
  7.6 1.2 %copy-start.2 = (bf16[1,27,128,128]{3,2,1,0:T(8,128)(2,1)S(1)}, bf16[1,27,128,128]{3,2,1,0:T(8,128)(2,1)}, u32[]{:S(2)}) copy-start(bf16[1,27,128,128]{3,2,1,0:T(8,128)(2,1)} %param.13) | copy-start | bytes 2654212
  8.8 1.0 %copy-start.5 = (bf16[3,256,256]{2,1,0:T(8,128)(2,1)S(1)}, bf16[3,256,256]{2,1,0:T(8,128)(2,1)}, u32[]{:S(2)}) copy-start(bf16[3,256,256]{2,1,0:T(8,128)(2,1)} %get-tuple-element.34.fields) | copy-start | bytes 1179652
  12.0 4.2 %copy-start.6 = (bf16[4,8,8,256]{3,2,1,0:T(8,128)(2,1)S(1)}, bf16[4,8,8,256]{3,2,1,0:T(8,128)(2,1)}, u32[]{:S(2)}) copy-start(bf16[4,8,8,256]{3,2,1,0:T(8,128)(2,1)} %param.10) | copy-start | bytes 393220
  12.0 4.2 %copy-start.7 = (bf16[4,8,8,256]{3,2,1,0:T(8,128)(2,1)S(1)}, bf16[4,8,8,256]{3,2,1,0:T(8,128)(2,1)}, u32[]{:S(2)}) copy-start(bf16[4,8,8,256]{3,2,1,0:T(8,128)(2,1)} %param.11) | copy-start | bytes 393220
  12.0 9.5 %copy-start.4 = (bf16[1,4,8,8,256]{4,3,2,1,0:T(8,128)(2,1)S(1)}, bf16[1,4,8,8,256]{4,3,2,1,0:T(8,128)(2,1)}, u32[]{:S(2)}) copy-start(bf16[1,4,8,8,256]{4,3,2,1,0:T(8,128)(2,1)} %param.9) | copy-start | bytes 393220
  14.6 7.7 %copy-start.1 = (bf16[1,27,128,128]{3,2,1,0:T(8,128)(2,1)S(1)}, bf16[1,27,128,128]{3,2,1,0:T(8,128)(2,1)}, u32[]{:S(2)}) copy-start(bf16[1,27,128,128]{3,2,1,0:T(8,128)(2,1)} %param.12) | copy-start | bytes 2654212
  14.6 7.7 %copy-start.3 = (bf16[1,27,128,128]{3,2,1,0:T(8,128)(2,1)S(1)}, bf16[1,27,128,128]{3,2,1,0:T(8,128)(2,1)}, u32[]{:S(2)}) copy-start(bf16[1,27,128,128]{3,2,1,0:T(8,128)(2,1)} %param.13) | copy-start | bytes 2654212
  14.6 1.6 %collective-permute-start.2 = (bf16[2,256,256]{2,1,0:T(8,128)(2,1)S(1)}, bf16[2,256,256]{2,1,0:T(8,128)(2,1)S(1)}, u32[]{:S(2)}, u32[]{:S(2)}) collective-permute-start(bf16[2,256,256]{2,1,0:T(8,128)(2,1)S(1)} %get-tuple-element.45), channel_id=1, source_target_pairs={{0,16},{16,0},{1,17},{17,1},{2,18},{18,2},{3,19},{19,3},{4,20},{20... | collective-permute-start | bytes 786440 | tf_op jit(solution)/shard_map/ppermute | solution.py:531
  16.4 8.4 %collective-permute-start.3 = (bf16[576,128]{1,0:T(8,128)(2,1)S(1)}, bf16[576,128]{1,0:T(8,128)(2,1)S(1)}, u32[]{:S(2)}, u32[]{:S(2)}) collective-permute-start(bf16[576,128]{1,0:T(8,128)(2,1)S(1)} %get-tuple-element.49), channel_id=1, source_target_pairs={{0,1},{1,0},{2,3},{3,2},{4,5},{5,4},{6,7},{7,6},{8,9},{9,8},{10,11... | collective-permute-start | bytes 442376 | tf_op jit(solution)/shard_map/ppermute | solution.py:467
  20.7 4.2 %collective-permute-start.4 = (bf16[576,128]{1,0:T(8,128)(2,1)S(1)}, bf16[576,128]{1,0:T(8,128)(2,1)S(1)}, u32[]{:S(2)}, u32[]{:S(2)}) collective-permute-start(bf16[576,128]{1,0:T(8,128)(2,1)S(1)} %get-tuple-element.50), channel_id=1, source_target_pairs={{1,2},{2,1},{3,4},{4,3},{5,6},{6,5},{7,8},{8,7},{9,10},{10,9},{11,... | collective-permute-start | bytes 442376 | tf_op jit(solution)/shard_map/ppermute | solution.py:466
  29.8 12.4 %collective-permute-start.5 = (bf16[8,144,128]{2,1,0:T(8,128)(2,1)S(1)}, bf16[8,144,128]{2,1,0:T(8,128)(2,1)S(1)}, u32[]{:S(2)}, u32[]{:S(2)}) collective-permute-start(bf16[8,144,128]{2,1,0:T(8,128)(2,1)S(1)} %get-tuple-element.58), channel_id=1, source_target_pairs={{0,1},{1,0},{2,3},{3,2},{4,5},{5,4},{6,7},{7,6},{8,9},{9,8},{10,11... | collective-permute-start | bytes 884744 | tf_op jit(solution)/shard_map/ppermute | solution.py:430
  35.8 8.0 %collective-permute-start.8 = (bf16[8,144,128]{2,1,0:T(8,128)(2,1)S(1)}, bf16[8,144,128]{2,1,0:T(8,128)(2,1)S(1)}, u32[]{:S(2)}, u32[]{:S(2)}) collective-permute-start(bf16[8,144,128]{2,1,0:T(8,128)(2,1)S(1)} %get-tuple-element.60), channel_id=1, source_target_pairs={{0,2},{1,3},{2,0},{3,1},{4,6},{5,7},{6,4},{7,5},{8,10},{9,11},{10,... | collective-permute-start | bytes 884744 | tf_op jit(solution)/shard_map/ppermute | solution.py:430
  36.9 8.6 %collective-permute-start.11 = (bf16[8,144,128]{2,1,0:T(8,128)(2,1)S(1)}, bf16[8,144,128]{2,1,0:T(8,128)(2,1)S(1)}, u32[]{:S(2)}, u32[]{:S(2)}) collective-permute-start(bf16[8,144,128]{2,1,0:T(8,128)(2,1)S(1)} %get-tuple-element.62), channel_id=1, source_target_pairs={{0,4},{1,5},{2,6},{3,7},{4,0},{5,1},{6,2},{7,3},{8,12},{9,13},{10,... | collective-permute-start | bytes 884744 | tf_op jit(solution)/shard_map/ppermute | solution.py:430
  42.4 5.2 %collective-permute-start.6 = (bf16[4,144,128]{2,1,0:T(8,128)(2,1)S(1)}, bf16[4,144,128]{2,1,0:T(8,128)(2,1)S(1)}, u32[]{:S(2)}, u32[]{:S(2)}) collective-permute-start(bf16[4,144,128]{2,1,0:T(8,128)(2,1)S(1)} %dynamic-slice_bitcast_fusion.2), channel_id=1, source_target_pairs={{0,2},{1,3},{2,0},{3,1},{4,6},{5,7},{6,4},{7,5},{8,10},{9,11},{10,... | collective-permute-start | bytes 442376 | tf_op jit(solution)/shard_map/ppermute | solution.py:430
  43.9 6.1 %collective-permute-start.9 = (bf16[4,144,128]{2,1,0:T(8,128)(2,1)S(1)}, bf16[4,144,128]{2,1,0:T(8,128)(2,1)S(1)}, u32[]{:S(2)}, u32[]{:S(2)}) collective-permute-start(bf16[4,144,128]{2,1,0:T(8,128)(2,1)S(1)} %dynamic-slice_bitcast_fusion.1), channel_id=1, source_target_pairs={{0,4},{1,5},{2,6},{3,7},{4,0},{5,1},{6,2},{7,3},{8,12},{9,13},{10,... | collective-permute-start | bytes 442376 | tf_op jit(solution)/shard_map/ppermute | solution.py:430
  45.6 6.0 %collective-permute-start.12 = (bf16[4,144,128]{2,1,0:T(8,128)(2,1)S(1)}, bf16[4,144,128]{2,1,0:T(8,128)(2,1)S(1)}, u32[]{:S(2)}, u32[]{:S(2)}) collective-permute-start(bf16[4,144,128]{2,1,0:T(8,128)(2,1)S(1)} %dynamic-slice_bitcast_fusion), channel_id=1, source_target_pairs={{0,1},{1,0},{2,3},{3,2},{4,5},{5,4},{6,7},{7,6},{8,9},{9,8},{10,11... | collective-permute-start | bytes 442376 | tf_op jit(solution)/shard_map/ppermute | solution.py:430
  47.6 5.2 %collective-permute-start.7 = (bf16[2,144,128]{2,1,0:T(8,128)(2,1)S(1)}, bf16[2,144,128]{2,1,0:T(8,128)(2,1)S(1)}, u32[]{:S(2)}, u32[]{:S(2)}) collective-permute-start(bf16[2,144,128]{2,1,0:T(8,128)(2,1)S(1)} %dynamic-slice_bitcast_fusion.5), channel_id=1, source_target_pairs={{0,4},{1,5},{2,6},{3,7},{4,0},{5,1},{6,2},{7,3},{8,12},{9,13},{10,... | collective-permute-start | bytes 221192 | tf_op jit(solution)/shard_map/ppermute | solution.py:430
  50.1 4.4 %collective-permute-start.10 = (bf16[2,144,128]{2,1,0:T(8,128)(2,1)S(1)}, bf16[2,144,128]{2,1,0:T(8,128)(2,1)S(1)}, u32[]{:S(2)}, u32[]{:S(2)}) collective-permute-start(bf16[2,144,128]{2,1,0:T(8,128)(2,1)S(1)} %dynamic-slice_bitcast_fusion.4), channel_id=1, source_target_pairs={{0,1},{1,0},{2,3},{3,2},{4,5},{5,4},{6,7},{7,6},{8,9},{9,8},{10,11... | collective-permute-start | bytes 221192 | tf_op jit(solution)/shard_map/ppermute | solution.py:430
  51.7 4.4 %collective-permute-start.13 = (bf16[2,144,128]{2,1,0:T(8,128)(2,1)S(1)}, bf16[2,144,128]{2,1,0:T(8,128)(2,1)S(1)}, u32[]{:S(2)}, u32[]{:S(2)}) collective-permute-start(bf16[2,144,128]{2,1,0:T(8,128)(2,1)S(1)} %dynamic-slice_bitcast_fusion.3), channel_id=1, source_target_pairs={{0,2},{1,3},{2,0},{3,1},{4,6},{5,7},{6,4},{7,5},{8,10},{9,11},{10,... | collective-permute-start | bytes 221192 | tf_op jit(solution)/shard_map/ppermute | solution.py:430
  56.2 6.9 %collective-permute-start.14 = (bf16[432,128]{1,0:T(8,128)(2,1)S(1)}, bf16[432,128]{1,0:T(8,128)(2,1)S(1)}, u32[]{:S(2)}, u32[]{:S(2)}) collective-permute-start(bf16[432,128]{1,0:T(8,128)(2,1)S(1)} %pad_maximum_fusion), channel_id=1, source_target_pairs={{0,8},{1,9},{2,10},{3,11},{4,12},{5,13},{6,14},{7,15},{8,0},{9,1},... | collective-permute-start | bytes 331784 | tf_op jit(solution)/shard_map/ppermute | solution.py:430

commit v12 on v11

--- a/solution.py
+++ b/solution.py
@@ -91,29 +91,16 @@
         put((6 + index) * plane, plane, source, half)
 
 
-def edges_kernel(plane, state, act, grad, near_out, far_out, fields_out, near, far, fields,
-                 sems):
-    width = state.shape[1] // 2
-    cells = state.shape[0]
-    left, right = pl.ds(0, width), pl.ds(width, width)
-    moves = []
-    for index, (source, half) in enumerate(((state, right), (act, left), (grad, right))):
-        moves.append((source, half, 2 * plane, index * 2 * plane))
-    for index, (source, half) in enumerate(((state, left), (act, right), (grad, left))):
-        moves.append((source, half, plane, (6 + index) * plane))
+def edges_kernel(plane, state, act, grad, near_out, far_out, fields_out, near, far, fields, sems):
     copies = Copies(sems)
-    odd = lax.rem(lax.axis_index("space"), 2)
-    for side, (out, high) in enumerate(((near, 1 - odd), (far, odd))):
-        for index, (source, half, size, at) in enumerate(moves):
-            start = pl.multiple_of(high * (cells - size), plane)
-            copies.start((side, index), source.at[pl.ds(start, size), half], out.at[pl.ds(at, size), :])
     for index, source in enumerate((state, act, grad)):
-        copies.start(("field", index), source, fields.at[index])
-    for side, (out, result) in enumerate(((near, near_out), (far, far_out))):
-        copies.need(*[(side, index) for index in range(len(moves))])
-        copies.start(side, out, result)
-    copies.need(*[("field", index) for index in range(3)])
+        copies.start(index, source, fields.at[index])
+    copies.finish()
+    odd = lax.rem(lax.axis_index("space"), 2) == 1
     copies.start("fields", fields, fields_out)
+    pack_edges(odd, fields.at[0], fields.at[1], fields.at[2], near, far, plane)
+    copies.start("near", near, near_out)
+    copies.start("far", far, far_out)
     copies.finish()
 
 
@@ -497,7 +484,7 @@
     fields_shape = array((3, cells, 2 * width), BF16)
     near, far, fields = call(
         functools.partial(edges_kernel, plane), "edges", (state, act, grad), (edge, edge, fields_shape),
-        (edge, edge, fields_shape), 65408 * 1024, 18, (hbm, hbm),
+        (edge, edge, fields_shape), 65408 * 1024, 6, (hbm, hbm),
     )
     near, far = exchange(near, far)
     held = call(

time: 64.1 us -> 63.9 us (level)
  no operation moved by 1% of the time
where the time goes in v12:
time: 63.9 us; the launch traced here: 63.6 us
  starting transfers between devices  29.6 us (46%)
  Pallas kernels  14.2 us (22%)
  waiting for transfers between devices  14.1 us (22%)
  local copies, waits for them, and re-layouts  4.21 us (7%)
  between operations  0.92 us (1%)
    ppermute x10, starting transfers between devices, swapped(): lax.ppermute(send, 'space', [(i, i ^ bit) for i in range(count)])  20.7 us
    pallas_call x8, Pallas kernels, call(): pl.pallas_call(kernel, out_shape=tuple(outs), in_specs=[places[0]] * (len...  14.2 us
    ppermute x10, waiting for transfers between devices, swapped(): lax.ppermute(send, 'space', [(i, i ^ bit) for i in range(count)])  11.8 us
    ppermute x2, starting transfers between devices, exchange(): near = lax.ppermute(near, 'space', beside)  7.29 us
    unnamed x16, local copies, waits for them, and re-layouts  3.36 us
    ppermute x1, waiting for transfers between devices, shards(): lifted = lowered = lax.ppermute(sent, 'section', [(0, 1), (1, 0)])  1.52 us
    ppermute x2, starting transfers between devices, exchange(): far = lax.ppermute(far, 'space', across)  1.5 us
  transfers between devices with their start and end apart: 15, of which 8 were waited for; matrix products, arithmetic and copies ran while one was open for 1% of the time, Pallas kernels for 7%

profile of v12, /device:TPU:0, one launch (start us, length us, event | category | flops | bytes accessed | tf_op | source)
XLA Modules:
  0.0 63.6 jit_solution(1631155078223821645)
XLA Ops:
  0.6 1.9 %edges.1 = (bf16[576,128]{1,0:T(8,128)(2,1)}, bf16[576,128]{1,0:T(8,128)(2,1)}, bf16[3,256,256]{2,1,0:T(8,128)(2,1)}) custom-call(bf16[256,256]{1,0:T(8,128)(2,1)} %bitcast.100, bf16[256,256]{1,0:T(8,128)(2,1)} %bitcast.101, bf16[256,256]{1,0:T(8,128)(2,1)} %bitcast.84), custom_call_target="tpu_custom_call" | custom-call | bytes 393216 | tf_op jit(solution)/shard_map/edges/pallas_call | solution.py:470
  2.6 3.0 %collective-permute-start = (bf16[576,128]{1,0:T(8,128)(2,1)}, bf16[576,128]{1,0:T(8,128)(2,1)S(1)}, u32[]{:S(2)}, u32[]{:S(2)}) collective-permute-start(bf16[576,128]{1,0:T(8,128)(2,1)} %get-tuple-element.38), channel_id=1, source_target_pairs={{0,1},{1,0},{2,3},{3,2},{4,5},{5,4},{6,7},{7,6},{8,9},{9,8},{10,11... | collective-permute-start | bytes 442376 | tf_op jit(solution)/shard_map/ppermute | solution.py:454
  5.6 0.7 %collective-permute-start.1 = (bf16[576,128]{1,0:T(8,128)(2,1)}, bf16[576,128]{1,0:T(8,128)(2,1)S(1)}, u32[]{:S(2)}, u32[]{:S(2)}) collective-permute-start(bf16[576,128]{1,0:T(8,128)(2,1)} %get-tuple-element.39), channel_id=1, source_target_pairs={{1,2},{2,1},{3,4},{4,3},{5,6},{6,5},{7,8},{8,7},{9,10},{10,9},{11,... | collective-permute-start | bytes 442376 | tf_op jit(solution)/shard_map/ppermute | solution.py:453
  6.2 1.2 %copy-done = bf16[1,27,128,128]{3,2,1,0:T(8,128)(2,1)S(1)} copy-done((bf16[1,27,128,128]{3,2,1,0:T(8,128)(2,1)S(1)}, bf16[1,27,128,128]{3,2,1,0:T(8,128)(2,1)}, u32[]{:S(2)}) %copy-start) | copy-done | bytes 884760
  7.4 1.2 %copy-done.2 = bf16[1,27,128,128]{3,2,1,0:T(8,128)(2,1)S(1)} copy-done((bf16[1,27,128,128]{3,2,1,0:T(8,128)(2,1)S(1)}, bf16[1,27,128,128]{3,2,1,0:T(8,128)(2,1)}, u32[]{:S(2)}) %copy-start.2) | copy-done | bytes 884760
  8.6 1.0 %copy-done.5 = bf16[3,256,256]{2,1,0:T(8,128)(2,1)S(1)} copy-done((bf16[3,256,256]{2,1,0:T(8,128)(2,1)S(1)}, bf16[3,256,256]{2,1,0:T(8,128)(2,1)}, u32[]{:S(2)}) %copy-start.5) | copy-done | bytes 393240
  9.6 0.6 flip.1
  10.2 1.6 %own_sums.2.partial = f32[3,384,128]{2,1,0:T(8,128)S(1)} custom-call(bf16[256,256]{1,0:T(8,128)(2,1)S(1)} %get-tuple-element.35.state, bf16[256,256]{1,0:T(8,128)(2,1)S(1)} %get-tuple-element.36.act, bf16[256,256]{1,0:T(8,128)(2,1)S(1)} %get-tuple-element.37.grad, bf16[3,1152,128]{2,1,0:T(8,128)(2,1)S(1)} %bitcast.78, bf16[3,1152,128]{2,1,0:T(8,128)(2,1)S(1)} %bitcast.80, ...), custom_call_target="tpu_custom_call" | custom-call | flops 452984832 | bytes 3047424 | tf_op jit(solution)/shard_map/own_sums/pallas_call | solution.py:470
  11.8 2.6 %tick_one.1 = (bf16[256,256]{1,0:T(8,128)(2,1)S(1)}, bf16[2,256,256]{2,1,0:T(8,128)(2,1)S(1)}, bf16[384,128]{1,0:T(8,128)(2,1)S(1)}, bf16[384,128]{1,0:T(8,128)(2,1)S(1)}, bf16[384,128]{1,0:T(8,128)(2,1)S(1)}) custom-call(bf16[256,256]{1,0:T(8,128)(2,1)S(1)} %get-tuple-element.35.state, bf16[256,256]{1,0:T(8,128)(2,1)S(1)} %get-tuple-element.36.act, ...), custom_call_target="tpu_custom_call" | custom-call | flops 1811939328 | bytes 4521984 | tf_op jit(solution)/shard_map/tick_one/pallas_call | solution.py:470
  14.5 1.5 %collective-permute-done.2.lifted.lowered = bf16[2,256,256]{2,1,0:T(8,128)(2,1)S(1)} collective-permute-done((bf16[2,256,256]{2,1,0:T(8,128)(2,1)S(1)}, bf16[2,256,256]{2,1,0:T(8,128)(2,1)S(1)}, u32[]{:S(2)}, u32[]{:S(2)}) %collective-permute-start.2) | collective-permute-done | bytes 262176 | tf_op jit(solution)/shard_map/ppermute | solution.py:518
  16.2 4.3 %collective-permute-start.3 = (bf16[576,128]{1,0:T(8,128)(2,1)S(1)}, bf16[576,128]{1,0:T(8,128)(2,1)S(1)}, u32[]{:S(2)}, u32[]{:S(2)}) collective-permute-start(bf16[576,128]{1,0:T(8,128)(2,1)S(1)} %get-tuple-element.49), channel_id=1, source_target_pairs={{0,1},{1,0},{2,3},{3,2},{4,5},{5,4},{6,7},{7,6},{8,9},{9,8},{10,11... | collective-permute-start | bytes 442376 | tf_op jit(solution)/shard_map/ppermute | solution.py:454
  20.4 0.8 %collective-permute-start.4 = (bf16[576,128]{1,0:T(8,128)(2,1)S(1)}, bf16[576,128]{1,0:T(8,128)(2,1)S(1)}, u32[]{:S(2)}, u32[]{:S(2)}) collective-permute-start(bf16[576,128]{1,0:T(8,128)(2,1)S(1)} %get-tuple-element.50), channel_id=1, source_target_pairs={{1,2},{2,1},{3,4},{4,3},{5,6},{6,5},{7,8},{8,7},{9,10},{10,9},{11,... | collective-permute-start | bytes 442376 | tf_op jit(solution)/shard_map/ppermute | solution.py:453
  21.3 0.8 %weight_grads.1.so_far = f32[2,3456,128]{2,1,0:T(8,128)S(1)} custom-call(bf16[256,256]{1,0:T(8,128)(2,1)S(1)} %bitcast.85, bf16[384,128]{1,0:T(8,128)(2,1)S(1)} %get-tuple-element.51.back, bf16[384,128]{1,0:T(8,128)(2,1)S(1)} %get-tuple-element.52.carry, bf16[384,128]{1,0:T(8,128)(2,1)S(1)} %get-tuple-element.53.gate), custom_call_target="tpu_custom_call" | custom-call | flops 452984832 | bytes 425984 | tf_op jit(solution)/shard_map/weight_grads/pallas_call | solution.py:470
  22.1 1.6 %own_sums.3.partial = f32[3,384,128]{2,1,0:T(8,128)S(1)} custom-call(bf16[256,256]{1,0:T(8,128)(2,1)S(1)} %get-tuple-element.46.state, bf16[256,256]{1,0:T(8,128)(2,1)S(1)} %get-tuple-element.47.act, bf16[256,256]{1,0:T(8,128)(2,1)S(1)} %get-tuple-element.48.grad, bf16[3,1152,128]{2,1,0:T(8,128)(2,1)S(1)} %bitcast.73, bf16[3,1152,128]{2,1,0:T(8,128)(2,1)S(1)} %bitcast.76, ...), custom_call_target="tpu_custom_call" | custom-call | flops 452984832 | bytes 3047424 | tf_op jit(solution)/shard_map/own_sums/pallas_call | solution.py:470
  23.7 0.9 %collective-permute-done.3.near = bf16[576,128]{1,0:T(8,128)(2,1)S(1)} collective-permute-done((bf16[576,128]{1,0:T(8,128)(2,1)S(1)}, bf16[576,128]{1,0:T(8,128)(2,1)S(1)}, u32[]{:S(2)}, u32[]{:S(2)}) %collective-permute-start.3) | collective-permute-done | bytes 147488 | tf_op jit(solution)/shard_map/ppermute | solution.py:454
  24.6 5.0 %tick_two.1 = (bf16[256,256]{1,0:T(8,128)(2,1)}, bf16[256,256]{1,0:T(8,128)(2,1)}, bf16[256,256]{1,0:T(8,128)(2,1)}, bf16[8,144,128]{2,1,0:T(8,128)(2,1)S(1)}, b...) custom-call(bf16[256,256]{1,0:T(8,128)(2,1)S(1)} %get-tuple-element., ...), custom_call_target="tpu_custom_call" | custom-call | flops 2038431744 | bytes 6291456 | tf_op jit(solution)/shard_map/tick_two/pallas_call | solution.py:470
  29.6 5.9 %collective-permute-start.5 = (bf16[8,144,128]{2,1,0:T(8,128)(2,1)S(1)}, bf16[8,144,128]{2,1,0:T(8,128)(2,1)S(1)}, u32[]{:S(2)}, u32[]{:S(2)}) collective-permute-start(bf16[8,144,128]{2,1,0:T(8,128)(2,1)S(1)} %get-tuple-element.58), channel_id=1, source_target_pairs={{0,1},{1,0},{2,3},{3,2},{4,5},{5,4},{6,7},{7,6},{8,9},{9,8},{10,11... | collective-permute-start | bytes 884744 | tf_op jit(solution)/shard_map/ppermute | solution.py:417
  35.6 1.1 %collective-permute-start.8 = (bf16[8,144,128]{2,1,0:T(8,128)(2,1)S(1)}, bf16[8,144,128]{2,1,0:T(8,128)(2,1)S(1)}, u32[]{:S(2)}, u32[]{:S(2)}) collective-permute-start(bf16[8,144,128]{2,1,0:T(8,128)(2,1)S(1)} %get-tuple-element.60), channel_id=1, source_target_pairs={{0,2},{1,3},{2,0},{3,1},{4,6},{5,7},{6,4},{7,5},{8,10},{9,11},{10,... | collective-permute-start | bytes 884744 | tf_op jit(solution)/shard_map/ppermute | solution.py:417
  36.7 1.6 %collective-permute-start.11 = (bf16[8,144,128]{2,1,0:T(8,128)(2,1)S(1)}, bf16[8,144,128]{2,1,0:T(8,128)(2,1)S(1)}, u32[]{:S(2)}, u32[]{:S(2)}) collective-permute-start(bf16[8,144,128]{2,1,0:T(8,128)(2,1)S(1)} %get-tuple-element.62), channel_id=1, source_target_pairs={{0,4},{1,5},{2,6},{3,7},{4,0},{5,1},{6,2},{7,3},{8,12},{9,13},{10,... | collective-permute-start | bytes 884744 | tf_op jit(solution)/shard_map/ppermute | solution.py:417
  38.2 3.8 %collective-permute-done.5 = bf16[8,144,128]{2,1,0:T(8,128)(2,1)S(1)} collective-permute-done((bf16[8,144,128]{2,1,0:T(8,128)(2,1)S(1)}, bf16[8,144,128]{2,1,0:T(8,128)(2,1)S(1)}, u32[]{:S(2)}, u32[]{:S(2)}) %collective-permute-start.5) | collective-permute-done | bytes 294944 | tf_op jit(solution)/shard_map/ppermute | solution.py:417
  42.1 1.4 %collective-permute-start.6 = (bf16[4,144,128]{2,1,0:T(8,128)(2,1)S(1)}, bf16[4,144,128]{2,1,0:T(8,128)(2,1)S(1)}, u32[]{:S(2)}, u32[]{:S(2)}) collective-permute-start(bf16[4,144,128]{2,1,0:T(8,128)(2,1)S(1)} %dynamic-slice_bitcast_fusion.2), channel_id=1, source_target_pairs={{0,2},{1,3},{2,0},{3,1},{4,6},{5,7},{6,4},{7,5},{8,10},{9,11},{10,... | collective-permute-start | bytes 442376 | tf_op jit(solution)/shard_map/ppermute | solution.py:417
  43.7 1.6 %collective-permute-start.9 = (bf16[4,144,128]{2,1,0:T(8,128)(2,1)S(1)}, bf16[4,144,128]{2,1,0:T(8,128)(2,1)S(1)}, u32[]{:S(2)}, u32[]{:S(2)}) collective-permute-start(bf16[4,144,128]{2,1,0:T(8,128)(2,1)S(1)} %dynamic-slice_bitcast_fusion.1), channel_id=1, source_target_pairs={{0,4},{1,5},{2,6},{3,7},{4,0},{5,1},{6,2},{7,3},{8,12},{9,13},{10,... | collective-permute-start | bytes 442376 | tf_op jit(solution)/shard_map/ppermute | solution.py:417
  45.4 1.6 %collective-permute-start.12 = (bf16[4,144,128]{2,1,0:T(8,128)(2,1)S(1)}, bf16[4,144,128]{2,1,0:T(8,128)(2,1)S(1)}, u32[]{:S(2)}, u32[]{:S(2)}) collective-permute-start(bf16[4,144,128]{2,1,0:T(8,128)(2,1)S(1)} %dynamic-slice_bitcast_fusion), channel_id=1, source_target_pairs={{0,1},{1,0},{2,3},{3,2},{4,5},{5,4},{6,7},{7,6},{8,9},{9,8},{10,11... | collective-permute-start | bytes 442376 | tf_op jit(solution)/shard_map/ppermute | solution.py:417
  47.0 0.3 collective-permute-done.6
  47.4 2.4 %collective-permute-start.7 = (bf16[2,144,128]{2,1,0:T(8,128)(2,1)S(1)}, bf16[2,144,128]{2,1,0:T(8,128)(2,1)S(1)}, u32[]{:S(2)}, u32[]{:S(2)}) collective-permute-start(bf16[2,144,128]{2,1,0:T(8,128)(2,1)S(1)} %dynamic-slice_bitcast_fusion.5), channel_id=1, source_target_pairs={{0,4},{1,5},{2,6},{3,7},{4,0},{5,1},{6,2},{7,3},{8,12},{9,13},{10,... | collective-permute-start | bytes 221192 | tf_op jit(solution)/shard_map/ppermute | solution.py:417
  49.8 1.5 %collective-permute-start.10 = (bf16[2,144,128]{2,1,0:T(8,128)(2,1)S(1)}, bf16[2,144,128]{2,1,0:T(8,128)(2,1)S(1)}, u32[]{:S(2)}, u32[]{:S(2)}) collective-permute-start(bf16[2,144,128]{2,1,0:T(8,128)(2,1)S(1)} %dynamic-slice_bitcast_fusion.4), channel_id=1, source_target_pairs={{0,1},{1,0},{2,3},{3,2},{4,5},{5,4},{6,7},{7,6},{8,9},{9,8},{10,11... | collective-permute-start | bytes 221192 | tf_op jit(solution)/shard_map/ppermute | solution.py:417
  51.5 1.2 %collective-permute-start.13 = (bf16[2,144,128]{2,1,0:T(8,128)(2,1)S(1)}, bf16[2,144,128]{2,1,0:T(8,128)(2,1)S(1)}, u32[]{:S(2)}, u32[]{:S(2)}) collective-permute-start(bf16[2,144,128]{2,1,0:T(8,128)(2,1)S(1)} %dynamic-slice_bitcast_fusion.3), channel_id=1, source_target_pairs={{0,2},{1,3},{2,0},{3,1},{4,6},{5,7},{6,4},{7,5},{8,10},{9,11},{10,... | collective-permute-start | bytes 221192 | tf_op jit(solution)/shard_map/ppermute | solution.py:417
  52.7 1.5 %collective-permute-done.10 = bf16[2,144,128]{2,1,0:T(8,128)(2,1)S(1)} collective-permute-done((bf16[2,144,128]{2,1,0:T(8,128)(2,1)S(1)}, bf16[2,144,128]{2,1,0:T(8,128)(2,1)S(1)}, u32[]{:S(2)}, u32[]{:S(2)}) %collective-permute-start.10) | collective-permute-done | bytes 73760 | tf_op jit(solution)/shard_map/ppermute | solution.py:417
  54.3 1.6 %collective-permute-done.13 = bf16[2,144,128]{2,1,0:T(8,128)(2,1)S(1)} collective-permute-done((bf16[2,144,128]{2,1,0:T(8,128)(2,1)S(1)}, bf16[2,144,128]{2,1,0:T(8,128)(2,1)S(1)}, u32[]{:S(2)}, u32[]{:S(2)}) %collective-permute-start.13) | collective-permute-done | bytes 73760 | tf_op jit(solution)/shard_map/ppermute | solution.py:417
  56.0 2.5 %collective-permute-start.14 = (bf16[432,128]{1,0:T(8,128)(2,1)S(1)}, bf16[432,128]{1,0:T(8,128)(2,1)S(1)}, u32[]{:S(2)}, u32[]{:S(2)}) collective-permute-start(bf16[432,128]{1,0:T(8,128)(2,1)S(1)} %pad_maximum_fusion), channel_id=1, source_target_pairs={{0,8},{1,9},{2,10},{3,11},{4,12},{5,13},{6,14},{7,15},{8,0},{9,1},... | collective-permute-start | bytes 331784 | tf_op jit(solution)/shard_map/ppermute | solution.py:417
  58.5 4.4 %collective-permute-done.14 = bf16[432,128]{1,0:T(8,128)(2,1)S(1)} collective-permute-done((bf16[432,128]{1,0:T(8,128)(2,1)S(1)}, bf16[432,128]{1,0:T(8,128)(2,1)S(1)}, u32[]{:S(2)}, u32[]{:S(2)}) %collective-permute-start.14) | collective-permute-done | bytes 110624 | tf_op jit(solution)/shard_map/ppermute | solution.py:417
  62.9 0.7 %slice_bitcast_fusion = (f32[1,216,128]{2,1,0:T(8,128)}, f32[1,216,128]{2,1,0:T(8,128)}) fusion(f32[432,128]{1,0:T(8,128)S(1)} %convert_add_fusion.3), kind=kLoop, calls=%fused_computation.19 | loop fusion | bytes 442368 | tf_op jit(solution)/shard_map/broadcast_in_dim | solution.py:561
  (43 shorter events, 1.0 us)
Async XLA Ops:
  2.6 9.2 %collective-permute-start = (bf16[576,128]{1,0:T(8,128)(2,1)}, bf16[576,128]{1,0:T(8,128)(2,1)S(1)}, u32[]{:S(2)}, u32[]{:S(2)}) collective-permute-start(bf16[576,128]{1,0:T(8,128)(2,1)} %get-tuple-element.38), channel_id=1, source_target_pairs={{0,1},{1,0},{2,3},{3,2},{4,5},{5,4},{6,7},{7,6},{8,9},{9,8},{10,11... | collective-permute-start | bytes 442376 | tf_op jit(solution)/shard_map/ppermute | solution.py:454
  5.6 6.2 %collective-permute-start.1 = (bf16[576,128]{1,0:T(8,128)(2,1)}, bf16[576,128]{1,0:T(8,128)(2,1)S(1)}, u32[]{:S(2)}, u32[]{:S(2)}) collective-permute-start(bf16[576,128]{1,0:T(8,128)(2,1)} %get-tuple-element.39), channel_id=1, source_target_pairs={{1,2},{2,1},{3,4},{4,3},{5,6},{6,5},{7,8},{8,7},{9,10},{10,9},{11,... | collective-permute-start | bytes 442376 | tf_op jit(solution)/shard_map/ppermute | solution.py:453
  6.2 1.2 %copy-start = (bf16[1,27,128,128]{3,2,1,0:T(8,128)(2,1)S(1)}, bf16[1,27,128,128]{3,2,1,0:T(8,128)(2,1)}, u32[]{:S(2)}) copy-start(bf16[1,27,128,128]{3,2,1,0:T(8,128)(2,1)} %param.12) | copy-start | bytes 2654212
  7.4 1.2 %copy-start.2 = (bf16[1,27,128,128]{3,2,1,0:T(8,128)(2,1)S(1)}, bf16[1,27,128,128]{3,2,1,0:T(8,128)(2,1)}, u32[]{:S(2)}) copy-start(bf16[1,27,128,128]{3,2,1,0:T(8,128)(2,1)} %param.13) | copy-start | bytes 2654212
  8.6 1.0 %copy-start.5 = (bf16[3,256,256]{2,1,0:T(8,128)(2,1)S(1)}, bf16[3,256,256]{2,1,0:T(8,128)(2,1)}, u32[]{:S(2)}) copy-start(bf16[3,256,256]{2,1,0:T(8,128)(2,1)} %get-tuple-element.34.fields) | copy-start | bytes 1179652
  11.8 4.2 %copy-start.6 = (bf16[4,8,8,256]{3,2,1,0:T(8,128)(2,1)S(1)}, bf16[4,8,8,256]{3,2,1,0:T(8,128)(2,1)}, u32[]{:S(2)}) copy-start(bf16[4,8,8,256]{3,2,1,0:T(8,128)(2,1)} %param.10) | copy-start | bytes 393220
  11.8 4.2 %copy-start.7 = (bf16[4,8,8,256]{3,2,1,0:T(8,128)(2,1)S(1)}, bf16[4,8,8,256]{3,2,1,0:T(8,128)(2,1)}, u32[]{:S(2)}) copy-start(bf16[4,8,8,256]{3,2,1,0:T(8,128)(2,1)} %param.11) | copy-start | bytes 393220
  11.8 9.5 %copy-start.4 = (bf16[1,4,8,8,256]{4,3,2,1,0:T(8,128)(2,1)S(1)}, bf16[1,4,8,8,256]{4,3,2,1,0:T(8,128)(2,1)}, u32[]{:S(2)}) copy-start(bf16[1,4,8,8,256]{4,3,2,1,0:T(8,128)(2,1)} %param.9) | copy-start | bytes 393220
  14.4 7.7 %copy-start.1 = (bf16[1,27,128,128]{3,2,1,0:T(8,128)(2,1)S(1)}, bf16[1,27,128,128]{3,2,1,0:T(8,128)(2,1)}, u32[]{:S(2)}) copy-start(bf16[1,27,128,128]{3,2,1,0:T(8,128)(2,1)} %param.12) | copy-start | bytes 2654212
  14.4 7.7 %copy-start.3 = (bf16[1,27,128,128]{3,2,1,0:T(8,128)(2,1)S(1)}, bf16[1,27,128,128]{3,2,1,0:T(8,128)(2,1)}, u32[]{:S(2)}) copy-start(bf16[1,27,128,128]{3,2,1,0:T(8,128)(2,1)} %param.13) | copy-start | bytes 2654212
  14.4 1.6 %collective-permute-start.2 = (bf16[2,256,256]{2,1,0:T(8,128)(2,1)S(1)}, bf16[2,256,256]{2,1,0:T(8,128)(2,1)S(1)}, u32[]{:S(2)}, u32[]{:S(2)}) collective-permute-start(bf16[2,256,256]{2,1,0:T(8,128)(2,1)S(1)} %get-tuple-element.45), channel_id=1, source_target_pairs={{0,16},{16,0},{1,17},{17,1},{2,18},{18,2},{3,19},{19,3},{4,20},{20... | collective-permute-start | bytes 786440 | tf_op jit(solution)/shard_map/ppermute | solution.py:518
  16.2 8.4 %collective-permute-start.3 = (bf16[576,128]{1,0:T(8,128)(2,1)S(1)}, bf16[576,128]{1,0:T(8,128)(2,1)S(1)}, u32[]{:S(2)}, u32[]{:S(2)}) collective-permute-start(bf16[576,128]{1,0:T(8,128)(2,1)S(1)} %get-tuple-element.49), channel_id=1, source_target_pairs={{0,1},{1,0},{2,3},{3,2},{4,5},{5,4},{6,7},{7,6},{8,9},{9,8},{10,11... | collective-permute-start | bytes 442376 | tf_op jit(solution)/shard_map/ppermute | solution.py:454
  20.4 4.2 %collective-permute-start.4 = (bf16[576,128]{1,0:T(8,128)(2,1)S(1)}, bf16[576,128]{1,0:T(8,128)(2,1)S(1)}, u32[]{:S(2)}, u32[]{:S(2)}) collective-permute-start(bf16[576,128]{1,0:T(8,128)(2,1)S(1)} %get-tuple-element.50), channel_id=1, source_target_pairs={{1,2},{2,1},{3,4},{4,3},{5,6},{6,5},{7,8},{8,7},{9,10},{10,9},{11,... | collective-permute-start | bytes 442376 | tf_op jit(solution)/shard_map/ppermute | solution.py:453
  29.6 12.4 %collective-permute-start.5 = (bf16[8,144,128]{2,1,0:T(8,128)(2,1)S(1)}, bf16[8,144,128]{2,1,0:T(8,128)(2,1)S(1)}, u32[]{:S(2)}, u32[]{:S(2)}) collective-permute-start(bf16[8,144,128]{2,1,0:T(8,128)(2,1)S(1)} %get-tuple-element.58), channel_id=1, source_target_pairs={{0,1},{1,0},{2,3},{3,2},{4,5},{5,4},{6,7},{7,6},{8,9},{9,8},{10,11... | collective-permute-start | bytes 884744 | tf_op jit(solution)/shard_map/ppermute | solution.py:417
  35.6 8.0 %collective-permute-start.8 = (bf16[8,144,128]{2,1,0:T(8,128)(2,1)S(1)}, bf16[8,144,128]{2,1,0:T(8,128)(2,1)S(1)}, u32[]{:S(2)}, u32[]{:S(2)}) collective-permute-start(bf16[8,144,128]{2,1,0:T(8,128)(2,1)S(1)} %get-tuple-element.60), channel_id=1, source_target_pairs={{0,2},{1,3},{2,0},{3,1},{4,6},{5,7},{6,4},{7,5},{8,10},{9,11},{10,... | collective-permute-start | bytes 884744 | tf_op jit(solution)/shard_map/ppermute | solution.py:417
  36.7 8.7 %collective-permute-start.11 = (bf16[8,144,128]{2,1,0:T(8,128)(2,1)S(1)}, bf16[8,144,128]{2,1,0:T(8,128)(2,1)S(1)}, u32[]{:S(2)}, u32[]{:S(2)}) collective-permute-start(bf16[8,144,128]{2,1,0:T(8,128)(2,1)S(1)} %get-tuple-element.62), channel_id=1, source_target_pairs={{0,4},{1,5},{2,6},{3,7},{4,0},{5,1},{6,2},{7,3},{8,12},{9,13},{10,... | collective-permute-start | bytes 884744 | tf_op jit(solution)/shard_map/ppermute | solution.py:417
  42.1 5.2 %collective-permute-start.6 = (bf16[4,144,128]{2,1,0:T(8,128)(2,1)S(1)}, bf16[4,144,128]{2,1,0:T(8,128)(2,1)S(1)}, u32[]{:S(2)}, u32[]{:S(2)}) collective-permute-start(bf16[4,144,128]{2,1,0:T(8,128)(2,1)S(1)} %dynamic-slice_bitcast_fusion.2), channel_id=1, source_target_pairs={{0,2},{1,3},{2,0},{3,1},{4,6},{5,7},{6,4},{7,5},{8,10},{9,11},{10,... | collective-permute-start | bytes 442376 | tf_op jit(solution)/shard_map/ppermute | solution.py:417
  43.7 6.1 %collective-permute-start.9 = (bf16[4,144,128]{2,1,0:T(8,128)(2,1)S(1)}, bf16[4,144,128]{2,1,0:T(8,128)(2,1)S(1)}, u32[]{:S(2)}, u32[]{:S(2)}) collective-permute-start(bf16[4,144,128]{2,1,0:T(8,128)(2,1)S(1)} %dynamic-slice_bitcast_fusion.1), channel_id=1, source_target_pairs={{0,4},{1,5},{2,6},{3,7},{4,0},{5,1},{6,2},{7,3},{8,12},{9,13},{10,... | collective-permute-start | bytes 442376 | tf_op jit(solution)/shard_map/ppermute | solution.py:417
  45.4 6.0 %collective-permute-start.12 = (bf16[4,144,128]{2,1,0:T(8,128)(2,1)S(1)}, bf16[4,144,128]{2,1,0:T(8,128)(2,1)S(1)}, u32[]{:S(2)}, u32[]{:S(2)}) collective-permute-start(bf16[4,144,128]{2,1,0:T(8,128)(2,1)S(1)} %dynamic-slice_bitcast_fusion), channel_id=1, source_target_pairs={{0,1},{1,0},{2,3},{3,2},{4,5},{5,4},{6,7},{7,6},{8,9},{9,8},{10,11... | collective-permute-start | bytes 442376 | tf_op jit(solution)/shard_map/ppermute | solution.py:417
  47.4 5.3 %collective-permute-start.7 = (bf16[2,144,128]{2,1,0:T(8,128)(2,1)S(1)}, bf16[2,144,128]{2,1,0:T(8,128)(2,1)S(1)}, u32[]{:S(2)}, u32[]{:S(2)}) collective-permute-start(bf16[2,144,128]{2,1,0:T(8,128)(2,1)S(1)} %dynamic-slice_bitcast_fusion.5), channel_id=1, source_target_pairs={{0,4},{1,5},{2,6},{3,7},{4,0},{5,1},{6,2},{7,3},{8,12},{9,13},{10,... | collective-permute-start | bytes 221192 | tf_op jit(solution)/shard_map/ppermute | solution.py:417
  49.8 4.4 %collective-permute-start.10 = (bf16[2,144,128]{2,1,0:T(8,128)(2,1)S(1)}, bf16[2,144,128]{2,1,0:T(8,128)(2,1)S(1)}, u32[]{:S(2)}, u32[]{:S(2)}) collective-permute-start(bf16[2,144,128]{2,1,0:T(8,128)(2,1)S(1)} %dynamic-slice_bitcast_fusion.4), channel_id=1, source_target_pairs={{0,1},{1,0},{2,3},{3,2},{4,5},{5,4},{6,7},{7,6},{8,9},{9,8},{10,11... | collective-permute-start | bytes 221192 | tf_op jit(solution)/shard_map/ppermute | solution.py:417
  51.5 4.4 %collective-permute-start.13 = (bf16[2,144,128]{2,1,0:T(8,128)(2,1)S(1)}, bf16[2,144,128]{2,1,0:T(8,128)(2,1)S(1)}, u32[]{:S(2)}, u32[]{:S(2)}) collective-permute-start(bf16[2,144,128]{2,1,0:T(8,128)(2,1)S(1)} %dynamic-slice_bitcast_fusion.3), channel_id=1, source_target_pairs={{0,2},{1,3},{2,0},{3,1},{4,6},{5,7},{6,4},{7,5},{8,10},{9,11},{10,... | collective-permute-start | bytes 221192 | tf_op jit(solution)/shard_map/ppermute | solution.py:417
  56.0 6.9 %collective-permute-start.14 = (bf16[432,128]{1,0:T(8,128)(2,1)S(1)}, bf16[432,128]{1,0:T(8,128)(2,1)S(1)}, u32[]{:S(2)}, u32[]{:S(2)}) collective-permute-start(bf16[432,128]{1,0:T(8,128)(2,1)S(1)} %pad_maximum_fusion), channel_id=1, source_target_pairs={{0,8},{1,9},{2,10},{3,11},{4,12},{5,13},{6,14},{7,15},{8,0},{9,1},... | collective-permute-start | bytes 331784 | tf_op jit(solution)/shard_map/ppermute | solution.py:417

commit v13 on v12

--- a/solution.py
+++ b/solution.py
@@ -135,12 +135,17 @@
     for index, (field, weight) in enumerate(zip(fields, weights)):
         fill_shifts(stack, field, ydim, zdim)
         cells = field.shape[0]
-        partial[index] = jnp.zeros(partial.shape[1:], F32)
-        for step in range(3):
-            at = (2 - step) * plane
-            partial[index, at : at + cells, :] += jnp.dot(
-                stack[0:cells, :], weight[step], preferred_element_type=F32
-            )
+        ahead, level, behind = [
+            jnp.dot(stack[0:cells, :], weight[step], preferred_element_type=F32) for step in range(3)
+        ]
+        end = cells - plane
+        partial[index, 0:plane, :] = behind[0:plane]
+        partial[index, plane : 2 * plane, :] = behind[plane : 2 * plane] + level[0:plane]
+        partial[index, 2 * plane : cells, :] = (
+            behind[2 * plane :] + level[plane:end] + ahead[0 : end - plane]
+        )
+        partial[index, cells : cells + plane, :] = level[end:] + ahead[end - plane : end]
+        partial[index, cells + plane :, :] = ahead[end:]
 
 
 def gated_fields(state, act, grad):

time: 63.9 us -> 64 us (level)
  no operation moved by 1% of the time
where the time goes in v13:
time: 64 us; the launch traced here: 63.7 us
  starting transfers between devices  29.6 us (46%)
  Pallas kernels  14.4 us (22%)
  waiting for transfers between devices  14.1 us (22%)
  local copies, waits for them, and re-layouts  4.21 us (7%)
  between operations  0.92 us (1%)
    ppermute x10, starting transfers between devices, swapped(): lax.ppermute(send, 'space', [(i, i ^ bit) for i in range(count)])  20.7 us
    pallas_call x8, Pallas kernels, call(): pl.pallas_call(kernel, out_shape=tuple(outs), in_specs=[places[0]] * (len...  14.4 us
    ppermute x10, waiting for transfers between devices, swapped(): lax.ppermute(send, 'space', [(i, i ^ bit) for i in range(count)])  11.8 us
    ppermute x2, starting transfers between devices, exchange(): near = lax.ppermute(near, 'space', beside)  7.29 us
    unnamed x16, local copies, waits for them, and re-layouts  3.36 us
    ppermute x1, waiting for transfers between devices, shards(): lifted = lowered = lax.ppermute(sent, 'section', [(0, 1), (1, 0)])  1.52 us
    ppermute x2, starting transfers between devices, exchange(): far = lax.ppermute(far, 'space', across)  1.5 us
  transfers between devices with their start and end apart: 15, of which 8 were waited for; matrix products, arithmetic and copies ran while one was open for 1% of the time, Pallas kernels for 7%

profile of v13, /device:TPU:0, one launch (start us, length us, event | category | flops | bytes accessed | tf_op | source)
XLA Modules:
  0.0 63.7 jit_solution(4428958152916253603)
XLA Ops:
  0.6 1.9 %edges.1 = (bf16[576,128]{1,0:T(8,128)(2,1)}, bf16[576,128]{1,0:T(8,128)(2,1)}, bf16[3,256,256]{2,1,0:T(8,128)(2,1)}) custom-call(bf16[256,256]{1,0:T(8,128)(2,1)} %bitcast.100, bf16[256,256]{1,0:T(8,128)(2,1)} %bitcast.101, bf16[256,256]{1,0:T(8,128)(2,1)} %bitcast.84), custom_call_target="tpu_custom_call" | custom-call | bytes 393216 | tf_op jit(solution)/shard_map/edges/pallas_call | solution.py:475
  2.6 3.0 %collective-permute-start = (bf16[576,128]{1,0:T(8,128)(2,1)}, bf16[576,128]{1,0:T(8,128)(2,1)S(1)}, u32[]{:S(2)}, u32[]{:S(2)}) collective-permute-start(bf16[576,128]{1,0:T(8,128)(2,1)} %get-tuple-element.38), channel_id=1, source_target_pairs={{0,1},{1,0},{2,3},{3,2},{4,5},{5,4},{6,7},{7,6},{8,9},{9,8},{10,11... | collective-permute-start | bytes 442376 | tf_op jit(solution)/shard_map/ppermute | solution.py:459
  5.6 0.7 %collective-permute-start.1 = (bf16[576,128]{1,0:T(8,128)(2,1)}, bf16[576,128]{1,0:T(8,128)(2,1)S(1)}, u32[]{:S(2)}, u32[]{:S(2)}) collective-permute-start(bf16[576,128]{1,0:T(8,128)(2,1)} %get-tuple-element.39), channel_id=1, source_target_pairs={{1,2},{2,1},{3,4},{4,3},{5,6},{6,5},{7,8},{8,7},{9,10},{10,9},{11,... | collective-permute-start | bytes 442376 | tf_op jit(solution)/shard_map/ppermute | solution.py:458
  6.2 1.2 %copy-done = bf16[1,27,128,128]{3,2,1,0:T(8,128)(2,1)S(1)} copy-done((bf16[1,27,128,128]{3,2,1,0:T(8,128)(2,1)S(1)}, bf16[1,27,128,128]{3,2,1,0:T(8,128)(2,1)}, u32[]{:S(2)}) %copy-start) | copy-done | bytes 884760
  7.4 1.2 %copy-done.2 = bf16[1,27,128,128]{3,2,1,0:T(8,128)(2,1)S(1)} copy-done((bf16[1,27,128,128]{3,2,1,0:T(8,128)(2,1)S(1)}, bf16[1,27,128,128]{3,2,1,0:T(8,128)(2,1)}, u32[]{:S(2)}) %copy-start.2) | copy-done | bytes 884760
  8.6 1.0 %copy-done.5 = bf16[3,256,256]{2,1,0:T(8,128)(2,1)S(1)} copy-done((bf16[3,256,256]{2,1,0:T(8,128)(2,1)S(1)}, bf16[3,256,256]{2,1,0:T(8,128)(2,1)}, u32[]{:S(2)}) %copy-start.5) | copy-done | bytes 393240
  9.6 0.6 flip.1
  10.2 1.7 %own_sums.2.partial = f32[3,384,128]{2,1,0:T(8,128)S(1)} custom-call(bf16[256,256]{1,0:T(8,128)(2,1)S(1)} %get-tuple-element.35.state, bf16[256,256]{1,0:T(8,128)(2,1)S(1)} %get-tuple-element.36.act, bf16[256,256]{1,0:T(8,128)(2,1)S(1)} %get-tuple-element.37.grad, bf16[3,1152,128]{2,1,0:T(8,128)(2,1)S(1)} %bitcast.78, bf16[3,1152,128]{2,1,0:T(8,128)(2,1)S(1)} %bitcast.80, ...), custom_call_target="tpu_custom_call" | custom-call | flops 452984832 | bytes 3047424 | tf_op jit(solution)/shard_map/own_sums/pallas_call | solution.py:475
  11.9 2.6 %tick_one.1 = (bf16[256,256]{1,0:T(8,128)(2,1)S(1)}, bf16[2,256,256]{2,1,0:T(8,128)(2,1)S(1)}, bf16[384,128]{1,0:T(8,128)(2,1)S(1)}, bf16[384,128]{1,0:T(8,128)(2,1)S(1)}, bf16[384,128]{1,0:T(8,128)(2,1)S(1)}) custom-call(bf16[256,256]{1,0:T(8,128)(2,1)S(1)} %get-tuple-element.35.state, bf16[256,256]{1,0:T(8,128)(2,1)S(1)} %get-tuple-element.36.act, ...), custom_call_target="tpu_custom_call" | custom-call | flops 1811939328 | bytes 4521984 | tf_op jit(solution)/shard_map/tick_one/pallas_call | solution.py:475
  14.6 1.5 %collective-permute-done.2.lifted.lowered = bf16[2,256,256]{2,1,0:T(8,128)(2,1)S(1)} collective-permute-done((bf16[2,256,256]{2,1,0:T(8,128)(2,1)S(1)}, bf16[2,256,256]{2,1,0:T(8,128)(2,1)S(1)}, u32[]{:S(2)}, u32[]{:S(2)}) %collective-permute-start.2) | collective-permute-done | bytes 262176 | tf_op jit(solution)/shard_map/ppermute | solution.py:523
  16.2 4.3 %collective-permute-start.3 = (bf16[576,128]{1,0:T(8,128)(2,1)S(1)}, bf16[576,128]{1,0:T(8,128)(2,1)S(1)}, u32[]{:S(2)}, u32[]{:S(2)}) collective-permute-start(bf16[576,128]{1,0:T(8,128)(2,1)S(1)} %get-tuple-element.49), channel_id=1, source_target_pairs={{0,1},{1,0},{2,3},{3,2},{4,5},{5,4},{6,7},{7,6},{8,9},{9,8},{10,11... | collective-permute-start | bytes 442376 | tf_op jit(solution)/shard_map/ppermute | solution.py:459
  20.5 0.8 %collective-permute-start.4 = (bf16[576,128]{1,0:T(8,128)(2,1)S(1)}, bf16[576,128]{1,0:T(8,128)(2,1)S(1)}, u32[]{:S(2)}, u32[]{:S(2)}) collective-permute-start(bf16[576,128]{1,0:T(8,128)(2,1)S(1)} %get-tuple-element.50), channel_id=1, source_target_pairs={{1,2},{2,1},{3,4},{4,3},{5,6},{6,5},{7,8},{8,7},{9,10},{10,9},{11,... | collective-permute-start | bytes 442376 | tf_op jit(solution)/shard_map/ppermute | solution.py:458
  21.4 0.8 %weight_grads.1.so_far = f32[2,3456,128]{2,1,0:T(8,128)S(1)} custom-call(bf16[256,256]{1,0:T(8,128)(2,1)S(1)} %bitcast.85, bf16[384,128]{1,0:T(8,128)(2,1)S(1)} %get-tuple-element.51.back, bf16[384,128]{1,0:T(8,128)(2,1)S(1)} %get-tuple-element.52.carry, bf16[384,128]{1,0:T(8,128)(2,1)S(1)} %get-tuple-element.53.gate), custom_call_target="tpu_custom_call" | custom-call | flops 452984832 | bytes 425984 | tf_op jit(solution)/shard_map/weight_grads/pallas_call | solution.py:475
  22.2 1.7 %own_sums.3.partial = f32[3,384,128]{2,1,0:T(8,128)S(1)} custom-call(bf16[256,256]{1,0:T(8,128)(2,1)S(1)} %get-tuple-element.46.state, bf16[256,256]{1,0:T(8,128)(2,1)S(1)} %get-tuple-element.47.act, bf16[256,256]{1,0:T(8,128)(2,1)S(1)} %get-tuple-element.48.grad, bf16[3,1152,128]{2,1,0:T(8,128)(2,1)S(1)} %bitcast.73, bf16[3,1152,128]{2,1,0:T(8,128)(2,1)S(1)} %bitcast.76, ...), custom_call_target="tpu_custom_call" | custom-call | flops 452984832 | bytes 3047424 | tf_op jit(solution)/shard_map/own_sums/pallas_call | solution.py:475
  23.9 0.8 %collective-permute-done.3.near = bf16[576,128]{1,0:T(8,128)(2,1)S(1)} collective-permute-done((bf16[576,128]{1,0:T(8,128)(2,1)S(1)}, bf16[576,128]{1,0:T(8,128)(2,1)S(1)}, u32[]{:S(2)}, u32[]{:S(2)}) %collective-permute-start.3) | collective-permute-done | bytes 147488 | tf_op jit(solution)/shard_map/ppermute | solution.py:459
  24.7 5.0 %tick_two.1 = (bf16[256,256]{1,0:T(8,128)(2,1)}, bf16[256,256]{1,0:T(8,128)(2,1)}, bf16[256,256]{1,0:T(8,128)(2,1)}, bf16[8,144,128]{2,1,0:T(8,128)(2,1)S(1)}, b...) custom-call(bf16[256,256]{1,0:T(8,128)(2,1)S(1)} %get-tuple-element., ...), custom_call_target="tpu_custom_call" | custom-call | flops 2038431744 | bytes 6291456 | tf_op jit(solution)/shard_map/tick_two/pallas_call | solution.py:475
  29.7 5.9 %collective-permute-start.5 = (bf16[8,144,128]{2,1,0:T(8,128)(2,1)S(1)}, bf16[8,144,128]{2,1,0:T(8,128)(2,1)S(1)}, u32[]{:S(2)}, u32[]{:S(2)}) collective-permute-start(bf16[8,144,128]{2,1,0:T(8,128)(2,1)S(1)} %get-tuple-element.58), channel_id=1, source_target_pairs={{0,1},{1,0},{2,3},{3,2},{4,5},{5,4},{6,7},{7,6},{8,9},{9,8},{10,11... | collective-permute-start | bytes 884744 | tf_op jit(solution)/shard_map/ppermute | solution.py:422
  35.6 1.1 %collective-permute-start.8 = (bf16[8,144,128]{2,1,0:T(8,128)(2,1)S(1)}, bf16[8,144,128]{2,1,0:T(8,128)(2,1)S(1)}, u32[]{:S(2)}, u32[]{:S(2)}) collective-permute-start(bf16[8,144,128]{2,1,0:T(8,128)(2,1)S(1)} %get-tuple-element.60), channel_id=1, source_target_pairs={{0,2},{1,3},{2,0},{3,1},{4,6},{5,7},{6,4},{7,5},{8,10},{9,11},{10,... | collective-permute-start | bytes 884744 | tf_op jit(solution)/shard_map/ppermute | solution.py:422
  36.7 1.6 %collective-permute-start.11 = (bf16[8,144,128]{2,1,0:T(8,128)(2,1)S(1)}, bf16[8,144,128]{2,1,0:T(8,128)(2,1)S(1)}, u32[]{:S(2)}, u32[]{:S(2)}) collective-permute-start(bf16[8,144,128]{2,1,0:T(8,128)(2,1)S(1)} %get-tuple-element.62), channel_id=1, source_target_pairs={{0,4},{1,5},{2,6},{3,7},{4,0},{5,1},{6,2},{7,3},{8,12},{9,13},{10,... | collective-permute-start | bytes 884744 | tf_op jit(solution)/shard_map/ppermute | solution.py:422
  38.3 3.8 %collective-permute-done.5 = bf16[8,144,128]{2,1,0:T(8,128)(2,1)S(1)} collective-permute-done((bf16[8,144,128]{2,1,0:T(8,128)(2,1)S(1)}, bf16[8,144,128]{2,1,0:T(8,128)(2,1)S(1)}, u32[]{:S(2)}, u32[]{:S(2)}) %collective-permute-start.5) | collective-permute-done | bytes 294944 | tf_op jit(solution)/shard_map/ppermute | solution.py:422
  42.2 1.4 %collective-permute-start.6 = (bf16[4,144,128]{2,1,0:T(8,128)(2,1)S(1)}, bf16[4,144,128]{2,1,0:T(8,128)(2,1)S(1)}, u32[]{:S(2)}, u32[]{:S(2)}) collective-permute-start(bf16[4,144,128]{2,1,0:T(8,128)(2,1)S(1)} %dynamic-slice_bitcast_fusion.2), channel_id=1, source_target_pairs={{0,2},{1,3},{2,0},{3,1},{4,6},{5,7},{6,4},{7,5},{8,10},{9,11},{10,... | collective-permute-start | bytes 442376 | tf_op jit(solution)/shard_map/ppermute | solution.py:422
  43.7 1.6 %collective-permute-start.9 = (bf16[4,144,128]{2,1,0:T(8,128)(2,1)S(1)}, bf16[4,144,128]{2,1,0:T(8,128)(2,1)S(1)}, u32[]{:S(2)}, u32[]{:S(2)}) collective-permute-start(bf16[4,144,128]{2,1,0:T(8,128)(2,1)S(1)} %dynamic-slice_bitcast_fusion.1), channel_id=1, source_target_pairs={{0,4},{1,5},{2,6},{3,7},{4,0},{5,1},{6,2},{7,3},{8,12},{9,13},{10,... | collective-permute-start | bytes 442376 | tf_op jit(solution)/shard_map/ppermute | solution.py:422
  45.5 1.6 %collective-permute-start.12 = (bf16[4,144,128]{2,1,0:T(8,128)(2,1)S(1)}, bf16[4,144,128]{2,1,0:T(8,128)(2,1)S(1)}, u32[]{:S(2)}, u32[]{:S(2)}) collective-permute-start(bf16[4,144,128]{2,1,0:T(8,128)(2,1)S(1)} %dynamic-slice_bitcast_fusion), channel_id=1, source_target_pairs={{0,1},{1,0},{2,3},{3,2},{4,5},{5,4},{6,7},{7,6},{8,9},{9,8},{10,11... | collective-permute-start | bytes 442376 | tf_op jit(solution)/shard_map/ppermute | solution.py:422
  47.1 0.3 collective-permute-done.6
  47.5 2.3 %collective-permute-start.7 = (bf16[2,144,128]{2,1,0:T(8,128)(2,1)S(1)}, bf16[2,144,128]{2,1,0:T(8,128)(2,1)S(1)}, u32[]{:S(2)}, u32[]{:S(2)}) collective-permute-start(bf16[2,144,128]{2,1,0:T(8,128)(2,1)S(1)} %dynamic-slice_bitcast_fusion.5), channel_id=1, source_target_pairs={{0,4},{1,5},{2,6},{3,7},{4,0},{5,1},{6,2},{7,3},{8,12},{9,13},{10,... | collective-permute-start | bytes 221192 | tf_op jit(solution)/shard_map/ppermute | solution.py:422
  49.9 1.5 %collective-permute-start.10 = (bf16[2,144,128]{2,1,0:T(8,128)(2,1)S(1)}, bf16[2,144,128]{2,1,0:T(8,128)(2,1)S(1)}, u32[]{:S(2)}, u32[]{:S(2)}) collective-permute-start(bf16[2,144,128]{2,1,0:T(8,128)(2,1)S(1)} %dynamic-slice_bitcast_fusion.4), channel_id=1, source_target_pairs={{0,1},{1,0},{2,3},{3,2},{4,5},{5,4},{6,7},{7,6},{8,9},{9,8},{10,11... | collective-permute-start | bytes 221192 | tf_op jit(solution)/shard_map/ppermute | solution.py:422
  51.6 1.2 %collective-permute-start.13 = (bf16[2,144,128]{2,1,0:T(8,128)(2,1)S(1)}, bf16[2,144,128]{2,1,0:T(8,128)(2,1)S(1)}, u32[]{:S(2)}, u32[]{:S(2)}) collective-permute-start(bf16[2,144,128]{2,1,0:T(8,128)(2,1)S(1)} %dynamic-slice_bitcast_fusion.3), channel_id=1, source_target_pairs={{0,2},{1,3},{2,0},{3,1},{4,6},{5,7},{6,4},{7,5},{8,10},{9,11},{10,... | collective-permute-start | bytes 221192 | tf_op jit(solution)/shard_map/ppermute | solution.py:422
  52.8 1.5 %collective-permute-done.10 = bf16[2,144,128]{2,1,0:T(8,128)(2,1)S(1)} collective-permute-done((bf16[2,144,128]{2,1,0:T(8,128)(2,1)S(1)}, bf16[2,144,128]{2,1,0:T(8,128)(2,1)S(1)}, u32[]{:S(2)}, u32[]{:S(2)}) %collective-permute-start.10) | collective-permute-done | bytes 73760 | tf_op jit(solution)/shard_map/ppermute | solution.py:422
  54.4 1.6 %collective-permute-done.13 = bf16[2,144,128]{2,1,0:T(8,128)(2,1)S(1)} collective-permute-done((bf16[2,144,128]{2,1,0:T(8,128)(2,1)S(1)}, bf16[2,144,128]{2,1,0:T(8,128)(2,1)S(1)}, u32[]{:S(2)}, u32[]{:S(2)}) %collective-permute-start.13) | collective-permute-done | bytes 73760 | tf_op jit(solution)/shard_map/ppermute | solution.py:422
  56.1 2.5 %collective-permute-start.14 = (bf16[432,128]{1,0:T(8,128)(2,1)S(1)}, bf16[432,128]{1,0:T(8,128)(2,1)S(1)}, u32[]{:S(2)}, u32[]{:S(2)}) collective-permute-start(bf16[432,128]{1,0:T(8,128)(2,1)S(1)} %pad_maximum_fusion), channel_id=1, source_target_pairs={{0,8},{1,9},{2,10},{3,11},{4,12},{5,13},{6,14},{7,15},{8,0},{9,1},... | collective-permute-start | bytes 331784 | tf_op jit(solution)/shard_map/ppermute | solution.py:422
  58.6 4.4 %collective-permute-done.14 = bf16[432,128]{1,0:T(8,128)(2,1)S(1)} collective-permute-done((bf16[432,128]{1,0:T(8,128)(2,1)S(1)}, bf16[432,128]{1,0:T(8,128)(2,1)S(1)}, u32[]{:S(2)}, u32[]{:S(2)}) %collective-permute-start.14) | collective-permute-done | bytes 110624 | tf_op jit(solution)/shard_map/ppermute | solution.py:422
  63.0 0.7 %slice_bitcast_fusion = (f32[1,216,128]{2,1,0:T(8,128)}, f32[1,216,128]{2,1,0:T(8,128)}) fusion(f32[432,128]{1,0:T(8,128)S(1)} %convert_add_fusion.3), kind=kLoop, calls=%fused_computation.19 | loop fusion | bytes 442368 | tf_op jit(solution)/shard_map/broadcast_in_dim | solution.py:566
  (43 shorter events, 1.0 us)
Async XLA Ops:
  2.6 9.3 %collective-permute-start = (bf16[576,128]{1,0:T(8,128)(2,1)}, bf16[576,128]{1,0:T(8,128)(2,1)S(1)}, u32[]{:S(2)}, u32[]{:S(2)}) collective-permute-start(bf16[576,128]{1,0:T(8,128)(2,1)} %get-tuple-element.38), channel_id=1, source_target_pairs={{0,1},{1,0},{2,3},{3,2},{4,5},{5,4},{6,7},{7,6},{8,9},{9,8},{10,11... | collective-permute-start | bytes 442376 | tf_op jit(solution)/shard_map/ppermute | solution.py:459
  5.6 6.3 %collective-permute-start.1 = (bf16[576,128]{1,0:T(8,128)(2,1)}, bf16[576,128]{1,0:T(8,128)(2,1)S(1)}, u32[]{:S(2)}, u32[]{:S(2)}) collective-permute-start(bf16[576,128]{1,0:T(8,128)(2,1)} %get-tuple-element.39), channel_id=1, source_target_pairs={{1,2},{2,1},{3,4},{4,3},{5,6},{6,5},{7,8},{8,7},{9,10},{10,9},{11,... | collective-permute-start | bytes 442376 | tf_op jit(solution)/shard_map/ppermute | solution.py:458
  6.2 1.2 %copy-start = (bf16[1,27,128,128]{3,2,1,0:T(8,128)(2,1)S(1)}, bf16[1,27,128,128]{3,2,1,0:T(8,128)(2,1)}, u32[]{:S(2)}) copy-start(bf16[1,27,128,128]{3,2,1,0:T(8,128)(2,1)} %param.12) | copy-start | bytes 2654212
  7.4 1.2 %copy-start.2 = (bf16[1,27,128,128]{3,2,1,0:T(8,128)(2,1)S(1)}, bf16[1,27,128,128]{3,2,1,0:T(8,128)(2,1)}, u32[]{:S(2)}) copy-start(bf16[1,27,128,128]{3,2,1,0:T(8,128)(2,1)} %param.13) | copy-start | bytes 2654212
  8.6 1.0 %copy-start.5 = (bf16[3,256,256]{2,1,0:T(8,128)(2,1)S(1)}, bf16[3,256,256]{2,1,0:T(8,128)(2,1)}, u32[]{:S(2)}) copy-start(bf16[3,256,256]{2,1,0:T(8,128)(2,1)} %get-tuple-element.34.fields) | copy-start | bytes 1179652
  11.9 4.2 %copy-start.6 = (bf16[4,8,8,256]{3,2,1,0:T(8,128)(2,1)S(1)}, bf16[4,8,8,256]{3,2,1,0:T(8,128)(2,1)}, u32[]{:S(2)}) copy-start(bf16[4,8,8,256]{3,2,1,0:T(8,128)(2,1)} %param.10) | copy-start | bytes 393220
  11.9 4.2 %copy-start.7 = (bf16[4,8,8,256]{3,2,1,0:T(8,128)(2,1)S(1)}, bf16[4,8,8,256]{3,2,1,0:T(8,128)(2,1)}, u32[]{:S(2)}) copy-start(bf16[4,8,8,256]{3,2,1,0:T(8,128)(2,1)} %param.11) | copy-start | bytes 393220
  11.9 9.5 %copy-start.4 = (bf16[1,4,8,8,256]{4,3,2,1,0:T(8,128)(2,1)S(1)}, bf16[1,4,8,8,256]{4,3,2,1,0:T(8,128)(2,1)}, u32[]{:S(2)}) copy-start(bf16[1,4,8,8,256]{4,3,2,1,0:T(8,128)(2,1)} %param.9) | copy-start | bytes 393220
  14.5 7.7 %copy-start.1 = (bf16[1,27,128,128]{3,2,1,0:T(8,128)(2,1)S(1)}, bf16[1,27,128,128]{3,2,1,0:T(8,128)(2,1)}, u32[]{:S(2)}) copy-start(bf16[1,27,128,128]{3,2,1,0:T(8,128)(2,1)} %param.12) | copy-start | bytes 2654212
  14.5 7.7 %copy-start.3 = (bf16[1,27,128,128]{3,2,1,0:T(8,128)(2,1)S(1)}, bf16[1,27,128,128]{3,2,1,0:T(8,128)(2,1)}, u32[]{:S(2)}) copy-start(bf16[1,27,128,128]{3,2,1,0:T(8,128)(2,1)} %param.13) | copy-start | bytes 2654212
  14.5 1.6 %collective-permute-start.2 = (bf16[2,256,256]{2,1,0:T(8,128)(2,1)S(1)}, bf16[2,256,256]{2,1,0:T(8,128)(2,1)S(1)}, u32[]{:S(2)}, u32[]{:S(2)}) collective-permute-start(bf16[2,256,256]{2,1,0:T(8,128)(2,1)S(1)} %get-tuple-element.45), channel_id=1, source_target_pairs={{0,16},{16,0},{1,17},{17,1},{2,18},{18,2},{3,19},{19,3},{4,20},{20... | collective-permute-start | bytes 786440 | tf_op jit(solution)/shard_map/ppermute | solution.py:523
  16.2 8.4 %collective-permute-start.3 = (bf16[576,128]{1,0:T(8,128)(2,1)S(1)}, bf16[576,128]{1,0:T(8,128)(2,1)S(1)}, u32[]{:S(2)}, u32[]{:S(2)}) collective-permute-start(bf16[576,128]{1,0:T(8,128)(2,1)S(1)} %get-tuple-element.49), channel_id=1, source_target_pairs={{0,1},{1,0},{2,3},{3,2},{4,5},{5,4},{6,7},{7,6},{8,9},{9,8},{10,11... | collective-permute-start | bytes 442376 | tf_op jit(solution)/shard_map/ppermute | solution.py:459
  20.5 4.2 %collective-permute-start.4 = (bf16[576,128]{1,0:T(8,128)(2,1)S(1)}, bf16[576,128]{1,0:T(8,128)(2,1)S(1)}, u32[]{:S(2)}, u32[]{:S(2)}) collective-permute-start(bf16[576,128]{1,0:T(8,128)(2,1)S(1)} %get-tuple-element.50), channel_id=1, source_target_pairs={{1,2},{2,1},{3,4},{4,3},{5,6},{6,5},{7,8},{8,7},{9,10},{10,9},{11,... | collective-permute-start | bytes 442376 | tf_op jit(solution)/shard_map/ppermute | solution.py:458
  29.7 12.4 %collective-permute-start.5 = (bf16[8,144,128]{2,1,0:T(8,128)(2,1)S(1)}, bf16[8,144,128]{2,1,0:T(8,128)(2,1)S(1)}, u32[]{:S(2)}, u32[]{:S(2)}) collective-permute-start(bf16[8,144,128]{2,1,0:T(8,128)(2,1)S(1)} %get-tuple-element.58), channel_id=1, source_target_pairs={{0,1},{1,0},{2,3},{3,2},{4,5},{5,4},{6,7},{7,6},{8,9},{9,8},{10,11... | collective-permute-start | bytes 884744 | tf_op jit(solution)/shard_map/ppermute | solution.py:422
  35.6 8.0 %collective-permute-start.8 = (bf16[8,144,128]{2,1,0:T(8,128)(2,1)S(1)}, bf16[8,144,128]{2,1,0:T(8,128)(2,1)S(1)}, u32[]{:S(2)}, u32[]{:S(2)}) collective-permute-start(bf16[8,144,128]{2,1,0:T(8,128)(2,1)S(1)} %get-tuple-element.60), channel_id=1, source_target_pairs={{0,2},{1,3},{2,0},{3,1},{4,6},{5,7},{6,4},{7,5},{8,10},{9,11},{10,... | collective-permute-start | bytes 884744 | tf_op jit(solution)/shard_map/ppermute | solution.py:422
  36.7 8.7 %collective-permute-start.11 = (bf16[8,144,128]{2,1,0:T(8,128)(2,1)S(1)}, bf16[8,144,128]{2,1,0:T(8,128)(2,1)S(1)}, u32[]{:S(2)}, u32[]{:S(2)}) collective-permute-start(bf16[8,144,128]{2,1,0:T(8,128)(2,1)S(1)} %get-tuple-element.62), channel_id=1, source_target_pairs={{0,4},{1,5},{2,6},{3,7},{4,0},{5,1},{6,2},{7,3},{8,12},{9,13},{10,... | collective-permute-start | bytes 884744 | tf_op jit(solution)/shard_map/ppermute | solution.py:422
  42.2 5.2 %collective-permute-start.6 = (bf16[4,144,128]{2,1,0:T(8,128)(2,1)S(1)}, bf16[4,144,128]{2,1,0:T(8,128)(2,1)S(1)}, u32[]{:S(2)}, u32[]{:S(2)}) collective-permute-start(bf16[4,144,128]{2,1,0:T(8,128)(2,1)S(1)} %dynamic-slice_bitcast_fusion.2), channel_id=1, source_target_pairs={{0,2},{1,3},{2,0},{3,1},{4,6},{5,7},{6,4},{7,5},{8,10},{9,11},{10,... | collective-permute-start | bytes 442376 | tf_op jit(solution)/shard_map/ppermute | solution.py:422
  43.7 6.1 %collective-permute-start.9 = (bf16[4,144,128]{2,1,0:T(8,128)(2,1)S(1)}, bf16[4,144,128]{2,1,0:T(8,128)(2,1)S(1)}, u32[]{:S(2)}, u32[]{:S(2)}) collective-permute-start(bf16[4,144,128]{2,1,0:T(8,128)(2,1)S(1)} %dynamic-slice_bitcast_fusion.1), channel_id=1, source_target_pairs={{0,4},{1,5},{2,6},{3,7},{4,0},{5,1},{6,2},{7,3},{8,12},{9,13},{10,... | collective-permute-start | bytes 442376 | tf_op jit(solution)/shard_map/ppermute | solution.py:422
  45.5 6.0 %collective-permute-start.12 = (bf16[4,144,128]{2,1,0:T(8,128)(2,1)S(1)}, bf16[4,144,128]{2,1,0:T(8,128)(2,1)S(1)}, u32[]{:S(2)}, u32[]{:S(2)}) collective-permute-start(bf16[4,144,128]{2,1,0:T(8,128)(2,1)S(1)} %dynamic-slice_bitcast_fusion), channel_id=1, source_target_pairs={{0,1},{1,0},{2,3},{3,2},{4,5},{5,4},{6,7},{7,6},{8,9},{9,8},{10,11... | collective-permute-start | bytes 442376 | tf_op jit(solution)/shard_map/ppermute | solution.py:422
  47.5 5.3 %collective-permute-start.7 = (bf16[2,144,128]{2,1,0:T(8,128)(2,1)S(1)}, bf16[2,144,128]{2,1,0:T(8,128)(2,1)S(1)}, u32[]{:S(2)}, u32[]{:S(2)}) collective-permute-start(bf16[2,144,128]{2,1,0:T(8,128)(2,1)S(1)} %dynamic-slice_bitcast_fusion.5), channel_id=1, source_target_pairs={{0,4},{1,5},{2,6},{3,7},{4,0},{5,1},{6,2},{7,3},{8,12},{9,13},{10,... | collective-permute-start | bytes 221192 | tf_op jit(solution)/shard_map/ppermute | solution.py:422
  49.9 4.4 %collective-permute-start.10 = (bf16[2,144,128]{2,1,0:T(8,128)(2,1)S(1)}, bf16[2,144,128]{2,1,0:T(8,128)(2,1)S(1)}, u32[]{:S(2)}, u32[]{:S(2)}) collective-permute-start(bf16[2,144,128]{2,1,0:T(8,128)(2,1)S(1)} %dynamic-slice_bitcast_fusion.4), channel_id=1, source_target_pairs={{0,1},{1,0},{2,3},{3,2},{4,5},{5,4},{6,7},{7,6},{8,9},{9,8},{10,11... | collective-permute-start | bytes 221192 | tf_op jit(solution)/shard_map/ppermute | solution.py:422
  51.6 4.4 %collective-permute-start.13 = (bf16[2,144,128]{2,1,0:T(8,128)(2,1)S(1)}, bf16[2,144,128]{2,1,0:T(8,128)(2,1)S(1)}, u32[]{:S(2)}, u32[]{:S(2)}) collective-permute-start(bf16[2,144,128]{2,1,0:T(8,128)(2,1)S(1)} %dynamic-slice_bitcast_fusion.3), channel_id=1, source_target_pairs={{0,2},{1,3},{2,0},{3,1},{4,6},{5,7},{6,4},{7,5},{8,10},{9,11},{10,... | collective-permute-start | bytes 221192 | tf_op jit(solution)/shard_map/ppermute | solution.py:422
  56.1 6.9 %collective-permute-start.14 = (bf16[432,128]{1,0:T(8,128)(2,1)S(1)}, bf16[432,128]{1,0:T(8,128)(2,1)S(1)}, u32[]{:S(2)}, u32[]{:S(2)}) collective-permute-start(bf16[432,128]{1,0:T(8,128)(2,1)S(1)} %pad_maximum_fusion), channel_id=1, source_target_pairs={{0,8},{1,9},{2,10},{3,11},{4,12},{5,13},{6,14},{7,15},{8,0},{9,1},... | collective-permute-start | bytes 331784 | tf_op jit(solution)/shard_map/ppermute | solution.py:422
